TPU v7x, 32 devices: a whole 2x2x4 slice. The times are simulated.
32 devices in a mesh: dp: 8 (over z, x), img: 4 (over y, core).
Axes of the slice: x: 2, y: 2, z: 4, core: 2. Of those that a mesh axis runs over, the one named last changes fastest.
Arguments:
- tokens: bfloat16 [4, 448, 56, 512], P('img', 'dp'), may hold values from -6 to 6
- regional: bfloat16 [4, 512, 512], P('img', 'dp'), may hold values from -6 to 6
- pad_mask: int32 [4, 448, 56], P('img', 'dp'), may hold values from 0 to 1, as said below
- keep_mask: int32 [4, 8], P('img'), may hold values 0 or 1
- window_slot: int32 [4, 512], P('img'), may hold values from 0 to 511, as said below
- ln1_gain: float32 [512], replicated, may hold values from 0.5 to 1.5
- ln1_bias: float32 [512], replicated, may hold values from -1.75 to 1.75
- w_qkv: bfloat16 [512, 1536], replicated, may hold values from -0.25 to 0.25
- bias_q: float32 [512], replicated, may hold values from -1.75 to 1.75
- bias_v: float32 [512], replicated, may hold values from -1.75 to 1.75
- w_out: bfloat16 [512, 512], replicated, may hold values from -1 to 1
- bias_out: float32 [512], replicated, may hold values from -1.75 to 1.75
- ln2_gain: float32 [512], replicated, may hold values from 0.5 to 1.5
- ln2_bias: float32 [512], replicated, may hold values from -1.75 to 1.75
- w_fc1: bfloat16 [512, 2048], replicated, may hold values from -0.25 to 0.25
- bias_fc1: float32 [2048], replicated, may hold values from -3 to 3
- w_fc2: bfloat16 [2048, 512], replicated, may hold values from -0.125 to 0.125
- bias_fc2: float32 [512], replicated, may hold values from -1.75 to 1.75
- cot_local: bfloat16 [4, 512, 49, 512], P('img', 'dp'), may hold values from -6 to 6
- cot_regional: bfloat16 [4, 512, 512], P('img', 'dp'), may hold values from -6 to 6
Outputs:
- out_local: bfloat16 [4, 512, 49, 512], P('img', 'dp')
- out_regional: bfloat16 [4, 512, 512], P('img', 'dp')
- grad_tokens: bfloat16 [4, 448, 56, 512], P('img', 'dp')
- grad_regional: bfloat16 [4, 512, 512], P('img', 'dp')
- grad_ln1_gain: float32 [512], replicated
- grad_ln1_bias: float32 [512], replicated
- grad_w_qkv: float32 [512, 1536], replicated
- grad_bias_q: float32 [512], replicated
- grad_bias_v: float32 [512], replicated
- grad_w_out: float32 [512, 512], replicated
- grad_bias_out: float32 [512], replicated
- grad_ln2_gain: float32 [512], replicated
- grad_ln2_bias: float32 [512], replicated
- grad_w_fc1: float32 [512, 2048], replicated
- grad_bias_fc1: float32 [2048], replicated
- grad_w_fc2: float32 [2048, 512], replicated
- grad_bias_fc2: float32 [512], replicated
Inputs may be any that keep to these rules, and one draw needn't show every extreme that they name: `pad_mask`: image i of a group holds rows i * 56 to (i + 1) * 56 - 1; its live patches form a top-left rectangle of more than 7 rows and more than 7 columns. Each group's row is a permutation. Window w lies on device w // 64 of dp and goes to slot window_slot[w] on device window_slot[w] // 64; every device sends exactly 8 windows to each device it sends to, never more.
All inputs are finite; a program needn't handle non-finite values. No bound on the sum of `keep_mask` on one device may be relied on, other than what follows from the above.
Results may differ from a plain program's by a relative error of at most 0.02.
Values may be sent and summed in bfloat16 or wider, within the bound.
No kernel may reach another device: no remote copies, remote signals or barrier semaphores. Data moves between devices by JAX's collectives and lax.ppermute only.
A program may use at most 320 MiB of HBM per device.

v0:
```python
import jax
import jax.numpy as jnp
from jax import lax
from jax.sharding import PartitionSpec as P

HEADS = 16
HDIM = 32
WIN_SIDE = 7
REG_SIDE = 8
REGIONS = 64


norm_eps = 1e-05
survive = 0.9


def layer_norm(values, scale_gain, shift_bias):
    centered = values - jnp.mean(values, axis=-1, keepdims=True)
    spread = jnp.mean(centered * centered, axis=-1, keepdims=True)
    return centered * lax.rsqrt(spread + norm_eps) * scale_gain + shift_bias


def gelu_exact(values):
    return jax.nn.gelu(values, approximate=False)


def split_heads(values):
    return values.reshape(values.shape[:-1] + (HEADS, HDIM))


def merge_heads(values):
    return values.reshape(values.shape[:-2] + (HEADS * HDIM,))


def linear(values, matrix):
    return jnp.einsum("...i,ij->...j", values, matrix, preferred_element_type=jnp.float32)


def linear_back(grads, matrix):
    return jnp.einsum("...j,ij->...i", grads, matrix, preferred_element_type=jnp.float32)


def outer_sum(values, grads):
    flat_values = values.reshape(-1, values.shape[-1])
    flat_grads = grads.reshape(-1, grads.shape[-1])
    return jnp.einsum("ti,tj->ij", flat_values, flat_grads, preferred_element_type=jnp.float32)


def row_total(grads):
    return jnp.sum(grads.astype(jnp.float32).reshape(-1, grads.shape[-1]), axis=0)


def project_heads(normed, w_qkv, bias_q, bias_v):
    combined = linear(normed, w_qkv)
    model_width = bias_q.shape[0]
    queries = (combined[..., :model_width] + bias_q).astype(jnp.bfloat16)
    key_rows = combined[..., model_width : 2 * model_width].astype(jnp.bfloat16)
    values = (combined[..., 2 * model_width :] + bias_v).astype(jnp.bfloat16)
    return (queries, key_rows, values)


def masked_scores(queries, key_heads, allowed):
    raw_scores = jnp.einsum(
        "bqhe,bkhe->bhqk", queries, key_heads, preferred_element_type=jnp.float32
    )
    return jnp.where(allowed, raw_scores * HDIM ** (-0.5), -1e30)


def attend_forward(queries, key_heads, values, allowed):
    scores = masked_scores(queries, key_heads, allowed)
    highest_score = jnp.max(scores, axis=-1, keepdims=True)
    weighted = jnp.exp(scores - highest_score)
    normal_sum = jnp.sum(weighted, axis=-1, keepdims=True)
    attn_probs = (weighted / normal_sum).astype(jnp.bfloat16)
    mixed_heads = jnp.einsum(
        "bhqk,bkhe->bqhe", attn_probs, values, preferred_element_type=jnp.float32
    )
    return (mixed_heads, highest_score + jnp.log(normal_sum))


def attend_backward(queries, key_heads, values, allowed, log_total, grad_mixed):
    attn_probs = jnp.exp(masked_scores(queries, key_heads, allowed) - log_total)
    grad_values = jnp.einsum(
        "bhqk,bqhe->bkhe",
        attn_probs.astype(jnp.bfloat16),
        grad_mixed,
        preferred_element_type=jnp.float32,
    )
    grad_probs = jnp.einsum(
        "bqhe,bkhe->bhqk", grad_mixed, values, preferred_element_type=jnp.float32
    )
    row_inner = jnp.sum(attn_probs * grad_probs, axis=-1, keepdims=True)
    grad_scores = (attn_probs * (grad_probs - row_inner)).astype(jnp.bfloat16)
    factor = HDIM ** (-0.5)
    grad_queries = (
        jnp.einsum("bhqk,bkhe->bqhe", grad_scores, key_heads, preferred_element_type=jnp.float32)
        * factor
    )
    grad_keys = (
        jnp.einsum("bhqk,bqhe->bkhe", grad_scores, queries, preferred_element_type=jnp.float32)
        * factor
    )
    return (grad_queries, grad_keys, grad_values)


def band_to_windows(band_values, win_count):
    trailing = band_values.shape[2:]
    blocks = band_values.reshape(
        (band_values.shape[0] // WIN_SIDE, WIN_SIDE, REG_SIDE, WIN_SIDE) + trailing
    )
    return jnp.swapaxes(blocks, 1, 2).reshape((win_count, WIN_SIDE * WIN_SIDE) + trailing)


def windows_to_band(windows, band_rows):
    trailing = windows.shape[2:]
    blocks = windows.reshape((band_rows // WIN_SIDE, REG_SIDE, WIN_SIDE, WIN_SIDE) + trailing)
    return jnp.swapaxes(blocks, 1, 2).reshape((band_rows, REG_SIDE * WIN_SIDE) + trailing)


def pick_rows(selector, values):
    return jnp.einsum("rc,cf->rf", selector, values, preferred_element_type=jnp.float32)


def keep_for(image_ids, keep_row):
    image_match = image_ids[:, None] == jnp.arange(keep_row.shape[0])[None, :]
    return (
        jnp.sum(jnp.where(image_match, keep_row[None, :], 0), axis=1).astype(jnp.float32) / survive
    )


def shards(
    tokens,
    regional,
    pad_mask,
    keep_mask,
    window_slot,
    ln1_gain,
    ln1_bias,
    w_qkv,
    bias_q,
    bias_v,
    w_out,
    bias_out,
    ln2_gain,
    ln2_bias,
    w_fc1,
    bias_fc1,
    w_fc2,
    bias_fc2,
    cot_local,
    cot_regional,
):
    devices = lax.axis_size("dp")
    own_rank = lax.axis_index("dp")
    win_count = regional.shape[1]
    all_windows = window_slot.shape[1]
    capacity = max(1, win_count // devices)
    buffer_rows = devices * capacity
    model_width = regional.shape[2]
    window_len = cot_local.shape[2]
    band_rows = tokens.shape[1]
    images_dev = win_count // REGIONS
    slot_of = window_slot[0]
    target = slot_of // win_count
    target_grid = target.reshape(devices, win_count)
    earlier = jnp.arange(win_count)[None, :] < jnp.arange(win_count)[:, None]
    send_rank = jnp.sum(
        (target_grid[:, :, None] == target_grid[:, None, :]) & earlier[None], axis=2
    ).reshape(all_windows)
    window_ids = jnp.arange(all_windows)
    send_row = target * capacity + send_rank
    recv_row = window_ids // win_count * capacity + send_rank
    own_send = lax.dynamic_slice_in_dim(send_row, own_rank * win_count, win_count)
    send_pick = (jnp.arange(buffer_rows)[:, None] == own_send[None, :]).astype(jnp.bfloat16)
    slot_hit = slot_of[None, :] == (own_rank * win_count + jnp.arange(win_count))[:, None]
    window_here = jnp.sum(jnp.where(slot_hit, window_ids[None, :], 0), axis=1)
    recv_here = jnp.sum(jnp.where(slot_hit, recv_row[None, :], 0), axis=1)
    recv_pick = (recv_here[:, None] == jnp.arange(buffer_rows)[None, :]).astype(jnp.bfloat16)
    image_here = window_here // REGIONS
    keep_here = keep_for(image_here, keep_mask[0])
    band_image = (own_rank * win_count + jnp.arange(win_count)) // REGIONS
    keep_band = keep_for(band_image, keep_mask[0])
    windows = band_to_windows(tokens[0], win_count).reshape(win_count, window_len * model_width)
    live_local = band_to_windows(pad_mask[0], win_count)
    region_shape = (images_dev, REGIONS, HEADS, HDIM)
    region_band = regional[0].astype(jnp.float32)
    normed_region = layer_norm(region_band, ln1_gain, ln1_bias).astype(jnp.bfloat16)
    queries_r, keys_r, values_r = project_heads(normed_region, w_qkv, bias_q, bias_v)
    query_heads_r = queries_r.reshape(region_shape)
    key_heads_r = keys_r.reshape(region_shape)
    value_heads_r = values_r.reshape(region_shape)
    region_allowed = (live_local[:, 0] != 0).reshape(images_dev, 1, 1, REGIONS)
    mixed_heads_r, total_r = attend_forward(
        query_heads_r, key_heads_r, value_heads_r, region_allowed
    )
    mixed_r = mixed_heads_r.reshape(win_count, model_width).astype(jnp.bfloat16)
    region_mid_band = (
        region_band + keep_band[:, None] * (linear(mixed_r, w_out) + bias_out)
    ).astype(jnp.bfloat16)
    send_region = pick_rows(send_pick, region_mid_band).astype(jnp.bfloat16)
    send_tokens = pick_rows(send_pick, windows).astype(jnp.bfloat16)
    send_live = pick_rows(send_pick, live_local.astype(jnp.bfloat16)).astype(jnp.bfloat16)
    got_tokens, got_region, got_live = (
        lax.all_to_all(send_tokens, "dp", split_axis=0, concat_axis=0, tiled=True),
        lax.all_to_all(send_region, "dp", split_axis=0, concat_axis=0, tiled=True),
        lax.all_to_all(send_live, "dp", split_axis=0, concat_axis=0, tiled=True),
    )
    here_tokens = pick_rows(recv_pick, got_tokens).reshape(win_count, window_len, model_width)
    region_rows = pick_rows(recv_pick, got_region)
    here_live = pick_rows(recv_pick, got_live) > 0.5
    joined = jnp.concatenate([region_rows[:, None, :], here_tokens], axis=1)
    normed_local = layer_norm(joined, ln1_gain, ln1_bias).astype(jnp.bfloat16)
    queries_l, keys_l, values_l = project_heads(normed_local, w_qkv, bias_q, bias_v)
    local_allowed = jnp.concatenate([jnp.ones((win_count, 1), bool), here_live], axis=1)[
        :, None, None, :
    ]
    query_heads_l = split_heads(queries_l)
    key_heads_l = split_heads(keys_l)
    value_heads_l = split_heads(values_l)
    mixed_l, total_l = attend_forward(query_heads_l, key_heads_l, value_heads_l, local_allowed)
    mixed_l = merge_heads(mixed_l).astype(jnp.bfloat16)
    keep_rows = keep_here[:, None, None]
    after_attention = joined + keep_rows * (linear(mixed_l, w_out) + bias_out)
    normed_mlp = layer_norm(after_attention, ln2_gain, ln2_bias).astype(jnp.bfloat16)
    pre_act = linear(normed_mlp, w_fc1) + bias_fc1
    hidden = gelu_exact(pre_act).astype(jnp.bfloat16)
    result = after_attention + keep_rows * (linear(hidden, w_fc2) + bias_fc2)
    out_local = result[:, 1:].astype(jnp.bfloat16)
    out_regional = result[:, 0].astype(jnp.bfloat16)
    grad_result = jnp.concatenate(
        [cot_regional[0].astype(jnp.float32)[:, None, :], cot_local[0].astype(jnp.float32)], axis=1
    )
    grad_mlp = (keep_rows * grad_result).astype(jnp.bfloat16)
    grad_w_fc2 = outer_sum(hidden, grad_mlp)
    grad_bias_fc2 = row_total(grad_mlp)
    unused, gelu_pull = jax.vjp(gelu_exact, pre_act)
    grad_pre = gelu_pull(linear_back(grad_mlp, w_fc2))[0].astype(jnp.bfloat16)
    grad_w_fc1 = outer_sum(normed_mlp, grad_pre)
    grad_bias_fc1 = row_total(grad_pre)
    unused, norm_pull = jax.vjp(layer_norm, after_attention, ln2_gain, ln2_bias)
    grad_norm_in, grad_ln2_gain, grad_ln2_bias = norm_pull(linear_back(grad_pre, w_fc1))
    grad_after = grad_result + grad_norm_in
    grad_branch_l = (keep_rows * grad_after).astype(jnp.bfloat16)
    grad_w_out = outer_sum(mixed_l, grad_branch_l)
    grad_bias_out = row_total(grad_branch_l)
    grad_mixed_l = split_heads(linear_back(grad_branch_l, w_out).astype(jnp.bfloat16))
    grad_q_l, grad_k_l, grad_v_l = attend_backward(
        query_heads_l, key_heads_l, value_heads_l, local_allowed, total_l, grad_mixed_l
    )
    grad_qkv_l = jnp.concatenate(
        [merge_heads(grad_q_l), merge_heads(grad_k_l), merge_heads(grad_v_l)], axis=-1
    ).astype(jnp.bfloat16)
    grad_w_qkv = outer_sum(normed_local, grad_qkv_l)
    grad_bias_q = row_total(grad_qkv_l[..., :model_width])
    grad_bias_v = row_total(grad_qkv_l[..., 2 * model_width :])
    unused, local_pull = jax.vjp(layer_norm, joined, ln1_gain, ln1_bias)
    grad_joined_in, grad_ln1_gain, grad_ln1_bias = local_pull(linear_back(grad_qkv_l, w_qkv))
    grad_joined = grad_after + grad_joined_in
    grad_mid_low = grad_joined[:, 0].astype(jnp.bfloat16)
    grad_windows = (
        grad_joined[:, 1:].astype(jnp.bfloat16).reshape(win_count, window_len * model_width)
    )
    back_tokens = jnp.einsum(
        "cr,cf->rf", recv_pick, grad_windows, preferred_element_type=jnp.float32
    ).astype(jnp.bfloat16)
    back_region = jnp.einsum(
        "cr,cf->rf", recv_pick, grad_mid_low, preferred_element_type=jnp.float32
    ).astype(jnp.bfloat16)
    came_tokens, came_region = (
        lax.all_to_all(back_tokens, "dp", split_axis=0, concat_axis=0, tiled=True),
        lax.all_to_all(back_region, "dp", split_axis=0, concat_axis=0, tiled=True),
    )
    raster_tokens = jnp.einsum(
        "rc,rf->cf", send_pick, came_tokens, preferred_element_type=jnp.float32
    ).astype(jnp.bfloat16)
    raster_came = jnp.einsum(
        "rc,rf->cf", send_pick, came_region, preferred_element_type=jnp.float32
    )
    grad_band = windows_to_band(
        raster_tokens.reshape(win_count, window_len, model_width), band_rows
    )
    grad_branch_r = (keep_band[:, None] * raster_came).astype(jnp.bfloat16)
    grad_w_out = grad_w_out + outer_sum(mixed_r, grad_branch_r)
    grad_bias_out = grad_bias_out + row_total(grad_branch_r)
    grad_mixed_r = linear_back(grad_branch_r, w_out).astype(jnp.bfloat16).reshape(region_shape)
    grad_q_r, grad_k_r, grad_v_r = attend_backward(
        query_heads_r, key_heads_r, value_heads_r, region_allowed, total_r, grad_mixed_r
    )
    grad_qkv_r = jnp.concatenate(
        [
            grad_q_r.reshape(win_count, model_width),
            grad_k_r.reshape(win_count, model_width),
            grad_v_r.reshape(win_count, model_width),
        ],
        axis=-1,
    ).astype(jnp.bfloat16)
    grad_w_qkv = grad_w_qkv + outer_sum(normed_region, grad_qkv_r)
    grad_bias_q = grad_bias_q + row_total(grad_qkv_r[..., :model_width])
    grad_bias_v = grad_bias_v + row_total(grad_qkv_r[..., 2 * model_width :])
    unused, region_pull = jax.vjp(layer_norm, region_band, ln1_gain, ln1_bias)
    grad_region_in, region_gain, region_bias = region_pull(linear_back(grad_qkv_r, w_qkv))
    grad_ln1_gain = grad_ln1_gain + region_gain
    grad_ln1_bias = grad_ln1_bias + region_bias
    raster_region = (raster_came + grad_region_in).astype(jnp.bfloat16)
    (
        grad_ln1_gain,
        grad_ln1_bias,
        grad_w_qkv,
        grad_bias_q,
        grad_bias_v,
        grad_w_out,
        grad_bias_out,
        grad_ln2_gain,
        grad_ln2_bias,
        grad_w_fc1,
        grad_bias_fc1,
        grad_w_fc2,
        grad_bias_fc2,
    ) = lax.psum(
        (
            grad_ln1_gain,
            grad_ln1_bias,
            grad_w_qkv,
            grad_bias_q,
            grad_bias_v,
            grad_w_out,
            grad_bias_out,
            grad_ln2_gain,
            grad_ln2_bias,
            grad_w_fc1,
            grad_bias_fc1,
            grad_w_fc2,
            grad_bias_fc2,
        ),
        ("dp", "img"),
    )
    return (
        out_local[None],
        out_regional[None],
        grad_band[None],
        raster_region[None],
        grad_ln1_gain,
        grad_ln1_bias,
        grad_w_qkv,
        grad_bias_q,
        grad_bias_v,
        grad_w_out,
        grad_bias_out,
        grad_ln2_gain,
        grad_ln2_bias,
        grad_w_fc1,
        grad_bias_fc1,
        grad_w_fc2,
        grad_bias_fc2,
    )


def solution(mesh):
    in_specs = (
        P("img", "dp", None, None),
        P("img", "dp", None),
        P("img", "dp", None),
        P("img", None),
        P("img", None),
        P(),
        P(),
        P(),
        P(),
        P(),
        P(),
        P(),
        P(),
        P(),
        P(),
        P(),
        P(),
        P(),
        P("img", "dp", None, None),
        P("img", "dp", None),
    )
    out_specs = (
        P("img", "dp", None, None),
        P("img", "dp", None),
        P("img", "dp", None, None),
        P("img", "dp", None),
        P(),
        P(),
        P(),
        P(),
        P(),
        P(),
        P(),
        P(),
        P(),
        P(),
        P(),
        P(),
        P(),
    )
    return jax.shard_map(shards, mesh=mesh, in_specs=in_specs, out_specs=out_specs, check_vma=False)
```

profile of v0, /device:TPU:0, one launch (start us, length us, event | category | flops | bytes accessed | tf_op | source)
XLA Modules:
  0.0 941.1 jit_solution(7364958400995034930)
XLA Ops:
  60.2 69.0 %all-to-all-done.1 = bf16[8,8,25088]{2,1,0:T(8,128)(2,1)} async-done(((bf16[8,8,25088]{2,1,0:T(8,128)(2,1)}), bf16[8,8,25088]{2,1,0:T(8,128)(2,1)}, u32[]{:S(2)}, u32[]{:S(2)}) %all-to-all-start.1) | async-done | bytes 3211296 | tf_op jit(solution)/shard_map/all_to_all | solution.py:204
  184.4 20.0 %fusion.14 = (f32[64,16,50]{2,1,0:T(8,128)S(1)}, f32[64,16,50,50]{2,3,1,0:T(8,128)}) fusion(pred[64,50]{1,0:T(8,128)(4,1)S(1)} %concatenate.21.clone, bf16[64,50,16,32]{1,3,2,0:T(8,128)(2,1)} %bitcast.235, bf16[64,50,16,32]{1,3,2,0:T(8,128)(2,1)} %bitcast.237), kind=kOutput, calls=%fused_computation.38 | convolution fusion | flops 171468800 | bytes 17001600 | tf_op jit(solution)/shard_map/bqhe,bkhe->bhqk/dot_general | solution.py:63
  204.4 19.2 %fusion.8 = f32[64,16,50]{2,1,0:T(8,128)S(1)} fusion(f32[64,16,50]{2,1,0:T(8,128)S(1)} %get-tuple-element.62, f32[64,16,50,50]{2,3,1,0:T(8,128)} %get-tuple-element.63, pred[64,50]{1,0:T(8,128)(4,1)S(1)} %concatenate.21.clone), kind=kLoop, calls=%fused_computation.29 | loop fusion | flops 10188800 | bytes 10652800 | tf_op jit(solution)/shard_map/reduce_sum | solution.py:73
  224.5 19.0 %fusion.15 = bf16[64,16,32,50]{3,2,1,0:T(8,128)(2,1)} fusion(bf16[64,50,16,32]{1,3,2,0:T(8,128)(2,1)} %bitcast.242, f32[64,16,50]{2,1,0:T(8,128)S(1)} %fusion.8, f32[64,16,50]{2,1,0:T(8,128)S(1)} %get-tuple-element.62, f32[64,16,50,50]{2,3,1,0:T(8,128)} %get-tuple-element.63, pred[64,50]{1,0:T(8,128)(4,1)S(1)} %concatenate.21.clone), kind=kOutput, calls=%fused_computation.44 | convolution fusion | flops 178278400 | bytes 17206400 | tf_op jit(solution)/shard_map/bhqk,bkhe->bqhe/dot_general | solution.py:75
  243.5 9.7 %copy.157 = bf16[64,50,512]{2,0,1:T(8,128)(2,1)} copy(bf16[64,50,512]{1,2,0:T(8,128)(2,1)} %bitcast.253) | data formatting | bytes 6553600 | tf_op jit(solution)/shard_map/convert_element_type | solution.py:221
  253.2 13.4 %fusion.129 = (f32[64,50]{0,1:T(8,128)S(1)}, f32[64,50,512]{2,0,1:T(8,128)S(1)}) fusion(f32[512]{0:T(512)S(1)} %copy-done.67, bf16[64,50,512]{2,0,1:T(8,128)(2,1)} %copy.157, bf16[512,512]{1,0:T(8,128)(2,1)S(1)} %copy-done.20, f32[64]{0:T(128)S(1)} %convert_multiply_fusion.1, f32[64,49,512]{2,0,1:T(8,128)} %copy-done.1, ...), kind=kOutput, calls=%fused_computation.255 | convolution fusion | flops 1685910400 | bytes 16923392 | tf_op jit(solution)/shard_map/...i,ij->...j/dot_general | solution.py:36
  269.4 67.0 %multiply_convert_fusion.1 = (bf16[64,50,2048]{2,0,1:T(8,128)(2,1)}, f32[64,50,2048]{2,0,1:T(8,128)}, f32[64,50,2048]{2,0,1:T(8,128)}) fusion(f32[2048]{0:T(1024)S(1)} %copy-done.78, bf16[512,2048]{1,0:T(8,128)(2,1)S(1)} %copy-done, f32[64,50,512]{2,0,1:T(8,128)S(1)} %get-tuple-element.65, f32[512]{0:T(512)S(1)} %copy-done.79, f32[512]{0:T(512)S(1)} %copy-done.68, ...), kind=kOutput, calls=%fused_computation.15 | convolution fusion | flops 7151616000 | bytes 74224640 | tf_op jit(solution)/shard_map/...i,ij->...j/dot_general | solution.py:36
  336.4 26.6 %convert_reduce_fusion = (f32[2048]{0:T(1024)}, bf16[64,50,2048]{2,0,1:T(8,128)(2,1)}) fusion(f32[64,50,2048]{2,0,1:T(8,128)} %get-tuple-element.52, bf16[2048,512]{1,0:T(8,128)(2,1)} %param.36, f32[64]{0:T(128)S(1)} %copy-done.76, bf16[64,49,512]{2,0,1:T(8,128)(2,1)S(1)} %bitcast.249, bf16[64,1,512]{2,0,1:T(8,128)(2,1)S(1)} %bitcast.272, ...), kind=kOutput, calls=%fused_computation.13 | convolution fusion | flops 6828849152 | bytes 70926592 | tf_op jit(solution)/shard_map/...j,ij->...i/dot_general | solution.py:40
  363.0 16.3 %convolution_bitcast_fusion.1 = f32[512,2048]{1,0:T(8,128)} fusion(bf16[64,50,2048]{2,0,1:T(8,128)(2,1)} %get-tuple-element.76, f32[64,50,512]{2,0,1:T(8,128)} %copy-done.3, f32[512]{0:T(512)S(1)} %copy-done.79, f32[512]{0:T(512)S(1)} %copy-done.68, f32[64,50]{0,1:T(8,128)S(1)} %fusion.84, f32[64,50]{0,1:T(8,128)S(1)} %broadcast_multiply_fusion), kind=kOutput, calls=%fused_computation.76 | convolution fusion | flops 6719078400 | bytes 23884800 | tf_op jit(solution)/shard_map/ti,tj->ij/dot_general | solution.py:46
  379.3 14.1 %multiply_reduce_fusion.1 = (f32[512]{0:T(512)}, f32[64,50]{0,1:T(8,128)S(1)}, f32[512]{0:T(512)}, f32[64,50,512]{2,0,1:T(8,128)}) fusion(f32[64,50,512]{2,0,1:T(8,128)S(1)} %copy-done.4, f32[64,50]{0,1:T(8,128)S(1)} %fusion.84, f32[64,50]{0,1:T(8,128)S(1)} %broadcast_multiply_fusion, f32[512]{0:T(512)S(1)} %copy-done.68, ...), kind=kOutput, calls=%fused_computation.54 | convolution fusion | flops 6723989504 | bytes 28356096 | tf_op jit(solution)/shard_map/...j,ij->...i/dot_general | solution.py:40
  415.8 18.7 %fusion.16 = bf16[64,16,32,50]{3,2,1,0:T(8,128)(2,1)} fusion(bf16[64,50,16,32]{1,3,2,0:T(8,128)(2,1)} %bitcast.233, f32[64,16,50]{2,1,0:T(8,128)S(1)} %copy-done.11, f32[64,16,50,50]{2,3,1,0:T(8,128)} %get-tuple-element.63, pred[64,50]{1,0:T(8,128)(4,1)S(1)} %copy-done.31), kind=kOutput, calls=%fused_computation.45 | convolution fusion | flops 175718400 | bytes 17001600 | tf_op jit(solution)/shard_map/bhqk,bqhe->bkhe/dot_general | solution.py:83
  434.5 27.4 %multiply_reduce_fusion = (f32[64,16,50]{2,1,0:T(8,128)S(1)}, f32[64,16,50,50]{2,3,1,0:T(8,128)}) fusion(f32[64,16,50]{2,1,0:T(8,128)S(1)} %copy-done.11, f32[64,16,50,50]{2,3,1,0:T(8,128)} %get-tuple-element.63, pred[64,50]{1,0:T(8,128)(4,1)S(1)} %copy-done.31, bf16[64,50,16,32]{1,3,2,0:T(8,128)(2,1)} %bitcast.234, bf16[64,50,16,32]{1,3,2,0:T(8,128)(2,1)} %bitcast.243), kind=kOutput, calls=%fused_computation.2 | convolution fusion | flops 176588800 | bytes 27446400 | tf_op jit(solution)/shard_map/bqhe,bkhe->bhqk/dot_general | solution.py:89
  461.9 27.4 %multiply_convert_fusion = bf16[64,16,50,50]{2,3,1,0:T(8,128)(2,1)} fusion(f32[64,16,50,50]{2,3,1,0:T(8,128)} %get-tuple-element.69, f32[64,16,50]{2,1,0:T(8,128)S(1)} %get-tuple-element.68, f32[64,16,50]{2,1,0:T(8,128)S(1)} %copy-done.11, f32[64,16,50,50]{2,3,1,0:T(8,128)} %get-tuple-element.63, pred[64,50]{1,0:T(8,128)(4,1)S(1)} %copy-done.31), kind=kLoop, calls=%fused_computation.1 | loop fusion | flops 15360000 | bytes 26012800 | tf_op jit(solution)/shard_map/convert_element_type | solution.py:93
  489.3 12.0 %multiply_convert_fusion.3 = bf16[64,16,32,50]{3,2,1,0:T(8,128)(2,1)} fusion(bf16[64,50,16,32]{1,3,2,0:T(8,128)(2,1)} %bitcast.238, bf16[64,16,50,50]{2,3,1,0:T(8,128)(2,1)} %multiply_convert_fusion), kind=kOutput, calls=%fused_computation.34 | convolution fusion | flops 167116800 | bytes 11673600 | tf_op jit(solution)/shard_map/bhqk,bkhe->bqhe/dot_general | solution.py:96
  501.2 14.2 %multiply_convert_fusion.2 = bf16[64,16,32,50]{3,2,1,0:T(8,128)(2,1)} fusion(bf16[64,50,16,32]{1,3,2,0:T(8,128)(2,1)} %bitcast.236, bf16[64,16,50,50]{2,3,1,0:T(8,128)(2,1)} %multiply_convert_fusion), kind=kOutput, calls=%fused_computation.33 | convolution fusion | flops 167116800 | bytes 11673600 | tf_op jit(solution)/shard_map/bhqk,bqhe->bkhe/dot_general | solution.py:100
  525.1 9.8 %copy.168 = bf16[64,50,512]{2,0,1:T(8,128)(2,1)} copy(bf16[64,50,512]{1,2,0:T(8,128)(2,1)} %bitcast.241) | data formatting | bytes 6553600 | tf_op jit(solution)/shard_map/reshape | solution.py:32
  534.9 9.9 %copy.167 = bf16[64,50,512]{2,0,1:T(8,128)(2,1)} copy(bf16[64,50,512]{1,2,0:T(8,128)(2,1)} %bitcast.240) | data formatting | bytes 6553600 | tf_op jit(solution)/shard_map/reshape | solution.py:32
  544.9 12.1 %fusion.26 = f32[512,1536]{1,0:T(8,128)} fusion(bf16[64,50,512]{2,0,1:T(8,128)(2,1)} %copy.169, bf16[64,50,512]{2,0,1:T(8,128)(2,1)} %copy.168, bf16[64,50,512]{2,0,1:T(8,128)(2,1)} %copy.167, f32[512]{0:T(512)S(1)} %copy-done.57, f32[512]{0:T(512)S(1)} %copy-done.48, f32[64,50]{0,1:T(8,128)S(1)} %copy-done.39, f32[64,50]{0,1:T(8,128)S(1)} %copy-done.36, ...), kind=kOutput, calls=%fused_computation.74 | convolution fusion | flops 5072486400 | bytes 19559424 | tf_op jit(solution)/shard_map/ti,tj->ij/dot_general | solution.py:46
  557.0 12.7 %fusion.124 = (f32[512]{0:T(512)}, f32[64,50]{0,1:T(8,128)S(1)}, f32[64,50,512]{2,0,1:T(8,128)}) fusion(f32[512]{0:T(512)S(1)} %copy-done.48, f32[64,50]{0,1:T(8,128)S(1)} %copy-done.36, f32[64,49,512]{2,0,1:T(8,128)} %copy-done.1, f32[64,1,512]{2,0,1:T(8,128)S(1)} %copy-done.15, bf16[512,1536]{1,0:T(8,128)(2,1)} %param.27, ...), kind=kOutput, calls=%fused_computation.251 | convolution fusion | flops 5072482816 | bytes 24540160 | tf_op jit(solution)/shard_map/...j,ij->...i/dot_general | solution.py:40
  569.7 11.9 %convolution_bitcast_fusion = f32[2048,512]{1,0:T(8,128)} fusion(bf16[64,50,2048]{2,0,1:T(8,128)(2,1)} %get-tuple-element.51, f32[64]{0:T(128)S(1)} %copy-done.76, bf16[64,49,512]{2,0,1:T(8,128)(2,1)S(1)} %bitcast.251, bf16[64,1,512]{2,0,1:T(8,128)(2,1)S(1)} %bitcast.274), kind=kOutput, calls=%fused_computation.75 | convolution fusion | flops 6717440000 | bytes 20578560 | tf_op jit(solution)/shard_map/ti,tj->ij/dot_general | solution.py:46
  599.6 10.4 %fusion.40 = f32[512,512]{1,0:T(8,128)} fusion(bf16[64,50,512]{1,2,0:T(8,128)(2,1)} %bitcast.254, bf16[64,50,512]{2,0,1:T(8,128)(2,1)} %copy-done.16), kind=kOutput, calls=%fused_computation.93 | convolution fusion | flops 1677721600 | bytes 7602176 | tf_op jit(solution)/shard_map/ti,tj->ij/dot_general | solution.py:46
  633.5 14.0 %add_convert_fusion.2 = bf16[64,50,512]{2,0,1:T(8,128)(2,1)S(1)} fusion(f32[64,50,512]{2,0,1:T(8,128)} %copy-done.3, f32[512]{0:T(512)S(1)} %copy-done.80, f32[64]{0:T(128)S(1)} %copy-done.77, bf16[64,50,2048]{2,0,1:T(8,128)(2,1)} %get-tuple-element.51, bf16[2048,512]{1,0:T(8,128)(2,1)} %param.36), kind=kOutput, calls=%fused_computation.61 | convolution fusion | flops 6717440000 | bytes 25037056 | tf_op jit(solution)/shard_map/...i,ij->...j/dot_general | solution.py:36
  661.9 99.6 %all-reduce.1 = (f32[512]{0:T(512)}, f32[512]{0:T(512)}, f32[512]{0:T(512)}, f32[512]{0:T(512)}, f32[512]{0:T(512)}, /*index=5*/f32[512]{0:T(512)}, f32[512]{0:T(512)}, f32[2048]{0:T(1024)}, f32[512]{0:T(512)}) all-reduce(f32[512]{0:T(512)S(1)} %add.292, f32[512]{0:T(512)S(1)} %add.293, ...), channel_id=1, replica_groups=mesh['dp'=8,'img'=4] {'dp','img'}, use_global_device_ids=true, to_apply=%region_25.26 | all-reduce | flops 6144 | bytes 49152 | tf_op jit(solution)/shard_map/psum | solution.py:319
  775.0 148.9 %all-reduce.5.cloned.1.call-done = (f32[512,1536]{1,0:T(8,128)}, f32[512,512]{1,0:T(8,128)}, f32[512,2048]{1,0:T(8,128)}, f32[2048,512]{1,0:T(8,128)}) async-done(((f32[512,1536]{1,0:T(8,128)}, f32[512,512]{1,0:T(8,128)}, f32[512,2048]{1,0:T(8,128)}, f32[2048,512]{1,0:T(8,128)}), (f32[512,1536]{1,0:T(8,128)}, f32[512,512]{1,0:T(8,128)}, f32[512,2048]{1,0:T(8,128)}, ...) | async-done | bytes 12582928 | tf_op jit(solution)/shard_map/psum | solution.py:319
  (286 shorter events, 222.1 us)
Async XLA Ops:
  7.2 262.1 %copy-start = (bf16[512,2048]{1,0:T(8,128)(2,1)S(1)}, bf16[512,2048]{1,0:T(8,128)(2,1)}, u32[]{:S(2)}) copy-start(bf16[512,2048]{1,0:T(8,128)(2,1)} %param.34) | copy-start | bytes 6291460
  7.2 21.5 %copy-start.17 = (bf16[1,64,512]{2,1,0:T(8,128)(2,1)S(1)}, bf16[1,64,512]{2,1,0:T(8,128)(2,1)}, u32[]{:S(2)}) copy-start(bf16[1,64,512]{2,1,0:T(8,128)(2,1)} %param.21) | copy-start | bytes 196612
  7.2 21.5 %copy-start.20 = (bf16[512,512]{1,0:T(8,128)(2,1)S(1)}, bf16[512,512]{1,0:T(8,128)(2,1)}, u32[]{:S(2)}) copy-start(bf16[512,512]{1,0:T(8,128)(2,1)} %param.30) | copy-start | bytes 1572868
  7.2 21.5 %copy-start.67 = (f32[512]{0:T(512)S(1)}, f32[512]{0:T(512)}, u32[]{:S(2)}) copy-start(f32[512]{0:T(512)} %param.31) | copy-start | bytes 6148
  11.8 35.5 %copy-start.49 = (s32[64]{0:T(128)}, s32[64]{0:T(128)S(1)}, u32[]{:S(2)}) copy-start(s32[64]{0:T(128)S(1)} %dynamic_slice.3) | copy-start | bytes 772
  12.8 28.5 %all-to-all-start.2 = ((bf16[8,2,196]{2,1,0:T(2,128)(2,1)}), bf16[8,2,196]{2,1,0:T(2,128)(2,1)S(1)}, u32[]{:S(2)}, u32[]{:S(2)}) async-start(bf16[8,2,196]{2,1,0:T(2,128)(2,1)} %reshape.530), calls=%async_computation.2 | async-start | bytes 16384 | tf_op jit(solution)/shard_map/all_to_all | solution.py:206
  23.5 105.8 %copy-start.53 = (s32[64]{0:T(128)}, s32[64]{0:T(128)S(1)}, u32[]{:S(2)}) copy-start(s32[64]{0:T(128)S(1)} %get-tuple-element.28) | copy-start | bytes 772
  41.3 12.9 %all-to-all-start = ((bf16[8,8,512]{2,1,0:T(8,128)(2,1)}), bf16[8,8,512]{2,1,0:T(8,128)(2,1)S(1)}, u32[]{:S(2)}, u32[]{:S(2)}) async-start(bf16[8,8,512]{2,1,0:T(8,128)(2,1)} %fusion.49), calls=%async_computation | async-start | bytes 131072 | tf_op jit(solution)/shard_map/all_to_all | solution.py:205
  54.2 75.1 %all-to-all-start.1 = ((bf16[8,8,25088]{2,1,0:T(8,128)(2,1)}), bf16[8,8,25088]{2,1,0:T(8,128)(2,1)}, u32[]{:S(2)}, u32[]{:S(2)}) async-start(bf16[8,8,25088]{2,1,0:T(8,128)(2,1)} %fusion), calls=%async_computation.1 | async-start | bytes 6422528 | tf_op jit(solution)/shard_map/all_to_all | solution.py:204
  58.9 194.3 %copy-start.75 = (f32[64]{0:T(128)}, f32[64]{0:T(128)S(1)}, u32[]{:S(2)}) copy-start(f32[64]{0:T(128)S(1)} %convert_multiply_fusion.1) | copy-start | bytes 772
  60.0 164.4 %copy-start.30 = (pred[64,50]{1,0:T(8,128)(4,1)}, pred[64,50]{1,0:T(8,128)(4,1)S(1)}, u32[]{:S(2)}) copy-start(pred[64,50]{1,0:T(8,128)(4,1)S(1)} %concatenate.21.clone) | copy-start | bytes 9604
  60.2 193.0 %copy-start.14 = (f32[64,1,512]{2,0,1:T(8,128)}, f32[64,1,512]{2,0,1:T(8,128)S(1)}, u32[]{:S(2)}) copy-start(f32[64,1,512]{2,0,1:T(8,128)S(1)} %convolution_bitcast_fusion.2) | copy-start | bytes 393220
  266.6 69.8 %copy-start.3 = (f32[64,50,512]{2,0,1:T(8,128)}, f32[64,50,512]{2,0,1:T(8,128)S(1)}, u32[]{:S(2)}) copy-start(f32[64,50,512]{2,0,1:T(8,128)S(1)} %get-tuple-element.65) | copy-start | bytes 19660804
  269.4 67.1 %copy-start.9 = (bf16[1,64,49,512]{3,1,2,0:T(8,128)(2,1)S(1)}, bf16[1,64,49,512]{3,1,2,0:T(8,128)(2,1)}, u32[]{:S(2)}) copy-start(bf16[1,64,49,512]{3,1,2,0:T(8,128)(2,1)} %param.38) | copy-start | bytes 9633796
  269.4 67.1 %copy-start.37 = (bf16[1,64,512]{2,1,0:T(8,128)(2,1)S(1)}, bf16[1,64,512]{2,1,0:T(8,128)(2,1)}, u32[]{:S(2)}) copy-start(bf16[1,64,512]{2,1,0:T(8,128)(2,1)} %param.39) | copy-start | bytes 196612
  269.4 67.1 %copy-start.76 = (f32[64]{0:T(128)S(1)}, f32[64]{0:T(128)}, u32[]{:S(2)}) copy-start(f32[64]{0:T(128)} %copy-done.75) | copy-start | bytes 772
  544.9 36.7 %slice-start = ((s8[6422528]{0:T(1024)(128)(4,1)}), s8[4194304]{0:T(1024)(128)(4,1)S(1)}, s32[]{:S(2)}) async-start(s8[6422528]{0:T(1024)(128)(4,1)} %bitcast.231), calls=%async_computation.6 | async-start | bytes 8388608
  557.0 24.6 %slice-start.1 = ((s8[6422528]{0:T(1024)(128)(4,1)}), s8[2228224]{0:T(1024)(128)(4,1)S(1)}, s32[]{:S(2)}) async-start(s8[6422528]{0:T(1024)(128)(4,1)} %bitcast.231), calls=%async_computation.7 | async-start | bytes 4456448
  595.3 14.7 %all-to-all-start.4 = ((bf16[8,8,512]{2,1,0:T(8,128)(2,1)}), bf16[8,8,512]{2,1,0:T(8,128)(2,1)}, u32[]{:S(2)}, u32[]{:S(2)}) async-start(bf16[8,8,512]{2,1,0:T(8,128)(2,1)} %fusion.50), calls=%async_computation.4 | async-start | bytes 131072 | tf_op jit(solution)/shard_map/all_to_all | solution.py:271
  599.3 16.6 %copy-start.28 = (bf16[64,512]{0,1:T(8,128)(2,1)S(1)}, bf16[64,512]{0,1:T(8,128)(2,1)}, u32[]{:S(2)}) copy-start(bf16[64,512]{0,1:T(8,128)(2,1)} %copy-done.27) | copy-start | bytes 196612
  599.3 16.8 %copy-start.26 = (bf16[64,512]{0,1:T(8,128)(2,1)S(1)}, bf16[64,512]{0,1:T(8,128)(2,1)}, u32[]{:S(2)}) copy-start(bf16[64,512]{0,1:T(8,128)(2,1)} %copy-done.25) | copy-start | bytes 196612
  599.3 324.5 %all-reduce.5.cloned.1.call-start = ((), (), s32[]{:S(2)}) async-start(), calls=%async_computation.5 | async-start | bytes 25165824 | tf_op jit(solution)/shard_map/psum | solution.py:319
  627.2 135.0 %all-to-all-start.3 = ((bf16[8,8,25088]{2,1,0:T(8,128)(2,1)}), bf16[8,8,25088]{2,1,0:T(8,128)(2,1)}, u32[]{:S(2)}, u32[]{:S(2)}) async-start(bf16[8,8,25088]{2,1,0:T(8,128)(2,1)} %fusion.1), calls=%async_computation.3 | async-start | bytes 6422528 | tf_op jit(solution)/shard_map/all_to_all | solution.py:270
  655.4 106.1 %copy-start.32 = (f32[64,512]{1,0:T(8,128)S(1)}, f32[64,512]{1,0:T(8,128)}, u32[]{:S(2)}) copy-start(f32[64,512]{1,0:T(8,128)} %get-tuple-element.71) | copy-start | bytes 393220
  (65 other events, 494.8 us)
Sparse Core Ops, SparseCore 0:
  622.2 301.6 all-reduce.4
where the time goes:
time: 949 us; the launch traced here: 941 us
  matrix products  353 us (37%)
  waiting for transfers between devices  220 us (23%)
  local copies, waits for them, and re-layouts  128 us (13%)
  blocking collectives  99.6 us (10%)
  other arithmetic  96.4 us (10%)
  starting transfers between devices  28.4 us (3%)
  between operations  15.8 us (2%)
    psum x1, waiting for transfers between devices, shards(): lax.psum((grad_ln1_gain, grad_ln1_bias, grad_w_qkv, grad_bias_q, grad_bia...  149 us
    dot_general x5, matrix products, linear(): jnp.einsum('...i,ij->...j', values, matrix, preferred_element_type=jnp.fl...  106 us
    psum x1, blocking collectives, shards(): lax.psum((grad_ln1_gain, grad_ln1_bias, grad_w_qkv, grad_bias_q, grad_bia...  99.6 us
    all_to_all x1, waiting for transfers between devices, shards(): lax.all_to_all(send_tokens, 'dp', split_axis=0, concat_axis=0, tiled=True)  69 us
    dot_general x6, matrix products, linear_back(): jnp.einsum('...j,ij->...i', grads, matrix, preferred_element_type=jnp.flo...  58.6 us
    dot_general x6, matrix products, outer_sum(): jnp.einsum('ti,tj->ij', flat_values, flat_grads, preferred_element_type=j...  56.3 us
    reshape x4, local copies, waits for them, and re-layouts, split_heads(): return values.reshape(values.shape[:-1] + (HEADS, HDIM))  36.2 us
    reshape x3, local copies, waits for them, and re-layouts, merge_heads(): return values.reshape(values.shape[:-2] + (HEADS * HDIM,))  29.4 us
  transfers between devices with their start and end apart: 6, of which 3 were waited for; matrix products, arithmetic and copies ran while one was open for 9% of the time, Pallas kernels for 0%

commit v1 on v0

--- a/solution.py
+++ b/solution.py
@@ -117,15 +117,108 @@
     return jnp.swapaxes(blocks, 1, 2).reshape((band_rows, REG_SIDE * WIN_SIDE) + trailing)
 
 
-def pick_rows(selector, values):
-    return jnp.einsum("rc,cf->rf", selector, values, preferred_element_type=jnp.float32)
-
-
 def keep_for(image_ids, keep_row):
     image_match = image_ids[:, None] == jnp.arange(keep_row.shape[0])[None, :]
     return (
         jnp.sum(jnp.where(image_match, keep_row[None, :], 0), axis=1).astype(jnp.float32) / survive
     )
+
+
+def rank_of(keys):
+    return jnp.sum(keys[None, :] < keys[:, None], axis=1)
+
+
+def reduce_stages():
+    img_bits = [("img", bit) for bit in range(lax.axis_size("img").bit_length() - 1)]
+    dp_bits = [("dp", bit) for bit in range(lax.axis_size("dp").bit_length() - 1)]
+    rest = img_bits[1:] + dp_bits
+    return [img_bits[:1]] + [rest[at : at + 2] for at in range(0, len(rest), 2)]
+
+
+def stage_peers(stage):
+    dp_size, img_size = lax.axis_size("dp"), lax.axis_size("img")
+    flat = lax.axis_index("dp") * img_size + lax.axis_index("img")
+    masks = [(1 << bit) * (img_size if name == "dp" else 1) for name, bit in stage]
+    own = sum(((flat // mask) % 2) << place for place, mask in enumerate(masks))
+    moves = []
+    for offset in range(1, 1 << len(masks)):
+        flip = sum(mask for place, mask in enumerate(masks) if offset >> place & 1)
+        moves.append((offset, [(at, at ^ flip) for at in range(dp_size * img_size)]))
+    return own, moves
+
+
+def reduce_shards(rows):
+    for stage in reduce_stages():
+        own, moves = stage_peers(stage)
+        parts = rows.reshape((1 << len(stage), -1) + rows.shape[1:])
+        got = [
+            lax.ppermute(
+                lax.dynamic_index_in_dim(parts, own ^ offset, 0, False), ("dp", "img"), pairs
+            )
+            for offset, pairs in moves
+        ]
+        total = lax.dynamic_index_in_dim(parts, own, 0, False).astype(jnp.float32)
+        for piece in got:
+            total = total + piece.astype(jnp.float32)
+        rows = total.astype(jnp.bfloat16)
+    return rows
+
+
+def gather_shards(rows):
+    for stage in reversed(reduce_stages()):
+        own, moves = stage_peers(stage)
+        got = [lax.ppermute(rows, ("dp", "img"), pairs) for offset, pairs in moves]
+        pieces = [rows] + got
+        ordered = []
+        for place in range(len(pieces)):
+            piece = pieces[0]
+            for offset in range(1, len(pieces)):
+                piece = jnp.where((own ^ place) == offset, pieces[offset], piece)
+            ordered.append(piece)
+        rows = jnp.concatenate(ordered, axis=0)
+    return rows
+
+
+def all_sum(rows):
+    return gather_shards(reduce_shards(rows.astype(jnp.bfloat16)))
+
+
+def small_rows(vectors, width):
+    flat = jnp.concatenate([vector.reshape(-1, width) for vector in vectors], axis=0)
+    return flat
+
+
+def pack(matrices, vectors, parts):
+    width = 512
+    blocks = []
+    for matrix in matrices:
+        columns = matrix.shape[1] // width
+        blocks.extend(matrix[:, at * width : (at + 1) * width] for at in range(columns))
+    main = jnp.concatenate(blocks, axis=0).astype(jnp.bfloat16)
+    small = jnp.concatenate([vector.reshape(-1, width) for vector in vectors], axis=0)
+    extra = jnp.zeros((parts, 8, width), jnp.bfloat16)
+    extra = extra.at[0, : small.shape[0]].set(small.astype(jnp.bfloat16))
+    main = main.reshape(parts, -1, width)
+    return jnp.concatenate([main, extra], axis=1).reshape(-1, width)
+
+
+def unpack(rows, shapes, vector_sizes, parts):
+    width = 512
+    rows = rows.reshape(parts, -1, width)
+    main = rows[:, :-8].reshape(-1, width)
+    small = rows[0, -8:].astype(jnp.float32)
+    outs, at = [], 0
+    for height, columns in shapes:
+        blocks = []
+        for _ in range(columns // width):
+            blocks.append(main[at : at + height])
+            at += height
+        outs.append(jnp.concatenate(blocks, axis=1).astype(jnp.float32))
+    vectors, at = [], 0
+    for size in vector_sizes:
+        vectors.append(small[at : at + size // width].reshape(size))
+        at += size // width
+    return outs, vectors
 
 
 def shards(
@@ -151,37 +244,37 @@
     cot_regional,
 ):
     devices = lax.axis_size("dp")
+    parts = devices * lax.axis_size("img")
     own_rank = lax.axis_index("dp")
     win_count = regional.shape[1]
     all_windows = window_slot.shape[1]
-    capacity = max(1, win_count // devices)
-    buffer_rows = devices * capacity
     model_width = regional.shape[2]
     window_len = cot_local.shape[2]
     band_rows = tokens.shape[1]
     images_dev = win_count // REGIONS
     slot_of = window_slot[0]
-    target = slot_of // win_count
-    target_grid = target.reshape(devices, win_count)
-    earlier = jnp.arange(win_count)[None, :] < jnp.arange(win_count)[:, None]
-    send_rank = jnp.sum(
-        (target_grid[:, :, None] == target_grid[:, None, :]) & earlier[None], axis=2
-    ).reshape(all_windows)
-    window_ids = jnp.arange(all_windows)
-    send_row = target * capacity + send_rank
-    recv_row = window_ids // win_count * capacity + send_rank
-    own_send = lax.dynamic_slice_in_dim(send_row, own_rank * win_count, win_count)
-    send_pick = (jnp.arange(buffer_rows)[:, None] == own_send[None, :]).astype(jnp.bfloat16)
-    slot_hit = slot_of[None, :] == (own_rank * win_count + jnp.arange(win_count))[:, None]
-    window_here = jnp.sum(jnp.where(slot_hit, window_ids[None, :], 0), axis=1)
-    recv_here = jnp.sum(jnp.where(slot_hit, recv_row[None, :], 0), axis=1)
-    recv_pick = (recv_here[:, None] == jnp.arange(buffer_rows)[None, :]).astype(jnp.bfloat16)
-    image_here = window_here // REGIONS
-    keep_here = keep_for(image_here, keep_mask[0])
-    band_image = (own_rank * win_count + jnp.arange(win_count)) // REGIONS
-    keep_band = keep_for(band_image, keep_mask[0])
-    windows = band_to_windows(tokens[0], win_count).reshape(win_count, window_len * model_width)
-    live_local = band_to_windows(pad_mask[0], win_count)
+    places = jnp.arange(win_count)
+    own_target = lax.dynamic_slice_in_dim(slot_of, own_rank * win_count, win_count) // win_count
+    own_place = rank_of(own_target * win_count + places)
+    slot_hit = slot_of[None, :] == (own_rank * win_count + places)[:, None]
+    window_here = jnp.sum(jnp.where(slot_hit, jnp.arange(all_windows)[None, :], 0), axis=1)
+    here_place = rank_of(window_here)
+    own_pick = (places[:, None] == own_place[None, :]).astype(jnp.bfloat16)
+    here_pick = (places[:, None] == here_place[None, :]).astype(jnp.bfloat16)
+
+    def deal(values, sender, receiver, name):
+        packed = jnp.einsum("ps,tsf->ptf", sender, values, preferred_element_type=jnp.float32)
+        packed = packed.astype(jnp.bfloat16)
+        came = lax.all_to_all(packed, "dp", split_axis=0, concat_axis=0, tiled=True)
+        return jnp.einsum(name, receiver, came, preferred_element_type=jnp.float32)
+
+    cot_rows = jnp.concatenate([cot_regional, jnp.swapaxes(cot_local[0], 0, 1)], axis=0)
+    grad_result = deal(cot_rows, here_pick, own_pick, "pw,ptf->wtf")
+    keep_rows = keep_for((own_rank * win_count) // REGIONS + jnp.arange(images_dev), keep_mask[0])
+    keep_rows = jnp.repeat(keep_rows, REGIONS)[:, None, None]
+    keep_band = keep_rows[:, 0, 0]
+    windows = band_to_windows(tokens[0], win_count)
+    live_local = band_to_windows(pad_mask[0], win_count) != 0
     region_shape = (images_dev, REGIONS, HEADS, HDIM)
     region_band = regional[0].astype(jnp.float32)
     normed_region = layer_norm(region_band, ln1_gain, ln1_bias).astype(jnp.bfloat16)
@@ -189,29 +282,18 @@
     query_heads_r = queries_r.reshape(region_shape)
     key_heads_r = keys_r.reshape(region_shape)
     value_heads_r = values_r.reshape(region_shape)
-    region_allowed = (live_local[:, 0] != 0).reshape(images_dev, 1, 1, REGIONS)
+    region_allowed = live_local[:, 0].reshape(images_dev, 1, 1, REGIONS)
     mixed_heads_r, total_r = attend_forward(
         query_heads_r, key_heads_r, value_heads_r, region_allowed
     )
     mixed_r = mixed_heads_r.reshape(win_count, model_width).astype(jnp.bfloat16)
-    region_mid_band = (
+    region_mid = (
         region_band + keep_band[:, None] * (linear(mixed_r, w_out) + bias_out)
     ).astype(jnp.bfloat16)
-    send_region = pick_rows(send_pick, region_mid_band).astype(jnp.bfloat16)
-    send_tokens = pick_rows(send_pick, windows).astype(jnp.bfloat16)
-    send_live = pick_rows(send_pick, live_local.astype(jnp.bfloat16)).astype(jnp.bfloat16)
-    got_tokens, got_region, got_live = (
-        lax.all_to_all(send_tokens, "dp", split_axis=0, concat_axis=0, tiled=True),
-        lax.all_to_all(send_region, "dp", split_axis=0, concat_axis=0, tiled=True),
-        lax.all_to_all(send_live, "dp", split_axis=0, concat_axis=0, tiled=True),
-    )
-    here_tokens = pick_rows(recv_pick, got_tokens).reshape(win_count, window_len, model_width)
-    region_rows = pick_rows(recv_pick, got_region)
-    here_live = pick_rows(recv_pick, got_live) > 0.5
-    joined = jnp.concatenate([region_rows[:, None, :], here_tokens], axis=1)
+    joined = jnp.concatenate([region_mid[:, None, :], windows], axis=1).astype(jnp.float32)
     normed_local = layer_norm(joined, ln1_gain, ln1_bias).astype(jnp.bfloat16)
     queries_l, keys_l, values_l = project_heads(normed_local, w_qkv, bias_q, bias_v)
-    local_allowed = jnp.concatenate([jnp.ones((win_count, 1), bool), here_live], axis=1)[
+    local_allowed = jnp.concatenate([jnp.ones((win_count, 1), bool), live_local], axis=1)[
         :, None, None, :
     ]
     query_heads_l = split_heads(queries_l)
@@ -219,17 +301,15 @@
     value_heads_l = split_heads(values_l)
     mixed_l, total_l = attend_forward(query_heads_l, key_heads_l, value_heads_l, local_allowed)
     mixed_l = merge_heads(mixed_l).astype(jnp.bfloat16)
-    keep_rows = keep_here[:, None, None]
     after_attention = joined + keep_rows * (linear(mixed_l, w_out) + bias_out)
     normed_mlp = layer_norm(after_attention, ln2_gain, ln2_bias).astype(jnp.bfloat16)
     pre_act = linear(normed_mlp, w_fc1) + bias_fc1
     hidden = gelu_exact(pre_act).astype(jnp.bfloat16)
     result = after_attention + keep_rows * (linear(hidden, w_fc2) + bias_fc2)
-    out_local = result[:, 1:].astype(jnp.bfloat16)
-    out_regional = result[:, 0].astype(jnp.bfloat16)
-    grad_result = jnp.concatenate(
-        [cot_regional[0].astype(jnp.float32)[:, None, :], cot_local[0].astype(jnp.float32)], axis=1
-    )
+    result_rows = jnp.swapaxes(result.astype(jnp.bfloat16), 0, 1)
+    out_rows = deal(result_rows, own_pick, here_pick, "ps,ptf->tsf").astype(jnp.bfloat16)
+    out_regional = out_rows[0]
+    out_local = jnp.swapaxes(out_rows[1:], 0, 1)
     grad_mlp = (keep_rows * grad_result).astype(jnp.bfloat16)
     grad_w_fc2 = outer_sum(hidden, grad_mlp)
     grad_bias_fc2 = row_total(grad_mlp)
@@ -239,6 +319,21 @@
     grad_bias_fc1 = row_total(grad_pre)
     unused, norm_pull = jax.vjp(layer_norm, after_attention, ln2_gain, ln2_bias)
     grad_norm_in, grad_ln2_gain, grad_ln2_bias = norm_pull(linear_back(grad_pre, w_fc1))
+    early = all_sum(
+        pack(
+            [grad_w_fc1, grad_w_fc2],
+            [grad_bias_fc1, grad_bias_fc2, grad_ln2_gain, grad_ln2_bias],
+            parts,
+        )
+    )
+    (grad_w_fc1, grad_w_fc2), (grad_bias_fc1, grad_bias_fc2, grad_ln2_gain, grad_ln2_bias) = (
+        unpack(
+            early,
+            [w_fc1.shape, w_fc2.shape],
+            [bias_fc1.shape[0], model_width, model_width, model_width],
+            parts,
+        )
+    )
     grad_after = grad_result + grad_norm_in
     grad_branch_l = (keep_rows * grad_after).astype(jnp.bfloat16)
     grad_w_out = outer_sum(mixed_l, grad_branch_l)
@@ -255,30 +350,9 @@
     grad_bias_v = row_total(grad_qkv_l[..., 2 * model_width :])
     unused, local_pull = jax.vjp(layer_norm, joined, ln1_gain, ln1_bias)
     grad_joined_in, grad_ln1_gain, grad_ln1_bias = local_pull(linear_back(grad_qkv_l, w_qkv))
-    grad_joined = grad_after + grad_joined_in
-    grad_mid_low = grad_joined[:, 0].astype(jnp.bfloat16)
-    grad_windows = (
-        grad_joined[:, 1:].astype(jnp.bfloat16).reshape(win_count, window_len * model_width)
-    )
-    back_tokens = jnp.einsum(
-        "cr,cf->rf", recv_pick, grad_windows, preferred_element_type=jnp.float32
-    ).astype(jnp.bfloat16)
-    back_region = jnp.einsum(
-        "cr,cf->rf", recv_pick, grad_mid_low, preferred_element_type=jnp.float32
-    ).astype(jnp.bfloat16)
-    came_tokens, came_region = (
-        lax.all_to_all(back_tokens, "dp", split_axis=0, concat_axis=0, tiled=True),
-        lax.all_to_all(back_region, "dp", split_axis=0, concat_axis=0, tiled=True),
-    )
-    raster_tokens = jnp.einsum(
-        "rc,rf->cf", send_pick, came_tokens, preferred_element_type=jnp.float32
-    ).astype(jnp.bfloat16)
-    raster_came = jnp.einsum(
-        "rc,rf->cf", send_pick, came_region, preferred_element_type=jnp.float32
-    )
-    grad_band = windows_to_band(
-        raster_tokens.reshape(win_count, window_len, model_width), band_rows
-    )
+    grad_joined = (grad_after + grad_joined_in).astype(jnp.bfloat16)
+    grad_band = windows_to_band(grad_joined[:, 1:], band_rows)
+    raster_came = grad_joined[:, 0].astype(jnp.float32)
     grad_branch_r = (keep_band[:, None] * raster_came).astype(jnp.bfloat16)
     grad_w_out = grad_w_out + outer_sum(mixed_r, grad_branch_r)
     grad_bias_out = grad_bias_out + row_total(grad_branch_r)
@@ -302,38 +376,17 @@
     grad_ln1_gain = grad_ln1_gain + region_gain
     grad_ln1_bias = grad_ln1_bias + region_bias
     raster_region = (raster_came + grad_region_in).astype(jnp.bfloat16)
-    (
-        grad_ln1_gain,
-        grad_ln1_bias,
-        grad_w_qkv,
-        grad_bias_q,
-        grad_bias_v,
-        grad_w_out,
-        grad_bias_out,
-        grad_ln2_gain,
-        grad_ln2_bias,
-        grad_w_fc1,
-        grad_bias_fc1,
-        grad_w_fc2,
-        grad_bias_fc2,
-    ) = lax.psum(
-        (
-            grad_ln1_gain,
-            grad_ln1_bias,
-            grad_w_qkv,
-            grad_bias_q,
-            grad_bias_v,
-            grad_w_out,
-            grad_bias_out,
-            grad_ln2_gain,
-            grad_ln2_bias,
-            grad_w_fc1,
-            grad_bias_fc1,
-            grad_w_fc2,
-            grad_bias_fc2,
-        ),
-        ("dp", "img"),
-    )
+    late = all_sum(
+        pack(
+            [grad_w_qkv, grad_w_out],
+            [grad_ln1_gain, grad_ln1_bias, grad_bias_q, grad_bias_v, grad_bias_out],
+            parts,
+        )
+    )
+    (grad_w_qkv, grad_w_out), late_vectors = unpack(
+        late, [w_qkv.shape, w_out.shape], [model_width] * 5, parts
+    )
+    grad_ln1_gain, grad_ln1_bias, grad_bias_q, grad_bias_v, grad_bias_out = late_vectors
     return (
         out_local[None],
         out_regional[None],

time: 949 us -> 717 us (0.76)
  waiting for transfers between devices: 220 us -> 59.3 us
  blocking collectives: 99.6 us -> 0 us
  other arithmetic: 96.4 us -> 124 us
  starting transfers between devices: 28.4 us -> 46.4 us
  matrix products: 353 us -> 337 us
  between operations: 15.8 us -> 3.19 us
  local copies, waits for them, and re-layouts: 128 us -> 140 us
    psum x1 -> x0, waiting for transfers between devices: 149 us -> none  [shards(): lax.psum((grad_ln1_gain, grad_ln1_bias, grad_w_qkv, grad_bias_q, grad_bia...]
    psum x1 -> x0, blocking collectives: 99.6 us -> none  [shards(): lax.psum((grad_ln1_gain, grad_ln1_bias, grad_w_qkv, grad_bias_q, grad_bia...]
    all_to_all x5 -> x2, waiting for transfers between devices: 71.4 us -> 0.01 us  [deal(): came = lax.all_to_all(packed, 'dp', split_axis=0, concat_axis=0, tiled=True)]
    ppermute x0 -> x28, waiting for transfers between devices: none -> 59.3 us  [the longest x14 41.1 us: reduce_shards(): lax.ppermute(lax.dynamic_index_in_dim(parts, own ^ offset, 0, False), ('d...]
    ppermute x0 -> x28, starting transfers between devices: none -> 32.2 us  [the longest x14 16.9 us: gather_shards(): got = [lax.ppermute(rows, ('dp', 'img'), pairs) for offset, pairs in moves]]
    convert_element_type x0 -> x13, other arithmetic: none -> 24.7 us  [the longest x6 8.85 us: reduce_shards(): rows = total.astype(jnp.bfloat16)]
    dot_general x5, matrix products: 106 us -> 86.5 us  [linear(): jnp.einsum('...i,ij->...j', values, matrix, preferred_element_type=jnp.fl...]
    all_to_all x5 -> x2, starting transfers between devices: 28.1 us -> 14.2 us  [deal(): came = lax.all_to_all(packed, 'dp', split_axis=0, concat_axis=0, tiled=True)]
  transfers between devices with their start and end apart: 6 -> 30, of which waited for: 3 -> 13; matrix products, arithmetic and copies ran while one was open for 9% -> 81% of each run, Pallas kernels for 0% -> 0%
where the time goes in v1:
time: 717 us; the launch traced here: 709 us
  matrix products  337 us (47%)
  local copies, waits for them, and re-layouts  140 us (20%)
  other arithmetic  124 us (17%)
  waiting for transfers between devices  59.3 us (8%)
  starting transfers between devices  46.4 us (6%)
    dot_general x5, matrix products, linear(): jnp.einsum('...i,ij->...j', values, matrix, preferred_element_type=jnp.fl...  86.5 us
    dot_general x6, matrix products, linear_back(): jnp.einsum('...j,ij->...i', grads, matrix, preferred_element_type=jnp.flo...  58.6 us
    dot_general x6, matrix products, outer_sum(): jnp.einsum('ti,tj->ij', flat_values, flat_grads, preferred_element_type=j...  50.7 us
    ppermute x14, waiting for transfers between devices, reduce_shards(): lax.ppermute(lax.dynamic_index_in_dim(parts, own ^ offset, 0, False), ('d...  41.1 us
    reshape x4, local copies, waits for them, and re-layouts, split_heads(): return values.reshape(values.shape[:-1] + (HEADS, HDIM))  36.4 us
    reshape x3, local copies, waits for them, and re-layouts, merge_heads(): return values.reshape(values.shape[:-2] + (HEADS * HDIM,))  29.7 us
    convert_element_type x2, other arithmetic, attend_backward(): grad_scores = (attn_probs * (grad_probs - row_inner)).astype(jnp.bfloat16)  27.9 us
    dot_general x2, matrix products, attend_backward(): jnp.einsum('bqhe,bkhe->bhqk', grad_mixed, values, preferred_element_type=...  27.4 us
  transfers between devices with their start and end apart: 30, of which 13 were waited for; matrix products, arithmetic and copies ran while one was open for 81% of the time, Pallas kernels for 0%

profile of v1, /device:TPU:0, one launch (start us, length us, event | category | flops | bytes accessed | tf_op | source)
XLA Modules:
  0.0 709.5 jit_solution(5325902144282755661)
XLA Ops:
  60.3 9.2 %copy.232 = bf16[64,50,512]{1,2,0:T(8,128)(2,1)} copy(bf16[64,50,512]{2,0,1:T(8,128)(2,1)} %slice.332) | data formatting | bytes 6553600 | tf_op jit(solution)/shard_map/reshape | solution.py:28
  78.6 20.1 %fusion.12 = (f32[64,16,50]{2,1,0:T(8,128)S(1)}, f32[64,16,50,50]{2,3,1,0:T(8,128)}) fusion(pred[64,50]{1,0:T(8,128)(4,1)S(1)} %concatenate.96.clone, bf16[64,50,16,32]{1,3,2,0:T(8,128)(2,1)} %bitcast.323, bf16[64,50,16,32]{1,3,2,0:T(8,128)(2,1)} %bitcast.325), kind=kOutput, calls=%fused_computation.32 | convolution fusion | flops 171468800 | bytes 17001600 | tf_op jit(solution)/shard_map/bqhe,bkhe->bhqk/dot_general | solution.py:63
  98.7 19.0 %fusion.6 = f32[64,16,50]{2,1,0:T(8,128)S(1)} fusion(f32[64,16,50]{2,1,0:T(8,128)S(1)} %get-tuple-element.119, f32[64,16,50,50]{2,3,1,0:T(8,128)} %get-tuple-element.120, pred[64,50]{1,0:T(8,128)(4,1)S(1)} %concatenate.96.clone), kind=kLoop, calls=%fused_computation.23 | loop fusion | flops 10188800 | bytes 10652800 | tf_op jit(solution)/shard_map/reduce_sum | solution.py:73
  117.7 19.1 %fusion.19 = bf16[64,16,32,50]{3,2,1,0:T(8,128)(2,1)} fusion(bf16[64,50,16,32]{1,3,2,0:T(8,128)(2,1)} %bitcast.340, f32[64,16,50]{2,1,0:T(8,128)S(1)} %fusion.6, f32[64,16,50]{2,1,0:T(8,128)S(1)} %get-tuple-element.119, f32[64,16,50,50]{2,3,1,0:T(8,128)} %get-tuple-element.120, pred[64,50]{1,0:T(8,128)(4,1)S(1)} %concatenate.96.clone), kind=kOutput, calls=%fused_computation.45 | convolution fusion | flops 178278400 | bytes 17206400 | tf_op jit(solution)/shard_map/bhqk,bkhe->bqhe/dot_general | solution.py:75
  136.8 9.7 %copy.192 = bf16[64,50,512]{2,0,1:T(8,128)(2,1)} copy(bf16[64,50,512]{1,2,0:T(8,128)(2,1)} %bitcast.358) | data formatting | bytes 6553600 | tf_op jit(solution)/shard_map/convert_element_type | solution.py:303
  146.5 11.6 %fusion.183 = (f32[64,50]{0,1:T(8,128)S(1)}, f32[64,50,512]{2,0,1:T(8,128)S(1)}) fusion(f32[512]{0:T(512)S(1)} %copy-done.68, bf16[64,50,512]{2,0,1:T(8,128)(2,1)} %copy.192, bf16[512,512]{1,0:T(8,128)(2,1)S(1)} %copy-done.21, f32[]{:T(128)S(6)} %div.163, bf16[64,49,512]{2,0,1:T(8,128)(2,1)} %bitcast.330, bf16[64,1,512]{2,0,1:T(8,128)(2,1)S(1)} %fusion.87), kind=kOutput, calls=%fused_computation.332 | convolution fusion | flops 1687548800 | bytes 13646340 | tf_op jit(solution)/shard_map/...i,ij->...j/dot_general | solution.py:36
  160.8 67.0 %multiply_convert_fusion.1 = (bf16[64,50,2048]{2,0,1:T(8,128)(2,1)}, f32[64,50,2048]{2,0,1:T(8,128)}, f32[64,50,2048]{2,0,1:T(8,128)}) fusion(f32[2048]{0:T(1024)S(1)} %copy-done.77, bf16[512,2048]{1,0:T(8,128)(2,1)S(1)} %copy-done, f32[64,50,512]{2,0,1:T(8,128)S(1)} %get-tuple-element.122, f32[512]{0:T(512)S(1)} %copy-done.79, f32[512]{0:T(512)S(1)} %copy-done.69, ...), kind=kOutput, calls=%fused_computation.9 | convolution fusion | flops 7151616000 | bytes 74224640 | tf_op jit(solution)/shard_map/...i,ij->...j/dot_general | solution.py:36
  228.2 14.0 %fusion.57 = bf16[64,50,512]{2,0,1:T(8,128)(2,1)} fusion(f32[64,50,512]{2,0,1:T(8,128)} %copy-done.4, f32[512]{0:T(512)S(1)} %copy-done.78, f32[]{:T(128)S(6)} %div.163, bf16[64,50,2048]{2,0,1:T(8,128)(2,1)} %get-tuple-element.58, bf16[2048,512]{1,0:T(8,128)(2,1)} %param.40, s32[64]{0:T(128)S(1)} %convert_reduce_fusion.9), kind=kOutput, calls=%fused_computation.105 | convolution fusion | flops 6928797696 | bytes 25037060 | tf_op jit(solution)/shard_map/ps,tsf->ptf/dot_general | solution.py:266
  264.2 29.2 %fusion.184 = (bf16[2048]{0:T(1024)(128)(2,1)}, bf16[64,50,2048]{2,0,1:T(8,128)(2,1)}) fusion(f32[64,50,2048]{2,0,1:T(8,128)} %get-tuple-element.59, bf16[64,50,512]{2,0,1:T(8,128)(2,1)} %get-tuple-element.53, bf16[2048,512]{1,0:T(8,128)(2,1)} %param.40, f32[64,50,2048]{2,0,1:T(8,128)} %get-tuple-element.123, f32[2048]{0:T(1024)S(1)} %copy-done.77), kind=kOutput, calls=%fused_computation.333 | convolution fusion | flops 6815741952 | bytes 70922240 | tf_op jit(solution)/shard_map/...j,ij->...i/dot_general | solution.py:40
  293.3 15.7 %bitcast_convert_fusion.1 = bf16[512,2048]{1,0:T(8,128)(2,1)} fusion(bf16[64,50,2048]{2,0,1:T(8,128)(2,1)} %get-tuple-element.133, f32[64,50,512]{2,0,1:T(8,128)} %copy-done.4, f32[512]{0:T(512)S(1)} %copy-done.79, f32[512]{0:T(512)S(1)} %copy-done.69, f32[64,50]{0,1:T(8,128)S(1)} %fusion.152, f32[64,50]{0,1:T(8,128)S(1)} %broadcast_multiply_fusion), kind=kOutput, calls=%fused_computation.74 | convolution fusion | flops 6720126976 | bytes 21787648 | tf_op jit(solution)/shard_map/ti,tj->ij/dot_general | solution.py:46
  309.0 14.9 %multiply_reduce_fusion.1 = (bf16[512]{0:T(512)(128)(2,1)}, f32[64,50]{0,1:T(8,128)S(1)}, bf16[512]{0:T(512)(128)(2,1)}, f32[64,50,512]{2,0,1:T(8,128)}) fusion(f32[64,50,512]{2,0,1:T(8,128)} %copy-done.4, f32[64,50]{0,1:T(8,128)S(1)} %fusion.152, f32[64,50]{0,1:T(8,128)S(1)} %broadcast_multiply_fusion, f32[512]{0:T(512)S(1)} %copy-done.69, ...), kind=kOutput, calls=%fused_computation.57 | convolution fusion | flops 6723989504 | bytes 28354048 | tf_op jit(solution)/shard_map/...j,ij->...i/dot_general | solution.py:40
  344.5 9.1 %copy.235 = bf16[64,50,512]{1,2,0:T(8,128)(2,1)} copy(bf16[64,50,512]{2,0,1:T(8,128)(2,1)} %convolution_convert_fusion) | data formatting | bytes 6553600 | tf_op jit(solution)/shard_map/reshape | solution.py:28
  353.6 18.7 %fusion.20 = bf16[64,16,32,50]{3,2,1,0:T(8,128)(2,1)} fusion(bf16[64,50,16,32]{1,3,2,0:T(8,128)(2,1)} %bitcast.321, f32[64,16,50]{2,1,0:T(8,128)S(1)} %log_add_fusion, f32[64,16,50,50]{2,3,1,0:T(8,128)} %get-tuple-element.120, pred[64,50]{1,0:T(8,128)(4,1)S(1)} %copy-done.34), kind=kOutput, calls=%fused_computation.46 | convolution fusion | flops 175718400 | bytes 17001600 | tf_op jit(solution)/shard_map/bhqk,bqhe->bkhe/dot_general | solution.py:83
  372.3 27.1 %multiply_reduce_fusion = (f32[64,16,50]{2,1,0:T(8,128)S(1)}, f32[64,16,50,50]{2,3,1,0:T(8,128)}) fusion(f32[64,16,50]{2,1,0:T(8,128)S(1)} %log_add_fusion, f32[64,16,50,50]{2,3,1,0:T(8,128)} %get-tuple-element.120, pred[64,50]{1,0:T(8,128)(4,1)S(1)} %copy-done.34, bf16[64,50,16,32]{1,3,2,0:T(8,128)(2,1)} %bitcast.322, bf16[64,50,16,32]{1,3,2,0:T(8,128)(2,1)} %bitcast.341), kind=kOutput, calls=%fused_computation.2 | convolution fusion | flops 176588800 | bytes 27446400 | tf_op jit(solution)/shard_map/bqhe,bkhe->bhqk/dot_general | solution.py:89
  399.4 27.8 %multiply_convert_fusion = bf16[64,16,50,50]{2,3,1,0:T(8,128)(2,1)} fusion(f32[64,16,50,50]{2,3,1,0:T(8,128)} %get-tuple-element.127, f32[64,16,50]{2,1,0:T(8,128)S(1)} %get-tuple-element.126, f32[64,16,50]{2,1,0:T(8,128)S(1)} %log_add_fusion, f32[64,16,50,50]{2,3,1,0:T(8,128)} %get-tuple-element.120, pred[64,50]{1,0:T(8,128)(4,1)S(1)} %copy-done.34), kind=kLoop, calls=%fused_computation.1 | loop fusion | flops 15360000 | bytes 26012800 | tf_op jit(solution)/shard_map/convert_element_type | solution.py:93
  427.2 12.0 %multiply_convert_fusion.3 = bf16[64,16,32,50]{3,2,1,0:T(8,128)(2,1)} fusion(bf16[64,50,16,32]{1,3,2,0:T(8,128)(2,1)} %bitcast.326, bf16[64,16,50,50]{2,3,1,0:T(8,128)(2,1)} %multiply_convert_fusion), kind=kOutput, calls=%fused_computation.28 | convolution fusion | flops 167116800 | bytes 11673600 | tf_op jit(solution)/shard_map/bhqk,bkhe->bqhe/dot_general | solution.py:96
  439.1 14.2 %multiply_convert_fusion.2 = bf16[64,16,32,50]{3,2,1,0:T(8,128)(2,1)} fusion(bf16[64,50,16,32]{1,3,2,0:T(8,128)(2,1)} %bitcast.324, bf16[64,16,50,50]{2,3,1,0:T(8,128)(2,1)} %multiply_convert_fusion), kind=kOutput, calls=%fused_computation.27 | convolution fusion | flops 167116800 | bytes 11673600 | tf_op jit(solution)/shard_map/bhqk,bqhe->bkhe/dot_general | solution.py:100
  458.4 9.7 %copy.210 = bf16[64,50,512]{2,0,1:T(8,128)(2,1)} copy(bf16[64,50,512]{1,2,0:T(8,128)(2,1)} %bitcast.327) | data formatting | bytes 6553600 | tf_op jit(solution)/shard_map/reshape | solution.py:32
  468.2 9.8 %copy.209 = bf16[64,50,512]{2,0,1:T(8,128)(2,1)} copy(bf16[64,50,512]{1,2,0:T(8,128)(2,1)} %bitcast.339) | data formatting | bytes 6553600 | tf_op jit(solution)/shard_map/reshape | solution.py:32
  483.1 10.2 %copy.208 = bf16[64,50,512]{2,0,1:T(8,128)(2,1)} copy(bf16[64,50,512]{1,2,0:T(8,128)(2,1)} %bitcast.328) | data formatting | bytes 6553600 | tf_op jit(solution)/shard_map/reshape | solution.py:32
  493.3 12.2 %fusion.49 = f32[512,1536]{1,0:T(8,128)} fusion(bf16[64,50,512]{2,0,1:T(8,128)(2,1)} %copy.210, bf16[64,50,512]{2,0,1:T(8,128)(2,1)} %copy.209, bf16[64,50,512]{2,0,1:T(8,128)(2,1)} %copy.208, f32[512]{0:T(512)S(1)} %copy-done.60, f32[512]{0:T(512)S(1)} %copy-done.53, f32[64,50]{0,1:T(8,128)S(1)} %copy-done.42, f32[64,50]{0,1:T(8,128)S(1)} %copy-done.40, ...), kind=kOutput, calls=%fused_computation.95 | convolution fusion | flops 5074124800 | bytes 16282624 | tf_op jit(solution)/shard_map/ti,tj->ij/dot_general | solution.py:46
  547.7 11.5 %fusion.50 = bf16[4096,512]{1,0:T(8,128)(2,1)} fusion(bf16[4096,512]{1,0:T(8,128)(2,1)} %slice_dynamic-update-slice_fusion, bf16[64,50,2048]{2,0,1:T(8,128)(2,1)} %get-tuple-element.58, bf16[64,50,512]{2,0,1:T(8,128)(2,1)S(1)} %copy-done.14), kind=kOutput, calls=%fused_computation.97 | convolution fusion | flops 6711934976 | bytes 18481152 | tf_op jit(solution)/shard_map/ti,tj->ij/dot_general | solution.py:46
  572.1 12.0 %collective-permute-done.1 = bf16[288,512]{1,0:T(8,128)(2,1)} collective-permute-done((bf16[288,512]{1,0:T(8,128)(2,1)}, bf16[288,512]{1,0:T(8,128)(2,1)}, u32[]{:S(2)}, u32[]{:S(2)}) %collective-permute-start.1) | collective-permute-done | bytes 294944 | tf_op jit(solution)/shard_map/ppermute | solution.py:155
  619.0 17.5 %collective-permute-done.15 = bf16[544,512]{1,0:T(8,128)(2,1)S(1)} collective-permute-done((bf16[544,512]{1,0:T(8,128)(2,1)}, bf16[544,512]{1,0:T(8,128)(2,1)S(1)}, u32[]{:S(2)}, u32[]{:S(2)}) %collective-permute-start.15) | collective-permute-done | bytes 557088 | tf_op jit(solution)/shard_map/ppermute | solution.py:155
  (377 shorter events, 285.1 us)
Async XLA Ops:
  9.2 240.4 %all-to-all-start.1 = ((bf16[64,50,512]{2,1,0:T(8,128)(2,1)}), bf16[64,50,512]{2,1,0:T(8,128)(2,1)}, u32[]{:S(2)}, u32[]{:S(2)}) async-start(bf16[64,50,512]{2,1,0:T(8,128)(2,1)} %copy.197), calls=%async_computation.1 | async-start | bytes 7340032 | tf_op jit(solution)/shard_map/all_to_all | solution.py:268
  249.6 362.8 %all-to-all-start = ((bf16[64,50,512]{2,1,0:T(8,128)(2,1)}), bf16[64,50,512]{2,1,0:T(8,128)(2,1)}, u32[]{:S(2)}, u32[]{:S(2)}) async-start(bf16[64,50,512]{2,1,0:T(8,128)(2,1)} %copy.194), calls=%async_computation | async-start | bytes 7340032 | tf_op jit(solution)/shard_map/all_to_all | solution.py:268
  547.5 18.1 %collective-permute-start = (bf16[1152,512]{1,0:T(8,128)(2,1)S(1)}, bf16[1152,512]{1,0:T(8,128)(2,1)}, u32[]{:S(2)}, u32[]{:S(2)}) collective-permute-start(bf16[1152,512]{1,0:T(8,128)(2,1)S(1)} %dynamic-slice_bitcast_fusion.1), channel_id=1, source_target_pairs={{0,1},{1,0},{2,3},{3,2},{4,5},{5,4},{6,7},{7,6},{8,9},{9,8},{10,11... | collective-permute-start | bytes 3538952 | tf_op jit(solution)/shard_map/ppermute | solution.py:155
  565.2 38.3 %collective-permute-start.14 = (bf16[2176,512]{1,0:T(8,128)(2,1)}, bf16[2176,512]{1,0:T(8,128)(2,1)}, u32[]{:S(2)}, u32[]{:S(2)}) collective-permute-start(bf16[2176,512]{1,0:T(8,128)(2,1)} %dynamic-slice_bitcast_fusion), channel_id=1, source_target_pairs={{0,1},{1,0},{2,3},{3,2},{4,5},{5,4},{6,7},{7,6},{8,9},{9,8},{10,11... | collective-permute-start | bytes 6684680 | tf_op jit(solution)/shard_map/ppermute | solution.py:155
  568.5 15.6 %collective-permute-start.1 = (bf16[288,512]{1,0:T(8,128)(2,1)}, bf16[288,512]{1,0:T(8,128)(2,1)}, u32[]{:S(2)}, u32[]{:S(2)}) collective-permute-start(bf16[288,512]{1,0:T(8,128)(2,1)} %get-tuple-element.90), channel_id=1, source_target_pairs={{0,2},{1,3},{2,0},{3,1},{4,6},{5,7},{6,4},{7,5},{8,10},{9,11},{10,... | collective-permute-start | bytes 884744 | tf_op jit(solution)/shard_map/ppermute | solution.py:155
  570.0 14.1 %collective-permute-start.3 = (bf16[288,512]{1,0:T(8,128)(2,1)}, bf16[288,512]{1,0:T(8,128)(2,1)}, u32[]{:S(2)}, u32[]{:S(2)}) collective-permute-start(bf16[288,512]{1,0:T(8,128)(2,1)} %get-tuple-element.91), channel_id=1, source_target_pairs={{0,6},{1,7},{2,4},{3,5},{4,2},{5,3},{6,0},{7,1},{8,14},{9,15},{10,... | collective-permute-start | bytes 884744 | tf_op jit(solution)/shard_map/ppermute | solution.py:155
  572.0 13.6 %collective-permute-start.2 = (bf16[288,512]{1,0:T(8,128)(2,1)}, bf16[288,512]{1,0:T(8,128)(2,1)}, u32[]{:S(2)}, u32[]{:S(2)}) collective-permute-start(bf16[288,512]{1,0:T(8,128)(2,1)} %get-tuple-element.92), channel_id=1, source_target_pairs={{0,4},{1,5},{2,6},{3,7},{4,0},{5,1},{6,2},{7,3},{8,12},{9,13},{10,... | collective-permute-start | bytes 884744 | tf_op jit(solution)/shard_map/ppermute | solution.py:155
  599.0 12.8 %collective-permute-start.9 = (bf16[72,512]{1,0:T(8,128)(2,1)S(1)}, bf16[72,512]{1,0:T(8,128)(2,1)S(1)}, u32[]{:S(2)}, u32[]{:S(2)}) collective-permute-start(bf16[72,512]{1,0:T(8,128)(2,1)S(1)} %fusion.127), channel_id=1, source_target_pairs={{0,8},{1,9},{2,10},{3,11},{4,12},{5,13},{6,14},{7,15},{8,0},{9,1},... | collective-permute-start | bytes 221192 | tf_op jit(solution)/shard_map/ppermute | solution.py:170
  599.1 16.8 %collective-permute-start.8 = (bf16[72,512]{1,0:T(8,128)(2,1)S(1)}, bf16[72,512]{1,0:T(8,128)(2,1)S(1)}, u32[]{:S(2)}, u32[]{:S(2)}) collective-permute-start(bf16[72,512]{1,0:T(8,128)(2,1)S(1)} %fusion.127), channel_id=1, source_target_pairs={{0,16},{1,17},{2,18},{3,19},{4,20},{5,21},{6,22},{7,23},{8,24},{9,... | collective-permute-start | bytes 221192 | tf_op jit(solution)/shard_map/ppermute | solution.py:170
  602.1 13.8 %collective-permute-start.7 = (bf16[72,512]{1,0:T(8,128)(2,1)S(1)}, bf16[72,512]{1,0:T(8,128)(2,1)S(1)}, u32[]{:S(2)}, u32[]{:S(2)}) collective-permute-start(bf16[72,512]{1,0:T(8,128)(2,1)S(1)} %fusion.127), channel_id=1, source_target_pairs={{0,24},{1,25},{2,26},{3,27},{4,28},{5,29},{6,30},{7,31},{8,16},{9,... | collective-permute-start | bytes 221192 | tf_op jit(solution)/shard_map/ppermute | solution.py:170
  608.9 27.6 %collective-permute-start.15 = (bf16[544,512]{1,0:T(8,128)(2,1)}, bf16[544,512]{1,0:T(8,128)(2,1)S(1)}, u32[]{:S(2)}, u32[]{:S(2)}) collective-permute-start(bf16[544,512]{1,0:T(8,128)(2,1)} %get-tuple-element.80), channel_id=1, source_target_pairs={{0,2},{1,3},{2,0},{3,1},{4,6},{5,7},{6,4},{7,5},{8,10},{9,11},{10,... | collective-permute-start | bytes 1671176 | tf_op jit(solution)/shard_map/ppermute | solution.py:155
  610.4 27.5 %collective-permute-start.17 = (bf16[544,512]{1,0:T(8,128)(2,1)}, bf16[544,512]{1,0:T(8,128)(2,1)}, u32[]{:S(2)}, u32[]{:S(2)}) collective-permute-start(bf16[544,512]{1,0:T(8,128)(2,1)} %get-tuple-element.81), channel_id=1, source_target_pairs={{0,6},{1,7},{2,4},{3,5},{4,2},{5,3},{6,0},{7,1},{8,14},{9,15},{10,... | collective-permute-start | bytes 1671176 | tf_op jit(solution)/shard_map/ppermute | solution.py:155
  611.8 26.4 %collective-permute-start.16 = (bf16[544,512]{1,0:T(8,128)(2,1)S(1)}, bf16[544,512]{1,0:T(8,128)(2,1)}, u32[]{:S(2)}, u32[]{:S(2)}) collective-permute-start(bf16[544,512]{1,0:T(8,128)(2,1)S(1)} %get-tuple-element.82), channel_id=1, source_target_pairs={{0,4},{1,5},{2,6},{3,7},{4,0},{5,1},{6,2},{7,3},{8,12},{9,13},{10,... | collective-permute-start | bytes 1671176 | tf_op jit(solution)/shard_map/ppermute | solution.py:155
  616.0 26.5 %collective-permute-start.12 = (bf16[288,512]{1,0:T(8,128)(2,1)S(1)}, bf16[288,512]{1,0:T(8,128)(2,1)S(1)}, u32[]{:S(2)}, u32[]{:S(2)}) collective-permute-start(bf16[288,512]{1,0:T(8,128)(2,1)S(1)} %pad_maximum_fusion.14), channel_id=1, source_target_pairs={{0,2},{1,3},{2,0},{3,1},{4,6},{5,7},{6,4},{7,5},{8,10},{9,11},{10,... | collective-permute-start | bytes 884744 | tf_op jit(solution)/shard_map/ppermute | solution.py:170
  617.6 26.8 %collective-permute-start.11 = (bf16[288,512]{1,0:T(8,128)(2,1)S(1)}, bf16[288,512]{1,0:T(8,128)(2,1)S(1)}, u32[]{:S(2)}, u32[]{:S(2)}) collective-permute-start(bf16[288,512]{1,0:T(8,128)(2,1)S(1)} %pad_maximum_fusion.14), channel_id=1, source_target_pairs={{0,4},{1,5},{2,6},{3,7},{4,0},{5,1},{6,2},{7,3},{8,12},{9,13},{10,... | collective-permute-start | bytes 884744 | tf_op jit(solution)/shard_map/ppermute | solution.py:170
  636.5 12.5 %collective-permute-start.10 = (bf16[288,512]{1,0:T(8,128)(2,1)S(1)}, bf16[288,512]{1,0:T(8,128)(2,1)S(1)}, u32[]{:S(2)}, u32[]{:S(2)}) collective-permute-start(bf16[288,512]{1,0:T(8,128)(2,1)S(1)} %pad_maximum_fusion.14), channel_id=1, source_target_pairs={{0,6},{1,7},{2,4},{3,5},{4,2},{5,3},{6,0},{7,1},{8,14},{9,15},{10,... | collective-permute-start | bytes 884744 | tf_op jit(solution)/shard_map/ppermute | solution.py:170
  639.9 9.4 %collective-permute-start.18 = (bf16[136,512]{1,0:T(8,128)(2,1)S(1)}, bf16[136,512]{1,0:T(8,128)(2,1)S(1)}, u32[]{:S(2)}, u32[]{:S(2)}) collective-permute-start(bf16[136,512]{1,0:T(8,128)(2,1)S(1)} %get-tuple-element.97), channel_id=1, source_target_pairs={{0,8},{1,9},{2,10},{3,11},{4,12},{5,13},{6,14},{7,15},{8,0},{9,1},... | collective-permute-start | bytes 417800 | tf_op jit(solution)/shard_map/ppermute | solution.py:155
  642.5 10.3 %collective-permute-start.19 = (bf16[136,512]{1,0:T(8,128)(2,1)S(1)}, bf16[136,512]{1,0:T(8,128)(2,1)S(1)}, u32[]{:S(2)}, u32[]{:S(2)}) collective-permute-start(bf16[136,512]{1,0:T(8,128)(2,1)S(1)} %get-tuple-element.99), channel_id=1, source_target_pairs={{0,16},{1,17},{2,18},{3,19},{4,20},{5,21},{6,22},{7,23},{8,24},{9,... | collective-permute-start | bytes 417800 | tf_op jit(solution)/shard_map/ppermute | solution.py:155
  652.9 12.9 %collective-permute-start.22 = (bf16[136,512]{1,0:T(8,128)(2,1)S(1)}, bf16[136,512]{1,0:T(8,128)(2,1)S(1)}, u32[]{:S(2)}, u32[]{:S(2)}) collective-permute-start(bf16[136,512]{1,0:T(8,128)(2,1)S(1)} %fusion.105), channel_id=1, source_target_pairs={{0,16},{1,17},{2,18},{3,19},{4,20},{5,21},{6,22},{7,23},{8,24},{9,... | collective-permute-start | bytes 417800 | tf_op jit(solution)/shard_map/ppermute | solution.py:170
  654.8 11.0 %collective-permute-start.21 = (bf16[136,512]{1,0:T(8,128)(2,1)S(1)}, bf16[136,512]{1,0:T(8,128)(2,1)S(1)}, u32[]{:S(2)}, u32[]{:S(2)}) collective-permute-start(bf16[136,512]{1,0:T(8,128)(2,1)S(1)} %fusion.105), channel_id=1, source_target_pairs={{0,24},{1,25},{2,26},{3,27},{4,28},{5,29},{6,30},{7,31},{8,16},{9,... | collective-permute-start | bytes 417800 | tf_op jit(solution)/shard_map/ppermute | solution.py:170
  667.4 19.3 %collective-permute-start.26 = (bf16[544,512]{1,0:T(8,128)(2,1)}, bf16[544,512]{1,0:T(8,128)(2,1)}, u32[]{:S(2)}, u32[]{:S(2)}) collective-permute-start(bf16[544,512]{1,0:T(8,128)(2,1)} %pad_maximum_fusion.12), channel_id=1, source_target_pairs={{0,2},{1,3},{2,0},{3,1},{4,6},{5,7},{6,4},{7,5},{8,10},{9,11},{10,... | collective-permute-start | bytes 1671176 | tf_op jit(solution)/shard_map/ppermute | solution.py:170
  667.4 19.3 %collective-permute-start.25 = (bf16[544,512]{1,0:T(8,128)(2,1)}, bf16[544,512]{1,0:T(8,128)(2,1)}, u32[]{:S(2)}, u32[]{:S(2)}) collective-permute-start(bf16[544,512]{1,0:T(8,128)(2,1)} %pad_maximum_fusion.12), channel_id=1, source_target_pairs={{0,4},{1,5},{2,6},{3,7},{4,0},{5,1},{6,2},{7,3},{8,12},{9,13},{10,... | collective-permute-start | bytes 1671176 | tf_op jit(solution)/shard_map/ppermute | solution.py:170
  668.0 23.1 %collective-permute-start.24 = (bf16[544,512]{1,0:T(8,128)(2,1)}, bf16[544,512]{1,0:T(8,128)(2,1)}, u32[]{:S(2)}, u32[]{:S(2)}) collective-permute-start(bf16[544,512]{1,0:T(8,128)(2,1)} %pad_maximum_fusion.12), channel_id=1, source_target_pairs={{0,6},{1,7},{2,4},{3,5},{4,2},{5,3},{6,0},{7,1},{8,14},{9,15},{10,... | collective-permute-start | bytes 1671176 | tf_op jit(solution)/shard_map/ppermute | solution.py:170
  672.0 23.1 %collective-permute-start.13 = (bf16[1152,512]{1,0:T(8,128)(2,1)}, bf16[1152,512]{1,0:T(8,128)(2,1)}, u32[]{:S(2)}, u32[]{:S(2)}) collective-permute-start(bf16[1152,512]{1,0:T(8,128)(2,1)} %pad_maximum_fusion.11), channel_id=1, source_target_pairs={{0,1},{1,0},{2,3},{3,2},{4,5},{5,4},{6,7},{7,6},{8,9},{9,8},{10,11... | collective-permute-start | bytes 3538952 | tf_op jit(solution)/shard_map/ppermute | solution.py:170
  (92 other events, 1210.0 us)

commit v2 on v1

v2 whole, which is shorter than its diff:
```python
import math
import jax
import jax.numpy as jnp
import numpy as np
from jax import lax
from jax.experimental import pallas as pl
from jax.experimental.pallas import tpu as pltpu
from jax.sharding import PartitionSpec as P

HEADS = 16
HDIM = 32
WIN_SIDE = 7
REG_SIDE = 8
REGIONS = 64

norm_eps = 1e-05
survive = 0.9

WIDTH = 512
SLOT = 64
TALL = 56
TILE = 8
GROUP = 4
LANES = 128
VMEM_LIMIT = 60 * 1024 * 1024

f32 = jnp.float32
bf16 = jnp.bfloat16


def dot(left, right):
    return lax.dot_general(left, right, (((1,), (0,)), ((), ())), preferred_element_type=f32)


def dot_nt(left, right):
    return lax.dot_general(left, right, (((1,), (1,)), ((), ())), preferred_element_type=f32)


def head_masks():
    lane_head = np.arange(LANES) // HDIM
    plain = np.repeat(np.arange(GROUP), SLOT)
    mixed = np.repeat(np.array([0, 2, 1, 3]), SLOT)
    return (
        jnp.asarray(plain[:, None] == lane_head[None, :], bf16),
        jnp.asarray(mixed[:, None] == lane_head[None, :], bf16),
    )


def spread_heads(rows, mask):
    return jnp.concatenate([rows] * GROUP, axis=0) * mask


def turn(blocks):
    stacked = jnp.concatenate([blocks[:, :LANES], blocks[:, LANES:]], axis=0)
    turned = stacked.T
    return jnp.concatenate([turned[:SLOT], turned[SLOT:]], axis=1)


def attend_group(queries, key_rows, values, bias, plain, mixed):
    scores = dot_nt(key_rows, spread_heads(queries, plain)) + bias
    highest = jnp.max(scores, axis=0, keepdims=True)
    weighted = jnp.exp2((scores - highest) * (HDIM**-0.5 * math.log2(math.e)))
    total = jnp.sum(weighted, axis=0, keepdims=True)
    probs = (weighted * (1.0 / total)).astype(bf16)
    return probs, dot(turn(probs), spread_heads(values, mixed))


def attend_group_back(queries, key_rows, values, probs, grad_mixed, plain, mixed):
    grad_wide = spread_heads(grad_mixed, plain)
    grad_values = dot(probs, grad_wide)
    grad_probs = dot_nt(values, grad_wide)
    soft = probs.astype(f32)
    weighted = soft * grad_probs
    inner = jnp.sum(weighted, axis=0, keepdims=True)
    grad_scores = (weighted - soft * inner).astype(bf16)
    factor = HDIM**-0.5
    grad_keys = dot(grad_scores, spread_heads(queries, plain)) * factor
    grad_queries = dot(turn(grad_scores), spread_heads(key_rows, mixed)) * factor
    return grad_queries, grad_keys, grad_values


def normalize(rows):
    centered = rows - jnp.mean(rows, axis=-1, keepdims=True)
    spread = jnp.mean(centered * centered, axis=-1, keepdims=True)
    scale = lax.rsqrt(spread + norm_eps)
    return centered * scale, scale


def normalize_back(grad_unit, unit, scale):
    first = jnp.mean(grad_unit, axis=-1, keepdims=True)
    second = jnp.mean(grad_unit * unit, axis=-1, keepdims=True)
    return scale * (grad_unit - first - unit * second)


def gelu_pair(values):
    size = jnp.abs(values)
    spot = 1.0 / (1.0 + (0.3275911 * 0.7071067811865476) * size)
    bell = jnp.exp2(values * values * (-0.5 * math.log2(math.e)))
    tail = 0.5 * 1.061405429
    for factor in (-1.453152027, 1.421413741, -0.284496736, 0.254829592):
        tail = tail * spot + 0.5 * factor
    tail = tail * spot * bell
    below = jnp.where(values >= 0, 1.0 - tail, tail)
    return values * below, below + values * bell * 0.3989422804014327


def column_sum(rows):
    return jnp.sum(rows, axis=0, keepdims=True)


def attend_window(qkv, bias, plain, mixed, put_probs):
    outs = []
    wide_bias = jnp.concatenate([bias, bias], axis=1)
    for group in range(HEADS // GROUP):
        at = group * LANES
        probs, out = attend_group(
            qkv[:, at : at + LANES],
            qkv[:, WIDTH + at : WIDTH + at + LANES],
            qkv[:, 2 * WIDTH + at : 2 * WIDTH + at + LANES],
            wide_bias,
            plain,
            mixed,
        )
        put_probs(group, probs)
        outs.append(out)
    return jnp.concatenate(outs, axis=1)


def attend_window_back(qkv, probs_of, grad_mixed, plain, mixed):
    parts = []
    for group in range(HEADS // GROUP):
        at = group * LANES
        parts.append(
            attend_group_back(
                qkv[:, at : at + LANES],
                qkv[:, WIDTH + at : WIDTH + at + LANES],
                qkv[:, 2 * WIDTH + at : 2 * WIDTH + at + LANES],
                probs_of(group),
                grad_mixed[:, at : at + LANES],
                plain,
                mixed,
            )
        )
    return jnp.concatenate(
        [parts[g][which] for which in range(3) for g in range(len(parts))], axis=1
    ).astype(bf16)


def forward_kernel(
    order_ref, keep_ref,
    tokens_ref, regional_ref, window_bias_ref, region_bias_ref, spread_ref, squeeze_ref,
    plain_ref, mixed_mask_ref, gain1_ref, bias1_ref, w_qkv_ref, bias_qkv_ref, w_out_ref, bias_out_ref,
    gain2_ref, bias2_ref, w_fc1_ref, bias_fc1_ref, w_fc2_ref, bias_fc2_ref,
    out_ref, qkv_ref, probs_ref, joined_ref, mixed_ref, after_ref, hidden_ref, slope_ref,
    qkv_r_ref, probs_r_ref, mixed_r_ref,
    windows, normed, mixed_rows,
):
    step = pl.program_id(0)
    keep = keep_ref[0]
    plain = plain_ref[...]
    mixed = mixed_mask_ref[...]

    @pl.when(step == 0)
    def first():
        region = regional_ref[...].astype(f32)
        unit, _ = normalize(region)
        region_norm = (unit * gain1_ref[...] + bias1_ref[...]).astype(bf16)
        qkv_r_ref[...] = (dot(region_norm, w_qkv_ref[...]) + bias_qkv_ref[...]).astype(bf16)

        def put(group, probs):
            probs_r_ref[:, group * 2 * LANES : (group + 1) * 2 * LANES] = probs

        region_mixed = attend_window(
            qkv_r_ref[...], region_bias_ref[...], plain, mixed, put
        ).astype(bf16)
        mixed_r_ref[...] = region_mixed
        region_mid = region + keep * (dot(region_mixed, w_out_ref[...]) + bias_out_ref[...])
        region_mid = region_mid.astype(bf16)
        row = lax.broadcasted_iota(jnp.int32, (TILE * SLOT, REGIONS), 0)
        column = lax.broadcasted_iota(jnp.int32, (TILE * SLOT, REGIONS), 1)

        def relay(line, carry):
            pick = (row == (column - line * TILE) * SLOT).astype(bf16)
            rows = dot(spread_ref[...], tokens_ref[line]) + dot(pick, region_mid)
            windows[pl.ds(line * TILE, TILE)] = rows.reshape(TILE, SLOT, WIDTH)
            return carry

        lax.fori_loop(0, REG_SIDE, relay, 0)

    for at in range(TILE):
        rows = windows[order_ref[step * TILE + at]]
        joined_ref[at] = rows.astype(bf16)
        unit, _ = normalize(rows)
        normed[at * SLOT : (at + 1) * SLOT] = (unit * gain1_ref[...] + bias1_ref[...]).astype(bf16)
    for part in range(3):
        cols = slice(part * WIDTH, (part + 1) * WIDTH)
        qkv = dot(normed[...], w_qkv_ref[:, cols]) + bias_qkv_ref[:, cols]
        qkv_ref[:, :, cols] = qkv.astype(bf16).reshape(TILE, SLOT, WIDTH)

    def one(at, carry):
        def put(group, probs):
            probs_ref[at, :, group * 2 * LANES : (group + 1) * 2 * LANES] = probs

        mixed_rows[at] = attend_window(
            qkv_ref[at], window_bias_ref[order_ref[step * TILE + at]], plain, mixed, put
        )
        return carry

    lax.fori_loop(0, TILE, one, 0)
    rows_count = TILE * TALL
    mixed_low = mixed_rows[:, :TALL].reshape(rows_count, WIDTH).astype(bf16)
    mixed_ref[...] = mixed_low
    joined = joined_ref[...].astype(f32)[:, :TALL].reshape(rows_count, WIDTH)
    after = joined + keep * (dot(mixed_low, w_out_ref[...]) + bias_out_ref[...])
    after_ref[...] = after
    unit, _ = normalize(after)
    mlp_norm = (unit * gain2_ref[...] + bias2_ref[...]).astype(bf16)
    total = after + keep * bias_fc2_ref[...]
    chunk = 512
    for at in range(0, w_fc1_ref.shape[1], chunk):
        cols = slice(at, at + chunk)
        hidden, slope = gelu_pair(dot(mlp_norm, w_fc1_ref[:, cols]) + bias_fc1_ref[:, cols])
        hidden = hidden.astype(bf16)
        hidden_ref[:, cols] = hidden
        slope_ref[:, cols] = slope.astype(bf16)
        total = total + keep * dot(hidden, w_fc2_ref[cols, :])
    out_ref[0] = dot(squeeze_ref[...], total.astype(bf16)).astype(bf16)


def whole(shape):
    return pl.BlockSpec(shape, lambda step, *_: (0,) * len(shape))


def tiles(shape):
    return pl.BlockSpec(shape, lambda step, *_: (step,) + (0,) * (len(shape) - 1))


def run_forward(order, keep, tokens, regional, window_bias, region_bias, spread, squeeze, plain, mixed,
                gain1, bias1, w_qkv, bias_qkv, w_out, bias_out, gain2, bias2, w_fc1, bias_fc1, w_fc2, bias_fc2):
    windows = regional.shape[0]
    steps = windows // TILE
    rows = TILE * TALL
    hidden = w_fc1.shape[1]
    compact = squeeze.shape[0]
    args = (tokens, regional, window_bias, region_bias, spread, squeeze, plain, mixed,
            gain1, bias1, w_qkv, bias_qkv, w_out, bias_out, gain2, bias2, w_fc1, bias_fc1, w_fc2, bias_fc2)
    outs = [
        ((steps, compact, WIDTH), bf16, (1, compact, WIDTH)),
        ((windows, SLOT, 3 * WIDTH), bf16, (TILE, SLOT, 3 * WIDTH)),
        ((windows, SLOT, HEADS * SLOT), bf16, (TILE, SLOT, HEADS * SLOT)),
        ((windows, SLOT, WIDTH), bf16, (TILE, SLOT, WIDTH)),
        ((steps * rows, WIDTH), bf16, (rows, WIDTH)),
        ((steps * rows, WIDTH), f32, (rows, WIDTH)),
        ((steps * rows, hidden), bf16, (rows, hidden)),
        ((steps * rows, hidden), bf16, (rows, hidden)),
    ]
    fixed = [((REGIONS, 3 * WIDTH), bf16), ((REGIONS, HEADS * SLOT), bf16), ((REGIONS, WIDTH), bf16)]
    return pl.pallas_call(
        forward_kernel,
        grid_spec=pltpu.PrefetchScalarGridSpec(
            num_scalar_prefetch=2,
            grid=(steps,),
            in_specs=[whole(a.shape) for a in args],
            out_specs=[tiles(block) for _, _, block in outs] + [whole(s) for s, _ in fixed],
            scratch_shapes=[
                pltpu.VMEM((windows, SLOT, WIDTH), f32),
                pltpu.VMEM((TILE * SLOT, WIDTH), bf16),
                pltpu.VMEM((TILE, SLOT, WIDTH), f32),
            ],
        ),
        out_shape=[jax.ShapeDtypeStruct(s, d) for s, d, _ in outs]
        + [jax.ShapeDtypeStruct(s, d) for s, d in fixed],
        compiler_params=pltpu.CompilerParams(
            dimension_semantics=("arbitrary",), vmem_limit_bytes=VMEM_LIMIT
        ),
        cost_estimate=pl.CostEstimate(flops=30_000_000_000, bytes_accessed=60_000_000, transcendentals=20_000_000),
        name="forward",
    )(order, keep, *args)


def back_mlp_kernel(
    keep_ref, cot_ref, after_ref, mixed_ref, hidden_ref, slope_ref, stretch_ref,
    gain2_ref, bias2_ref, w_fc1_ref, w_fc2_ref, w_out_ref,
    grad_after_ref, grad_mixed_ref, early_ref, grad_out_ref, small_ref, bias_row_ref,
    sum_fc1, sum_fc2, sum_out, sums, sum_hidden,
):
    step = pl.program_id(0)
    last = pl.num_programs(0) - 1
    keep = keep_ref[0]

    @pl.when(step == 0)
    def clear():
        for ref in (sum_fc1, sum_fc2, sum_out, sums, sum_hidden):
            ref[...] = jnp.zeros_like(ref)

    unit, scale = normalize(after_ref[...])
    mlp_norm = (unit * gain2_ref[...] + bias2_ref[...]).astype(bf16)
    norm_turned = mlp_norm.T
    cot = dot(stretch_ref[...], cot_ref[0])
    grad_mlp = (keep * cot).astype(bf16)
    grad_turned = grad_mlp.T
    sums[0:1] += column_sum(grad_mlp.astype(f32))
    grad_norm = jnp.zeros(after_ref.shape, f32)
    chunk = 512
    for at in range(0, w_fc1_ref.shape[1], chunk):
        cols = slice(at, at + chunk)
        grad_hidden = dot_nt(grad_mlp, w_fc2_ref[cols, :])
        grad_pre = (slope_ref[:, cols].astype(f32) * grad_hidden).astype(bf16)
        sum_fc2[:, cols] += dot(grad_turned, hidden_ref[:, cols])
        sum_fc1[:, cols] += dot(norm_turned, grad_pre)
        sum_hidden[0:1, cols] += column_sum(grad_pre.astype(f32))
        grad_norm = grad_norm + dot_nt(grad_pre, w_fc1_ref[:, cols])
    sums[1:2] += column_sum(grad_norm * unit)
    sums[2:3] += column_sum(grad_norm)
    grad_after = cot + normalize_back(grad_norm * gain2_ref[...], unit, scale)
    grad_after_ref[...] = grad_after
    grad_branch = (keep * grad_after).astype(bf16)
    sums[3:4] += column_sum(grad_branch.astype(f32))
    sum_out[...] += dot(mixed_ref[...].T, grad_branch)
    grad_mixed = dot_nt(grad_branch, w_out_ref[...]).reshape(TILE, TALL, WIDTH)
    empty = jnp.zeros((TILE, SLOT - TALL, WIDTH), f32)
    grad_mixed_ref[...] = jnp.concatenate([grad_mixed, empty], axis=1).astype(bf16)

    @pl.when(step == last)
    def finish():
        for at in range(4):
            cols = slice(at * WIDTH, (at + 1) * WIDTH)
            early_ref[cols, :] = sum_fc1[:, cols].astype(bf16)
            early_ref[4 * WIDTH + at * WIDTH : 4 * WIDTH + (at + 1) * WIDTH, :] = (
                sum_fc2[:, cols].T.astype(bf16)
            )
        grad_out_ref[...] = sum_out[...]
        small_ref[...] = sums[...]
        bias_row_ref[...] = sum_hidden[...]


def run_back_mlp(keep, cot, after, mixed, hidden, slope, stretch, gain2, bias2, w_fc1, w_fc2, w_out):
    steps, compact, _ = cot.shape
    rows = TILE * TALL
    units = w_fc1.shape[1]
    tiled = [(1, compact, WIDTH), (rows, WIDTH), (rows, WIDTH), (rows, units), (rows, units)]
    fixed = (stretch, gain2, bias2, w_fc1, w_fc2, w_out)
    outs = [
        ((steps * rows, WIDTH), f32, (rows, WIDTH)),
        ((steps * TILE, SLOT, WIDTH), bf16, (TILE, SLOT, WIDTH)),
    ]
    whole_outs = [((2 * units, WIDTH), bf16), ((WIDTH, WIDTH), f32), ((8, WIDTH), f32), ((8, units), f32)]
    return pl.pallas_call(
        back_mlp_kernel,
        grid_spec=pltpu.PrefetchScalarGridSpec(
            num_scalar_prefetch=1,
            grid=(steps,),
            in_specs=[tiles(b) for b in tiled] + [whole(a.shape) for a in fixed],
            out_specs=[tiles(block) for _, _, block in outs] + [whole(s) for s, _ in whole_outs],
            scratch_shapes=[
                pltpu.VMEM((WIDTH, units), f32),
                pltpu.VMEM((WIDTH, units), f32),
                pltpu.VMEM((WIDTH, WIDTH), f32),
                pltpu.VMEM((8, WIDTH), f32),
                pltpu.VMEM((8, units), f32),
            ],
        ),
        out_shape=[jax.ShapeDtypeStruct(s, d) for s, d, _ in outs]
        + [jax.ShapeDtypeStruct(s, d) for s, d in whole_outs],
        compiler_params=pltpu.CompilerParams(
            dimension_semantics=("arbitrary",), vmem_limit_bytes=VMEM_LIMIT
        ),
        cost_estimate=pl.CostEstimate(flops=40_000_000_000, bytes_accessed=60_000_000, transcendentals=0),
        name="back_mlp",
    )(keep, cot, after, mixed, hidden, slope, *fixed)


def back_attention_kernel(
    order_ref, keep_ref,
    qkv_ref, probs_ref, joined_ref, grad_mixed_ref, grad_after_ref, grad_out_ref,
    gather_ref, plain_ref, mixed_mask_ref, regional_ref, qkv_r_ref, probs_r_ref, mixed_r_ref,
    gain1_ref, bias1_ref, w_qkv_ref, w_out_ref,
    tokens_out_ref, regional_out_ref, late_ref, small_ref,
    windows, grads, sum_qkv, sums, region_grad,
):
    step = pl.program_id(0)
    last = pl.num_programs(0) - 1
    keep = keep_ref[0]
    plain = plain_ref[...]
    mixed = mixed_mask_ref[...]
    gain1 = gain1_ref[...]

    @pl.when(step == 0)
    def clear():
        sum_qkv[...] = jnp.zeros_like(sum_qkv)
        sums[...] = jnp.zeros_like(sums)

    def one(at, carry):
        def probs_of(group):
            return probs_ref[at, :, group * 2 * LANES : (group + 1) * 2 * LANES]

        grads[pl.ds(pl.multiple_of(at * SLOT, SLOT), SLOT)] = attend_window_back(
            qkv_ref[at], probs_of, grad_mixed_ref[at], plain, mixed
        )
        return carry

    lax.fori_loop(0, TILE, one, 0)
    joined = joined_ref[...].astype(f32).reshape(TILE * SLOT, WIDTH)
    unit, scale = normalize(joined)
    normed = (unit * gain1 + bias1_ref[...]).astype(bf16)
    grad_qkv = grads[...]
    sum_qkv[...] += dot(normed.T, grad_qkv)
    sums[2:3] += column_sum(grad_qkv[:, :WIDTH].astype(f32))
    sums[3:4] += column_sum(grad_qkv[:, 2 * WIDTH :].astype(f32))
    grad_normed = dot_nt(grad_qkv, w_qkv_ref[...])
    sums[0:1] += column_sum(grad_normed * unit)
    sums[1:2] += column_sum(grad_normed)
    grad_in = normalize_back(grad_normed * gain1, unit, scale)
    for at in range(TILE):
        rows = grad_in[at * SLOT : at * SLOT + TALL] + grad_after_ref[at * TALL : (at + 1) * TALL]
        windows[order_ref[step * TILE + at], :TALL] = rows

    @pl.when(step == last)
    def finish():
        def relay(line, carry):
            block = windows[pl.ds(line * TILE, TILE)][:, :TALL].reshape(TILE * TALL, WIDTH)
            rows = dot(gather_ref[...], block.astype(bf16))
            tokens_out_ref[line] = rows[: rows.shape[0] - TILE].astype(bf16)
            region_grad[pl.ds(pl.multiple_of(line * TILE, TILE), TILE)] = rows[rows.shape[0] - TILE :]
            return carry

        lax.fori_loop(0, REG_SIDE, relay, 0)
        came = region_grad[...]
        grad_branch = (keep * came).astype(bf16)
        grad_mixed = dot_nt(grad_branch, w_out_ref[...]).astype(bf16)

        def probs_of(group):
            return probs_r_ref[:, group * 2 * LANES : (group + 1) * 2 * LANES]

        grad_qkv_r = attend_window_back(qkv_r_ref[...], probs_of, grad_mixed, plain, mixed)
        region = regional_ref[...].astype(f32)
        unit_r, scale_r = normalize(region)
        normed_r = (unit_r * gain1 + bias1_ref[...]).astype(bf16)
        total = sum_qkv[...] + dot(normed_r.T, grad_qkv_r)
        for part in range(3):
            cols = slice(part * WIDTH, (part + 1) * WIDTH)
            late_ref[cols, :] = total[:, cols].astype(bf16)
        late_ref[3 * WIDTH :, :] = (
            grad_out_ref[...] + dot(mixed_r_ref[...].T, grad_branch)
        ).astype(bf16)
        grad_normed_r = dot_nt(grad_qkv_r, w_qkv_ref[...])
        sums[0:1] += column_sum(grad_normed_r * unit_r)
        sums[1:2] += column_sum(grad_normed_r)
        sums[2:3] += column_sum(grad_qkv_r[:, :WIDTH].astype(f32))
        sums[3:4] += column_sum(grad_qkv_r[:, 2 * WIDTH :].astype(f32))
        sums[4:5] += column_sum(grad_branch.astype(f32))
        regional_out_ref[...] = (
            came + normalize_back(grad_normed_r * gain1, unit_r, scale_r)
        ).astype(bf16)
        small_ref[...] = sums[...]


def run_back_attention(order, keep, qkv, probs, joined, grad_mixed, grad_after, grad_out, gather, plain, mixed,
                       regional, qkv_r, probs_r, mixed_r, gain1, bias1, w_qkv, w_out):
    windows = regional.shape[0]
    steps = windows // TILE
    rows = TILE * TALL
    lines = gather.shape[0] - TILE
    tiled = [(TILE, SLOT, 3 * WIDTH), (TILE, SLOT, HEADS * SLOT), (TILE, SLOT, WIDTH), (TILE, SLOT, WIDTH), (rows, WIDTH)]
    fixed = (grad_out, gather, plain, mixed, regional, qkv_r, probs_r, mixed_r, gain1, bias1, w_qkv, w_out)
    whole_outs = [((REG_SIDE, lines, WIDTH), bf16), ((windows, WIDTH), bf16), ((4 * WIDTH, WIDTH), bf16), ((8, WIDTH), f32)]
    return pl.pallas_call(
        back_attention_kernel,
        grid_spec=pltpu.PrefetchScalarGridSpec(
            num_scalar_prefetch=2,
            grid=(steps,),
            in_specs=[tiles(b) for b in tiled] + [whole(a.shape) for a in fixed],
            out_specs=[whole(s) for s, _ in whole_outs],
            scratch_shapes=[
                pltpu.VMEM((windows, SLOT, WIDTH), f32),
                pltpu.VMEM((TILE * SLOT, 3 * WIDTH), bf16),
                pltpu.VMEM((WIDTH, 3 * WIDTH), f32),
                pltpu.VMEM((8, WIDTH), f32),
                pltpu.VMEM((windows, WIDTH), f32),
            ],
        ),
        out_shape=[jax.ShapeDtypeStruct(s, d) for s, d in whole_outs],
        compiler_params=pltpu.CompilerParams(
            dimension_semantics=("arbitrary",), vmem_limit_bytes=VMEM_LIMIT
        ),
        cost_estimate=pl.CostEstimate(flops=30_000_000_000, bytes_accessed=60_000_000, transcendentals=0),
        name="back_attention",
    )(order, keep, qkv, probs, joined, grad_mixed, grad_after, *fixed)


def band_to_windows(band_values, win_count):
    trailing = band_values.shape[2:]
    blocks = band_values.reshape(
        (band_values.shape[0] // WIN_SIDE, WIN_SIDE, REG_SIDE, WIN_SIDE) + trailing
    )
    return jnp.swapaxes(blocks, 1, 2).reshape((win_count, WIN_SIDE * WIN_SIDE) + trailing)


def rank_of(keys):
    return jnp.sum(keys[None, :] < keys[:, None], axis=1)


def reduce_stages():
    img_bits = [("img", bit) for bit in range(lax.axis_size("img").bit_length() - 1)]
    dp_bits = [("dp", bit) for bit in range(lax.axis_size("dp").bit_length() - 1)]
    rest = img_bits[1:] + dp_bits
    return [img_bits[:1]] + [rest[at : at + 2] for at in range(0, len(rest), 2)]


def stage_peers(stage):
    dp_size, img_size = lax.axis_size("dp"), lax.axis_size("img")
    flat = lax.axis_index("dp") * img_size + lax.axis_index("img")
    masks = [(1 << bit) * (img_size if name == "dp" else 1) for name, bit in stage]
    own = sum(((flat // mask) % 2) << place for place, mask in enumerate(masks))
    moves = []
    for offset in range(1, 1 << len(masks)):
        flip = sum(mask for place, mask in enumerate(masks) if offset >> place & 1)
        moves.append((offset, [(at, at ^ flip) for at in range(dp_size * img_size)]))
    return own, moves


def reduce_shards(rows):
    for stage in reduce_stages():
        own, moves = stage_peers(stage)
        parts = rows.reshape((1 << len(stage), -1) + rows.shape[1:])
        got = [
            lax.ppermute(
                lax.dynamic_index_in_dim(parts, own ^ offset, 0, False), ("dp", "img"), pairs
            )
            for offset, pairs in moves
        ]
        total = lax.dynamic_index_in_dim(parts, own, 0, False).astype(jnp.float32)
        for piece in got:
            total = total + piece.astype(jnp.float32)
        rows = total.astype(jnp.bfloat16)
    return rows


def gather_shards(rows):
    for stage in reversed(reduce_stages()):
        own, moves = stage_peers(stage)
        got = [lax.ppermute(rows, ("dp", "img"), pairs) for offset, pairs in moves]
        pieces = [rows] + got
        ordered = []
        for place in range(len(pieces)):
            piece = pieces[0]
            for offset in range(1, len(pieces)):
                piece = jnp.where((own ^ place) == offset, pieces[offset], piece)
            ordered.append(piece)
        rows = jnp.concatenate(ordered, axis=0)
    return rows


def all_sum(rows):
    return gather_shards(reduce_shards(rows.astype(jnp.bfloat16)))


def deal_kernel(pick_ref, region_ref, local_ref, out_ref):
    groups = out_ref.shape[0]
    for pair in range(out_ref.shape[1] // 16):
        head = region_ref[...] if pair == 0 else local_ref[2 * pair - 1]
        rows = jnp.concatenate([head, local_ref[2 * pair]], axis=0)
        out_ref[:, 16 * pair : 16 * pair + 16, :] = (
            dot(pick_ref[...], rows).astype(bf16).reshape(groups, 16, WIDTH)
        )


def collect_kernel(pick_ref, came_ref, region_ref, local_ref):
    slots = region_ref.shape[0]
    for pair in range(came_ref.shape[1] // 16):
        rows = came_ref[:, 16 * pair : 16 * pair + 16, :].reshape(2 * slots, WIDTH)
        rows = dot(pick_ref[...], rows).astype(bf16)
        if pair == 0:
            region_ref[...] = rows[:slots]
        else:
            local_ref[2 * pair - 1] = rows[:slots]
        local_ref[2 * pair] = rows[slots:]


def run_deal(pick, region, local):
    count = region.shape[0] // TILE
    return pl.pallas_call(
        deal_kernel,
        out_shape=jax.ShapeDtypeStruct((count, (local.shape[0] + 1) * TILE, WIDTH), bf16),
        compiler_params=pltpu.CompilerParams(vmem_limit_bytes=VMEM_LIMIT),
        cost_estimate=pl.CostEstimate(flops=1_000_000_000, bytes_accessed=7_000_000, transcendentals=0),
        name="deal",
    )(pick, region, local)


def run_collect(pick, came):
    slots = came.shape[0] * TILE
    return pl.pallas_call(
        collect_kernel,
        out_shape=[
            jax.ShapeDtypeStruct((slots, WIDTH), bf16),
            jax.ShapeDtypeStruct((came.shape[1] // TILE - 1, slots, WIDTH), bf16),
        ],
        compiler_params=pltpu.CompilerParams(vmem_limit_bytes=VMEM_LIMIT),
        cost_estimate=pl.CostEstimate(flops=1_000_000_000, bytes_accessed=7_000_000, transcendentals=0),
        name="collect",
    )(pick, came)


def swap_tiles(tiles_sent, devices):
    count, rows, width = tiles_sent.shape
    share = count * TILE // devices
    if share == TILE:
        return lax.all_to_all(tiles_sent, "dp", split_axis=0, concat_axis=0, tiled=True)
    places = rows // TILE
    sent = tiles_sent.reshape(count, places, TILE, width).transpose(1, 0, 2, 3)
    sent = sent.reshape(places, devices, share, width).transpose(1, 0, 2, 3)
    came = lax.all_to_all(sent, "dp", split_axis=0, concat_axis=0, tiled=True)
    came = came.transpose(1, 0, 2, 3).reshape(places, count, TILE, width)
    return came.transpose(1, 0, 2, 3).reshape(count, rows, width)


def row_maps():
    window = np.arange(TILE)[:, None]
    place = np.arange(WIN_SIDE * WIN_SIDE)[None, :]
    raster = place // WIN_SIDE * (TILE * WIN_SIDE) + window * WIN_SIDE + place % WIN_SIDE
    band = TILE * WIN_SIDE * WIN_SIDE
    spread = np.zeros((TILE * SLOT, band), np.float32)
    spread[window * SLOT + 1 + place, raster] = 1
    gather = np.zeros((band + TILE, TILE * TALL), np.float32)
    gather[raster, window * TALL + 1 + place] = 1
    gather[band + window, window * TALL] = 1
    place = np.arange(WIN_SIDE * WIN_SIDE + 1)[None, :]
    squeeze = np.zeros(((WIN_SIDE * WIN_SIDE + 1) * TILE, TILE * TALL), np.float32)
    squeeze[place * TILE + window, window * TALL + place] = 1
    return [jnp.asarray(table, bf16) for table in (spread, gather, squeeze, squeeze.T)]


def shards(
    tokens,
    regional,
    pad_mask,
    keep_mask,
    window_slot,
    ln1_gain,
    ln1_bias,
    w_qkv,
    bias_q,
    bias_v,
    w_out,
    bias_out,
    ln2_gain,
    ln2_bias,
    w_fc1,
    bias_fc1,
    w_fc2,
    bias_fc2,
    cot_local,
    cot_regional,
):
    devices = lax.axis_size("dp")
    parts = devices * lax.axis_size("img")
    own_rank = lax.axis_index("dp")
    win_count = regional.shape[1]
    all_windows = window_slot.shape[1]
    slot_of = window_slot[0]
    places = jnp.arange(win_count)
    own_target = lax.dynamic_slice_in_dim(slot_of, own_rank * win_count, win_count) // win_count
    own_place = rank_of(own_target * win_count + places)
    order = jnp.sum(jnp.where(own_place[None, :] == places[:, None], places[None, :], 0), axis=1)
    slot_hit = slot_of[None, :] == (own_rank * win_count + places)[:, None]
    window_here = jnp.sum(jnp.where(slot_hit, jnp.arange(all_windows)[None, :], 0), axis=1)
    here_place = rank_of(window_here)
    deal_row = jnp.arange(2 * win_count)
    row_place = deal_row // (2 * TILE) * TILE + deal_row % TILE
    row_half = deal_row // TILE % 2
    column_hit = row_place[:, None] == jnp.concatenate([here_place, here_place])[None, :]
    pick = (column_hit & (row_half[:, None] == (deal_row // win_count)[None, :])).astype(bf16)
    pick_back = (column_hit & (row_half[:, None] == (deal_row // win_count)[None, :])).T.astype(bf16)
    cot = swap_tiles(
        run_deal(pick, cot_regional[0], jnp.swapaxes(cot_local[0], 0, 1)), devices
    )
    image = own_rank * win_count // REGIONS
    keep = lax.dynamic_slice_in_dim(keep_mask[0], image, 1).astype(f32) / survive
    live = band_to_windows(pad_mask[0], win_count) != 0
    allowed = jnp.concatenate(
        [jnp.ones((win_count, 1), bool), live, jnp.zeros((win_count, SLOT - 1 - live.shape[1]), bool)],
        axis=1,
    )
    window_bias = jnp.broadcast_to(
        jnp.where(allowed, 0.0, -1e30).astype(f32)[:, :, None], (win_count, SLOT, LANES)
    )
    region_bias = jnp.broadcast_to(
        jnp.where(live[:, 0], 0.0, -1e30).astype(f32)[:, None], (win_count, LANES)
    )
    spread, gather, squeeze, stretch = row_maps()
    plain, mixed_mask = head_masks()
    bias_qkv = jnp.concatenate([bias_q, jnp.zeros_like(bias_q), bias_v])[None]
    gain1, bias1, gain2, bias2 = ln1_gain[None], ln1_bias[None], ln2_gain[None], ln2_bias[None]
    out, qkv, probs, joined, mixed, after, hidden, slope, qkv_r, probs_r, mixed_r = run_forward(
        order, keep, tokens.reshape(REG_SIDE, -1, WIDTH), regional[0], window_bias, region_bias,
        spread, squeeze, plain, mixed_mask, gain1, bias1, w_qkv, bias_qkv, w_out, bias_out[None],
        gain2, bias2, w_fc1, bias_fc1[None], w_fc2, bias_fc2[None],
    )
    came = swap_tiles(out, devices)
    grad_after, grad_mixed, early, grad_out, small, row_fc1 = run_back_mlp(
        keep, cot, after, mixed, hidden, slope, stretch, gain2, bias2, w_fc1, w_fc2, w_out
    )
    early = all_sum(early)
    tokens_out, regional_out, late, small_late = run_back_attention(
        order, keep, qkv, probs, joined, grad_mixed, grad_after, grad_out, gather, plain, mixed_mask,
        regional[0], qkv_r, probs_r, mixed_r, gain1, bias1, w_qkv, w_out,
    )
    out_regional, out_local = run_collect(pick_back, came)
    vectors = jnp.concatenate(
        [
            small_late[0:4],
            (small[3] + small_late[4])[None],
            small[1:3],
            small[0:1],
            row_fc1[0].reshape(-1, WIDTH),
        ],
        axis=0,
    )
    late_share = late.shape[0] // parts
    extra = jnp.zeros((2 * 8, WIDTH), bf16).at[: vectors.shape[0]].set(vectors.astype(bf16))
    extra = jnp.concatenate([extra.reshape(2, 8, WIDTH), jnp.zeros((parts - 2, 8, WIDTH), bf16)])
    late = jnp.concatenate([late.reshape(parts, late_share, WIDTH), extra], axis=1)
    late = all_sum(late.reshape(-1, WIDTH)).reshape(parts, late_share + 8, WIDTH)
    vectors = late[:2, late_share:].reshape(-1, WIDTH).astype(f32)
    late = late[:, :late_share].reshape(-1, WIDTH)
    grad_w_qkv = jnp.concatenate([late[at * WIDTH : (at + 1) * WIDTH] for at in range(3)], axis=1)
    units = w_fc1.shape[1]
    grad_w_fc1 = jnp.concatenate(
        [early[at : at + WIDTH] for at in range(0, units, WIDTH)], axis=1
    )
    return (
        jnp.swapaxes(out_local, 0, 1)[None],
        out_regional[None],
        tokens_out.reshape(tokens.shape),
        regional_out[None],
        vectors[0],
        vectors[1],
        grad_w_qkv.astype(f32),
        vectors[2],
        vectors[3],
        late[3 * WIDTH :].astype(f32),
        vectors[4],
        vectors[5],
        vectors[6],
        grad_w_fc1.astype(f32),
        vectors[8:12].reshape(-1),
        early[units:].astype(f32),
        vectors[7],
    )


def solution(mesh):
    in_specs = (
        P("img", "dp", None, None),
        P("img", "dp", None),
        P("img", "dp", None),
        P("img", None),
        P("img", None),
        P(),
        P(),
        P(),
        P(),
        P(),
        P(),
        P(),
        P(),
        P(),
        P(),
        P(),
        P(),
        P(),
        P("img", "dp", None, None),
        P("img", "dp", None),
    )
    out_specs = (
        P("img", "dp", None, None),
        P("img", "dp", None),
        P("img", "dp", None, None),
        P("img", "dp", None),
        P(),
        P(),
        P(),
        P(),
        P(),
        P(),
        P(),
        P(),
        P(),
        P(),
        P(),
        P(),
        P(),
    )
    return jax.shard_map(shards, mesh=mesh, in_specs=in_specs, out_specs=out_specs, check_vma=False)
```

time: 717 us -> 496 us (0.69)
  matrix products: 337 us -> 0 us
  Pallas kernels: 0 us -> 311 us
  local copies, waits for them, and re-layouts: 140 us -> 13.2 us
  other arithmetic: 124 us -> 25.8 us
  waiting for transfers between devices: 59.3 us -> 97 us
    dot_general x33 -> x0, matrix products: 337 us -> none  [the longest x5 86.5 us: linear(): jnp.einsum('...i,ij->...j', values, matrix, preferred_element_type=jnp.fl...]
    pallas_call x0 -> x5, Pallas kernels: none -> 311 us  [the longest x1 144 us: run_forward(): pl.pallas_call(forward_kernel, grid_spec=pltpu.PrefetchScalarGridSpec(num...]
    reshape x8 -> x1, local copies, waits for them, and re-layouts: 71.3 us -> 0.01 us  [shards(): extra.reshape(2, 8, WIDTH)]
    reduce_sum x17 -> x1, other arithmetic: 48.4 us -> 0.64 us  [shards(): jnp.sum(jnp.where(own_place[None, :] == places[:, None], places[None, :],...]
    convert_element_type x11 -> x7, other arithmetic: 47.7 us -> 9.48 us  [the longest x1 2.56 us: shards(): grad_w_fc1.astype(f32)]
    ppermute x14, waiting for transfers between devices: 41.1 us -> 62.9 us  [reduce_shards(): lax.ppermute(lax.dynamic_index_in_dim(parts, own ^ offset, 0, False), ('d...]
    convert_element_type x6 -> x0, local copies, waits for them, and re-layouts: 19.5 us -> none  [the longest x1 9.72 us: shards(): mixed_l = merge_heads(mixed_l).astype(jnp.bfloat16)]
    unnamed x177 -> x16, local copies, waits for them, and re-layouts: 19.2 us -> 2.34 us
  transfers between devices with their start and end apart: 30 -> 30, of which waited for: 13 -> 14; matrix products, arithmetic and copies ran while one was open for 81% -> 5% of each run, Pallas kernels for 0% -> 30%
where the time goes in v2:
time: 496 us; the launch traced here: 495 us
  Pallas kernels  311 us (63%)
  waiting for transfers between devices  97 us (20%)
  starting transfers between devices  46.2 us (9%)
  other arithmetic  25.8 us (5%)
  local copies, waits for them, and re-layouts  13.2 us (3%)
    pallas_call x1, Pallas kernels, run_forward(): pl.pallas_call(forward_kernel, grid_spec=pltpu.PrefetchScalarGridSpec(num...  144 us
    pallas_call x1, Pallas kernels, run_back_attention(): pl.pallas_call(back_attention_kernel, grid_spec=pltpu.PrefetchScalarGridS...  103 us
    ppermute x14, waiting for transfers between devices, reduce_shards(): lax.ppermute(lax.dynamic_index_in_dim(parts, own ^ offset, 0, False), ('d...  62.9 us
    pallas_call x1, Pallas kernels, run_back_mlp(): pl.pallas_call(back_mlp_kernel, grid_spec=pltpu.PrefetchScalarGridSpec(nu...  54.5 us
    ppermute x14, waiting for transfers between devices, gather_shards(): got = [lax.ppermute(rows, ('dp', 'img'), pairs) for offset, pairs in moves]  34.1 us
    ppermute x14, starting transfers between devices, gather_shards(): got = [lax.ppermute(rows, ('dp', 'img'), pairs) for offset, pairs in moves]  17.4 us
    ppermute x14, starting transfers between devices, reduce_shards(): lax.ppermute(lax.dynamic_index_in_dim(parts, own ^ offset, 0, False), ('d...  15.4 us
    all_to_all x2, starting transfers between devices, swap_tiles(): lax.all_to_all(tiles_sent, 'dp', split_axis=0, concat_axis=0, tiled=True)  13.4 us
  transfers between devices with their start and end apart: 30, of which 14 were waited for; matrix products, arithmetic and copies ran while one was open for 5% of the time, Pallas kernels for 30%

profile of v2, /device:TPU:0, one launch (start us, length us, event | category | flops | bytes accessed | tf_op | source)
XLA Modules:
  0.0 495.2 jit_solution(8982444050012186760)
XLA Ops:
  2.6 4.7 deal.1
  7.3 7.4 %all-to-all-start.1 = ((bf16[8,400,512]{2,1,0:T(8,128)(2,1)}), bf16[8,400,512]{2,1,0:T(8,128)(2,1)S(1)}, u32[]{:S(2)}, u32[]{:S(2)}) async-start(bf16[8,400,512]{2,1,0:T(8,128)(2,1)} %deal.1), calls=%async_computation.1 | async-start | bytes 6553600 | tf_op jit(solution)/shard_map/all_to_all | solution.py:609
  21.2 144.5 %forward.1 = (bf16[8,400,512]{2,1,0:T(8,128)(2,1)}, bf16[64,64,1536]{2,1,0:T(8,128)(2,1)}, bf16[64,64,1024]{2,1,0:T(8,128)(2,1)}, bf16[64,64,512]{2,1,0:T(8,128)...) custom-call(s32[64]{0:T(128)} %select_reduce_fusion.1.order_ref, ...), custom_call_target="tpu_custom_call" | custom-call | flops 30000001024 | bytes 60000000 | tf_op jit(solution)/shard_map/forward/pallas_call | solution.py:258
  167.4 54.5 %back_mlp.1 = (f32[3584,512]{1,0:T(8,128)}, bf16[64,64,512]{2,1,0:T(8,128)(2,1)}, bf16[4096,512]{1,0:T(8,128)(2,1)}, f32[512,512]{1,0:T(8,128)}, f32[8,512]{1,0:T(8,128)}, /*index=5*/f32[8,2048]{1,0:T(8,128)}) custom-call(f32[1]{0:T(128)} %bitcast.3.keep_ref, bf16[8,400,512]{2,1,0:T(8,128)(2,1)} %copy-done, f32[3584,512]{1,0:T(8,128)} %get-tuple-element.58.after_ref, ...), custom_call_target="tpu_custom_call" | custom-call | flops 40000000000 | bytes 60000000 | tf_op jit(solution)/shard_map/back_mlp/pallas_call | solution.py:348
  221.9 103.0 %back_attention.1 = (bf16[8,392,512]{2,1,0:T(8,128)(2,1)}, bf16[64,512]{1,0:T(8,128)(2,1)}, bf16[2048,512]{1,0:T(8,128)(2,1)}, f32[8,512]{1,0:T(8,128)}) custom-call(s32[64]{0:T(128)} %select_reduce_fusion.1.order_ref, f32[1]{0:T(128)} %bitcast.3.keep_ref, bf16[64,64,1536]{2,1,0:T(8,128)(2,1)} %get-tuple-element.55.qkv_ref, ...), custom_call_target="tpu_custom_call" | custom-call | flops 30000001024 | bytes 60000000 | tf_op jit(solution)/shard_map/back_attention/pallas_call | solution.py:467
  329.4 6.0 %all-to-all-start = ((bf16[8,400,512]{2,1,0:T(8,128)(2,1)}), bf16[8,400,512]{2,1,0:T(8,128)(2,1)}, u32[]{:S(2)}, u32[]{:S(2)}) async-start(bf16[8,400,512]{2,1,0:T(8,128)(2,1)} %get-tuple-element.52), calls=%async_computation | async-start | bytes 6553600 | tf_op jit(solution)/shard_map/all_to_all | solution.py:609
  335.4 3.0 dynamic-slice_bitcast_fusion
  340.3 2.8 collective-permute-start.3
  343.8 26.4 %collective-permute-done.3 = bf16[288,512]{1,0:T(8,128)(2,1)S(1)} collective-permute-done((bf16[288,512]{1,0:T(8,128)(2,1)S(1)}, bf16[288,512]{1,0:T(8,128)(2,1)S(1)}, u32[]{:S(2)}, u32[]{:S(2)}) %collective-permute-start.3) | collective-permute-done | bytes 294944 | tf_op jit(solution)/shard_map/ppermute | solution.py:527
  370.3 15.8 %collective-permute-done.2 = bf16[288,512]{1,0:T(8,128)(2,1)S(1)} collective-permute-done((bf16[288,512]{1,0:T(8,128)(2,1)S(1)}, bf16[288,512]{1,0:T(8,128)(2,1)S(1)}, u32[]{:S(2)}, u32[]{:S(2)}) %collective-permute-start.2) | collective-permute-done | bytes 294944 | tf_op jit(solution)/shard_map/ppermute | solution.py:527
  386.3 3.4 collective-permute-start.6
  390.8 2.8 fusion.1
  398.0 17.8 %collective-permute-done.5 = bf16[72,512]{1,0:T(8,128)(2,1)S(1)} collective-permute-done((bf16[72,512]{1,0:T(8,128)(2,1)S(1)}, bf16[72,512]{1,0:T(8,128)(2,1)S(1)}, u32[]{:S(2)}, u32[]{:S(2)}) %collective-permute-start.5) | collective-permute-done | bytes 73760 | tf_op jit(solution)/shard_map/ppermute | solution.py:527
  418.7 3.5 collective-permute-done.7
  422.2 2.7 collective-permute-start.9
  438.3 3.3 collective-permute-done.11
  444.7 2.7 collective-permute-start.21
  449.4 2.8 collective-permute-done.21
  452.1 3.9 collective-permute-done.22
  456.9 3.2 collective-permute-start.24
  461.8 4.6 collect.1
  466.5 6.8 %collective-permute-done.24 = bf16[512,512]{1,0:T(8,128)(2,1)S(1)} collective-permute-done((bf16[512,512]{1,0:T(8,128)(2,1)}, bf16[512,512]{1,0:T(8,128)(2,1)S(1)}, u32[]{:S(2)}, u32[]{:S(2)}) %collective-permute-start.24) | collective-permute-done | bytes 524320 | tf_op jit(solution)/shard_map/ppermute | solution.py:542
  473.3 9.4 %collective-permute-done.25 = bf16[512,512]{1,0:T(8,128)(2,1)S(1)} collective-permute-done((bf16[512,512]{1,0:T(8,128)(2,1)}, bf16[512,512]{1,0:T(8,128)(2,1)S(1)}, u32[]{:S(2)}, u32[]{:S(2)}) %collective-permute-start.25) | collective-permute-done | bytes 524320 | tf_op jit(solution)/shard_map/ppermute | solution.py:542
  492.6 2.6 maximum_convert_fusion
  (125 shorter events, 55.7 us)
Async XLA Ops:
  7.3 158.4 %all-to-all-start.1 = ((bf16[8,400,512]{2,1,0:T(8,128)(2,1)}), bf16[8,400,512]{2,1,0:T(8,128)(2,1)S(1)}, u32[]{:S(2)}, u32[]{:S(2)}) async-start(bf16[8,400,512]{2,1,0:T(8,128)(2,1)} %deal.1), calls=%async_computation.1 | async-start | bytes 6553600 | tf_op jit(solution)/shard_map/all_to_all | solution.py:609
  329.3 9.3 %collective-permute-start = (bf16[1152,512]{1,0:T(8,128)(2,1)S(1)}, bf16[1152,512]{1,0:T(8,128)(2,1)}, u32[]{:S(2)}, u32[]{:S(2)}) collective-permute-start(bf16[1152,512]{1,0:T(8,128)(2,1)S(1)} %dynamic-slice_bitcast_fusion.1), channel_id=1, source_target_pairs={{0,1},{1,0},{2,3},{3,2},{4,5},{5,4},{6,7},{7,6},{8,9},{9,8},{10,11... | collective-permute-start | bytes 3538952 | tf_op jit(solution)/shard_map/ppermute | solution.py:527
  329.4 132.5 %all-to-all-start = ((bf16[8,400,512]{2,1,0:T(8,128)(2,1)}), bf16[8,400,512]{2,1,0:T(8,128)(2,1)}, u32[]{:S(2)}, u32[]{:S(2)}) async-start(bf16[8,400,512]{2,1,0:T(8,128)(2,1)} %get-tuple-element.52), calls=%async_computation | async-start | bytes 6553600 | tf_op jit(solution)/shard_map/all_to_all | solution.py:609
  338.4 52.4 %collective-permute-start.14 = (bf16[2048,512]{1,0:T(8,128)(2,1)}, bf16[2048,512]{1,0:T(8,128)(2,1)}, u32[]{:S(2)}, u32[]{:S(2)}) collective-permute-start(bf16[2048,512]{1,0:T(8,128)(2,1)} %dynamic-slice_bitcast_fusion), channel_id=1, source_target_pairs={{0,1},{1,0},{2,3},{3,2},{4,5},{5,4},{6,7},{7,6},{8,9},{9,8},{10,11... | collective-permute-start | bytes 6291464 | tf_op jit(solution)/shard_map/ppermute | solution.py:527
  340.3 30.0 %collective-permute-start.3 = (bf16[288,512]{1,0:T(8,128)(2,1)S(1)}, bf16[288,512]{1,0:T(8,128)(2,1)S(1)}, u32[]{:S(2)}, u32[]{:S(2)}) collective-permute-start(bf16[288,512]{1,0:T(8,128)(2,1)S(1)} %get-tuple-element.99), channel_id=1, source_target_pairs={{0,6},{1,7},{2,4},{3,5},{4,2},{5,3},{6,0},{7,1},{8,14},{9,15},{10,... | collective-permute-start | bytes 884744 | tf_op jit(solution)/shard_map/ppermute | solution.py:527
  343.1 43.0 %collective-permute-start.2 = (bf16[288,512]{1,0:T(8,128)(2,1)S(1)}, bf16[288,512]{1,0:T(8,128)(2,1)S(1)}, u32[]{:S(2)}, u32[]{:S(2)}) collective-permute-start(bf16[288,512]{1,0:T(8,128)(2,1)S(1)} %get-tuple-element.100), channel_id=1, source_target_pairs={{0,4},{1,5},{2,6},{3,7},{4,0},{5,1},{6,2},{7,3},{8,12},{9,13},{10,... | collective-permute-start | bytes 884744 | tf_op jit(solution)/shard_map/ppermute | solution.py:527
  343.3 42.8 %collective-permute-start.1 = (bf16[288,512]{1,0:T(8,128)(2,1)S(1)}, bf16[288,512]{1,0:T(8,128)(2,1)S(1)}, u32[]{:S(2)}, u32[]{:S(2)}) collective-permute-start(bf16[288,512]{1,0:T(8,128)(2,1)S(1)} %get-tuple-element.98), channel_id=1, source_target_pairs={{0,2},{1,3},{2,0},{3,1},{4,6},{5,7},{6,4},{7,5},{8,10},{9,11},{10,... | collective-permute-start | bytes 884744 | tf_op jit(solution)/shard_map/ppermute | solution.py:527
  386.3 11.2 %collective-permute-start.6 = (bf16[72,512]{1,0:T(8,128)(2,1)S(1)}, bf16[72,512]{1,0:T(8,128)(2,1)S(1)}, u32[]{:S(2)}, u32[]{:S(2)}) collective-permute-start(bf16[72,512]{1,0:T(8,128)(2,1)S(1)} %get-tuple-element.113), channel_id=1, source_target_pairs={{0,24},{1,25},{2,26},{3,27},{4,28},{5,29},{6,30},{7,31},{8,16},{9,... | collective-permute-start | bytes 221192 | tf_op jit(solution)/shard_map/ppermute | solution.py:527
  389.7 26.2 %collective-permute-start.5 = (bf16[72,512]{1,0:T(8,128)(2,1)S(1)}, bf16[72,512]{1,0:T(8,128)(2,1)S(1)}, u32[]{:S(2)}, u32[]{:S(2)}) collective-permute-start(bf16[72,512]{1,0:T(8,128)(2,1)S(1)} %get-tuple-element.114), channel_id=1, source_target_pairs={{0,16},{1,17},{2,18},{3,19},{4,20},{5,21},{6,22},{7,23},{8,24},{9,... | collective-permute-start | bytes 221192 | tf_op jit(solution)/shard_map/ppermute | solution.py:527
  389.7 26.2 %collective-permute-start.4 = (bf16[72,512]{1,0:T(8,128)(2,1)S(1)}, bf16[72,512]{1,0:T(8,128)(2,1)S(1)}, u32[]{:S(2)}, u32[]{:S(2)}) collective-permute-start(bf16[72,512]{1,0:T(8,128)(2,1)S(1)} %get-tuple-element.112), channel_id=1, source_target_pairs={{0,8},{1,9},{2,10},{3,11},{4,12},{5,13},{6,14},{7,15},{8,0},{9,1},... | collective-permute-start | bytes 221192 | tf_op jit(solution)/shard_map/ppermute | solution.py:527
  394.5 35.2 %collective-permute-start.17 = (bf16[512,512]{1,0:T(8,128)(2,1)}, bf16[512,512]{1,0:T(8,128)(2,1)}, u32[]{:S(2)}, u32[]{:S(2)}) collective-permute-start(bf16[512,512]{1,0:T(8,128)(2,1)} %get-tuple-element.92), channel_id=1, source_target_pairs={{0,6},{1,7},{2,4},{3,5},{4,2},{5,3},{6,0},{7,1},{8,14},{9,15},{10,... | collective-permute-start | bytes 1572872 | tf_op jit(solution)/shard_map/ppermute | solution.py:527
  395.0 35.9 %collective-permute-start.16 = (bf16[512,512]{1,0:T(8,128)(2,1)S(1)}, bf16[512,512]{1,0:T(8,128)(2,1)}, u32[]{:S(2)}, u32[]{:S(2)}) collective-permute-start(bf16[512,512]{1,0:T(8,128)(2,1)S(1)} %get-tuple-element.93), channel_id=1, source_target_pairs={{0,4},{1,5},{2,6},{3,7},{4,0},{5,1},{6,2},{7,3},{8,12},{9,13},{10,... | collective-permute-start | bytes 1572872 | tf_op jit(solution)/shard_map/ppermute | solution.py:527
  397.5 33.4 %collective-permute-start.15 = (bf16[512,512]{1,0:T(8,128)(2,1)S(1)}, bf16[512,512]{1,0:T(8,128)(2,1)}, u32[]{:S(2)}, u32[]{:S(2)}) collective-permute-start(bf16[512,512]{1,0:T(8,128)(2,1)S(1)} %get-tuple-element.91), channel_id=1, source_target_pairs={{0,2},{1,3},{2,0},{3,1},{4,6},{5,7},{6,4},{7,5},{8,10},{9,11},{10,... | collective-permute-start | bytes 1572872 | tf_op jit(solution)/shard_map/ppermute | solution.py:527
  427.3 10.9 %collective-permute-start.10 = (bf16[288,512]{1,0:T(8,128)(2,1)S(1)}, bf16[288,512]{1,0:T(8,128)(2,1)S(1)}, u32[]{:S(2)}, u32[]{:S(2)}) collective-permute-start(bf16[288,512]{1,0:T(8,128)(2,1)S(1)} %pad_maximum_fusion.4), channel_id=1, source_target_pairs={{0,6},{1,7},{2,4},{3,5},{4,2},{5,3},{6,0},{7,1},{8,14},{9,15},{10,... | collective-permute-start | bytes 884744 | tf_op jit(solution)/shard_map/ppermute | solution.py:542
  429.3 12.3 %collective-permute-start.11 = (bf16[288,512]{1,0:T(8,128)(2,1)S(1)}, bf16[288,512]{1,0:T(8,128)(2,1)S(1)}, u32[]{:S(2)}, u32[]{:S(2)}) collective-permute-start(bf16[288,512]{1,0:T(8,128)(2,1)S(1)} %pad_maximum_fusion.4), channel_id=1, source_target_pairs={{0,4},{1,5},{2,6},{3,7},{4,0},{5,1},{6,2},{7,3},{8,12},{9,13},{10,... | collective-permute-start | bytes 884744 | tf_op jit(solution)/shard_map/ppermute | solution.py:542
  429.7 11.9 %collective-permute-start.12 = (bf16[288,512]{1,0:T(8,128)(2,1)S(1)}, bf16[288,512]{1,0:T(8,128)(2,1)S(1)}, u32[]{:S(2)}, u32[]{:S(2)}) collective-permute-start(bf16[288,512]{1,0:T(8,128)(2,1)S(1)} %pad_maximum_fusion.4), channel_id=1, source_target_pairs={{0,2},{1,3},{2,0},{3,1},{4,6},{5,7},{6,4},{7,5},{8,10},{9,11},{10,... | collective-permute-start | bytes 884744 | tf_op jit(solution)/shard_map/ppermute | solution.py:542
  432.6 9.2 %collective-permute-start.20 = (bf16[128,512]{1,0:T(8,128)(2,1)S(1)}, bf16[128,512]{1,0:T(8,128)(2,1)S(1)}, u32[]{:S(2)}, u32[]{:S(2)}) collective-permute-start(bf16[128,512]{1,0:T(8,128)(2,1)S(1)} %get-tuple-element.106), channel_id=1, source_target_pairs={{0,24},{1,25},{2,26},{3,27},{4,28},{5,29},{6,30},{7,31},{8,16},{9,... | collective-permute-start | bytes 393224 | tf_op jit(solution)/shard_map/ppermute | solution.py:527
  434.9 9.2 %collective-permute-start.19 = (bf16[128,512]{1,0:T(8,128)(2,1)S(1)}, bf16[128,512]{1,0:T(8,128)(2,1)S(1)}, u32[]{:S(2)}, u32[]{:S(2)}) collective-permute-start(bf16[128,512]{1,0:T(8,128)(2,1)S(1)} %get-tuple-element.107), channel_id=1, source_target_pairs={{0,16},{1,17},{2,18},{3,19},{4,20},{5,21},{6,22},{7,23},{8,24},{9,... | collective-permute-start | bytes 393224 | tf_op jit(solution)/shard_map/ppermute | solution.py:527
  447.5 8.6 %collective-permute-start.22 = (bf16[128,512]{1,0:T(8,128)(2,1)S(1)}, bf16[128,512]{1,0:T(8,128)(2,1)S(1)}, u32[]{:S(2)}, u32[]{:S(2)}) collective-permute-start(bf16[128,512]{1,0:T(8,128)(2,1)S(1)} %fusion.12), channel_id=1, source_target_pairs={{0,16},{1,17},{2,18},{3,19},{4,20},{5,21},{6,22},{7,23},{8,24},{9,... | collective-permute-start | bytes 393224 | tf_op jit(solution)/shard_map/ppermute | solution.py:542
  447.5 8.6 %collective-permute-start.23 = (bf16[128,512]{1,0:T(8,128)(2,1)S(1)}, bf16[128,512]{1,0:T(8,128)(2,1)S(1)}, u32[]{:S(2)}, u32[]{:S(2)}) collective-permute-start(bf16[128,512]{1,0:T(8,128)(2,1)S(1)} %fusion.12), channel_id=1, source_target_pairs={{0,8},{1,9},{2,10},{3,11},{4,12},{5,13},{6,14},{7,15},{8,0},{9,1},... | collective-permute-start | bytes 393224 | tf_op jit(solution)/shard_map/ppermute | solution.py:542
  456.9 16.3 %collective-permute-start.24 = (bf16[512,512]{1,0:T(8,128)(2,1)}, bf16[512,512]{1,0:T(8,128)(2,1)S(1)}, u32[]{:S(2)}, u32[]{:S(2)}) collective-permute-start(bf16[512,512]{1,0:T(8,128)(2,1)} %pad_maximum_fusion.3), channel_id=1, source_target_pairs={{0,6},{1,7},{2,4},{3,5},{4,2},{5,3},{6,0},{7,1},{8,14},{9,15},{10,... | collective-permute-start | bytes 1572872 | tf_op jit(solution)/shard_map/ppermute | solution.py:542
  460.2 22.5 %collective-permute-start.25 = (bf16[512,512]{1,0:T(8,128)(2,1)}, bf16[512,512]{1,0:T(8,128)(2,1)S(1)}, u32[]{:S(2)}, u32[]{:S(2)}) collective-permute-start(bf16[512,512]{1,0:T(8,128)(2,1)} %pad_maximum_fusion.3), channel_id=1, source_target_pairs={{0,4},{1,5},{2,6},{3,7},{4,0},{5,1},{6,2},{7,3},{8,12},{9,13},{10,... | collective-permute-start | bytes 1572872 | tf_op jit(solution)/shard_map/ppermute | solution.py:542
  460.6 22.1 %collective-permute-start.26 = (bf16[512,512]{1,0:T(8,128)(2,1)}, bf16[512,512]{1,0:T(8,128)(2,1)S(1)}, u32[]{:S(2)}, u32[]{:S(2)}) collective-permute-start(bf16[512,512]{1,0:T(8,128)(2,1)} %pad_maximum_fusion.3), channel_id=1, source_target_pairs={{0,2},{1,3},{2,0},{3,1},{4,6},{5,7},{6,4},{7,5},{8,10},{9,11},{10,... | collective-permute-start | bytes 1572872 | tf_op jit(solution)/shard_map/ppermute | solution.py:542
  461.8 21.8 %collective-permute-start.13 = (bf16[1152,512]{1,0:T(8,128)(2,1)}, bf16[1152,512]{1,0:T(8,128)(2,1)}, u32[]{:S(2)}, u32[]{:S(2)}) collective-permute-start(bf16[1152,512]{1,0:T(8,128)(2,1)} %pad_maximum_fusion.2), channel_id=1, source_target_pairs={{0,1},{1,0},{2,3},{3,2},{4,5},{5,4},{6,7},{7,6},{8,9},{9,8},{10,11... | collective-permute-start | bytes 3538952 | tf_op jit(solution)/shard_map/ppermute | solution.py:542
  (13 other events, 188.2 us)

commit v3 on v2

--- a/solution.py
+++ b/solution.py
@@ -1,3 +1,4 @@
+import functools
 import math
 import jax
 import jax.numpy as jnp
@@ -21,7 +22,11 @@
 TALL = 56
 TILE = 8
 GROUP = 4
+GROUPS = HEADS // GROUP
+TOGETHER = 8
 LANES = 128
+FIRST_TILES = 2
+CHUNK = 512
 VMEM_LIMIT = 60 * 1024 * 1024
 
 f32 = jnp.float32
@@ -56,27 +61,35 @@
     return jnp.concatenate([turned[:SLOT], turned[SLOT:]], axis=1)
 
 
-def attend_group(queries, key_rows, values, bias, plain, mixed):
-    scores = dot_nt(key_rows, spread_heads(queries, plain)) + bias
-    highest = jnp.max(scores, axis=0, keepdims=True)
-    weighted = jnp.exp2((scores - highest) * (HDIM**-0.5 * math.log2(math.e)))
-    total = jnp.sum(weighted, axis=0, keepdims=True)
-    probs = (weighted * (1.0 / total)).astype(bf16)
-    return probs, dot(turn(probs), spread_heads(values, mixed))
-
-
-def attend_group_back(queries, key_rows, values, probs, grad_mixed, plain, mixed):
-    grad_wide = spread_heads(grad_mixed, plain)
-    grad_values = dot(probs, grad_wide)
-    grad_probs = dot_nt(values, grad_wide)
-    soft = probs.astype(f32)
-    weighted = soft * grad_probs
-    inner = jnp.sum(weighted, axis=0, keepdims=True)
-    grad_scores = (weighted - soft * inner).astype(bf16)
+def attend(items, plain, mixed):
+    scores = [dot_nt(key_rows, spread_heads(queries, plain)) for queries, key_rows, _, _ in items]
+    probs = []
+    for rows, (_, _, _, bias) in zip(scores, items):
+        rows = rows + bias
+        highest = jnp.max(rows, axis=0, keepdims=True)
+        weighted = jnp.exp2((rows - highest) * (HDIM**-0.5 * math.log2(math.e)))
+        total = jnp.sum(weighted, axis=0, keepdims=True)
+        probs.append((weighted * (1.0 / total)).astype(bf16))
+    turned = [turn(rows) for rows in probs]
+    outs = [dot(rows, spread_heads(item[2], mixed)) for rows, item in zip(turned, items)]
+    return probs, outs
+
+
+def attend_back(items, plain, mixed):
+    wide = [spread_heads(item[4], plain) for item in items]
+    grad_probs = [dot_nt(item[2], rows) for item, rows in zip(items, wide)]
+    grad_values = [dot(item[3], rows) for item, rows in zip(items, wide)]
+    scores = []
+    for rows, item in zip(grad_probs, items):
+        soft = item[3].astype(f32)
+        weighted = soft * rows
+        inner = jnp.sum(weighted, axis=0, keepdims=True)
+        scores.append((weighted - soft * inner).astype(bf16))
+    turned = [turn(rows) for rows in scores]
     factor = HDIM**-0.5
-    grad_keys = dot(grad_scores, spread_heads(queries, plain)) * factor
-    grad_queries = dot(turn(grad_scores), spread_heads(key_rows, mixed)) * factor
-    return grad_queries, grad_keys, grad_values
+    grad_keys = [dot(rows, spread_heads(item[0], plain)) * factor for rows, item in zip(scores, items)]
+    grad_queries = [dot(rows, spread_heads(item[1], mixed)) * factor for rows, item in zip(turned, items)]
+    return list(zip(grad_queries, grad_keys, grad_values))
 
 
 def normalize(rows):
@@ -108,42 +121,34 @@
     return jnp.sum(rows, axis=0, keepdims=True)
 
 
-def attend_window(qkv, bias, plain, mixed, put_probs):
-    outs = []
-    wide_bias = jnp.concatenate([bias, bias], axis=1)
-    for group in range(HEADS // GROUP):
-        at = group * LANES
-        probs, out = attend_group(
-            qkv[:, at : at + LANES],
-            qkv[:, WIDTH + at : WIDTH + at + LANES],
-            qkv[:, 2 * WIDTH + at : 2 * WIDTH + at + LANES],
-            wide_bias,
-            plain,
-            mixed,
-        )
-        put_probs(group, probs)
-        outs.append(out)
-    return jnp.concatenate(outs, axis=1)
-
-
-def attend_window_back(qkv, probs_of, grad_mixed, plain, mixed):
-    parts = []
-    for group in range(HEADS // GROUP):
-        at = group * LANES
-        parts.append(
-            attend_group_back(
-                qkv[:, at : at + LANES],
-                qkv[:, WIDTH + at : WIDTH + at + LANES],
-                qkv[:, 2 * WIDTH + at : 2 * WIDTH + at + LANES],
-                probs_of(group),
-                grad_mixed[:, at : at + LANES],
-                plain,
-                mixed,
+def attend_windows(windows, plain, mixed):
+    items = []
+    for qkv_of, bias, _, _ in windows:
+        wide = jnp.concatenate([bias, bias], axis=1)
+        for group in range(GROUPS):
+            items.append((qkv_of(group), qkv_of(GROUPS + group), qkv_of(2 * GROUPS + group), wide))
+    probs, outs = attend(items, plain, mixed)
+    for at, (_, _, put_probs, put_mixed) in enumerate(windows):
+        for group in range(GROUPS):
+            rows = probs[at * GROUPS + group]
+            put_probs(2 * group, rows[:, :LANES])
+            put_probs(2 * group + 1, rows[:, LANES:])
+            put_mixed(group, outs[at * GROUPS + group])
+
+
+def attend_windows_back(windows, plain, mixed):
+    items = []
+    for qkv_of, probs_of, grad_of, _ in windows:
+        for group in range(GROUPS):
+            probs = jnp.concatenate([probs_of(2 * group), probs_of(2 * group + 1)], axis=1)
+            items.append(
+                (qkv_of(group), qkv_of(GROUPS + group), qkv_of(2 * GROUPS + group), probs, grad_of(group))
             )
-        )
-    return jnp.concatenate(
-        [parts[g][which] for which in range(3) for g in range(len(parts))], axis=1
-    ).astype(bf16)
+    grads = attend_back(items, plain, mixed)
+    for at, (_, _, _, put_grad) in enumerate(windows):
+        for group in range(GROUPS):
+            for part in range(3):
+                put_grad(part * GROUPS + group, grads[at * GROUPS + group][part].astype(bf16))
 
 
 def forward_kernel(
@@ -165,15 +170,20 @@
         region = regional_ref[...].astype(f32)
         unit, _ = normalize(region)
         region_norm = (unit * gain1_ref[...] + bias1_ref[...]).astype(bf16)
-        qkv_r_ref[...] = (dot(region_norm, w_qkv_ref[...]) + bias_qkv_ref[...]).astype(bf16)
-
-        def put(group, probs):
-            probs_r_ref[:, group * 2 * LANES : (group + 1) * 2 * LANES] = probs
-
-        region_mixed = attend_window(
-            qkv_r_ref[...], region_bias_ref[...], plain, mixed, put
-        ).astype(bf16)
-        mixed_r_ref[...] = region_mixed
+        region_qkv = (dot(region_norm, w_qkv_ref[...]) + bias_qkv_ref[...]).astype(bf16)
+        for at in range(3 * GROUPS):
+            qkv_r_ref[at] = region_qkv[:, at * LANES : (at + 1) * LANES]
+
+        def put_probs(at, probs):
+            probs_r_ref[at] = probs
+
+        def put_mixed(at, rows):
+            mixed_r_ref[:, at * LANES : (at + 1) * LANES] = rows.astype(bf16)
+
+        attend_windows(
+            [(lambda at: qkv_r_ref[at], region_bias_ref[...], put_probs, put_mixed)], plain, mixed
+        )
+        region_mixed = mixed_r_ref[...]
         region_mid = region + keep * (dot(region_mixed, w_out_ref[...]) + bias_out_ref[...])
         region_mid = region_mid.astype(bf16)
         row = lax.broadcasted_iota(jnp.int32, (TILE * SLOT, REGIONS), 0)
@@ -195,18 +205,25 @@
     for part in range(3):
         cols = slice(part * WIDTH, (part + 1) * WIDTH)
         qkv = dot(normed[...], w_qkv_ref[:, cols]) + bias_qkv_ref[:, cols]
-        qkv_ref[:, :, cols] = qkv.astype(bf16).reshape(TILE, SLOT, WIDTH)
-
-    def one(at, carry):
-        def put(group, probs):
-            probs_ref[at, :, group * 2 * LANES : (group + 1) * 2 * LANES] = probs
-
-        mixed_rows[at] = attend_window(
-            qkv_ref[at], window_bias_ref[order_ref[step * TILE + at]], plain, mixed, put
-        )
+        qkv = qkv.astype(bf16).reshape(TILE, SLOT, WIDTH)
+        for group in range(GROUPS):
+            qkv_ref[:, part * GROUPS + group] = qkv[:, :, group * LANES : (group + 1) * LANES]
+
+    def some(batch, carry):
+        def window(at):
+            def put_probs(place, probs):
+                probs_ref[at, place] = probs
+
+            def put_mixed(group, rows):
+                mixed_rows[at, :, group * LANES : (group + 1) * LANES] = rows
+
+            bias = window_bias_ref[order_ref[step * TILE + at]]
+            return lambda place: qkv_ref[at, place], bias, put_probs, put_mixed
+
+        attend_windows([window(batch * TOGETHER + at) for at in range(TOGETHER)], plain, mixed)
         return carry
 
-    lax.fori_loop(0, TILE, one, 0)
+    lax.fori_loop(0, TILE // TOGETHER, some, 0)
     rows_count = TILE * TALL
     mixed_low = mixed_rows[:, :TALL].reshape(rows_count, WIDTH).astype(bf16)
     mixed_ref[...] = mixed_low
@@ -216,10 +233,13 @@
     unit, _ = normalize(after)
     mlp_norm = (unit * gain2_ref[...] + bias2_ref[...]).astype(bf16)
     total = after + keep * bias_fc2_ref[...]
-    chunk = 512
-    for at in range(0, w_fc1_ref.shape[1], chunk):
-        cols = slice(at, at + chunk)
-        hidden, slope = gelu_pair(dot(mlp_norm, w_fc1_ref[:, cols]) + bias_fc1_ref[:, cols])
+    chunks = [slice(at, at + CHUNK) for at in range(0, w_fc1_ref.shape[1], CHUNK)]
+    ahead = dot(mlp_norm, w_fc1_ref[:, chunks[0]])
+    for at, cols in enumerate(chunks):
+        pre_act = ahead + bias_fc1_ref[:, cols]
+        if at + 1 < len(chunks):
+            ahead = dot(mlp_norm, w_fc1_ref[:, chunks[at + 1]])
+        hidden, slope = gelu_pair(pre_act)
         hidden = hidden.astype(bf16)
         hidden_ref[:, cols] = hidden
         slope_ref[:, cols] = slope.astype(bf16)
@@ -246,15 +266,19 @@
             gain1, bias1, w_qkv, bias_qkv, w_out, bias_out, gain2, bias2, w_fc1, bias_fc1, w_fc2, bias_fc2)
     outs = [
         ((steps, compact, WIDTH), bf16, (1, compact, WIDTH)),
-        ((windows, SLOT, 3 * WIDTH), bf16, (TILE, SLOT, 3 * WIDTH)),
-        ((windows, SLOT, HEADS * SLOT), bf16, (TILE, SLOT, HEADS * SLOT)),
+        ((windows, 3 * GROUPS, SLOT, LANES), bf16, (TILE, 3 * GROUPS, SLOT, LANES)),
+        ((windows, 2 * GROUPS, SLOT, LANES), bf16, (TILE, 2 * GROUPS, SLOT, LANES)),
         ((windows, SLOT, WIDTH), bf16, (TILE, SLOT, WIDTH)),
         ((steps * rows, WIDTH), bf16, (rows, WIDTH)),
         ((steps * rows, WIDTH), f32, (rows, WIDTH)),
         ((steps * rows, hidden), bf16, (rows, hidden)),
         ((steps * rows, hidden), bf16, (rows, hidden)),
     ]
-    fixed = [((REGIONS, 3 * WIDTH), bf16), ((REGIONS, HEADS * SLOT), bf16), ((REGIONS, WIDTH), bf16)]
+    fixed = [
+        ((3 * GROUPS, REGIONS, LANES), bf16),
+        ((2 * GROUPS, REGIONS, LANES), bf16),
+        ((REGIONS, WIDTH), bf16),
+    ]
     return pl.pallas_call(
         forward_kernel,
         grid_spec=pltpu.PrefetchScalarGridSpec(
@@ -301,12 +325,14 @@
     grad_turned = grad_mlp.T
     sums[0:1] += column_sum(grad_mlp.astype(f32))
     grad_norm = jnp.zeros(after_ref.shape, f32)
-    chunk = 512
-    for at in range(0, w_fc1_ref.shape[1], chunk):
-        cols = slice(at, at + chunk)
-        grad_hidden = dot_nt(grad_mlp, w_fc2_ref[cols, :])
+    chunks = [slice(at, at + CHUNK) for at in range(0, w_fc1_ref.shape[1], CHUNK)]
+    ahead = dot_nt(grad_mlp, w_fc2_ref[chunks[0], :])
+    for at, cols in enumerate(chunks):
+        grad_hidden = ahead
+        if at + 1 < len(chunks):
+            ahead = dot_nt(grad_mlp, w_fc2_ref[chunks[at + 1], :])
+        sum_fc2[:, cols] += dot(grad_turned, hidden_ref[:, cols])
         grad_pre = (slope_ref[:, cols].astype(f32) * grad_hidden).astype(bf16)
-        sum_fc2[:, cols] += dot(grad_turned, hidden_ref[:, cols])
         sum_fc1[:, cols] += dot(norm_turned, grad_pre)
         sum_hidden[0:1, cols] += column_sum(grad_pre.astype(f32))
         grad_norm = grad_norm + dot_nt(grad_pre, w_fc1_ref[:, cols])
@@ -319,7 +345,9 @@
     sum_out[...] += dot(mixed_ref[...].T, grad_branch)
     grad_mixed = dot_nt(grad_branch, w_out_ref[...]).reshape(TILE, TALL, WIDTH)
     empty = jnp.zeros((TILE, SLOT - TALL, WIDTH), f32)
-    grad_mixed_ref[...] = jnp.concatenate([grad_mixed, empty], axis=1).astype(bf16)
+    grad_mixed = jnp.concatenate([grad_mixed, empty], axis=1).astype(bf16)
+    for group in range(GROUPS):
+        grad_mixed_ref[:, group] = grad_mixed[:, :, group * LANES : (group + 1) * LANES]
 
     @pl.when(step == last)
     def finish():
@@ -342,7 +370,7 @@
     fixed = (stretch, gain2, bias2, w_fc1, w_fc2, w_out)
     outs = [
         ((steps * rows, WIDTH), f32, (rows, WIDTH)),
-        ((steps * TILE, SLOT, WIDTH), bf16, (TILE, SLOT, WIDTH)),
+        ((steps * TILE, GROUPS, SLOT, LANES), bf16, (TILE, GROUPS, SLOT, LANES)),
     ]
     whole_outs = [((2 * units, WIDTH), bf16), ((WIDTH, WIDTH), f32), ((8, WIDTH), f32), ((8, units), f32)]
     return pl.pallas_call(
@@ -371,70 +399,92 @@
 
 
 def back_attention_kernel(
-    order_ref, keep_ref,
-    qkv_ref, probs_ref, joined_ref, grad_mixed_ref, grad_after_ref, grad_out_ref,
-    gather_ref, plain_ref, mixed_mask_ref, regional_ref, qkv_r_ref, probs_r_ref, mixed_r_ref,
-    gain1_ref, bias1_ref, w_qkv_ref, w_out_ref,
-    tokens_out_ref, regional_out_ref, late_ref, small_ref,
-    windows, grads, sum_qkv, sums, region_grad,
+    first, last, order_ref, keep_ref,
+    qkv_ref, probs_ref, joined_ref, grad_mixed_ref, grad_after_ref,
+    plain_ref, mixed_mask_ref, head_ref, gain1_ref, bias1_ref, *refs,
 ):
+    if first:
+        held_in = ()
+    else:
+        held_in, refs = refs[:4], refs[5:]
+    if last:
+        (grad_out_ref, order_row_ref, regional_ref, qkv_r_ref, probs_r_ref, mixed_r_ref, w_qkv_ref, w_out_ref), refs = (
+            refs[:8],
+            refs[8:],
+        )
+        grad_qkv_ref, late_ref, regional_out_ref, small_ref, sum_qkv, sums, heads, after_heads = refs
+    else:
+        grad_qkv_ref, sum_qkv, sums, heads, after_heads = refs
     step = pl.program_id(0)
-    last = pl.num_programs(0) - 1
-    keep = keep_ref[0]
     plain = plain_ref[...]
     mixed = mixed_mask_ref[...]
-    gain1 = gain1_ref[...]
 
     @pl.when(step == 0)
-    def clear():
-        sum_qkv[...] = jnp.zeros_like(sum_qkv)
-        sums[...] = jnp.zeros_like(sums)
-
-    def one(at, carry):
-        def probs_of(group):
-            return probs_ref[at, :, group * 2 * LANES : (group + 1) * 2 * LANES]
-
-        grads[pl.ds(pl.multiple_of(at * SLOT, SLOT), SLOT)] = attend_window_back(
-            qkv_ref[at], probs_of, grad_mixed_ref[at], plain, mixed
-        )
+    def begin():
+        for at, ref in enumerate((sum_qkv, sums, heads, after_heads)):
+            ref[...] = jnp.zeros_like(ref) if first else held_in[at][...]
+
+    def some(batch, carry):
+        def window(at):
+            rows = pl.ds(pl.multiple_of(at * SLOT, SLOT), SLOT)
+
+            def put_grad(place, values):
+                grad_qkv_ref[rows, place * LANES : (place + 1) * LANES] = values
+
+            return (
+                lambda place: qkv_ref[at, place],
+                lambda place: probs_ref[at, place],
+                lambda place: grad_mixed_ref[at, place],
+                put_grad,
+            )
+
+        attend_windows_back([window(batch * TOGETHER + at) for at in range(TOGETHER)], plain, mixed)
         return carry
 
-    lax.fori_loop(0, TILE, one, 0)
-    joined = joined_ref[...].astype(f32).reshape(TILE * SLOT, WIDTH)
-    unit, scale = normalize(joined)
-    normed = (unit * gain1 + bias1_ref[...]).astype(bf16)
-    grad_qkv = grads[...]
+    lax.fori_loop(0, TILE // TOGETHER, some, 0)
+    joined = joined_ref[...].reshape(TILE * SLOT, WIDTH)
+    unit, _ = normalize(joined.astype(f32))
+    normed = (unit * gain1_ref[...] + bias1_ref[...]).astype(bf16)
+    grad_qkv = grad_qkv_ref[...]
     sum_qkv[...] += dot(normed.T, grad_qkv)
     sums[2:3] += column_sum(grad_qkv[:, :WIDTH].astype(f32))
     sums[3:4] += column_sum(grad_qkv[:, 2 * WIDTH :].astype(f32))
-    grad_normed = dot_nt(grad_qkv, w_qkv_ref[...])
-    sums[0:1] += column_sum(grad_normed * unit)
-    sums[1:2] += column_sum(grad_normed)
-    grad_in = normalize_back(grad_normed * gain1, unit, scale)
-    for at in range(TILE):
-        rows = grad_in[at * SLOT : at * SLOT + TALL] + grad_after_ref[at * TALL : (at + 1) * TALL]
-        windows[order_ref[step * TILE + at], :TALL] = rows
-
-    @pl.when(step == last)
+    rows = pl.ds(pl.multiple_of((step + (0 if first else FIRST_TILES)) * TILE, TILE), TILE)
+    heads[rows, : 3 * WIDTH] = dot(head_ref[...], grad_qkv)
+    heads[rows, 3 * WIDTH :] = dot(head_ref[...], joined)
+    after_heads[rows] = jnp.concatenate(
+        [grad_after_ref[at * TALL : at * TALL + 1] for at in range(TILE)], axis=0
+    )
+    if not last:
+        return
+
+    @pl.when(step == pl.num_programs(0) - 1)
     def finish():
-        def relay(line, carry):
-            block = windows[pl.ds(line * TILE, TILE)][:, :TALL].reshape(TILE * TALL, WIDTH)
-            rows = dot(gather_ref[...], block.astype(bf16))
-            tokens_out_ref[line] = rows[: rows.shape[0] - TILE].astype(bf16)
-            region_grad[pl.ds(pl.multiple_of(line * TILE, TILE), TILE)] = rows[rows.shape[0] - TILE :]
-            return carry
-
-        lax.fori_loop(0, REG_SIDE, relay, 0)
-        came = region_grad[...]
+        keep = keep_ref[0]
+        gain1 = gain1_ref[...]
+        grad_normed = dot_nt(heads[:, : 3 * WIDTH].astype(bf16), w_qkv_ref[...])
+        unit, scale = normalize(heads[:, 3 * WIDTH :])
+        grad_mid = after_heads[...] + normalize_back(grad_normed * gain1, unit, scale)
+        windows = grad_mid.shape[0]
+        raster = lax.broadcasted_iota(jnp.int32, (windows, windows), 0)
+        came = dot((raster == order_row_ref[...]).astype(bf16), grad_mid.astype(bf16))
         grad_branch = (keep * came).astype(bf16)
         grad_mixed = dot_nt(grad_branch, w_out_ref[...]).astype(bf16)
-
-        def probs_of(group):
-            return probs_r_ref[:, group * 2 * LANES : (group + 1) * 2 * LANES]
-
-        grad_qkv_r = attend_window_back(qkv_r_ref[...], probs_of, grad_mixed, plain, mixed)
-        region = regional_ref[...].astype(f32)
-        unit_r, scale_r = normalize(region)
+        parts = {}
+        attend_windows_back(
+            [
+                (
+                    lambda place: qkv_r_ref[place],
+                    lambda place: probs_r_ref[place],
+                    lambda place: grad_mixed[:, place * LANES : (place + 1) * LANES],
+                    parts.__setitem__,
+                )
+            ],
+            plain,
+            mixed,
+        )
+        grad_qkv_r = jnp.concatenate([parts[place] for place in range(3 * GROUPS)], axis=1)
+        unit_r, scale_r = normalize(regional_ref[...].astype(f32))
         normed_r = (unit_r * gain1 + bias1_ref[...]).astype(bf16)
         total = sum_qkv[...] + dot(normed_r.T, grad_qkv_r)
         for part in range(3):
@@ -444,48 +494,130 @@
             grad_out_ref[...] + dot(mixed_r_ref[...].T, grad_branch)
         ).astype(bf16)
         grad_normed_r = dot_nt(grad_qkv_r, w_qkv_ref[...])
-        sums[0:1] += column_sum(grad_normed_r * unit_r)
-        sums[1:2] += column_sum(grad_normed_r)
-        sums[2:3] += column_sum(grad_qkv_r[:, :WIDTH].astype(f32))
-        sums[3:4] += column_sum(grad_qkv_r[:, 2 * WIDTH :].astype(f32))
-        sums[4:5] += column_sum(grad_branch.astype(f32))
+        small_ref[...] = sums[...]
+        small_ref[0:1] = column_sum(grad_normed_r * unit_r)
+        small_ref[1:2] = column_sum(grad_normed_r)
+        small_ref[2:3] += column_sum(grad_qkv_r[:, :WIDTH].astype(f32))
+        small_ref[3:4] += column_sum(grad_qkv_r[:, 2 * WIDTH :].astype(f32))
+        small_ref[4:5] = column_sum(grad_branch.astype(f32))
         regional_out_ref[...] = (
             came + normalize_back(grad_normed_r * gain1, unit_r, scale_r)
         ).astype(bf16)
-        small_ref[...] = sums[...]
-
-
-def run_back_attention(order, keep, qkv, probs, joined, grad_mixed, grad_after, grad_out, gather, plain, mixed,
-                       regional, qkv_r, probs_r, mixed_r, gain1, bias1, w_qkv, w_out):
-    windows = regional.shape[0]
+
+
+def run_back_attention(order, keep, qkv, probs, joined, grad_mixed, grad_after, plain, mixed, head, gain1, bias1,
+                       held=None, ending=None):
+    windows = qkv.shape[0]
     steps = windows // TILE
     rows = TILE * TALL
-    lines = gather.shape[0] - TILE
-    tiled = [(TILE, SLOT, 3 * WIDTH), (TILE, SLOT, HEADS * SLOT), (TILE, SLOT, WIDTH), (TILE, SLOT, WIDTH), (rows, WIDTH)]
-    fixed = (grad_out, gather, plain, mixed, regional, qkv_r, probs_r, mixed_r, gain1, bias1, w_qkv, w_out)
-    whole_outs = [((REG_SIDE, lines, WIDTH), bf16), ((windows, WIDTH), bf16), ((4 * WIDTH, WIDTH), bf16), ((8, WIDTH), f32)]
+    begin = 0 if held is None else FIRST_TILES
+    count = FIRST_TILES if held is None else steps - FIRST_TILES
+
+    def tile(shape):
+        return pl.BlockSpec(shape, lambda step, *_: (step + begin,) + (0,) * (len(shape) - 1))
+
+    tiled = [
+        (TILE, 3 * GROUPS, SLOT, LANES),
+        (TILE, 2 * GROUPS, SLOT, LANES),
+        (TILE, SLOT, WIDTH),
+        (TILE, GROUPS, SLOT, LANES),
+        (rows, WIDTH),
+    ]
+    fixed = [plain, mixed, head, gain1, bias1]
+    in_specs = [tile(b) for b in tiled] + [whole(a.shape) for a in fixed]
+    args = [qkv, probs, joined, grad_mixed, grad_after] + fixed
+    aliases = {}
+    if held is not None:
+        in_specs += [whole(a.shape) for a in held[:4]] + [pl.BlockSpec(memory_space=pl.ANY)]
+        args += list(held)
+        aliases = {2 + len(args) - 1: 0}
+    if ending is not None:
+        in_specs += [whole(a.shape) for a in ending]
+        args += list(ending)
+    held_shapes = [(WIDTH, 3 * WIDTH), (8, WIDTH), (windows, 4 * WIDTH), (windows, WIDTH)]
+    outs = [((steps * TILE * SLOT, 3 * WIDTH), bf16, tile((TILE * SLOT, 3 * WIDTH)))]
+    scratch = []
+    if ending is None:
+        outs += [(s, f32, whole(s)) for s in held_shapes]
+    else:
+        outs += [
+            ((4 * WIDTH, WIDTH), bf16, whole((4 * WIDTH, WIDTH))),
+            ((windows, WIDTH), bf16, whole((windows, WIDTH))),
+            ((8, WIDTH), f32, whole((8, WIDTH))),
+        ]
+        scratch = [pltpu.VMEM(s, f32) for s in held_shapes]
     return pl.pallas_call(
-        back_attention_kernel,
+        functools.partial(back_attention_kernel, held is None, ending is not None),
         grid_spec=pltpu.PrefetchScalarGridSpec(
             num_scalar_prefetch=2,
-            grid=(steps,),
-            in_specs=[tiles(b) for b in tiled] + [whole(a.shape) for a in fixed],
-            out_specs=[whole(s) for s, _ in whole_outs],
-            scratch_shapes=[
-                pltpu.VMEM((windows, SLOT, WIDTH), f32),
-                pltpu.VMEM((TILE * SLOT, 3 * WIDTH), bf16),
-                pltpu.VMEM((WIDTH, 3 * WIDTH), f32),
-                pltpu.VMEM((8, WIDTH), f32),
-                pltpu.VMEM((windows, WIDTH), f32),
-            ],
+            grid=(count,),
+            in_specs=in_specs,
+            out_specs=[spec for _, _, spec in outs],
+            scratch_shapes=scratch,
         ),
-        out_shape=[jax.ShapeDtypeStruct(s, d) for s, d in whole_outs],
+        out_shape=[jax.ShapeDtypeStruct(s, d) for s, d, _ in outs],
+        input_output_aliases=aliases,
         compiler_params=pltpu.CompilerParams(
             dimension_semantics=("arbitrary",), vmem_limit_bytes=VMEM_LIMIT
         ),
-        cost_estimate=pl.CostEstimate(flops=30_000_000_000, bytes_accessed=60_000_000, transcendentals=0),
+        cost_estimate=pl.CostEstimate(
+            flops=4_500_000_000 * count, bytes_accessed=5_000_000 * count, transcendentals=0
+        ),
         name="back_attention",
-    )(order, keep, qkv, probs, joined, grad_mixed, grad_after, *fixed)
+    )(order, keep, *args)
+
+
+def back_rows_kernel(
+    order_ref, grad_qkv_ref, joined_ref, grad_after_ref, gather_ref, gain1_ref, w_qkv_ref,
+    tokens_out_ref, small_ref, windows,
+):
+    step = pl.program_id(0)
+    gain1 = gain1_ref[...]
+
+    @pl.when(step == 0)
+    def clear():
+        small_ref[...] = jnp.zeros_like(small_ref)
+
+    unit, scale = normalize(joined_ref[...].astype(f32).reshape(TILE * SLOT, WIDTH))
+    grad_normed = dot_nt(grad_qkv_ref[...], w_qkv_ref[...])
+    small_ref[0:1] += column_sum(grad_normed * unit)
+    small_ref[1:2] += column_sum(grad_normed)
+    grad_in = normalize_back(grad_normed * gain1, unit, scale)
+    for at in range(TILE):
+        rows = grad_in[at * SLOT : at * SLOT + TALL] + grad_after_ref[at * TALL : (at + 1) * TALL]
+        windows[order_ref[step * TILE + at], :TALL] = rows
+
+    @pl.when(step == pl.num_programs(0) - 1)
+    def finish():
+        def relay(line, carry):
+            block = windows[pl.ds(line * TILE, TILE)][:, :TALL].reshape(TILE * TALL, WIDTH)
+            tokens_out_ref[line] = dot(gather_ref[...], block.astype(bf16)).astype(bf16)
+            return carry
+
+        lax.fori_loop(0, REG_SIDE, relay, 0)
+
+
+def run_back_rows(order, grad_qkv, joined, grad_after, gather, gain1, w_qkv):
+    windows = joined.shape[0]
+    tiled = [(TILE * SLOT, 3 * WIDTH), (TILE, SLOT, WIDTH), (TILE * TALL, WIDTH)]
+    fixed = (gather, gain1, w_qkv)
+    outs = [((REG_SIDE, gather.shape[0], WIDTH), bf16), ((8, WIDTH), f32)]
+    return pl.pallas_call(
+        back_rows_kernel,
+        grid_spec=pltpu.PrefetchScalarGridSpec(
+            num_scalar_prefetch=1,
+            grid=(windows // TILE,),
+            in_specs=[tiles(b) for b in tiled] + [whole(a.shape) for a in fixed],
+            out_specs=[whole(s) for s, _ in outs],
+            scratch_shapes=[pltpu.VMEM((windows, SLOT, WIDTH), f32)],
+        ),
+        out_shape=[jax.ShapeDtypeStruct(s, d) for s, d in outs],
+        compiler_params=pltpu.CompilerParams(
+            dimension_semantics=("arbitrary",), vmem_limit_bytes=VMEM_LIMIT
+        ),
+        cost_estimate=pl.CostEstimate(flops=15_000_000_000, bytes_accessed=30_000_000, transcendentals=0),
+        name="back_rows",
+    )(order, grad_qkv, joined, grad_after, *fixed)
 
 
 def band_to_windows(band_values, win_count):
@@ -519,40 +651,38 @@
     return own, moves
 
 
-def reduce_shards(rows):
-    for stage in reduce_stages():
-        own, moves = stage_peers(stage)
-        parts = rows.reshape((1 << len(stage), -1) + rows.shape[1:])
-        got = [
-            lax.ppermute(
-                lax.dynamic_index_in_dim(parts, own ^ offset, 0, False), ("dp", "img"), pairs
-            )
-            for offset, pairs in moves
-        ]
-        total = lax.dynamic_index_in_dim(parts, own, 0, False).astype(jnp.float32)
+def sum_stage(rows, stage):
+    own, moves = stage_peers(stage)
+    parts = rows.reshape((1 << len(stage), -1) + rows.shape[1:])
+    got = [
+        lax.ppermute(lax.dynamic_index_in_dim(parts, own ^ offset, 0, False), ("dp", "img"), pairs)
+        for offset, pairs in moves
+    ]
+    total = lax.dynamic_index_in_dim(parts, own, 0, False).astype(f32)
+    for piece in got:
+        total = total + piece.astype(f32)
+    return total.astype(bf16)
+
+
+def gather_stage(rows, stage):
+    own, moves = stage_peers(stage)
+    pieces = [rows] + [lax.ppermute(rows, ("dp", "img"), pairs) for _, pairs in moves]
+    ordered = []
+    for place in range(len(pieces)):
+        piece = pieces[0]
+        for offset in range(1, len(pieces)):
+            piece = jnp.where((own ^ place) == offset, pieces[offset], piece)
+        ordered.append(piece)
+    return jnp.concatenate(ordered, axis=0)
+
+
+def sum_small(rows, stages):
+    for stage in stages:
+        _, moves = stage_peers(stage)
+        got = [lax.ppermute(rows, ("dp", "img"), pairs) for _, pairs in moves]
         for piece in got:
-            total = total + piece.astype(jnp.float32)
-        rows = total.astype(jnp.bfloat16)
+            rows = rows + piece
     return rows
-
-
-def gather_shards(rows):
-    for stage in reversed(reduce_stages()):
-        own, moves = stage_peers(stage)
-        got = [lax.ppermute(rows, ("dp", "img"), pairs) for offset, pairs in moves]
-        pieces = [rows] + got
-        ordered = []
-        for place in range(len(pieces)):
-            piece = pieces[0]
-            for offset in range(1, len(pieces)):
-                piece = jnp.where((own ^ place) == offset, pieces[offset], piece)
-            ordered.append(piece)
-        rows = jnp.concatenate(ordered, axis=0)
-    return rows
-
-
-def all_sum(rows):
-    return gather_shards(reduce_shards(rows.astype(jnp.bfloat16)))
 
 
 def deal_kernel(pick_ref, region_ref, local_ref, out_ref):
@@ -622,13 +752,14 @@
     band = TILE * WIN_SIDE * WIN_SIDE
     spread = np.zeros((TILE * SLOT, band), np.float32)
     spread[window * SLOT + 1 + place, raster] = 1
-    gather = np.zeros((band + TILE, TILE * TALL), np.float32)
+    gather = np.zeros((band, TILE * TALL), np.float32)
     gather[raster, window * TALL + 1 + place] = 1
-    gather[band + window, window * TALL] = 1
+    head = np.zeros((TILE, TILE * SLOT), np.float32)
+    head[np.arange(TILE), np.arange(TILE) * SLOT] = 1
     place = np.arange(WIN_SIDE * WIN_SIDE + 1)[None, :]
     squeeze = np.zeros(((WIN_SIDE * WIN_SIDE + 1) * TILE, TILE * TALL), np.float32)
     squeeze[place * TILE + window, window * TALL + place] = 1
-    return [jnp.asarray(table, bf16) for table in (spread, gather, squeeze, squeeze.T)]
+    return [jnp.asarray(table, bf16) for table in (spread, gather, head, squeeze, squeeze.T)]
 
 
 def shards(
@@ -654,7 +785,7 @@
     cot_regional,
 ):
     devices = lax.axis_size("dp")
-    parts = devices * lax.axis_size("img")
+    stages = reduce_stages()
     own_rank = lax.axis_index("dp")
     win_count = regional.shape[1]
     all_windows = window_slot.shape[1]
@@ -688,7 +819,7 @@
     region_bias = jnp.broadcast_to(
         jnp.where(live[:, 0], 0.0, -1e30).astype(f32)[:, None], (win_count, LANES)
     )
-    spread, gather, squeeze, stretch = row_maps()
+    spread, gather, head, squeeze, stretch = row_maps()
     plain, mixed_mask = head_masks()
     bias_qkv = jnp.concatenate([bias_q, jnp.zeros_like(bias_q), bias_v])[None]
     gain1, bias1, gain2, bias2 = ln1_gain[None], ln1_bias[None], ln2_gain[None], ln2_bias[None]
@@ -701,29 +832,41 @@
     grad_after, grad_mixed, early, grad_out, small, row_fc1 = run_back_mlp(
         keep, cot, after, mixed, hidden, slope, stretch, gain2, bias2, w_fc1, w_fc2, w_out
     )
-    early = all_sum(early)
-    tokens_out, regional_out, late, small_late = run_back_attention(
-        order, keep, qkv, probs, joined, grad_mixed, grad_after, grad_out, gather, plain, mixed_mask,
-        regional[0], qkv_r, probs_r, mixed_r, gain1, bias1, w_qkv, w_out,
-    )
+    early = sum_stage(early, stages[0])
+    attention = (order, keep, qkv, probs, joined, grad_mixed, grad_after, plain, mixed_mask, head, gain1, bias1)
+    grad_qkv, *held = run_back_attention(*attention)
+    held, early = lax.optimization_barrier((held, early))
+    early = sum_stage(early, stages[1])
+    grad_qkv, late, regional_out, small_late = run_back_attention(
+        *attention,
+        held=(*held, grad_qkv),
+        ending=(grad_out, order[None], regional[0], qkv_r, probs_r, mixed_r, w_qkv, w_out),
+    )
+    late = sum_stage(late, stages[0])
+    grad_qkv, early, came = lax.optimization_barrier((grad_qkv, early, came))
+    for stage in stages[2:]:
+        early = sum_stage(early, stage)
+    tokens_out, small_rows = run_back_rows(order, grad_qkv, joined, grad_after, gather, gain1, w_qkv)
     out_regional, out_local = run_collect(pick_back, came)
     vectors = jnp.concatenate(
         [
-            small_late[0:4],
-            (small[3] + small_late[4])[None],
+            small_late[0:2] + small_rows[0:2],
+            small_late[2:4],
+            small[3:4] + small_late[4:5],
             small[1:3],
             small[0:1],
             row_fc1[0].reshape(-1, WIDTH),
+            jnp.zeros((4, WIDTH), f32),
         ],
         axis=0,
     )
-    late_share = late.shape[0] // parts
-    extra = jnp.zeros((2 * 8, WIDTH), bf16).at[: vectors.shape[0]].set(vectors.astype(bf16))
-    extra = jnp.concatenate([extra.reshape(2, 8, WIDTH), jnp.zeros((parts - 2, 8, WIDTH), bf16)])
-    late = jnp.concatenate([late.reshape(parts, late_share, WIDTH), extra], axis=1)
-    late = all_sum(late.reshape(-1, WIDTH)).reshape(parts, late_share + 8, WIDTH)
-    vectors = late[:2, late_share:].reshape(-1, WIDTH).astype(f32)
-    late = late[:, :late_share].reshape(-1, WIDTH)
+    for stage in stages[1:]:
+        late = sum_stage(late, stage)
+    for stage in reversed(stages):
+        early = gather_stage(early, stage)
+    for stage in reversed(stages):
+        late = gather_stage(late, stage)
+    vectors = sum_small(vectors, stages)
     grad_w_qkv = jnp.concatenate([late[at * WIDTH : (at + 1) * WIDTH] for at in range(3)], axis=1)
     units = w_fc1.shape[1]
     grad_w_fc1 = jnp.concatenate(

time: 496 us -> 352 us (0.71)
  Pallas kernels: 311 us -> 202 us
  waiting for transfers between devices: 97 us -> 51.6 us
  starting transfers between devices: 46.2 us -> 55 us
    pallas_call x1, Pallas kernels: 144 us -> 75.6 us  [run_forward(): pl.pallas_call(forward_kernel, grid_spec=pltpu.PrefetchScalarGridSpec(num...]
    ppermute x28 -> x35, waiting for transfers between devices: 97 us -> 40.5 us  [the longest x14 24.7 us: sum_stage(): lax.ppermute(lax.dynamic_index_in_dim(parts, own ^ offset, 0, False), ('d...]
    pallas_call x1 -> x3, Pallas kernels: 103 us -> 62.2 us  [the longest x2 41.6 us: run_back_attention(): pl.pallas_call(functools.partial(back_attention_kernel, held is None, end...]
    all_to_all x2, waiting for transfers between devices: 0.01 us -> 11 us  [swap_tiles(): lax.all_to_all(tiles_sent, 'dp', split_axis=0, concat_axis=0, tiled=True)]
    ppermute x28 -> x35, starting transfers between devices: 32.8 us -> 41.6 us  [the longest x14 17.5 us: gather_stage(): lax.ppermute(rows, ('dp', 'img'), pairs)]
  transfers between devices with their start and end apart: 30 -> 37, of which waited for: 14 -> 14; matrix products, arithmetic and copies ran while one was open for 5% -> 8% of each run, Pallas kernels for 30% -> 41%
where the time goes in v3:
time: 352 us; the launch traced here: 351 us
  Pallas kernels  202 us (57%)
  starting transfers between devices  55 us (16%)
  waiting for transfers between devices  51.6 us (15%)
  other arithmetic  27.8 us (8%)
  local copies, waits for them, and re-layouts  13.2 us (4%)
    pallas_call x1, Pallas kernels, run_forward(): pl.pallas_call(forward_kernel, grid_spec=pltpu.PrefetchScalarGridSpec(num...  75.6 us
    pallas_call x1, Pallas kernels, run_back_mlp(): pl.pallas_call(back_mlp_kernel, grid_spec=pltpu.PrefetchScalarGridSpec(nu...  54.7 us
    pallas_call x2, Pallas kernels, run_back_attention(): pl.pallas_call(functools.partial(back_attention_kernel, held is None, end...  41.6 us
    ppermute x14, waiting for transfers between devices, sum_stage(): lax.ppermute(lax.dynamic_index_in_dim(parts, own ^ offset, 0, False), ('d...  24.7 us
    pallas_call x1, Pallas kernels, run_back_rows(): pl.pallas_call(back_rows_kernel, grid_spec=pltpu.PrefetchScalarGridSpec(n...  20.6 us
    ppermute x14, starting transfers between devices, gather_stage(): lax.ppermute(rows, ('dp', 'img'), pairs)  17.5 us
    ppermute x14, starting transfers between devices, sum_stage(): lax.ppermute(lax.dynamic_index_in_dim(parts, own ^ offset, 0, False), ('d...  17.2 us
    ppermute x14, waiting for transfers between devices, gather_stage(): lax.ppermute(rows, ('dp', 'img'), pairs)  14.7 us
  transfers between devices with their start and end apart: 37, of which 14 were waited for; matrix products, arithmetic and copies ran while one was open for 8% of the time, Pallas kernels for 41%

profile of v3, /device:TPU:0, one launch (start us, length us, event | category | flops | bytes accessed | tf_op | source)
XLA Modules:
  0.0 351.1 jit_solution(2268013037314243213)
XLA Ops:
  2.6 4.7 %deal.1 = bf16[8,400,512]{2,1,0:T(8,128)(2,1)} custom-call(bf16[128,128]{1,0:T(8,128)(2,1)} %get-tuple-element.145.pick_ref, bf16[64,512]{1,0:T(8,128)(2,1)} %bitcast.119, bf16[49,64,512]{2,1,0:T(8,128)(2,1)} %bitcast.111), custom_call_target="tpu_custom_call" | custom-call | flops 1000000000 | bytes 7000000 | tf_op jit(solution)/shard_map/deal/pallas_call | solution.py:712
  7.3 7.4 %all-to-all-start = ((bf16[8,400,512]{2,1,0:T(8,128)(2,1)}), bf16[8,400,512]{2,1,0:T(8,128)(2,1)S(1)}, u32[]{:S(2)}, u32[]{:S(2)}) async-start(bf16[8,400,512]{2,1,0:T(8,128)(2,1)} %deal.1), calls=%async_computation | async-start | bytes 6553600 | tf_op jit(solution)/shard_map/all_to_all | solution.py:739
  21.2 75.6 %forward.1 = (bf16[8,400,512]{2,1,0:T(8,128)(2,1)}, bf16[64,12,64,128]{3,2,1,0:T(8,128)(2,1)}, bf16[64,8,64,128]{3,2,1,0:T(8,128)(2,1)}, bf16[64,64,512]{2,1,0:T...) custom-call(s32[64]{0:T(128)} %select_reduce_fusion.1.order_ref, ...), custom_call_target="tpu_custom_call" | custom-call | flops 30000001024 | bytes 60000000 | tf_op jit(solution)/shard_map/forward/pallas_call | solution.py:282
  98.6 54.7 %back_mlp.1 = (f32[3584,512]{1,0:T(8,128)}, bf16[64,4,64,128]{3,2,1,0:T(8,128)(2,1)}, bf16[4096,512]{1,0:T(8,128)(2,1)}, f32[512,512]{1,0:T(8,128)}, f32[8,512]{1,0:T(8,128)}, /*index=5*/f32[8,2048]{1,0:T(8,128)}) custom-call(f32[1]{0:T(128)} %bitcast.3.keep_ref, bf16[8,400,512]{2,1,0:T(8,128)(2,1)} %copy-done, f32[3584,512]{1,0:T(8,128)} %get-tuple-element.58.after_ref, ...), custom_call_target="tpu_custom_call" | custom-call | flops 40000000000 | bytes 60000000 | tf_op jit(solution)/shard_map/back_mlp/pallas_call | solution.py:376
  155.2 6.0 %all-to-all-start.1 = ((bf16[8,400,512]{2,1,0:T(8,128)(2,1)}), bf16[8,400,512]{2,1,0:T(8,128)(2,1)}, u32[]{:S(2)}, u32[]{:S(2)}) async-start(bf16[8,400,512]{2,1,0:T(8,128)(2,1)} %get-tuple-element.80), calls=%async_computation.1 | async-start | bytes 6553600 | tf_op jit(solution)/shard_map/all_to_all | solution.py:739
  162.1 12.2 %back_attention.2 = (bf16[4096,1536]{1,0:T(8,128)(2,1)}, f32[512,1536]{1,0:T(8,128)}, f32[8,512]{1,0:T(8,128)}, f32[64,2048]{1,0:T(8,128)}, f32[64,512]{1,0:T(8,128)}) custom-call(s32[64]{0:T(128)} %select_reduce_fusion.1.order_ref, f32[1]{0:T(128)} %bitcast.3.keep_ref, bf16[64,12,64,128]{3,2,1,0:T(8,128)(2,1)} %get-tuple-element.55.qkv_ref, ...), custom_call_target="tpu_custom_call" | custom-call | flops 8999999488 | bytes 10000000 | tf_op jit(solution)/shard_map/back_attention/pallas_call | solution.py:549
  174.3 2.8 fusion
  178.2 3.0 collective-permute-start.3
  181.7 29.4 %back_attention.3 = (bf16[4096,1536]{1,0:T(8,128)(2,1)}, bf16[2048,512]{1,0:T(8,128)(2,1)}, bf16[64,512]{1,0:T(8,128)(2,1)}, f32[8,512]{1,0:T(8,128)}) custom-call(s32[64]{0:T(128)} %select_reduce_fusion.1.order_ref, f32[1]{0:T(128)} %bitcast.3.keep_ref, bf16[64,12,64,128]{3,2,1,0:T(8,128)(2,1)} %get-tuple-element.55.qkv_ref, ...), custom_call_target="tpu_custom_call", output_to_operand_aliasing={{0}: (16, {})} | custom-call | flops 27000000512 | bytes 30000000 | tf_op jit(solution)/shard_map/back_attention/pallas_call | solution.py:549
  213.3 9.7 %collective-permute-done.2 = bf16[512,512]{1,0:T(8,128)(2,1)} collective-permute-done((bf16[512,512]{1,0:T(8,128)(2,1)}, bf16[512,512]{1,0:T(8,128)(2,1)}, u32[]{:S(2)}, u32[]{:S(2)}) %collective-permute-start.2) | collective-permute-done | bytes 524320 | tf_op jit(solution)/shard_map/ppermute | solution.py:658
  224.5 11.0 %all-to-all-done.1.came_ref = bf16[8,400,512]{2,1,0:T(8,128)(2,1)} async-done(((bf16[8,400,512]{2,1,0:T(8,128)(2,1)}), bf16[8,400,512]{2,1,0:T(8,128)(2,1)}, u32[]{:S(2)}, u32[]{:S(2)}) %all-to-all-start.1) | async-done | bytes 3276832 | tf_op jit(solution)/shard_map/all_to_all | solution.py:739
  240.7 20.6 %back_rows.1 = (bf16[8,392,512]{2,1,0:T(8,128)(2,1)}, f32[8,512]{1,0:T(8,128)}) custom-call(s32[64]{0:T(128)} %select_reduce_fusion.1.order_ref, bf16[4096,1536]{1,0:T(8,128)(2,1)} %get-tuple-element.84.grad_qkv_ref, bf16[64,64,512]{2,1,0:T(8,128)(2,1)} %get-tuple-element.57.joined_ref, f32[3584,512]{1,0:T(8,128)} %get-tuple-element.63.grad_after_ref, ...), custom_call_target="tpu_custom_call" | custom-call | flops 15000000512 | bytes 30000000 | tf_op jit(solution)/shard_map/back_rows/pallas_call | solution.py:605
  268.3 2.5 collective-permute-start.14
  272.0 3.2 collective-permute-done.29
  275.3 2.5 collective-permute-start.31
  280.1 4.1 %collective-permute-done.13 = bf16[256,512]{1,0:T(8,128)(2,1)S(1)} collective-permute-done((bf16[256,512]{1,0:T(8,128)(2,1)S(1)}, bf16[256,512]{1,0:T(8,128)(2,1)S(1)}, u32[]{:S(2)}, u32[]{:S(2)}) %collective-permute-start.13) | collective-permute-done | bytes 262176 | tf_op jit(solution)/shard_map/ppermute | solution.py:658
  284.2 7.7 %collective-permute-done.12 = bf16[256,512]{1,0:T(8,128)(2,1)S(1)} collective-permute-done((bf16[256,512]{1,0:T(8,128)(2,1)S(1)}, bf16[256,512]{1,0:T(8,128)(2,1)S(1)}, u32[]{:S(2)}, u32[]{:S(2)}) %collective-permute-start.12) | collective-permute-done | bytes 262176 | tf_op jit(solution)/shard_map/ppermute | solution.py:658
  299.5 3.0 collective-permute-done.16
  306.1 2.4 collective-permute-start.19
  318.4 4.8 %collective-permute-done.21 = bf16[256,512]{1,0:T(8,128)(2,1)S(1)} collective-permute-done((bf16[256,512]{1,0:T(8,128)(2,1)S(1)}, bf16[256,512]{1,0:T(8,128)(2,1)S(1)}, u32[]{:S(2)}, u32[]{:S(2)}) %collective-permute-start.21) | collective-permute-done | bytes 262176 | tf_op jit(solution)/shard_map/ppermute | solution.py:669
  329.6 2.6 collective-permute-start.10
  334.0 4.6 %collect.1 = (bf16[64,512]{1,0:T(8,128)(2,1)}, bf16[49,64,512]{2,1,0:T(8,128)(2,1)}) custom-call(bf16[128,128]{1,0:T(8,128)(2,1)} %get-tuple-element.146.pick_ref, bf16[8,400,512]{2,1,0:T(8,128)(2,1)} %all-to-all-done.1.came_ref), custom_call_target="tpu_custom_call" | custom-call | flops 1000000000 | bytes 7000000 | tf_op jit(solution)/shard_map/collect/pallas_call | solution.py:723
  344.8 3.6 %select_convert_fusion = (f32[2048,512]{1,0:T(8,128)}, bf16[2048,512]{1,0:T(8,128)(2,1)S(1)}) fusion(bf16[2048,512]{1,0:T(8,128)(2,1)} %collective-permute-done.34, pred[]{:T(512)S(6)} %eq.247, bf16[512,512]{1,0:T(8,128)(2,1)S(1)} %get-tuple-element.100, bf16[512,512]{1,0:T(8,128)(2,1)S(1)} %get-tuple-element.102, ...), kind=kLoop, calls=%fused_computation.6 | loop fusion | flops 11534336 | bytes 10485762 | tf_op jit(solution)/shard_map/convert_element_type | solution.py:891
  348.6 2.6 maximum_convert_fusion
  (145 shorter events, 68.9 us)
Async XLA Ops:
  7.3 89.5 %all-to-all-start = ((bf16[8,400,512]{2,1,0:T(8,128)(2,1)}), bf16[8,400,512]{2,1,0:T(8,128)(2,1)S(1)}, u32[]{:S(2)}, u32[]{:S(2)}) async-start(bf16[8,400,512]{2,1,0:T(8,128)(2,1)} %deal.1), calls=%async_computation | async-start | bytes 6553600 | tf_op jit(solution)/shard_map/all_to_all | solution.py:739
  155.1 19.2 %collective-permute-start = (bf16[2048,512]{1,0:T(8,128)(2,1)S(1)}, bf16[2048,512]{1,0:T(8,128)(2,1)}, u32[]{:S(2)}, u32[]{:S(2)}) collective-permute-start(bf16[2048,512]{1,0:T(8,128)(2,1)S(1)} %dynamic-slice_bitcast_fusion), channel_id=1, source_target_pairs={{0,1},{1,0},{2,3},{3,2},{4,5},{5,4},{6,7},{7,6},{8,9},{9,8},{10,11... | collective-permute-start | bytes 6291464 | tf_op jit(solution)/shard_map/ppermute | solution.py:658
  155.2 80.4 %all-to-all-start.1 = ((bf16[8,400,512]{2,1,0:T(8,128)(2,1)}), bf16[8,400,512]{2,1,0:T(8,128)(2,1)}, u32[]{:S(2)}, u32[]{:S(2)}) async-start(bf16[8,400,512]{2,1,0:T(8,128)(2,1)} %get-tuple-element.80), calls=%async_computation.1 | async-start | bytes 6553600 | tf_op jit(solution)/shard_map/all_to_all | solution.py:739
  178.2 35.1 %collective-permute-start.3 = (bf16[512,512]{1,0:T(8,128)(2,1)}, bf16[512,512]{1,0:T(8,128)(2,1)}, u32[]{:S(2)}, u32[]{:S(2)}) collective-permute-start(bf16[512,512]{1,0:T(8,128)(2,1)} %get-tuple-element.106), channel_id=1, source_target_pairs={{0,6},{1,7},{2,4},{3,5},{4,2},{5,3},{6,0},{7,1},{8,14},{9,15},{10,... | collective-permute-start | bytes 1572872 | tf_op jit(solution)/shard_map/ppermute | solution.py:658
  181.2 41.8 %collective-permute-start.2 = (bf16[512,512]{1,0:T(8,128)(2,1)}, bf16[512,512]{1,0:T(8,128)(2,1)}, u32[]{:S(2)}, u32[]{:S(2)}) collective-permute-start(bf16[512,512]{1,0:T(8,128)(2,1)} %get-tuple-element.107), channel_id=1, source_target_pairs={{0,4},{1,5},{2,6},{3,7},{4,0},{5,1},{6,2},{7,3},{8,12},{9,13},{10,... | collective-permute-start | bytes 1572872 | tf_op jit(solution)/shard_map/ppermute | solution.py:658
  181.2 41.8 %collective-permute-start.1 = (bf16[512,512]{1,0:T(8,128)(2,1)S(1)}, bf16[512,512]{1,0:T(8,128)(2,1)}, u32[]{:S(2)}, u32[]{:S(2)}) collective-permute-start(bf16[512,512]{1,0:T(8,128)(2,1)S(1)} %get-tuple-element.105), channel_id=1, source_target_pairs={{0,2},{1,3},{2,0},{3,1},{4,6},{5,7},{6,4},{7,5},{8,10},{9,11},{10,... | collective-permute-start | bytes 1572872 | tf_op jit(solution)/shard_map/ppermute | solution.py:658
  212.5 54.2 %collective-permute-start.11 = (bf16[1024,512]{1,0:T(8,128)(2,1)S(1)}, bf16[1024,512]{1,0:T(8,128)(2,1)}, u32[]{:S(2)}, u32[]{:S(2)}) collective-permute-start(bf16[1024,512]{1,0:T(8,128)(2,1)S(1)} %dynamic-slice_bitcast_fusion.1), channel_id=1, source_target_pairs={{0,1},{1,0},{2,3},{3,2},{4,5},{5,4},{6,7},{7,6},{8,9},{9,8},{10,11... | collective-permute-start | bytes 3145736 | tf_op jit(solution)/shard_map/ppermute | solution.py:658
  236.3 24.9 %collective-permute-start.27 = (bf16[128,512]{1,0:T(8,128)(2,1)}, bf16[128,512]{1,0:T(8,128)(2,1)S(1)}, u32[]{:S(2)}, u32[]{:S(2)}) collective-permute-start(bf16[128,512]{1,0:T(8,128)(2,1)} %get-tuple-element.124), channel_id=1, source_target_pairs={{0,24},{1,25},{2,26},{3,27},{4,28},{5,29},{6,30},{7,31},{8,16},{9,... | collective-permute-start | bytes 393224 | tf_op jit(solution)/shard_map/ppermute | solution.py:658
  238.6 22.7 %collective-permute-start.26 = (bf16[128,512]{1,0:T(8,128)(2,1)}, bf16[128,512]{1,0:T(8,128)(2,1)S(1)}, u32[]{:S(2)}, u32[]{:S(2)}) collective-permute-start(bf16[128,512]{1,0:T(8,128)(2,1)} %get-tuple-element.125), channel_id=1, source_target_pairs={{0,16},{1,17},{2,18},{3,19},{4,20},{5,21},{6,22},{7,23},{8,24},{9,... | collective-permute-start | bytes 393224 | tf_op jit(solution)/shard_map/ppermute | solution.py:658
  238.6 22.7 %collective-permute-start.25 = (bf16[128,512]{1,0:T(8,128)(2,1)S(1)}, bf16[128,512]{1,0:T(8,128)(2,1)}, u32[]{:S(2)}, u32[]{:S(2)}) collective-permute-start(bf16[128,512]{1,0:T(8,128)(2,1)S(1)} %get-tuple-element.123), channel_id=1, source_target_pairs={{0,8},{1,9},{2,10},{3,11},{4,12},{5,13},{6,14},{7,15},{8,0},{9,1},... | collective-permute-start | bytes 393224 | tf_op jit(solution)/shard_map/ppermute | solution.py:658
  264.6 10.6 %collective-permute-start.29 = (bf16[128,512]{1,0:T(8,128)(2,1)S(1)}, bf16[128,512]{1,0:T(8,128)(2,1)S(1)}, u32[]{:S(2)}, u32[]{:S(2)}) collective-permute-start(bf16[128,512]{1,0:T(8,128)(2,1)S(1)} %fusion.10), channel_id=1, source_target_pairs={{0,16},{1,17},{2,18},{3,19},{4,20},{5,21},{6,22},{7,23},{8,24},{9,... | collective-permute-start | bytes 393224 | tf_op jit(solution)/shard_map/ppermute | solution.py:669
  264.6 10.6 %collective-permute-start.30 = (bf16[128,512]{1,0:T(8,128)(2,1)S(1)}, bf16[128,512]{1,0:T(8,128)(2,1)S(1)}, u32[]{:S(2)}, u32[]{:S(2)}) collective-permute-start(bf16[128,512]{1,0:T(8,128)(2,1)S(1)} %fusion.10), channel_id=1, source_target_pairs={{0,8},{1,9},{2,10},{3,11},{4,12},{5,13},{6,14},{7,15},{8,0},{9,1},... | collective-permute-start | bytes 393224 | tf_op jit(solution)/shard_map/ppermute | solution.py:669
  268.3 10.3 %collective-permute-start.14 = (bf16[256,512]{1,0:T(8,128)(2,1)S(1)}, bf16[256,512]{1,0:T(8,128)(2,1)S(1)}, u32[]{:S(2)}, u32[]{:S(2)}) collective-permute-start(bf16[256,512]{1,0:T(8,128)(2,1)S(1)} %get-tuple-element.117), channel_id=1, source_target_pairs={{0,6},{1,7},{2,4},{3,5},{4,2},{5,3},{6,0},{7,1},{8,14},{9,15},{10,... | collective-permute-start | bytes 786440 | tf_op jit(solution)/shard_map/ppermute | solution.py:658
  270.8 13.4 %collective-permute-start.13 = (bf16[256,512]{1,0:T(8,128)(2,1)S(1)}, bf16[256,512]{1,0:T(8,128)(2,1)S(1)}, u32[]{:S(2)}, u32[]{:S(2)}) collective-permute-start(bf16[256,512]{1,0:T(8,128)(2,1)S(1)} %get-tuple-element.118), channel_id=1, source_target_pairs={{0,4},{1,5},{2,6},{3,7},{4,0},{5,1},{6,2},{7,3},{8,12},{9,13},{10,... | collective-permute-start | bytes 786440 | tf_op jit(solution)/shard_map/ppermute | solution.py:658
  271.3 20.5 %collective-permute-start.12 = (bf16[256,512]{1,0:T(8,128)(2,1)S(1)}, bf16[256,512]{1,0:T(8,128)(2,1)S(1)}, u32[]{:S(2)}, u32[]{:S(2)}) collective-permute-start(bf16[256,512]{1,0:T(8,128)(2,1)S(1)} %get-tuple-element.116), channel_id=1, source_target_pairs={{0,2},{1,3},{2,0},{3,1},{4,6},{5,7},{6,4},{7,5},{8,10},{9,11},{10,... | collective-permute-start | bytes 786440 | tf_op jit(solution)/shard_map/ppermute | solution.py:658
  275.3 29.4 %collective-permute-start.31 = (bf16[512,512]{1,0:T(8,128)(2,1)S(1)}, bf16[512,512]{1,0:T(8,128)(2,1)S(1)}, u32[]{:S(2)}, u32[]{:S(2)}) collective-permute-start(bf16[512,512]{1,0:T(8,128)(2,1)S(1)} %pad_maximum_fusion.2), channel_id=1, source_target_pairs={{0,6},{1,7},{2,4},{3,5},{4,2},{5,3},{6,0},{7,1},{8,14},{9,15},{10,... | collective-permute-start | bytes 1572872 | tf_op jit(solution)/shard_map/ppermute | solution.py:669
  277.8 28.3 %collective-permute-start.32 = (bf16[512,512]{1,0:T(8,128)(2,1)S(1)}, bf16[512,512]{1,0:T(8,128)(2,1)S(1)}, u32[]{:S(2)}, u32[]{:S(2)}) collective-permute-start(bf16[512,512]{1,0:T(8,128)(2,1)S(1)} %pad_maximum_fusion.2), channel_id=1, source_target_pairs={{0,4},{1,5},{2,6},{3,7},{4,0},{5,1},{6,2},{7,3},{8,12},{9,13},{10,... | collective-permute-start | bytes 1572872 | tf_op jit(solution)/shard_map/ppermute | solution.py:669
  278.6 30.0 %collective-permute-start.33 = (bf16[512,512]{1,0:T(8,128)(2,1)S(1)}, bf16[512,512]{1,0:T(8,128)(2,1)S(1)}, u32[]{:S(2)}, u32[]{:S(2)}) collective-permute-start(bf16[512,512]{1,0:T(8,128)(2,1)S(1)} %pad_maximum_fusion.2), channel_id=1, source_target_pairs={{0,2},{1,3},{2,0},{3,1},{4,6},{5,7},{6,4},{7,5},{8,10},{9,11},{10,... | collective-permute-start | bytes 1572872 | tf_op jit(solution)/shard_map/ppermute | solution.py:669
  302.5 27.1 %collective-permute-start.7 = (f32[16,512]{1,0:T(8,128)S(1)}, f32[16,512]{1,0:T(8,128)S(1)}, u32[]{:S(2)}, u32[]{:S(2)}) collective-permute-start(f32[16,512]{1,0:T(8,128)S(1)} %add.282), channel_id=1, source_target_pairs={{0,6},{1,7},{2,4},{3,5},{4,2},{5,3},{6,0},{7,1},{8,14},{9,15},{10,... | collective-permute-start | bytes 98312 | tf_op jit(solution)/shard_map/ppermute | solution.py:682
  304.7 24.9 %collective-permute-start.6 = (f32[16,512]{1,0:T(8,128)S(1)}, f32[16,512]{1,0:T(8,128)S(1)}, u32[]{:S(2)}, u32[]{:S(2)}) collective-permute-start(f32[16,512]{1,0:T(8,128)S(1)} %add.282), channel_id=1, source_target_pairs={{0,4},{1,5},{2,6},{3,7},{4,0},{5,1},{6,2},{7,3},{8,12},{9,13},{10,... | collective-permute-start | bytes 98312 | tf_op jit(solution)/shard_map/ppermute | solution.py:682
  314.8 9.8 %collective-permute-start.22 = (bf16[256,512]{1,0:T(8,128)(2,1)S(1)}, bf16[256,512]{1,0:T(8,128)(2,1)S(1)}, u32[]{:S(2)}, u32[]{:S(2)}) collective-permute-start(bf16[256,512]{1,0:T(8,128)(2,1)S(1)} %pad_maximum_fusion.3), channel_id=1, source_target_pairs={{0,4},{1,5},{2,6},{3,7},{4,0},{5,1},{6,2},{7,3},{8,12},{9,13},{10,... | collective-permute-start | bytes 786440 | tf_op jit(solution)/shard_map/ppermute | solution.py:669
  315.7 10.4 %collective-permute-start.23 = (bf16[256,512]{1,0:T(8,128)(2,1)S(1)}, bf16[256,512]{1,0:T(8,128)(2,1)S(1)}, u32[]{:S(2)}, u32[]{:S(2)}) collective-permute-start(bf16[256,512]{1,0:T(8,128)(2,1)S(1)} %pad_maximum_fusion.3), channel_id=1, source_target_pairs={{0,2},{1,3},{2,0},{3,1},{4,6},{5,7},{6,4},{7,5},{8,10},{9,11},{10,... | collective-permute-start | bytes 786440 | tf_op jit(solution)/shard_map/ppermute | solution.py:669
  327.6 12.3 %collective-permute-start.24 = (bf16[1024,512]{1,0:T(8,128)(2,1)}, bf16[1024,512]{1,0:T(8,128)(2,1)}, u32[]{:S(2)}, u32[]{:S(2)}) collective-permute-start(bf16[1024,512]{1,0:T(8,128)(2,1)} %pad_maximum_fusion.1), channel_id=1, source_target_pairs={{0,1},{1,0},{2,3},{3,2},{4,5},{5,4},{6,7},{7,6},{8,9},{9,8},{10,11... | collective-permute-start | bytes 3145736 | tf_op jit(solution)/shard_map/ppermute | solution.py:669
  329.0 15.8 %collective-permute-start.34 = (bf16[2048,512]{1,0:T(8,128)(2,1)}, bf16[2048,512]{1,0:T(8,128)(2,1)}, u32[]{:S(2)}, u32[]{:S(2)}) collective-permute-start(bf16[2048,512]{1,0:T(8,128)(2,1)} %pad_maximum_fusion), channel_id=1, source_target_pairs={{0,1},{1,0},{2,3},{3,2},{4,5},{5,4},{6,7},{7,6},{8,9},{9,8},{10,11... | collective-permute-start | bytes 6291464 | tf_op jit(solution)/shard_map/ppermute | solution.py:669
  (23 other events, 226.2 us)

commit v4 on v3

--- a/solution.py
+++ b/solution.py
@@ -25,11 +25,17 @@
 GROUPS = HEADS // GROUP
 TOGETHER = 8
 LANES = 128
-FIRST_TILES = 2
+ROWS_FIRST = 2
+FIRST_TILES = 3
 CHUNK = 512
 VMEM_LIMIT = 60 * 1024 * 1024
 
 f32 = jnp.float32
+
+
+def took(micros):
+    return pl.CostEstimate(flops=int(micros * 1.15e9), bytes_accessed=1_000_000, transcendentals=0)
+
 bf16 = jnp.bfloat16
 
 
@@ -61,8 +67,11 @@
     return jnp.concatenate([turned[:SLOT], turned[SLOT:]], axis=1)
 
 
-def attend(items, plain, mixed):
-    scores = [dot_nt(key_rows, spread_heads(queries, plain)) for queries, key_rows, _, _ in items]
+def attend_scores(items, plain):
+    return [dot_nt(key_rows, spread_heads(queries, plain)) for queries, key_rows, _, _ in items]
+
+
+def attend_probs(items, scores):
     probs = []
     for rows, (_, _, _, bias) in zip(scores, items):
         rows = rows + bias
@@ -70,9 +79,11 @@
         weighted = jnp.exp2((rows - highest) * (HDIM**-0.5 * math.log2(math.e)))
         total = jnp.sum(weighted, axis=0, keepdims=True)
         probs.append((weighted * (1.0 / total)).astype(bf16))
-    turned = [turn(rows) for rows in probs]
-    outs = [dot(rows, spread_heads(item[2], mixed)) for rows, item in zip(turned, items)]
-    return probs, outs
+    return probs
+
+
+def attend_mix(items, turned, mixed):
+    return [dot(rows, spread_heads(item[2], mixed)) for rows, item in zip(turned, items)]
 
 
 def attend_back(items, plain, mixed):
@@ -106,34 +117,24 @@
 
 
 def gelu_pair(values):
-    size = jnp.abs(values)
-    spot = 1.0 / (1.0 + (0.3275911 * 0.7071067811865476) * size)
+    below = 0.5 + 0.5 * lax.erf(values * 0.7071067811865476)
     bell = jnp.exp2(values * values * (-0.5 * math.log2(math.e)))
-    tail = 0.5 * 1.061405429
-    for factor in (-1.453152027, 1.421413741, -0.284496736, 0.254829592):
-        tail = tail * spot + 0.5 * factor
-    tail = tail * spot * bell
-    below = jnp.where(values >= 0, 1.0 - tail, tail)
     return values * below, below + values * bell * 0.3989422804014327
+
+
+def fold_lanes(rows):
+    return sum(rows[:, at : at + LANES] for at in range(0, rows.shape[1], LANES))
 
 
 def column_sum(rows):
     return jnp.sum(rows, axis=0, keepdims=True)
 
 
-def attend_windows(windows, plain, mixed):
-    items = []
-    for qkv_of, bias, _, _ in windows:
-        wide = jnp.concatenate([bias, bias], axis=1)
-        for group in range(GROUPS):
-            items.append((qkv_of(group), qkv_of(GROUPS + group), qkv_of(2 * GROUPS + group), wide))
-    probs, outs = attend(items, plain, mixed)
-    for at, (_, _, put_probs, put_mixed) in enumerate(windows):
-        for group in range(GROUPS):
-            rows = probs[at * GROUPS + group]
-            put_probs(2 * group, rows[:, :LANES])
-            put_probs(2 * group + 1, rows[:, LANES:])
-            put_mixed(group, outs[at * GROUPS + group])
+def window_items(qkv_of, bias):
+    wide = jnp.concatenate([bias, bias], axis=1)
+    return [
+        (qkv_of(group), qkv_of(GROUPS + group), qkv_of(2 * GROUPS + group), wide) for group in range(GROUPS)
+    ]
 
 
 def attend_windows_back(windows, plain, mixed):
@@ -158,12 +159,16 @@
     gain2_ref, bias2_ref, w_fc1_ref, bias_fc1_ref, w_fc2_ref, bias_fc2_ref,
     out_ref, qkv_ref, probs_ref, joined_ref, mixed_ref, after_ref, hidden_ref, slope_ref,
     qkv_r_ref, probs_r_ref, mixed_r_ref,
-    windows, normed, mixed_rows,
+    windows, normed, mixed_rows, joined_rows,
 ):
     step = pl.program_id(0)
+    last = pl.num_programs(0) - 1
     keep = keep_ref[0]
     plain = plain_ref[...]
     mixed = mixed_mask_ref[...]
+    count = TILE * TALL
+    chunks = [slice(at, at + CHUNK) for at in range(0, w_fc1_ref.shape[1], CHUNK)]
+    tile = {}
 
     @pl.when(step == 0)
     def first():
@@ -173,17 +178,14 @@
         region_qkv = (dot(region_norm, w_qkv_ref[...]) + bias_qkv_ref[...]).astype(bf16)
         for at in range(3 * GROUPS):
             qkv_r_ref[at] = region_qkv[:, at * LANES : (at + 1) * LANES]
-
-        def put_probs(at, probs):
-            probs_r_ref[at] = probs
-
-        def put_mixed(at, rows):
-            mixed_r_ref[:, at * LANES : (at + 1) * LANES] = rows.astype(bf16)
-
-        attend_windows(
-            [(lambda at: qkv_r_ref[at], region_bias_ref[...], put_probs, put_mixed)], plain, mixed
-        )
-        region_mixed = mixed_r_ref[...]
+        items = window_items(lambda at: region_qkv[:, at * LANES : (at + 1) * LANES], region_bias_ref[...])
+        probs = attend_probs(items, attend_scores(items, plain))
+        for group in range(GROUPS):
+            probs_r_ref[2 * group] = probs[group][:, :LANES]
+            probs_r_ref[2 * group + 1] = probs[group][:, LANES:]
+        outs = attend_mix(items, [turn(rows) for rows in probs], mixed)
+        region_mixed = jnp.concatenate(outs, axis=1).astype(bf16)
+        mixed_r_ref[...] = region_mixed
         region_mid = region + keep * (dot(region_mixed, w_out_ref[...]) + bias_out_ref[...])
         region_mid = region_mid.astype(bf16)
         row = lax.broadcasted_iota(jnp.int32, (TILE * SLOT, REGIONS), 0)
@@ -197,54 +199,130 @@
 
         lax.fori_loop(0, REG_SIDE, relay, 0)
 
-    for at in range(TILE):
-        rows = windows[order_ref[step * TILE + at]]
-        joined_ref[at] = rows.astype(bf16)
-        unit, _ = normalize(rows)
-        normed[at * SLOT : (at + 1) * SLOT] = (unit * gain1_ref[...] + bias1_ref[...]).astype(bf16)
-    for part in range(3):
+
+    def norm_rows():
+        for at in range(TILE):
+            rows = windows[order_ref[step * TILE + at]]
+            joined_ref[at] = rows.astype(bf16)
+            unit, _ = normalize(rows)
+            normed[at * SLOT : (at + 1) * SLOT] = (unit * gain1_ref[...] + bias1_ref[...]).astype(bf16)
+
+    def project(part):
         cols = slice(part * WIDTH, (part + 1) * WIDTH)
         qkv = dot(normed[...], w_qkv_ref[:, cols]) + bias_qkv_ref[:, cols]
         qkv = qkv.astype(bf16).reshape(TILE, SLOT, WIDTH)
         for group in range(GROUPS):
             qkv_ref[:, part * GROUPS + group] = qkv[:, :, group * LANES : (group + 1) * LANES]
 
-    def some(batch, carry):
-        def window(at):
-            def put_probs(place, probs):
-                probs_ref[at, place] = probs
-
-            def put_mixed(group, rows):
-                mixed_rows[at, :, group * LANES : (group + 1) * LANES] = rows
-
+    def score(half):
+        items = []
+        for at in half:
             bias = window_bias_ref[order_ref[step * TILE + at]]
-            return lambda place: qkv_ref[at, place], bias, put_probs, put_mixed
-
-        attend_windows([window(batch * TOGETHER + at) for at in range(TOGETHER)], plain, mixed)
-        return carry
-
-    lax.fori_loop(0, TILE // TOGETHER, some, 0)
-    rows_count = TILE * TALL
-    mixed_low = mixed_rows[:, :TALL].reshape(rows_count, WIDTH).astype(bf16)
-    mixed_ref[...] = mixed_low
-    joined = joined_ref[...].astype(f32)[:, :TALL].reshape(rows_count, WIDTH)
-    after = joined + keep * (dot(mixed_low, w_out_ref[...]) + bias_out_ref[...])
-    after_ref[...] = after
-    unit, _ = normalize(after)
-    mlp_norm = (unit * gain2_ref[...] + bias2_ref[...]).astype(bf16)
-    total = after + keep * bias_fc2_ref[...]
-    chunks = [slice(at, at + CHUNK) for at in range(0, w_fc1_ref.shape[1], CHUNK)]
-    ahead = dot(mlp_norm, w_fc1_ref[:, chunks[0]])
-    for at, cols in enumerate(chunks):
-        pre_act = ahead + bias_fc1_ref[:, cols]
-        if at + 1 < len(chunks):
-            ahead = dot(mlp_norm, w_fc1_ref[:, chunks[at + 1]])
-        hidden, slope = gelu_pair(pre_act)
-        hidden = hidden.astype(bf16)
-        hidden_ref[:, cols] = hidden
+            items += window_items(lambda place, at=at: qkv_ref[at, place], bias)
+        return items, attend_scores(items, plain)
+
+    def soften(half, items, scores):
+        probs = attend_probs(items, scores)
+        for at, rows in enumerate(probs):
+            window, group = half[at // GROUPS], at % GROUPS
+            probs_ref[window, 2 * group] = rows[:, :LANES]
+            probs_ref[window, 2 * group + 1] = rows[:, LANES:]
+        return [turn(rows) for rows in probs]
+
+    def mix(half, items, turned):
+        outs = attend_mix(items, turned, mixed)
+        for at, rows in enumerate(outs):
+            window, group = half[at // GROUPS], at % GROUPS
+            mixed_rows[window, :, group * LANES : (group + 1) * LANES] = rows
+
+    def keep_joined():
+        for at in range(TILE):
+            joined_rows[at] = joined_ref[at].astype(f32)
+
+
+    def branch():
+        mixed_low = mixed_rows[:, :TALL].reshape(count, WIDTH).astype(bf16)
+        mixed_ref[...] = mixed_low
+        after = joined_rows[:, :TALL].reshape(count, WIDTH) + keep * (
+            dot(mixed_low, w_out_ref[...]) + bias_out_ref[...]
+        )
+        after_ref[...] = after
+
+    def norm_after():
+        unit, _ = normalize(after_ref[...])
+        tile["norm"] = (unit * gain2_ref[...] + bias2_ref[...]).astype(bf16)
+        tile["total"] = jnp.zeros((count, WIDTH), f32)
+
+    def widen(at):
+        tile[at] = dot(tile["norm"], w_fc1_ref[:, chunks[at]])
+
+    def bend(at):
+        cols = chunks[at]
+        hidden, slope = gelu_pair(tile[at] + bias_fc1_ref[:, cols])
+        tile[at] = hidden.astype(bf16)
+        hidden_ref[:, cols] = tile[at]
         slope_ref[:, cols] = slope.astype(bf16)
-        total = total + keep * dot(hidden, w_fc2_ref[cols, :])
-    out_ref[0] = dot(squeeze_ref[...], total.astype(bf16)).astype(bf16)
+
+    def narrow(at):
+        tile["total"] = tile["total"] + dot(tile[at], w_fc2_ref[chunks[at], :])
+
+    def send():
+        result = after_ref[...] + keep * (tile["total"] + bias_fc2_ref[...])
+        out_ref[0] = dot(squeeze_ref[...], result.astype(bf16)).astype(bf16)
+
+    halves = [list(range(TILE // 2)), list(range(TILE // 2, TILE))]
+
+    @pl.when(step == 0)
+    def attention_only():
+        norm_rows()
+        for part in range(3):
+            project(part)
+        scored = [score(half) for half in halves]
+        turned = [soften(half, *pair) for half, pair in zip(halves, scored)]
+        for half, pair, rows in zip(halves, scored, turned):
+            mix(half, pair[0], rows)
+        keep_joined()
+
+    @pl.when((step > 0) & (step < last))
+    def both():
+        branch()
+        norm_rows()
+        project(0)
+        norm_after()
+        project(1)
+        widen(0)
+        project(2)
+        widen(1)
+        bend(0)
+        scored = [score(halves[0]), None]
+        narrow(0)
+        bend(1)
+        widen(2)
+        scored[1] = score(halves[1])
+        turned = [soften(halves[0], *scored[0]), None]
+        narrow(1)
+        widen(3)
+        bend(2)
+        mix(halves[0], scored[0][0], turned[0])
+        turned[1] = soften(halves[1], *scored[1])
+        narrow(2)
+        bend(3)
+        mix(halves[1], scored[1][0], turned[1])
+        narrow(3)
+        send()
+        keep_joined()
+
+    @pl.when(step == last)
+    def feed_only():
+        branch()
+        norm_after()
+        widen(0)
+        for at in range(len(chunks)):
+            if at + 1 < len(chunks):
+                widen(at + 1)
+            bend(at)
+            narrow(at)
+        send()
 
 
 def whole(shape):
@@ -264,15 +342,23 @@
     compact = squeeze.shape[0]
     args = (tokens, regional, window_bias, region_bias, spread, squeeze, plain, mixed,
             gain1, bias1, w_qkv, bias_qkv, w_out, bias_out, gain2, bias2, w_fc1, bias_fc1, w_fc2, bias_fc2)
+    def ahead(shape):
+        return pl.BlockSpec(
+            shape, lambda step, *_: (jnp.minimum(step, steps - 1),) + (0,) * (len(shape) - 1)
+        )
+
+    def behind(shape):
+        return pl.BlockSpec(shape, lambda step, *_: (jnp.maximum(step - 1, 0),) + (0,) * (len(shape) - 1))
+
     outs = [
-        ((steps, compact, WIDTH), bf16, (1, compact, WIDTH)),
-        ((windows, 3 * GROUPS, SLOT, LANES), bf16, (TILE, 3 * GROUPS, SLOT, LANES)),
-        ((windows, 2 * GROUPS, SLOT, LANES), bf16, (TILE, 2 * GROUPS, SLOT, LANES)),
-        ((windows, SLOT, WIDTH), bf16, (TILE, SLOT, WIDTH)),
-        ((steps * rows, WIDTH), bf16, (rows, WIDTH)),
-        ((steps * rows, WIDTH), f32, (rows, WIDTH)),
-        ((steps * rows, hidden), bf16, (rows, hidden)),
-        ((steps * rows, hidden), bf16, (rows, hidden)),
+        ((steps, compact, WIDTH), bf16, behind((1, compact, WIDTH))),
+        ((windows, 3 * GROUPS, SLOT, LANES), bf16, ahead((TILE, 3 * GROUPS, SLOT, LANES))),
+        ((windows, 2 * GROUPS, SLOT, LANES), bf16, ahead((TILE, 2 * GROUPS, SLOT, LANES))),
+        ((windows, SLOT, WIDTH), bf16, ahead((TILE, SLOT, WIDTH))),
+        ((steps * rows, WIDTH), bf16, behind((rows, WIDTH))),
+        ((steps * rows, WIDTH), f32, behind((rows, WIDTH))),
+        ((steps * rows, hidden), bf16, behind((rows, hidden))),
+        ((steps * rows, hidden), bf16, behind((rows, hidden))),
     ]
     fixed = [
         ((3 * GROUPS, REGIONS, LANES), bf16),
@@ -283,12 +369,13 @@
         forward_kernel,
         grid_spec=pltpu.PrefetchScalarGridSpec(
             num_scalar_prefetch=2,
-            grid=(steps,),
+            grid=(steps + 1,),
             in_specs=[whole(a.shape) for a in args],
-            out_specs=[tiles(block) for _, _, block in outs] + [whole(s) for s, _ in fixed],
+            out_specs=[spec for _, _, spec in outs] + [whole(s) for s, _ in fixed],
             scratch_shapes=[
                 pltpu.VMEM((windows, SLOT, WIDTH), f32),
                 pltpu.VMEM((TILE * SLOT, WIDTH), bf16),
+                pltpu.VMEM((TILE, SLOT, WIDTH), f32),
                 pltpu.VMEM((TILE, SLOT, WIDTH), f32),
             ],
         ),
@@ -297,16 +384,33 @@
         compiler_params=pltpu.CompilerParams(
             dimension_semantics=("arbitrary",), vmem_limit_bytes=VMEM_LIMIT
         ),
-        cost_estimate=pl.CostEstimate(flops=30_000_000_000, bytes_accessed=60_000_000, transcendentals=20_000_000),
+        cost_estimate=took(61),
         name="forward",
     )(order, keep, *args)
 
 
+def put_shares(own, keep_ref, send_ref, chunk_of):
+    half = keep_ref.shape[0]
+
+    def fill(refs):
+        for which, ref in enumerate(refs):
+            for at in range(half):
+                ref[at ^ (own % half)] = chunk_of(which * half + at)
+
+    @pl.when(own < half)
+    def low():
+        fill((keep_ref, send_ref))
+
+    @pl.when(own >= half)
+    def high():
+        fill((send_ref, keep_ref))
+
+
 def back_mlp_kernel(
-    keep_ref, cot_ref, after_ref, mixed_ref, hidden_ref, slope_ref, stretch_ref,
+    keep_ref, own_ref, cot_ref, after_ref, mixed_ref, hidden_ref, slope_ref, stretch_ref,
     gain2_ref, bias2_ref, w_fc1_ref, w_fc2_ref, w_out_ref,
-    grad_after_ref, grad_mixed_ref, early_ref, grad_out_ref, small_ref, bias_row_ref,
-    sum_fc1, sum_fc2, sum_out, sums, sum_hidden,
+    grad_after_ref, grad_mixed_ref, stay_ref, send_ref, grad_out_ref, small_ref, bias_row_ref,
+    sum_fc1, sum_fc2, sum_out, sums, sum_hidden, early_rows,
 ):
     step = pl.program_id(0)
     last = pl.num_programs(0) - 1
@@ -353,16 +457,20 @@
     def finish():
         for at in range(4):
             cols = slice(at * WIDTH, (at + 1) * WIDTH)
-            early_ref[cols, :] = sum_fc1[:, cols].astype(bf16)
-            early_ref[4 * WIDTH + at * WIDTH : 4 * WIDTH + (at + 1) * WIDTH, :] = (
+            early_rows[cols, :] = sum_fc1[:, cols].astype(bf16)
+            early_rows[4 * WIDTH + at * WIDTH : 4 * WIDTH + (at + 1) * WIDTH, :] = (
                 sum_fc2[:, cols].T.astype(bf16)
             )
+        rows = stay_ref.shape[1]
+        put_shares(
+            own_ref[0], stay_ref, send_ref, lambda at: early_rows[at * rows : (at + 1) * rows, :]
+        )
         grad_out_ref[...] = sum_out[...]
         small_ref[...] = sums[...]
         bias_row_ref[...] = sum_hidden[...]
 
 
-def run_back_mlp(keep, cot, after, mixed, hidden, slope, stretch, gain2, bias2, w_fc1, w_fc2, w_out):
+def run_back_mlp(parts, keep, own, cot, after, mixed, hidden, slope, stretch, gain2, bias2, w_fc1, w_fc2, w_out):
     steps, compact, _ = cot.shape
     rows = TILE * TALL
     units = w_fc1.shape[1]
@@ -372,11 +480,12 @@
         ((steps * rows, WIDTH), f32, (rows, WIDTH)),
         ((steps * TILE, GROUPS, SLOT, LANES), bf16, (TILE, GROUPS, SLOT, LANES)),
     ]
-    whole_outs = [((2 * units, WIDTH), bf16), ((WIDTH, WIDTH), f32), ((8, WIDTH), f32), ((8, units), f32)]
+    share = (parts // 2, 2 * units // parts, WIDTH)
+    whole_outs = [(share, bf16), (share, bf16), ((WIDTH, WIDTH), f32), ((8, WIDTH), f32), ((8, units), f32)]
     return pl.pallas_call(
         back_mlp_kernel,
         grid_spec=pltpu.PrefetchScalarGridSpec(
-            num_scalar_prefetch=1,
+            num_scalar_prefetch=2,
             grid=(steps,),
             in_specs=[tiles(b) for b in tiled] + [whole(a.shape) for a in fixed],
             out_specs=[tiles(block) for _, _, block in outs] + [whole(s) for s, _ in whole_outs],
@@ -386,6 +495,7 @@
                 pltpu.VMEM((WIDTH, WIDTH), f32),
                 pltpu.VMEM((8, WIDTH), f32),
                 pltpu.VMEM((8, units), f32),
+                pltpu.VMEM((2 * units, WIDTH), bf16),
             ],
         ),
         out_shape=[jax.ShapeDtypeStruct(s, d) for s, d, _ in outs]
@@ -393,13 +503,13 @@
         compiler_params=pltpu.CompilerParams(
             dimension_semantics=("arbitrary",), vmem_limit_bytes=VMEM_LIMIT
         ),
-        cost_estimate=pl.CostEstimate(flops=40_000_000_000, bytes_accessed=60_000_000, transcendentals=0),
+        cost_estimate=took(55),
         name="back_mlp",
-    )(keep, cot, after, mixed, hidden, slope, *fixed)
+    )(keep, own, cot, after, mixed, hidden, slope, *fixed)
 
 
 def back_attention_kernel(
-    first, last, order_ref, keep_ref,
+    first, last, order_ref, keep_ref, own_ref,
     qkv_ref, probs_ref, joined_ref, grad_mixed_ref, grad_after_ref,
     plain_ref, mixed_mask_ref, head_ref, gain1_ref, bias1_ref, *refs,
 ):
@@ -408,11 +518,10 @@
     else:
         held_in, refs = refs[:4], refs[5:]
     if last:
-        (grad_out_ref, order_row_ref, regional_ref, qkv_r_ref, probs_r_ref, mixed_r_ref, w_qkv_ref, w_out_ref), refs = (
-            refs[:8],
-            refs[8:],
-        )
-        grad_qkv_ref, late_ref, regional_out_ref, small_ref, sum_qkv, sums, heads, after_heads = refs
+        ending, refs = refs[:10], refs[10:]
+        grad_out_ref, order_row_ref, regional_ref, qkv_r_ref, probs_r_ref, mixed_r_ref = ending[:6]
+        w_qkv_ref, w_out_ref, sums_mlp_ref, row_fc1_ref = ending[6:]
+        grad_qkv_ref, stay_ref, send_ref, regional_out_ref, sum_qkv, sums, heads, after_heads, late_rows = refs
     else:
         grad_qkv_ref, sum_qkv, sums, heads, after_heads = refs
     step = pl.program_id(0)
@@ -447,8 +556,7 @@
     normed = (unit * gain1_ref[...] + bias1_ref[...]).astype(bf16)
     grad_qkv = grad_qkv_ref[...]
     sum_qkv[...] += dot(normed.T, grad_qkv)
-    sums[2:3] += column_sum(grad_qkv[:, :WIDTH].astype(f32))
-    sums[3:4] += column_sum(grad_qkv[:, 2 * WIDTH :].astype(f32))
+    sums[0:1] += column_sum(grad_qkv.astype(f32))
     rows = pl.ds(pl.multiple_of((step + (0 if first else FIRST_TILES)) * TILE, TILE), TILE)
     heads[rows, : 3 * WIDTH] = dot(head_ref[...], grad_qkv)
     heads[rows, 3 * WIDTH :] = dot(head_ref[...], joined)
@@ -487,26 +595,51 @@
         unit_r, scale_r = normalize(regional_ref[...].astype(f32))
         normed_r = (unit_r * gain1 + bias1_ref[...]).astype(bf16)
         total = sum_qkv[...] + dot(normed_r.T, grad_qkv_r)
+        columns = sums[0:1] + column_sum(grad_qkv_r.astype(f32))
         for part in range(3):
             cols = slice(part * WIDTH, (part + 1) * WIDTH)
-            late_ref[cols, :] = total[:, cols].astype(bf16)
-        late_ref[3 * WIDTH :, :] = (
+            late_rows[cols, :] = total[:, cols].astype(bf16)
+        late_rows[3 * WIDTH :, :] = (
             grad_out_ref[...] + dot(mixed_r_ref[...].T, grad_branch)
         ).astype(bf16)
+        weights = w_qkv_ref[...].astype(f32)
+        by_bias = weights * columns
+        by_gain = weights * total
+        turned_bias = fold_lanes(by_bias).T
+        turned_gain = fold_lanes(by_gain).T
+        grad_bias1 = column_sum(turned_bias)
+        grad_gain1 = (column_sum(turned_gain) - bias1_ref[...] * grad_bias1) / gain1
+        small = [
+            grad_gain1,
+            grad_bias1,
+            columns[:, :WIDTH],
+            columns[:, 2 * WIDTH :],
+            sums_mlp_ref[3:4] + column_sum(grad_branch.astype(f32)),
+            sums_mlp_ref[1:2],
+            sums_mlp_ref[2:3],
+            sums_mlp_ref[0:1],
+        ]
+        units = row_fc1_ref.shape[1] // WIDTH
+        more = [row_fc1_ref[0:1, at * WIDTH : (at + 1) * WIDTH] for at in range(units)]
+        more.append(jnp.zeros((8 - units, WIDTH), f32))
+        share = stay_ref.shape[1] - 8
+
+        def chunk_of(part):
+            extra = jnp.zeros((8, WIDTH), f32)
+            if part < 2:
+                extra = jnp.concatenate(more if part else small, axis=0)
+            rows = late_rows[part * share : (part + 1) * share]
+            return jnp.concatenate([rows, extra.astype(bf16)], axis=0)
+
+        put_shares(own_ref[0], stay_ref, send_ref, chunk_of)
         grad_normed_r = dot_nt(grad_qkv_r, w_qkv_ref[...])
-        small_ref[...] = sums[...]
-        small_ref[0:1] = column_sum(grad_normed_r * unit_r)
-        small_ref[1:2] = column_sum(grad_normed_r)
-        small_ref[2:3] += column_sum(grad_qkv_r[:, :WIDTH].astype(f32))
-        small_ref[3:4] += column_sum(grad_qkv_r[:, 2 * WIDTH :].astype(f32))
-        small_ref[4:5] = column_sum(grad_branch.astype(f32))
         regional_out_ref[...] = (
             came + normalize_back(grad_normed_r * gain1, unit_r, scale_r)
         ).astype(bf16)
 
 
-def run_back_attention(order, keep, qkv, probs, joined, grad_mixed, grad_after, plain, mixed, head, gain1, bias1,
-                       held=None, ending=None):
+def run_back_attention(order, keep, own, qkv, probs, joined, grad_mixed, grad_after, plain, mixed, head, gain1, bias1,
+                       held=None, ending=None, parts=1):
     windows = qkv.shape[0]
     steps = windows // TILE
     rows = TILE * TALL
@@ -530,26 +663,27 @@
     if held is not None:
         in_specs += [whole(a.shape) for a in held[:4]] + [pl.BlockSpec(memory_space=pl.ANY)]
         args += list(held)
-        aliases = {2 + len(args) - 1: 0}
+        aliases = {3 + len(args) - 1: 0}
     if ending is not None:
         in_specs += [whole(a.shape) for a in ending]
         args += list(ending)
-    held_shapes = [(WIDTH, 3 * WIDTH), (8, WIDTH), (windows, 4 * WIDTH), (windows, WIDTH)]
+    held_shapes = [(WIDTH, 3 * WIDTH), (8, 3 * WIDTH), (windows, 4 * WIDTH), (windows, WIDTH)]
     outs = [((steps * TILE * SLOT, 3 * WIDTH), bf16, tile((TILE * SLOT, 3 * WIDTH)))]
     scratch = []
+    late_shape = (parts // 2, 4 * WIDTH // parts + 8, WIDTH)
     if ending is None:
         outs += [(s, f32, whole(s)) for s in held_shapes]
     else:
         outs += [
-            ((4 * WIDTH, WIDTH), bf16, whole((4 * WIDTH, WIDTH))),
+            (late_shape, bf16, whole(late_shape)),
+            (late_shape, bf16, whole(late_shape)),
             ((windows, WIDTH), bf16, whole((windows, WIDTH))),
-            ((8, WIDTH), f32, whole((8, WIDTH))),
         ]
-        scratch = [pltpu.VMEM(s, f32) for s in held_shapes]
+        scratch = [pltpu.VMEM(s, f32) for s in held_shapes] + [pltpu.VMEM((4 * WIDTH, WIDTH), bf16)]
     return pl.pallas_call(
         functools.partial(back_attention_kernel, held is None, ending is not None),
         grid_spec=pltpu.PrefetchScalarGridSpec(
-            num_scalar_prefetch=2,
+            num_scalar_prefetch=3,
             grid=(count,),
             in_specs=in_specs,
             out_specs=[spec for _, _, spec in outs],
@@ -560,64 +694,203 @@
         compiler_params=pltpu.CompilerParams(
             dimension_semantics=("arbitrary",), vmem_limit_bytes=VMEM_LIMIT
         ),
-        cost_estimate=pl.CostEstimate(
-            flops=4_500_000_000 * count, bytes_accessed=5_000_000 * count, transcendentals=0
-        ),
+        cost_estimate=took(5 * count),
         name="back_attention",
-    )(order, keep, *args)
-
-
-def back_rows_kernel(
-    order_ref, grad_qkv_ref, joined_ref, grad_after_ref, gather_ref, gain1_ref, w_qkv_ref,
-    tokens_out_ref, small_ref, windows,
-):
+    )(order, keep, own, *args)
+
+
+def back_rows_kernel(begin, order_ref, grad_qkv_ref, joined_ref, grad_after_ref, gain1_ref, w_qkv_ref, *refs):
+    windows_ref, rows_low, done = refs[-3:]
     step = pl.program_id(0)
-    gain1 = gain1_ref[...]
-
-    @pl.when(step == 0)
-    def clear():
-        small_ref[...] = jnp.zeros_like(small_ref)
+
+    def copies(at_step):
+        places = [order_ref[(begin + at_step) * TILE + at] for at in range(TILE)]
+        return [
+            pltpu.make_async_copy(rows_low.at[at], windows_ref.at[place], done.at[at])
+            for at, place in enumerate(places)
+        ]
 
     unit, scale = normalize(joined_ref[...].astype(f32).reshape(TILE * SLOT, WIDTH))
     grad_normed = dot_nt(grad_qkv_ref[...], w_qkv_ref[...])
-    small_ref[0:1] += column_sum(grad_normed * unit)
-    small_ref[1:2] += column_sum(grad_normed)
-    grad_in = normalize_back(grad_normed * gain1, unit, scale)
+    grad_in = normalize_back(grad_normed * gain1_ref[...], unit, scale)
+
+    @pl.when(step > 0)
+    def drain():
+        for copy in copies(step - 1):
+            copy.wait()
+
+    empty = jnp.zeros((SLOT - TALL, WIDTH), f32)
     for at in range(TILE):
         rows = grad_in[at * SLOT : at * SLOT + TALL] + grad_after_ref[at * TALL : (at + 1) * TALL]
-        windows[order_ref[step * TILE + at], :TALL] = rows
+        rows_low[at] = jnp.concatenate([rows, empty], axis=0).astype(bf16)
+    for copy in copies(step):
+        copy.start()
 
     @pl.when(step == pl.num_programs(0) - 1)
     def finish():
-        def relay(line, carry):
-            block = windows[pl.ds(line * TILE, TILE)][:, :TALL].reshape(TILE * TALL, WIDTH)
-            tokens_out_ref[line] = dot(gather_ref[...], block.astype(bf16)).astype(bf16)
-            return carry
-
-        lax.fori_loop(0, REG_SIDE, relay, 0)
-
-
-def run_back_rows(order, grad_qkv, joined, grad_after, gather, gain1, w_qkv):
+        for copy in copies(step):
+            copy.wait()
+
+
+def run_back_rows(order, grad_qkv, joined, grad_after, gain1, w_qkv, begin, count, held=None):
     windows = joined.shape[0]
+
+    def tile(shape):
+        return pl.BlockSpec(shape, lambda step, *_: (step + begin,) + (0,) * (len(shape) - 1))
+
     tiled = [(TILE * SLOT, 3 * WIDTH), (TILE, SLOT, WIDTH), (TILE * TALL, WIDTH)]
-    fixed = (gather, gain1, w_qkv)
-    outs = [((REG_SIDE, gather.shape[0], WIDTH), bf16), ((8, WIDTH), f32)]
+    fixed = [gain1, w_qkv]
+    in_specs = [tile(b) for b in tiled] + [whole(a.shape) for a in fixed]
+    args = [grad_qkv, joined, grad_after] + fixed
+    aliases = {}
+    if held is not None:
+        in_specs.append(pl.BlockSpec(memory_space=pl.ANY))
+        args.append(held)
+        aliases = {len(args): 0}
     return pl.pallas_call(
-        back_rows_kernel,
+        functools.partial(back_rows_kernel, begin),
         grid_spec=pltpu.PrefetchScalarGridSpec(
             num_scalar_prefetch=1,
-            grid=(windows // TILE,),
-            in_specs=[tiles(b) for b in tiled] + [whole(a.shape) for a in fixed],
-            out_specs=[whole(s) for s, _ in outs],
-            scratch_shapes=[pltpu.VMEM((windows, SLOT, WIDTH), f32)],
+            grid=(count,),
+            in_specs=in_specs,
+            out_specs=pl.BlockSpec(memory_space=pl.ANY),
+            scratch_shapes=[pltpu.VMEM((TILE, SLOT, WIDTH), bf16), pltpu.SemaphoreType.DMA((TILE,))],
         ),
-        out_shape=[jax.ShapeDtypeStruct(s, d) for s, d in outs],
+        out_shape=jax.ShapeDtypeStruct((windows, SLOT, WIDTH), bf16),
+        input_output_aliases=aliases,
         compiler_params=pltpu.CompilerParams(
             dimension_semantics=("arbitrary",), vmem_limit_bytes=VMEM_LIMIT
         ),
-        cost_estimate=pl.CostEstimate(flops=15_000_000_000, bytes_accessed=30_000_000, transcendentals=0),
+        cost_estimate=took(2.5 * count),
         name="back_rows",
-    )(order, grad_qkv, joined, grad_after, *fixed)
+    )(order, *args)
+
+
+def relay_kernel(gather_ref, windows_ref, tokens_out_ref):
+    for line in range(tokens_out_ref.shape[0]):
+        rows = windows_ref[line * TILE : (line + 1) * TILE].reshape(TILE * SLOT, WIDTH)
+        tokens_out_ref[line] = dot(gather_ref[...], rows).astype(bf16)
+
+
+def run_relay(gather, windows):
+    lines = windows.shape[0] // TILE
+    return pl.pallas_call(
+        relay_kernel,
+        grid=(lines // 2,),
+        in_specs=[whole(gather.shape), tiles((2 * TILE, SLOT, WIDTH))],
+        out_specs=tiles((2, gather.shape[0], WIDTH)),
+        out_shape=jax.ShapeDtypeStruct((lines, gather.shape[0], WIDTH), bf16),
+        compiler_params=pltpu.CompilerParams(
+            dimension_semantics=("arbitrary",), vmem_limit_bytes=VMEM_LIMIT
+        ),
+        cost_estimate=took(5),
+        name="relay",
+    )(gather, windows)
+
+
+def early_out_kernel(own_ref, near_ref, far_ref, fc1_ref, fc2_ref):
+    block = pl.program_id(0)
+    per, share, _ = near_ref.shape
+    inner = own_ref[0] % per
+    place = block ^ (own_ref[0] // per)
+
+    def fill(rows_ref):
+        @pl.when(block < 2)
+        def first():
+            for at in range(per):
+                start = at * share
+                column = start // WIDTH * WIDTH
+                fc1_ref[start - column : start - column + share, column : column + WIDTH] = rows_ref[
+                    at ^ inner
+                ].astype(f32)
+
+        @pl.when(block >= 2)
+        def second():
+            for at in range(per):
+                fc2_ref[at * share : (at + 1) * share] = rows_ref[at ^ inner].astype(f32)
+
+    @pl.when(place < 2)
+    def near():
+        fill(near_ref)
+
+    @pl.when(place >= 2)
+    def far():
+        fill(far_ref)
+
+
+def run_early_out(own, near, far, units):
+    half, share, _ = near.shape
+    per = half // 2
+    return pl.pallas_call(
+        early_out_kernel,
+        grid_spec=pltpu.PrefetchScalarGridSpec(
+            num_scalar_prefetch=1,
+            grid=(4,),
+            in_specs=[
+                pl.BlockSpec((per, share, WIDTH), lambda at, own: (jnp.minimum(at ^ (own[0] // per), 1), 0, 0)),
+                pl.BlockSpec(
+                    (per, share, WIDTH), lambda at, own: (jnp.maximum((at ^ (own[0] // per)) - 2, 0), 0, 0)
+                ),
+            ],
+            out_specs=[
+                pl.BlockSpec((WIDTH, units // 2), lambda at, own: (0, jnp.minimum(at, 1))),
+                pl.BlockSpec((units // 2, WIDTH), lambda at, own: (jnp.maximum(at - 2, 0), 0)),
+            ],
+        ),
+        out_shape=[
+            jax.ShapeDtypeStruct((WIDTH, units), f32),
+            jax.ShapeDtypeStruct((units, WIDTH), f32),
+        ],
+        compiler_params=pltpu.CompilerParams(
+            dimension_semantics=("arbitrary",), vmem_limit_bytes=VMEM_LIMIT
+        ),
+        cost_estimate=took(7),
+        name="early_out",
+    )(own, near, far)
+
+
+def late_out_kernel(own_ref, near_ref, far_ref, qkv_ref, out_ref, small_ref):
+    half, share, _ = near_ref.shape
+    share -= 8
+    own = own_ref[0]
+
+    def fill(halves):
+        for at in range(2 * half):
+            rows = halves[at // half][(at % half) ^ (own % half)].astype(f32)
+            row, part = at * share % WIDTH, at * share // WIDTH
+            if part < 3:
+                qkv_ref[row : row + share, part * WIDTH : (part + 1) * WIDTH] = rows[:share]
+            else:
+                out_ref[row : row + share] = rows[:share]
+            if at < 2:
+                small_ref[8 * at : 8 * at + 8] = rows[share:]
+
+    @pl.when(own < half)
+    def low():
+        fill((near_ref, far_ref))
+
+    @pl.when(own >= half)
+    def high():
+        fill((far_ref, near_ref))
+
+
+def run_late_out(own, near, far):
+    return pl.pallas_call(
+        late_out_kernel,
+        in_specs=[
+            pl.BlockSpec(memory_space=pltpu.SMEM),
+            pl.BlockSpec(memory_space=pltpu.VMEM),
+            pl.BlockSpec(memory_space=pltpu.VMEM),
+        ],
+        out_shape=[
+            jax.ShapeDtypeStruct((WIDTH, 3 * WIDTH), f32),
+            jax.ShapeDtypeStruct((WIDTH, WIDTH), f32),
+            jax.ShapeDtypeStruct((16, WIDTH), f32),
+        ],
+        compiler_params=pltpu.CompilerParams(vmem_limit_bytes=VMEM_LIMIT),
+        cost_estimate=took(4),
+        name="late_out",
+    )(own, near, far)
 
 
 def band_to_windows(band_values, win_count):
@@ -639,49 +912,49 @@
     return [img_bits[:1]] + [rest[at : at + 2] for at in range(0, len(rest), 2)]
 
 
-def stage_peers(stage):
-    dp_size, img_size = lax.axis_size("dp"), lax.axis_size("img")
-    flat = lax.axis_index("dp") * img_size + lax.axis_index("img")
-    masks = [(1 << bit) * (img_size if name == "dp" else 1) for name, bit in stage]
-    own = sum(((flat // mask) % 2) << place for place, mask in enumerate(masks))
+def stage_masks(stage):
+    img_size = lax.axis_size("img")
+    return [(1 << bit) * (img_size if name == "dp" else 1) for name, bit in stage]
+
+
+def stage_moves(stage):
+    devices = lax.axis_size("dp") * lax.axis_size("img")
     moves = []
-    for offset in range(1, 1 << len(masks)):
-        flip = sum(mask for place, mask in enumerate(masks) if offset >> place & 1)
-        moves.append((offset, [(at, at ^ flip) for at in range(dp_size * img_size)]))
-    return own, moves
+    for offset in range(1, 1 << len(stage)):
+        flip = sum(mask for place, mask in enumerate(stage_masks(stage)) if offset >> place & 1)
+        moves.append((offset, [(at, at ^ flip) for at in range(devices)]))
+    return moves
+
+
+def own_share(stages):
+    flat = lax.axis_index("dp") * lax.axis_size("img") + lax.axis_index("img")
+    share = 0
+    for stage in stages:
+        own = sum(((flat // mask) % 2) << place for place, mask in enumerate(stage_masks(stage)))
+        share = (share << len(stage)) + own
+    return share
+
+
+def swap(rows, pairs):
+    return lax.ppermute(rows, ("dp", "img"), pairs)
+
+
+def add_up(pieces):
+    return sum(piece.astype(f32) for piece in pieces).astype(bf16)
 
 
 def sum_stage(rows, stage):
-    own, moves = stage_peers(stage)
     parts = rows.reshape((1 << len(stage), -1) + rows.shape[1:])
-    got = [
-        lax.ppermute(lax.dynamic_index_in_dim(parts, own ^ offset, 0, False), ("dp", "img"), pairs)
-        for offset, pairs in moves
-    ]
-    total = lax.dynamic_index_in_dim(parts, own, 0, False).astype(f32)
-    for piece in got:
-        total = total + piece.astype(f32)
-    return total.astype(bf16)
+    return add_up([parts[0]] + [swap(parts[offset], pairs) for offset, pairs in stage_moves(stage)])
 
 
 def gather_stage(rows, stage):
-    own, moves = stage_peers(stage)
-    pieces = [rows] + [lax.ppermute(rows, ("dp", "img"), pairs) for _, pairs in moves]
-    ordered = []
-    for place in range(len(pieces)):
-        piece = pieces[0]
-        for offset in range(1, len(pieces)):
-            piece = jnp.where((own ^ place) == offset, pieces[offset], piece)
-        ordered.append(piece)
-    return jnp.concatenate(ordered, axis=0)
-
-
-def sum_small(rows, stages):
+    return jnp.concatenate([rows] + [swap(rows, pairs) for _, pairs in stage_moves(stage)], axis=0)
+
+
+def sum_stages(rows, stages):
     for stage in stages:
-        _, moves = stage_peers(stage)
-        got = [lax.ppermute(rows, ("dp", "img"), pairs) for _, pairs in moves]
-        for piece in got:
-            rows = rows + piece
+        rows = sum_stage(rows, stage)
     return rows
 
 
@@ -713,7 +986,7 @@
         deal_kernel,
         out_shape=jax.ShapeDtypeStruct((count, (local.shape[0] + 1) * TILE, WIDTH), bf16),
         compiler_params=pltpu.CompilerParams(vmem_limit_bytes=VMEM_LIMIT),
-        cost_estimate=pl.CostEstimate(flops=1_000_000_000, bytes_accessed=7_000_000, transcendentals=0),
+        cost_estimate=took(5),
         name="deal",
     )(pick, region, local)
 
@@ -727,7 +1000,7 @@
             jax.ShapeDtypeStruct((came.shape[1] // TILE - 1, slots, WIDTH), bf16),
         ],
         compiler_params=pltpu.CompilerParams(vmem_limit_bytes=VMEM_LIMIT),
-        cost_estimate=pl.CostEstimate(flops=1_000_000_000, bytes_accessed=7_000_000, transcendentals=0),
+        cost_estimate=took(5),
         name="collect",
     )(pick, came)
 
@@ -752,8 +1025,8 @@
     band = TILE * WIN_SIDE * WIN_SIDE
     spread = np.zeros((TILE * SLOT, band), np.float32)
     spread[window * SLOT + 1 + place, raster] = 1
-    gather = np.zeros((band, TILE * TALL), np.float32)
-    gather[raster, window * TALL + 1 + place] = 1
+    gather = np.zeros((band, TILE * SLOT), np.float32)
+    gather[raster, window * SLOT + 1 + place] = 1
     head = np.zeros((TILE, TILE * SLOT), np.float32)
     head[np.arange(TILE), np.arange(TILE) * SLOT] = 1
     place = np.arange(WIN_SIDE * WIN_SIDE + 1)[None, :]
@@ -786,6 +1059,7 @@
 ):
     devices = lax.axis_size("dp")
     stages = reduce_stages()
+    parts = devices * lax.axis_size("img")
     own_rank = lax.axis_index("dp")
     win_count = regional.shape[1]
     all_windows = window_slot.shape[1]
@@ -829,49 +1103,52 @@
         gain2, bias2, w_fc1, bias_fc1[None], w_fc2, bias_fc2[None],
     )
     came = swap_tiles(out, devices)
-    grad_after, grad_mixed, early, grad_out, small, row_fc1 = run_back_mlp(
-        keep, cot, after, mixed, hidden, slope, stretch, gain2, bias2, w_fc1, w_fc2, w_out
-    )
-    early = sum_stage(early, stages[0])
-    attention = (order, keep, qkv, probs, joined, grad_mixed, grad_after, plain, mixed_mask, head, gain1, bias1)
+    own = own_share(stages)[None]
+    grad_after, grad_mixed, early, early_sent, grad_out, small, row_fc1 = run_back_mlp(
+        parts, keep, own, cot, after, mixed, hidden, slope, stretch, gain2, bias2, w_fc1, w_fc2, w_out
+    )
+    (_, pairs), = stage_moves(stages[0])
+    early_came = swap(early_sent, pairs)
+    attention = (
+        order, keep, own, qkv, probs, joined, grad_mixed, grad_after, plain, mixed_mask, head, gain1, bias1
+    )
     grad_qkv, *held = run_back_attention(*attention)
-    held, early = lax.optimization_barrier((held, early))
+    early = add_up([early, early_came])
+    held, early, came = lax.optimization_barrier((held, early, came))
     early = sum_stage(early, stages[1])
-    grad_qkv, late, regional_out, small_late = run_back_attention(
+    grad_qkv, late, late_sent, regional_out = run_back_attention(
         *attention,
         held=(*held, grad_qkv),
-        ending=(grad_out, order[None], regional[0], qkv_r, probs_r, mixed_r, w_qkv, w_out),
-    )
-    late = sum_stage(late, stages[0])
-    grad_qkv, early, came = lax.optimization_barrier((grad_qkv, early, came))
-    for stage in stages[2:]:
-        early = sum_stage(early, stage)
-    tokens_out, small_rows = run_back_rows(order, grad_qkv, joined, grad_after, gather, gain1, w_qkv)
+        ending=(grad_out, order[None], regional[0], qkv_r, probs_r, mixed_r, w_qkv, w_out, small, row_fc1),
+        parts=parts,
+    )
+    late_came = swap(late_sent, pairs)
+    grad_qkv, early = lax.optimization_barrier((grad_qkv, early))
+    early = sum_stages(early, stages[2:])
+    rows = (order, grad_qkv, joined, grad_after, gain1, w_qkv)
+    windows = run_back_rows(*rows, 0, ROWS_FIRST)
+    windows, early, late_came = lax.optimization_barrier((windows, early, late_came))
+    late = sum_stage(add_up([late, late_came]), stages[1])
+    for stage in reversed(stages[2:]):
+        early = gather_stage(early, stage)
+    windows = run_back_rows(*rows, ROWS_FIRST, win_count // TILE - ROWS_FIRST, held=windows)
+    windows, early, late = lax.optimization_barrier((windows, early, late))
+    late = sum_stages(late, stages[2:])
+    moves = stage_moves(stages[1])
+    direct = [swap(early, moves[at][1]) for at in (0, 1)]
+    tokens_out = run_relay(gather, windows)
+    tokens_out, came, late, early, direct = lax.optimization_barrier((tokens_out, came, late, early, direct))
+    for stage in reversed(stages[2:]):
+        late = gather_stage(late, stage)
     out_regional, out_local = run_collect(pick_back, came)
-    vectors = jnp.concatenate(
-        [
-            small_late[0:2] + small_rows[0:2],
-            small_late[2:4],
-            small[3:4] + small_late[4:5],
-            small[1:3],
-            small[0:1],
-            row_fc1[0].reshape(-1, WIDTH),
-            jnp.zeros((4, WIDTH), f32),
-        ],
-        axis=0,
-    )
-    for stage in stages[1:]:
-        late = sum_stage(late, stage)
-    for stage in reversed(stages):
-        early = gather_stage(early, stage)
-    for stage in reversed(stages):
-        late = gather_stage(late, stage)
-    vectors = sum_small(vectors, stages)
-    grad_w_qkv = jnp.concatenate([late[at * WIDTH : (at + 1) * WIDTH] for at in range(3)], axis=1)
-    units = w_fc1.shape[1]
-    grad_w_fc1 = jnp.concatenate(
-        [early[at : at + WIDTH] for at in range(0, units, WIDTH)], axis=1
-    )
+    early = jnp.concatenate([early] + direct + [swap(early, pairs) for _, pairs in moves[2:]], axis=0)
+    out_local, early, late = lax.optimization_barrier((out_local, early, late))
+    late = gather_stage(late, stages[1])
+    early_far = swap(early, pairs)
+    grad_w_fc1, grad_w_fc2 = run_early_out(own, early, early_far, w_fc1.shape[1])
+    grad_w_fc1, grad_w_fc2, late = lax.optimization_barrier((grad_w_fc1, grad_w_fc2, late))
+    late_far = swap(late, pairs)
+    grad_w_qkv, grad_w_out, vectors = run_late_out(own, late, late_far)
     return (
         jnp.swapaxes(out_local, 0, 1)[None],
         out_regional[None],
@@ -879,16 +1156,16 @@
         regional_out[None],
         vectors[0],
         vectors[1],
-        grad_w_qkv.astype(f32),
+        grad_w_qkv,
         vectors[2],
         vectors[3],
-        late[3 * WIDTH :].astype(f32),
+        grad_w_out,
         vectors[4],
         vectors[5],
         vectors[6],
-        grad_w_fc1.astype(f32),
+        grad_w_fc1,
         vectors[8:12].reshape(-1),
-        early[units:].astype(f32),
+        grad_w_fc2,
         vectors[7],
     )
 

time: 352 us -> 312 us (0.89)
  waiting for transfers between devices: 51.6 us -> 30.6 us
  other arithmetic: 27.8 us -> 11.2 us
  starting transfers between devices: 55 us -> 44.9 us
  Pallas kernels: 202 us -> 206 us
    pallas_call x1 -> x5, Pallas kernels: 20.6 us -> 37.2 us  [the longest x2 20.3 us: run_back_rows(): pl.pallas_call(functools.partial(back_rows_kernel, begin), grid_spec=pltp...]
    ppermute x35 -> x28, waiting for transfers between devices: 40.5 us -> 25.7 us  [swap(): return lax.ppermute(rows, ('dp', 'img'), pairs)]
    pallas_call x1, Pallas kernels: 75.6 us -> 62.1 us  [run_forward(): pl.pallas_call(forward_kernel, grid_spec=pltpu.PrefetchScalarGridSpec(num...]
    convert_element_type x10 -> x6, other arithmetic: 16.5 us -> 5.14 us  [add_up(): return sum((piece.astype(f32) for piece in pieces)).astype(bf16)]
    ppermute x35 -> x28, starting transfers between devices: 41.6 us -> 32.8 us  [swap(): return lax.ppermute(rows, ('dp', 'img'), pairs)]
    all_to_all x2, waiting for transfers between devices: 11 us -> 4.94 us  [swap_tiles(): lax.all_to_all(tiles_sent, 'dp', split_axis=0, concat_axis=0, tiled=True)]
    squeeze x6 -> x0, local copies, waits for them, and re-layouts: 4.92 us -> none  [sum_stage(): lax.dynamic_index_in_dim(parts, own ^ offset, 0, False)]
    unnamed x22 -> x28, local copies, waits for them, and re-layouts: 2.43 us -> 6.82 us
  transfers between devices with their start and end apart: 37 -> 30, of which waited for: 14 -> 9; matrix products, arithmetic and copies ran while one was open for 8% -> 4% of each run, Pallas kernels for 41% -> 62%
where the time goes in v4:
time: 312 us; the launch traced here: 308 us
  Pallas kernels  206 us (66%)
  starting transfers between devices  44.9 us (14%)
  waiting for transfers between devices  30.6 us (10%)
  local copies, waits for them, and re-layouts  13.9 us (4%)
  other arithmetic  11.2 us (4%)
    pallas_call x1, Pallas kernels, run_forward(): pl.pallas_call(forward_kernel, grid_spec=pltpu.PrefetchScalarGridSpec(num...  62.1 us
    pallas_call x1, Pallas kernels, run_back_mlp(): pl.pallas_call(back_mlp_kernel, grid_spec=pltpu.PrefetchScalarGridSpec(nu...  54.9 us
    pallas_call x2, Pallas kernels, run_back_attention(): pl.pallas_call(functools.partial(back_attention_kernel, held is None, end...  42.3 us
    ppermute x28, starting transfers between devices, swap(): return lax.ppermute(rows, ('dp', 'img'), pairs)  32.8 us
    ppermute x28, waiting for transfers between devices, swap(): return lax.ppermute(rows, ('dp', 'img'), pairs)  25.7 us
    pallas_call x2, Pallas kernels, run_back_rows(): pl.pallas_call(functools.partial(back_rows_kernel, begin), grid_spec=pltp...  20.3 us
    all_to_all x2, starting transfers between devices, swap_tiles(): lax.all_to_all(tiles_sent, 'dp', split_axis=0, concat_axis=0, tiled=True)  12.1 us
    pallas_call x1, Pallas kernels, run_early_out(): pl.pallas_call(early_out_kernel, grid_spec=pltpu.PrefetchScalarGridSpec(n...  7.19 us
  transfers between devices with their start and end apart: 30, of which 9 were waited for; matrix products, arithmetic and copies ran while one was open for 4% of the time, Pallas kernels for 62%

profile of v4, /device:TPU:0, one launch (start us, length us, event | category | flops | bytes accessed | tf_op | source)
XLA Modules:
  0.0 308.4 jit_solution(369789585281497920)
XLA Ops:
  2.6 4.7 %deal.1 = bf16[8,400,512]{2,1,0:T(8,128)(2,1)} custom-call(bf16[128,128]{1,0:T(8,128)(2,1)} %get-tuple-element.157.pick_ref, bf16[64,512]{1,0:T(8,128)(2,1)} %bitcast.73, bf16[49,64,512]{2,1,0:T(8,128)(2,1)} %bitcast.71), custom_call_target="tpu_custom_call" | custom-call | flops 5750000128 | bytes 1000000 | tf_op jit(solution)/shard_map/deal/pallas_call | solution.py:985
  7.3 7.4 %all-to-all-start = ((bf16[8,400,512]{2,1,0:T(8,128)(2,1)}), bf16[8,400,512]{2,1,0:T(8,128)(2,1)S(1)}, u32[]{:S(2)}, u32[]{:S(2)}) async-start(bf16[8,400,512]{2,1,0:T(8,128)(2,1)} %deal.1), calls=%async_computation | async-start | bytes 6553600 | tf_op jit(solution)/shard_map/all_to_all | solution.py:1012
  21.2 62.1 %forward.1 = (bf16[8,400,512]{2,1,0:T(8,128)(2,1)}, bf16[64,12,64,128]{3,2,1,0:T(8,128)(2,1)}, bf16[64,8,64,128]{3,2,1,0:T(8,128)(2,1)}, bf16[64,64,512]{2,1,0:T...) custom-call(s32[64]{0:T(128)} %select_reduce_fusion.1.order_ref, ...), custom_call_target="tpu_custom_call" | custom-call | flops 70149996544 | bytes 1000000 | tf_op jit(solution)/shard_map/forward/pallas_call | solution.py:368
  83.3 4.9 %all-to-all-done.cot_ref = bf16[8,400,512]{2,1,0:T(8,128)(2,1)S(1)} async-done(((bf16[8,400,512]{2,1,0:T(8,128)(2,1)}), bf16[8,400,512]{2,1,0:T(8,128)(2,1)S(1)}, u32[]{:S(2)}, u32[]{:S(2)}) %all-to-all-start) | async-done | bytes 3276832 | tf_op jit(solution)/shard_map/all_to_all | solution.py:1012
  89.9 4.7 %all-to-all-start.1 = ((bf16[8,400,512]{2,1,0:T(8,128)(2,1)}), bf16[8,400,512]{2,1,0:T(8,128)(2,1)}, u32[]{:S(2)}, u32[]{:S(2)}) async-start(bf16[8,400,512]{2,1,0:T(8,128)(2,1)} %get-tuple-element.92), calls=%async_computation.1 | async-start | bytes 6553600 | tf_op jit(solution)/shard_map/all_to_all | solution.py:1012
  94.6 54.9 %back_mlp.1 = (f32[3584,512]{1,0:T(8,128)}, bf16[64,4,64,128]{3,2,1,0:T(8,128)(2,1)}, bf16[16,128,512]{2,1,0:T(8,128)(2,1)}, bf16[16,128,512]{2,1,0:T(8,128)(2,1...) custom-call(f32[1]{0:T(128)} %bitcast.3.keep_ref, s32[1]{0:T(128)} %bitcast.4.own_ref, ...), custom_call_target="tpu_custom_call" | custom-call | flops 63250001920 | bytes 1000000 | tf_op jit(solution)/shard_map/back_mlp/pallas_call | solution.py:485
  149.5 15.3 %back_attention.2 = (bf16[4096,1536]{1,0:T(8,128)(2,1)}, f32[512,1536]{1,0:T(8,128)}, f32[8,1536]{1,0:T(8,128)}, f32[64,2048]{1,0:T(8,128)}, f32[64,512]{1,0:T(8,128)}) custom-call(s32[64]{0:T(128)} %select_reduce_fusion.1.order_ref, f32[1]{0:T(128)} %bitcast.3.keep_ref, s32[1]{0:T(128)} %bitcast.4.own_ref, ...), custom_call_target="tpu_custom_call" | custom-call | flops 17250000896 | bytes 1000000 | tf_op jit(solution)/shard_map/back_attention/pallas_call | solution.py:683
  166.2 2.9 add_convert_fusion
  173.8 27.0 %back_attention.3 = (bf16[4096,1536]{1,0:T(8,128)(2,1)}, bf16[16,72,512]{2,1,0:T(8,128)(2,1)}, bf16[16,72,512]{2,1,0:T(8,128)(2,1)}, bf16[64,512]{1,0:T(8,128)(2,1)}) custom-call(s32[64]{0:T(128)} %select_reduce_fusion.1.order_ref, f32[1]{0:T(128)} %bitcast.3.keep_ref, s32[1]{0:T(128)} %bitcast.4.own_ref, ...), custom_call_target="tpu_custom_call", output_to_operand_aliasing={{0}: (17, {})} | custom-call | flops 28750000128 | bytes 1000000 | tf_op jit(solution)/shard_map/back_attention/pallas_call | solution.py:683
  205.4 2.4 collective-permute-start.6
  207.8 6.8 %back_rows.2.refs_0_ = bf16[64,64,512]{2,1,0:T(8,128)(2,1)} custom-call(s32[64]{0:T(128)} %select_reduce_fusion.1.order_ref, bf16[4096,1536]{1,0:T(8,128)(2,1)} %get-tuple-element.106.grad_qkv_ref, bf16[64,64,512]{2,1,0:T(8,128)(2,1)} %get-tuple-element.79.joined_ref, f32[3584,512]{1,0:T(8,128)} %get-tuple-element.85.grad_after_ref, f32[1,512]{1,0:T(1,128)} %bitcast.59, ...), custom_call_target="tpu_custom_call" | custom-call | flops 5750000128 | bytes 1000000 | tf_op jit(solution)/shard_map/back_rows/pallas_call | solution.py:750
  214.9 5.1 %collective-permute-done.5 = bf16[1,128,512]{2,1,0:T(8,128)(2,1)S(1)} collective-permute-done((bf16[1,128,512]{2,1,0:T(8,128)(2,1)S(1)}, bf16[1,128,512]{2,1,0:T(8,128)(2,1)S(1)}, u32[]{:S(2)}, u32[]{:S(2)}) %collective-permute-start.5) | collective-permute-done | bytes 131104 | tf_op jit(solution)/shard_map/ppermute | solution.py:939
  220.2 2.7 collective-permute-start.10
  229.9 13.5 %back_rows.3.windows_ref = bf16[64,64,512]{2,1,0:T(8,128)(2,1)} custom-call(s32[64]{0:T(128)} %select_reduce_fusion.1.order_ref, bf16[4096,1536]{1,0:T(8,128)(2,1)} %get-tuple-element.106.grad_qkv_ref, bf16[64,64,512]{2,1,0:T(8,128)(2,1)} %get-tuple-element.79.joined_ref, ...), custom_call_target="tpu_custom_call", output_to_operand_aliasing={{}: (6, {})} | custom-call | flops 17250000896 | bytes 1000000 | tf_op jit(solution)/shard_map/back_rows/pallas_call | solution.py:750
  251.1 5.8 %relay.1 = bf16[8,392,512]{2,1,0:T(8,128)(2,1)} custom-call(bf16[392,512]{1,0:T(8,128)(2,1)} %constant.195.clone.gather_ref, bf16[64,64,512]{2,1,0:T(8,128)(2,1)} %back_rows.3.windows_ref), custom_call_target="tpu_custom_call" | custom-call | flops 5750000128 | bytes 1000000 | tf_op jit(solution)/shard_map/relay/pallas_call | solution.py:777
  257.1 2.7 collective-permute-start.22
  261.5 2.2 collective-permute-start.19
  263.7 4.6 %collect.1 = (bf16[64,512]{1,0:T(8,128)(2,1)}, bf16[49,64,512]{2,1,0:T(8,128)(2,1)}) custom-call(bf16[128,128]{1,0:T(8,128)(2,1)} %get-tuple-element.158.pick_ref, bf16[8,400,512]{2,1,0:T(8,128)(2,1)} %all-to-all-done.1.came_ref), custom_call_target="tpu_custom_call" | custom-call | flops 5750000128 | bytes 1000000 | tf_op jit(solution)/shard_map/collect/pallas_call | solution.py:996
  268.4 3.5 %collective-permute-done.19 = bf16[4,128,512]{2,1,0:T(8,128)(2,1)} collective-permute-done((bf16[4,128,512]{2,1,0:T(8,128)(2,1)S(1)}, bf16[4,128,512]{2,1,0:T(8,128)(2,1)}, u32[]{:S(2)}, u32[]{:S(2)}) %collective-permute-start.19) | collective-permute-done | bytes 524320 | tf_op jit(solution)/shard_map/ppermute | solution.py:939
  276.8 7.3 %collective-permute-done.26 = bf16[4,72,512]{2,1,0:T(8,128)(2,1)S(1)} collective-permute-done((bf16[4,72,512]{2,1,0:T(8,128)(2,1)S(1)}, bf16[4,72,512]{2,1,0:T(8,128)(2,1)S(1)}, u32[]{:S(2)}, u32[]{:S(2)}) %collective-permute-start.26) | collective-permute-done | bytes 294944 | tf_op jit(solution)/shard_map/ppermute | solution.py:939
  284.1 6.0 %collective-permute-done.25 = bf16[4,72,512]{2,1,0:T(8,128)(2,1)S(1)} collective-permute-done((bf16[4,72,512]{2,1,0:T(8,128)(2,1)S(1)}, bf16[4,72,512]{2,1,0:T(8,128)(2,1)S(1)}, u32[]{:S(2)}, u32[]{:S(2)}) %collective-permute-start.25) | collective-permute-done | bytes 294944 | tf_op jit(solution)/shard_map/ppermute | solution.py:939
  290.2 7.2 %early_out.1 = (f32[512,2048]{1,0:T(8,128)}, f32[2048,512]{1,0:T(8,128)}) custom-call(s32[1]{0:T(128)} %bitcast.4.own_ref, bf16[16,128,512]{2,1,0:T(8,128)(2,1)} %copy-done.2, bf16[16,128,512]{2,1,0:T(8,128)(2,1)} %collective-permute-done.23.far_ref), custom_call_target="tpu_custom_call" | custom-call | flops 8049999872 | bytes 1000000 | tf_op jit(solution)/shard_map/early_out/pallas_call | solution.py:824
  297.4 2.8 collective-permute-done.27.far_ref
  301.3 3.9 %late_out.1 = (f32[512,1536]{1,0:T(8,128)}, f32[512,512]{1,0:T(8,128)}, f32[16,512]{1,0:T(8,128)}) custom-call(s32[1]{0:T(128)} %bitcast.4.own_ref, bf16[16,72,512]{2,1,0:T(8,128)(2,1)} %copy-done.4, bf16[16,72,512]{2,1,0:T(8,128)(2,1)} %copy-done.11), custom_call_target="tpu_custom_call" | custom-call | flops 4600000000 | bytes 1000000 | tf_op jit(solution)/shard_map/late_out/pallas_call | solution.py:878
  (116 shorter events, 46.1 us)
Async XLA Ops:
  7.3 80.9 %all-to-all-start = ((bf16[8,400,512]{2,1,0:T(8,128)(2,1)}), bf16[8,400,512]{2,1,0:T(8,128)(2,1)S(1)}, u32[]{:S(2)}, u32[]{:S(2)}) async-start(bf16[8,400,512]{2,1,0:T(8,128)(2,1)} %deal.1), calls=%async_computation | async-start | bytes 6553600 | tf_op jit(solution)/shard_map/all_to_all | solution.py:1012
  89.9 79.2 %all-to-all-start.1 = ((bf16[8,400,512]{2,1,0:T(8,128)(2,1)}), bf16[8,400,512]{2,1,0:T(8,128)(2,1)}, u32[]{:S(2)}, u32[]{:S(2)}) async-start(bf16[8,400,512]{2,1,0:T(8,128)(2,1)} %get-tuple-element.92), calls=%async_computation.1 | async-start | bytes 6553600 | tf_op jit(solution)/shard_map/all_to_all | solution.py:1012
  149.4 15.4 %collective-permute-start = (bf16[16,128,512]{2,1,0:T(8,128)(2,1)}, bf16[16,128,512]{2,1,0:T(8,128)(2,1)S(1)}, u32[]{:S(2)}, u32[]{:S(2)}) collective-permute-start(bf16[16,128,512]{2,1,0:T(8,128)(2,1)} %get-tuple-element.91), channel_id=1, source_target_pairs={{0,1},{1,0},{2,3},{3,2},{4,5},{5,4},{6,7},{7,6},{8,9},{9,8},{10,11... | collective-permute-start | bytes 6291464 | tf_op jit(solution)/shard_map/ppermute | solution.py:939
  170.3 30.6 %collective-permute-start.1 = (bf16[4,128,512]{2,1,0:T(8,128)(2,1)}, bf16[4,128,512]{2,1,0:T(8,128)(2,1)S(1)}, u32[]{:S(2)}, u32[]{:S(2)}) collective-permute-start(bf16[4,128,512]{2,1,0:T(8,128)(2,1)} %get-tuple-element.137), channel_id=1, source_target_pairs={{0,2},{1,3},{2,0},{3,1},{4,6},{5,7},{6,4},{7,5},{8,10},{9,11},{10,... | collective-permute-start | bytes 1572872 | tf_op jit(solution)/shard_map/ppermute | solution.py:939
  171.8 29.1 %collective-permute-start.3 = (bf16[4,128,512]{2,1,0:T(8,128)(2,1)}, bf16[4,128,512]{2,1,0:T(8,128)(2,1)}, u32[]{:S(2)}, u32[]{:S(2)}) collective-permute-start(bf16[4,128,512]{2,1,0:T(8,128)(2,1)} %get-tuple-element.138), channel_id=1, source_target_pairs={{0,6},{1,7},{2,4},{3,5},{4,2},{5,3},{6,0},{7,1},{8,14},{9,15},{10,... | collective-permute-start | bytes 1572872 | tf_op jit(solution)/shard_map/ppermute | solution.py:939
  173.7 28.0 %collective-permute-start.2 = (bf16[4,128,512]{2,1,0:T(8,128)(2,1)}, bf16[4,128,512]{2,1,0:T(8,128)(2,1)}, u32[]{:S(2)}, u32[]{:S(2)}) collective-permute-start(bf16[4,128,512]{2,1,0:T(8,128)(2,1)} %get-tuple-element.139), channel_id=1, source_target_pairs={{0,4},{1,5},{2,6},{3,7},{4,0},{5,1},{6,2},{7,3},{8,12},{9,13},{10,... | collective-permute-start | bytes 1572872 | tf_op jit(solution)/shard_map/ppermute | solution.py:939
  200.8 19.3 %collective-permute-start.7 = (bf16[16,72,512]{2,1,0:T(8,128)(2,1)}, bf16[16,72,512]{2,1,0:T(8,128)(2,1)S(1)}, u32[]{:S(2)}, u32[]{:S(2)}) collective-permute-start(bf16[16,72,512]{2,1,0:T(8,128)(2,1)} %get-tuple-element.108), channel_id=1, source_target_pairs={{0,1},{1,0},{2,3},{3,2},{4,5},{5,4},{6,7},{7,6},{8,9},{9,8},{10,11... | collective-permute-start | bytes 3538952 | tf_op jit(solution)/shard_map/ppermute | solution.py:939
  203.4 11.2 %collective-permute-start.4 = (bf16[1,128,512]{2,1,0:T(8,128)(2,1)S(1)}, bf16[1,128,512]{2,1,0:T(8,128)(2,1)S(1)}, u32[]{:S(2)}, u32[]{:S(2)}) collective-permute-start(bf16[1,128,512]{2,1,0:T(8,128)(2,1)S(1)} %get-tuple-element.143), channel_id=1, source_target_pairs={{0,8},{1,9},{2,10},{3,11},{4,12},{5,13},{6,14},{7,15},{8,0},{9,1},... | collective-permute-start | bytes 393224 | tf_op jit(solution)/shard_map/ppermute | solution.py:939
  205.4 9.5 %collective-permute-start.6 = (bf16[1,128,512]{2,1,0:T(8,128)(2,1)S(1)}, bf16[1,128,512]{2,1,0:T(8,128)(2,1)S(1)}, u32[]{:S(2)}, u32[]{:S(2)}) collective-permute-start(bf16[1,128,512]{2,1,0:T(8,128)(2,1)S(1)} %get-tuple-element.144), channel_id=1, source_target_pairs={{0,24},{1,25},{2,26},{3,27},{4,28},{5,29},{6,30},{7,31},{8,16},{9,... | collective-permute-start | bytes 393224 | tf_op jit(solution)/shard_map/ppermute | solution.py:939
  207.8 12.3 %collective-permute-start.5 = (bf16[1,128,512]{2,1,0:T(8,128)(2,1)S(1)}, bf16[1,128,512]{2,1,0:T(8,128)(2,1)S(1)}, u32[]{:S(2)}, u32[]{:S(2)}) collective-permute-start(bf16[1,128,512]{2,1,0:T(8,128)(2,1)S(1)} %get-tuple-element.145), channel_id=1, source_target_pairs={{0,16},{1,17},{2,18},{3,19},{4,20},{5,21},{6,22},{7,23},{8,24},{9,... | collective-permute-start | bytes 393224 | tf_op jit(solution)/shard_map/ppermute | solution.py:939
  222.9 20.6 %collective-permute-start.9 = (bf16[1,128,512]{2,1,0:T(8,128)(2,1)S(1)}, bf16[1,128,512]{2,1,0:T(8,128)(2,1)S(1)}, u32[]{:S(2)}, u32[]{:S(2)}) collective-permute-start(bf16[1,128,512]{2,1,0:T(8,128)(2,1)S(1)} %add_convert_fusion.4), channel_id=1, source_target_pairs={{0,16},{1,17},{2,18},{3,19},{4,20},{5,21},{6,22},{7,23},{8,24},{9,... | collective-permute-start | bytes 393224 | tf_op jit(solution)/shard_map/ppermute | solution.py:939
  222.9 21.3 %collective-permute-start.8 = (bf16[1,128,512]{2,1,0:T(8,128)(2,1)S(1)}, bf16[1,128,512]{2,1,0:T(8,128)(2,1)}, u32[]{:S(2)}, u32[]{:S(2)}) collective-permute-start(bf16[1,128,512]{2,1,0:T(8,128)(2,1)S(1)} %add_convert_fusion.4), channel_id=1, source_target_pairs={{0,8},{1,9},{2,10},{3,11},{4,12},{5,13},{6,14},{7,15},{8,0},{9,1},... | collective-permute-start | bytes 393224 | tf_op jit(solution)/shard_map/ppermute | solution.py:939
  225.0 20.2 %collective-permute-start.11 = (bf16[4,72,512]{2,1,0:T(8,128)(2,1)S(1)}, bf16[4,72,512]{2,1,0:T(8,128)(2,1)S(1)}, u32[]{:S(2)}, u32[]{:S(2)}) collective-permute-start(bf16[4,72,512]{2,1,0:T(8,128)(2,1)S(1)} %get-tuple-element.140), channel_id=1, source_target_pairs={{0,2},{1,3},{2,0},{3,1},{4,6},{5,7},{6,4},{7,5},{8,10},{9,11},{10,... | collective-permute-start | bytes 884744 | tf_op jit(solution)/shard_map/ppermute | solution.py:939
  226.6 18.6 %collective-permute-start.13 = (bf16[4,72,512]{2,1,0:T(8,128)(2,1)S(1)}, bf16[4,72,512]{2,1,0:T(8,128)(2,1)S(1)}, u32[]{:S(2)}, u32[]{:S(2)}) collective-permute-start(bf16[4,72,512]{2,1,0:T(8,128)(2,1)S(1)} %get-tuple-element.141), channel_id=1, source_target_pairs={{0,6},{1,7},{2,4},{3,5},{4,2},{5,3},{6,0},{7,1},{8,14},{9,15},{10,... | collective-permute-start | bytes 884744 | tf_op jit(solution)/shard_map/ppermute | solution.py:939
  228.5 16.7 %collective-permute-start.12 = (bf16[4,72,512]{2,1,0:T(8,128)(2,1)S(1)}, bf16[4,72,512]{2,1,0:T(8,128)(2,1)S(1)}, u32[]{:S(2)}, u32[]{:S(2)}) collective-permute-start(bf16[4,72,512]{2,1,0:T(8,128)(2,1)S(1)} %get-tuple-element.142), channel_id=1, source_target_pairs={{0,4},{1,5},{2,6},{3,7},{4,0},{5,1},{6,2},{7,3},{8,12},{9,13},{10,... | collective-permute-start | bytes 884744 | tf_op jit(solution)/shard_map/ppermute | solution.py:939
  245.4 11.6 %collective-permute-start.18 = (bf16[4,128,512]{2,1,0:T(8,128)(2,1)S(1)}, bf16[4,128,512]{2,1,0:T(8,128)(2,1)S(1)}, u32[]{:S(2)}, u32[]{:S(2)}) collective-permute-start(bf16[4,128,512]{2,1,0:T(8,128)(2,1)S(1)} %pad_maximum_fusion.2), channel_id=1, source_target_pairs={{0,4},{1,5},{2,6},{3,7},{4,0},{5,1},{6,2},{7,3},{8,12},{9,13},{10,... | collective-permute-start | bytes 1572872 | tf_op jit(solution)/shard_map/ppermute | solution.py:939
  246.0 11.1 %collective-permute-start.17 = (bf16[4,128,512]{2,1,0:T(8,128)(2,1)S(1)}, bf16[4,128,512]{2,1,0:T(8,128)(2,1)S(1)}, u32[]{:S(2)}, u32[]{:S(2)}) collective-permute-start(bf16[4,128,512]{2,1,0:T(8,128)(2,1)S(1)} %pad_maximum_fusion.2), channel_id=1, source_target_pairs={{0,2},{1,3},{2,0},{3,1},{4,6},{5,7},{6,4},{7,5},{8,10},{9,11},{10,... | collective-permute-start | bytes 1572872 | tf_op jit(solution)/shard_map/ppermute | solution.py:939
  247.6 9.4 %collective-permute-start.14 = (bf16[1,72,512]{2,1,0:T(8,128)(2,1)S(1)}, bf16[1,72,512]{2,1,0:T(8,128)(2,1)S(1)}, u32[]{:S(2)}, u32[]{:S(2)}) collective-permute-start(bf16[1,72,512]{2,1,0:T(8,128)(2,1)S(1)} %get-tuple-element.146), channel_id=1, source_target_pairs={{0,8},{1,9},{2,10},{3,11},{4,12},{5,13},{6,14},{7,15},{8,0},{9,1},... | collective-permute-start | bytes 221192 | tf_op jit(solution)/shard_map/ppermute | solution.py:939
  257.1 11.2 %collective-permute-start.22 = (bf16[1,72,512]{2,1,0:T(8,128)(2,1)S(1)}, bf16[1,72,512]{2,1,0:T(8,128)(2,1)S(1)}, u32[]{:S(2)}, u32[]{:S(2)}) collective-permute-start(bf16[1,72,512]{2,1,0:T(8,128)(2,1)S(1)} %add_convert_fusion.5), channel_id=1, source_target_pairs={{0,24},{1,25},{2,26},{3,27},{4,28},{5,29},{6,30},{7,31},{8,16},{9,... | collective-permute-start | bytes 221192 | tf_op jit(solution)/shard_map/ppermute | solution.py:939
  261.5 10.3 %collective-permute-start.19 = (bf16[4,128,512]{2,1,0:T(8,128)(2,1)S(1)}, bf16[4,128,512]{2,1,0:T(8,128)(2,1)}, u32[]{:S(2)}, u32[]{:S(2)}) collective-permute-start(bf16[4,128,512]{2,1,0:T(8,128)(2,1)S(1)} %pad_maximum_fusion.2), channel_id=1, source_target_pairs={{0,6},{1,7},{2,4},{3,5},{4,2},{5,3},{6,0},{7,1},{8,14},{9,15},{10,... | collective-permute-start | bytes 1572872 | tf_op jit(solution)/shard_map/ppermute | solution.py:939
  273.2 17.0 %collective-permute-start.23 = (bf16[16,128,512]{2,1,0:T(8,128)(2,1)S(1)}, bf16[16,128,512]{2,1,0:T(8,128)(2,1)}, u32[]{:S(2)}, u32[]{:S(2)}) collective-permute-start(bf16[16,128,512]{2,1,0:T(8,128)(2,1)S(1)} %pad_maximum_fusion.near_ref), channel_id=1, source_target_pairs={{0,1},{1,0},{2,3},{3,2},{4,5},{5,4},{6,7},{7,6},{8,9},{9,8},{10,11... | collective-permute-start | bytes 6291464 | tf_op jit(solution)/shard_map/ppermute | solution.py:939
  273.2 10.8 %collective-permute-start.26 = (bf16[4,72,512]{2,1,0:T(8,128)(2,1)S(1)}, bf16[4,72,512]{2,1,0:T(8,128)(2,1)S(1)}, u32[]{:S(2)}, u32[]{:S(2)}) collective-permute-start(bf16[4,72,512]{2,1,0:T(8,128)(2,1)S(1)} %pad_maximum_fusion.3), channel_id=1, source_target_pairs={{0,6},{1,7},{2,4},{3,5},{4,2},{5,3},{6,0},{7,1},{8,14},{9,15},{10,... | collective-permute-start | bytes 884744 | tf_op jit(solution)/shard_map/ppermute | solution.py:939
  275.3 14.7 %collective-permute-start.25 = (bf16[4,72,512]{2,1,0:T(8,128)(2,1)S(1)}, bf16[4,72,512]{2,1,0:T(8,128)(2,1)S(1)}, u32[]{:S(2)}, u32[]{:S(2)}) collective-permute-start(bf16[4,72,512]{2,1,0:T(8,128)(2,1)S(1)} %pad_maximum_fusion.3), channel_id=1, source_target_pairs={{0,4},{1,5},{2,6},{3,7},{4,0},{5,1},{6,2},{7,3},{8,12},{9,13},{10,... | collective-permute-start | bytes 884744 | tf_op jit(solution)/shard_map/ppermute | solution.py:939
  276.3 13.7 %collective-permute-start.24 = (bf16[4,72,512]{2,1,0:T(8,128)(2,1)S(1)}, bf16[4,72,512]{2,1,0:T(8,128)(2,1)S(1)}, u32[]{:S(2)}, u32[]{:S(2)}) collective-permute-start(bf16[4,72,512]{2,1,0:T(8,128)(2,1)S(1)} %pad_maximum_fusion.3), channel_id=1, source_target_pairs={{0,2},{1,3},{2,0},{3,1},{4,6},{5,7},{6,4},{7,5},{8,10},{9,11},{10,... | collective-permute-start | bytes 884744 | tf_op jit(solution)/shard_map/ppermute | solution.py:939
  (19 other events, 132.6 us)

commit v5 on v4

--- a/solution.py
+++ b/solution.py
@@ -27,6 +27,7 @@
 LANES = 128
 ROWS_FIRST = 2
 FIRST_TILES = 3
+ONES = 16
 CHUNK = 512
 VMEM_LIMIT = 60 * 1024 * 1024
 
@@ -131,7 +132,7 @@
 
 
 def window_items(qkv_of, bias):
-    wide = jnp.concatenate([bias, bias], axis=1)
+    wide = jnp.concatenate([bias, bias], axis=1).astype(f32)
     return [
         (qkv_of(group), qkv_of(GROUPS + group), qkv_of(2 * GROUPS + group), wide) for group in range(GROUPS)
     ]
@@ -155,7 +156,7 @@
 def forward_kernel(
     order_ref, keep_ref,
     tokens_ref, regional_ref, window_bias_ref, region_bias_ref, spread_ref, squeeze_ref,
-    plain_ref, mixed_mask_ref, gain1_ref, bias1_ref, w_qkv_ref, bias_qkv_ref, w_out_ref, bias_out_ref,
+    plain_ref, mixed_mask_ref, gain1_ref, bias1_ref, w_qkv_ref, bias_q_ref, bias_v_ref, w_out_ref, bias_out_ref,
     gain2_ref, bias2_ref, w_fc1_ref, bias_fc1_ref, w_fc2_ref, bias_fc2_ref,
     out_ref, qkv_ref, probs_ref, joined_ref, mixed_ref, after_ref, hidden_ref, slope_ref,
     qkv_r_ref, probs_r_ref, mixed_r_ref,
@@ -175,7 +176,15 @@
         region = regional_ref[...].astype(f32)
         unit, _ = normalize(region)
         region_norm = (unit * gain1_ref[...] + bias1_ref[...]).astype(bf16)
-        region_qkv = (dot(region_norm, w_qkv_ref[...]) + bias_qkv_ref[...]).astype(bf16)
+        region_qkv = dot(region_norm, w_qkv_ref[...])
+        region_qkv = jnp.concatenate(
+            [
+                region_qkv[:, :WIDTH] + bias_q_ref[...],
+                region_qkv[:, WIDTH : 2 * WIDTH],
+                region_qkv[:, 2 * WIDTH :] + bias_v_ref[...],
+            ],
+            axis=1,
+        ).astype(bf16)
         for at in range(3 * GROUPS):
             qkv_r_ref[at] = region_qkv[:, at * LANES : (at + 1) * LANES]
         items = window_items(lambda at: region_qkv[:, at * LANES : (at + 1) * LANES], region_bias_ref[...])
@@ -209,7 +218,9 @@
 
     def project(part):
         cols = slice(part * WIDTH, (part + 1) * WIDTH)
-        qkv = dot(normed[...], w_qkv_ref[:, cols]) + bias_qkv_ref[:, cols]
+        qkv = dot(normed[...], w_qkv_ref[:, cols])
+        if part != 1:
+            qkv = qkv + (bias_q_ref if part == 0 else bias_v_ref)[...]
         qkv = qkv.astype(bf16).reshape(TILE, SLOT, WIDTH)
         for group in range(GROUPS):
             qkv_ref[:, part * GROUPS + group] = qkv[:, :, group * LANES : (group + 1) * LANES]
@@ -334,14 +345,14 @@
 
 
 def run_forward(order, keep, tokens, regional, window_bias, region_bias, spread, squeeze, plain, mixed,
-                gain1, bias1, w_qkv, bias_qkv, w_out, bias_out, gain2, bias2, w_fc1, bias_fc1, w_fc2, bias_fc2):
+                gain1, bias1, w_qkv, bias_q, bias_v, w_out, bias_out, gain2, bias2, w_fc1, bias_fc1, w_fc2, bias_fc2):
     windows = regional.shape[0]
     steps = windows // TILE
     rows = TILE * TALL
     hidden = w_fc1.shape[1]
     compact = squeeze.shape[0]
     args = (tokens, regional, window_bias, region_bias, spread, squeeze, plain, mixed,
-            gain1, bias1, w_qkv, bias_qkv, w_out, bias_out, gain2, bias2, w_fc1, bias_fc1, w_fc2, bias_fc2)
+            gain1, bias1, w_qkv, bias_q, bias_v, w_out, bias_out, gain2, bias2, w_fc1, bias_fc1, w_fc2, bias_fc2)
     def ahead(shape):
         return pl.BlockSpec(
             shape, lambda step, *_: (jnp.minimum(step, steps - 1),) + (0,) * (len(shape) - 1)
@@ -511,26 +522,26 @@
 def back_attention_kernel(
     first, last, order_ref, keep_ref, own_ref,
     qkv_ref, probs_ref, joined_ref, grad_mixed_ref, grad_after_ref,
-    plain_ref, mixed_mask_ref, head_ref, gain1_ref, bias1_ref, *refs,
+    plain_ref, mixed_mask_ref, gain1_ref, bias1_ref, *refs,
 ):
     if first:
         held_in = ()
     else:
-        held_in, refs = refs[:4], refs[5:]
+        held_in, refs = refs[:3], refs[4:]
     if last:
         ending, refs = refs[:10], refs[10:]
         grad_out_ref, order_row_ref, regional_ref, qkv_r_ref, probs_r_ref, mixed_r_ref = ending[:6]
         w_qkv_ref, w_out_ref, sums_mlp_ref, row_fc1_ref = ending[6:]
-        grad_qkv_ref, stay_ref, send_ref, regional_out_ref, sum_qkv, sums, heads, after_heads, late_rows = refs
+        grad_qkv_ref, stay_ref, send_ref, regional_out_ref, sum_qkv, heads, after_heads, late_rows = refs
     else:
-        grad_qkv_ref, sum_qkv, sums, heads, after_heads = refs
+        grad_qkv_ref, sum_qkv, heads, after_heads = refs
     step = pl.program_id(0)
     plain = plain_ref[...]
     mixed = mixed_mask_ref[...]
 
     @pl.when(step == 0)
     def begin():
-        for at, ref in enumerate((sum_qkv, sums, heads, after_heads)):
+        for at, ref in enumerate((sum_qkv, heads, after_heads)):
             ref[...] = jnp.zeros_like(ref) if first else held_in[at][...]
 
     def some(batch, carry):
@@ -551,15 +562,16 @@
         return carry
 
     lax.fori_loop(0, TILE // TOGETHER, some, 0)
-    joined = joined_ref[...].reshape(TILE * SLOT, WIDTH)
-    unit, _ = normalize(joined.astype(f32))
+    joined = joined_ref[...].reshape(TILE * SLOT, WIDTH).astype(f32)
+    unit, _ = normalize(joined)
     normed = (unit * gain1_ref[...] + bias1_ref[...]).astype(bf16)
-    grad_qkv = grad_qkv_ref[...]
-    sum_qkv[...] += dot(normed.T, grad_qkv)
-    sums[0:1] += column_sum(grad_qkv.astype(f32))
+    turned = jnp.concatenate([normed.T, jnp.ones((ONES, TILE * SLOT), bf16)], axis=0)
+    sum_qkv[...] += dot(turned, grad_qkv_ref[...])
     rows = pl.ds(pl.multiple_of((step + (0 if first else FIRST_TILES)) * TILE, TILE), TILE)
-    heads[rows, : 3 * WIDTH] = dot(head_ref[...], grad_qkv)
-    heads[rows, 3 * WIDTH :] = dot(head_ref[...], joined)
+    heads[rows, : 3 * WIDTH] = jnp.concatenate(
+        [grad_qkv_ref[at * SLOT : at * SLOT + 16].astype(f32)[:1] for at in range(TILE)], axis=0
+    )
+    heads[rows, 3 * WIDTH :] = jnp.concatenate([joined_ref[at, :16].astype(f32)[:1] for at in range(TILE)], axis=0)
     after_heads[rows] = jnp.concatenate(
         [grad_after_ref[at * TALL : at * TALL + 1] for at in range(TILE)], axis=0
     )
@@ -594,8 +606,8 @@
         grad_qkv_r = jnp.concatenate([parts[place] for place in range(3 * GROUPS)], axis=1)
         unit_r, scale_r = normalize(regional_ref[...].astype(f32))
         normed_r = (unit_r * gain1 + bias1_ref[...]).astype(bf16)
-        total = sum_qkv[...] + dot(normed_r.T, grad_qkv_r)
-        columns = sums[0:1] + column_sum(grad_qkv_r.astype(f32))
+        total = sum_qkv[:WIDTH] + dot(normed_r.T, grad_qkv_r)
+        columns = sum_qkv[WIDTH : WIDTH + 1] + column_sum(grad_qkv_r.astype(f32))
         for part in range(3):
             cols = slice(part * WIDTH, (part + 1) * WIDTH)
             late_rows[cols, :] = total[:, cols].astype(bf16)
@@ -638,7 +650,7 @@
         ).astype(bf16)
 
 
-def run_back_attention(order, keep, own, qkv, probs, joined, grad_mixed, grad_after, plain, mixed, head, gain1, bias1,
+def run_back_attention(order, keep, own, qkv, probs, joined, grad_mixed, grad_after, plain, mixed, gain1, bias1,
                        held=None, ending=None, parts=1):
     windows = qkv.shape[0]
     steps = windows // TILE
@@ -656,18 +668,18 @@
         (TILE, GROUPS, SLOT, LANES),
         (rows, WIDTH),
     ]
-    fixed = [plain, mixed, head, gain1, bias1]
+    fixed = [plain, mixed, gain1, bias1]
     in_specs = [tile(b) for b in tiled] + [whole(a.shape) for a in fixed]
     args = [qkv, probs, joined, grad_mixed, grad_after] + fixed
     aliases = {}
     if held is not None:
-        in_specs += [whole(a.shape) for a in held[:4]] + [pl.BlockSpec(memory_space=pl.ANY)]
+        in_specs += [whole(a.shape) for a in held[:3]] + [pl.BlockSpec(memory_space=pl.ANY)]
         args += list(held)
         aliases = {3 + len(args) - 1: 0}
     if ending is not None:
         in_specs += [whole(a.shape) for a in ending]
         args += list(ending)
-    held_shapes = [(WIDTH, 3 * WIDTH), (8, 3 * WIDTH), (windows, 4 * WIDTH), (windows, WIDTH)]
+    held_shapes = [(WIDTH + ONES, 3 * WIDTH), (windows, 4 * WIDTH), (windows, WIDTH)]
     outs = [((steps * TILE * SLOT, 3 * WIDTH), bf16, tile((TILE * SLOT, 3 * WIDTH)))]
     scratch = []
     late_shape = (parts // 2, 4 * WIDTH // parts + 8, WIDTH)
@@ -788,109 +800,121 @@
     )(gather, windows)
 
 
-def early_out_kernel(own_ref, near_ref, far_ref, fc1_ref, fc2_ref):
-    block = pl.program_id(0)
-    per, share, _ = near_ref.shape
-    inner = own_ref[0] % per
-    place = block ^ (own_ref[0] // per)
-
-    def fill(rows_ref):
-        @pl.when(block < 2)
-        def first():
-            for at in range(per):
-                start = at * share
-                column = start // WIDTH * WIDTH
-                fc1_ref[start - column : start - column + share, column : column + WIDTH] = rows_ref[
-                    at ^ inner
-                ].astype(f32)
-
-        @pl.when(block >= 2)
-        def second():
-            for at in range(per):
-                fc2_ref[at * share : (at + 1) * share] = rows_ref[at ^ inner].astype(f32)
-
-    @pl.when(place < 2)
-    def near():
-        fill(near_ref)
-
-    @pl.when(place >= 2)
-    def far():
-        fill(far_ref)
-
-
-def run_early_out(own, near, far, units):
-    half, share, _ = near.shape
-    per = half // 2
+def early_out_kernel(own_ref, *refs):
+    pieces, (fc1_ref, fc2_ref, wide, done) = refs[:-4], refs[-4:]
+    per, share, _ = pieces[0].shape
+    own = own_ref[0]
+    half = len(pieces) // 2
+
+    def copy_first(block):
+        columns = pl.ds(pl.multiple_of(block * WIDTH, WIDTH), WIDTH)
+        return pltpu.make_async_copy(wide.at[block], fc1_ref.at[:, columns], done.at[block])
+
+    def copy_second(block):
+        rows = pl.ds(pl.multiple_of((block - half) * WIDTH, WIDTH), WIDTH)
+        return pltpu.make_async_copy(wide.at[block], fc2_ref.at[rows, :], done.at[block])
+
+    for at, piece in enumerate(pieces):
+        block = at ^ (own // per)
+        for chunk in range(per):
+            row = pl.multiple_of((chunk ^ (own % per)) * share, share)
+            wide[block, pl.ds(row, share)] = piece[chunk].astype(f32)
+
+        @pl.when(block < half)
+        def first(block=block):
+            copy_first(block).start()
+
+        @pl.when(block >= half)
+        def second(block=block):
+            copy_second(block).start()
+
+    for block in range(len(pieces)):
+        (copy_first if block < half else copy_second)(block).wait()
+
+
+def run_early_out(own, pieces, units):
+    count = len(pieces)
     return pl.pallas_call(
         early_out_kernel,
-        grid_spec=pltpu.PrefetchScalarGridSpec(
-            num_scalar_prefetch=1,
-            grid=(4,),
-            in_specs=[
-                pl.BlockSpec((per, share, WIDTH), lambda at, own: (jnp.minimum(at ^ (own[0] // per), 1), 0, 0)),
-                pl.BlockSpec(
-                    (per, share, WIDTH), lambda at, own: (jnp.maximum((at ^ (own[0] // per)) - 2, 0), 0, 0)
-                ),
-            ],
-            out_specs=[
-                pl.BlockSpec((WIDTH, units // 2), lambda at, own: (0, jnp.minimum(at, 1))),
-                pl.BlockSpec((units // 2, WIDTH), lambda at, own: (jnp.maximum(at - 2, 0), 0)),
-            ],
-        ),
+        in_specs=[pl.BlockSpec(memory_space=pltpu.SMEM)] + [pl.BlockSpec(memory_space=pltpu.VMEM)] * count,
+        out_specs=[pl.BlockSpec(memory_space=pl.ANY)] * 2,
         out_shape=[
             jax.ShapeDtypeStruct((WIDTH, units), f32),
             jax.ShapeDtypeStruct((units, WIDTH), f32),
         ],
-        compiler_params=pltpu.CompilerParams(
-            dimension_semantics=("arbitrary",), vmem_limit_bytes=VMEM_LIMIT
-        ),
-        cost_estimate=took(7),
+        scratch_shapes=[pltpu.VMEM((count, WIDTH, WIDTH), f32), pltpu.SemaphoreType.DMA((count,))],
+        compiler_params=pltpu.CompilerParams(vmem_limit_bytes=VMEM_LIMIT),
+        cost_estimate=took(5),
         name="early_out",
-    )(own, near, far)
-
-
-def late_out_kernel(own_ref, near_ref, far_ref, qkv_ref, out_ref, small_ref):
-    half, share, _ = near_ref.shape
+    )(own, *pieces)
+
+
+def late_out_kernel(own_ref, *refs):
+    pieces, (qkv_ref, out_ref), small_refs, (wide, done) = refs[:-13], refs[-13:-11], refs[-11:-2], refs[-2:]
+    per, share, _ = pieces[0].shape
     share -= 8
     own = own_ref[0]
-
-    def fill(halves):
-        for at in range(2 * half):
-            rows = halves[at // half][(at % half) ^ (own % half)].astype(f32)
-            row, part = at * share % WIDTH, at * share // WIDTH
-            if part < 3:
-                qkv_ref[row : row + share, part * WIDTH : (part + 1) * WIDTH] = rows[:share]
-            else:
-                out_ref[row : row + share] = rows[:share]
-            if at < 2:
-                small_ref[8 * at : 8 * at + 8] = rows[share:]
-
-    @pl.when(own < half)
-    def low():
-        fill((near_ref, far_ref))
-
-    @pl.when(own >= half)
-    def high():
-        fill((far_ref, near_ref))
-
-
-def run_late_out(own, near, far):
+    count = len(pieces)
+    height = per * share
+    split = WIDTH // height
+
+    def copy_first(block):
+        rows = pl.ds(pl.multiple_of(block % split * height, height), height)
+        columns = pl.ds(pl.multiple_of(block // split * WIDTH, WIDTH), WIDTH)
+        return pltpu.make_async_copy(wide.at[block], qkv_ref.at[rows, columns], done.at[block])
+
+    def copy_second(block):
+        rows = pl.ds(pl.multiple_of((block - 3 * split) * height, height), height)
+        return pltpu.make_async_copy(wide.at[block], out_ref.at[rows, :], done.at[block])
+
+    for at, piece in enumerate(pieces):
+        block = at ^ (own // per)
+        for chunk in range(per):
+            row = pl.multiple_of((chunk ^ (own % per)) * share, share)
+            wide[block, pl.ds(row, share)] = piece[chunk][:share].astype(f32)
+
+        @pl.when(block < 3 * split)
+        def first(block=block):
+            copy_first(block).start()
+
+        @pl.when(block >= 3 * split)
+        def second(block=block):
+            copy_second(block).start()
+
+        @pl.when(block == 0)
+        def vectors(piece=piece):
+            lines = piece[own % per][share:].astype(f32)
+            for line in range(8):
+                small_refs[line][...] = lines[line : line + 1]
+            lines = piece[1 ^ (own % per)][share:].astype(f32)
+            for line in range(small_refs[8].shape[1] // WIDTH):
+                small_refs[8][:, line * WIDTH : (line + 1) * WIDTH] = lines[line : line + 1]
+
+    for block in range(count):
+        (copy_first if block < 3 * split else copy_second)(block).wait()
+
+
+def run_late_out(own, pieces, units):
+    count = len(pieces)
+    per, share, _ = pieces[0].shape
     return pl.pallas_call(
         late_out_kernel,
-        in_specs=[
-            pl.BlockSpec(memory_space=pltpu.SMEM),
-            pl.BlockSpec(memory_space=pltpu.VMEM),
-            pl.BlockSpec(memory_space=pltpu.VMEM),
-        ],
+        in_specs=[pl.BlockSpec(memory_space=pltpu.SMEM)] + [pl.BlockSpec(memory_space=pltpu.VMEM)] * count,
+        out_specs=[pl.BlockSpec(memory_space=pl.ANY)] * 2 + [pl.BlockSpec(memory_space=pltpu.VMEM)] * 9,
         out_shape=[
             jax.ShapeDtypeStruct((WIDTH, 3 * WIDTH), f32),
             jax.ShapeDtypeStruct((WIDTH, WIDTH), f32),
-            jax.ShapeDtypeStruct((16, WIDTH), f32),
+            *[jax.ShapeDtypeStruct((1, WIDTH), f32)] * 8,
+            jax.ShapeDtypeStruct((1, units), f32),
+        ],
+        scratch_shapes=[
+            pltpu.VMEM((count, per * (share - 8), WIDTH), f32),
+            pltpu.SemaphoreType.DMA((count,)),
         ],
         compiler_params=pltpu.CompilerParams(vmem_limit_bytes=VMEM_LIMIT),
-        cost_estimate=took(4),
+        cost_estimate=took(3),
         name="late_out",
-    )(own, near, far)
+    )(own, *pieces)
 
 
 def band_to_windows(band_values, win_count):
@@ -943,9 +967,17 @@
     return sum(piece.astype(f32) for piece in pieces).astype(bf16)
 
 
+def split_sum(pieces, stage):
+    parts = [piece.reshape((1 << len(stage), -1) + piece.shape[1:]) for piece in pieces]
+    return [add_up([part[place] for part in parts]) for place in range(1 << len(stage))]
+
+
+def sum_parts(parts, stage):
+    return [parts[0]] + [swap(parts[offset], pairs) for offset, pairs in stage_moves(stage)]
+
+
 def sum_stage(rows, stage):
-    parts = rows.reshape((1 << len(stage), -1) + rows.shape[1:])
-    return add_up([parts[0]] + [swap(parts[offset], pairs) for offset, pairs in stage_moves(stage)])
+    return add_up(sum_parts(rows.reshape((1 << len(stage), -1) + rows.shape[1:]), stage))
 
 
 def gather_stage(rows, stage):
@@ -1027,12 +1059,10 @@
     spread[window * SLOT + 1 + place, raster] = 1
     gather = np.zeros((band, TILE * SLOT), np.float32)
     gather[raster, window * SLOT + 1 + place] = 1
-    head = np.zeros((TILE, TILE * SLOT), np.float32)
-    head[np.arange(TILE), np.arange(TILE) * SLOT] = 1
     place = np.arange(WIN_SIDE * WIN_SIDE + 1)[None, :]
     squeeze = np.zeros(((WIN_SIDE * WIN_SIDE + 1) * TILE, TILE * TALL), np.float32)
     squeeze[place * TILE + window, window * TALL + place] = 1
-    return [jnp.asarray(table, bf16) for table in (spread, gather, head, squeeze, squeeze.T)]
+    return [jnp.asarray(table, bf16) for table in (spread, gather, squeeze, squeeze.T)]
 
 
 def shards(
@@ -1088,18 +1118,17 @@
         axis=1,
     )
     window_bias = jnp.broadcast_to(
-        jnp.where(allowed, 0.0, -1e30).astype(f32)[:, :, None], (win_count, SLOT, LANES)
+        jnp.where(allowed, 0.0, -1e30).astype(bf16)[:, :, None], (win_count, SLOT, LANES)
     )
     region_bias = jnp.broadcast_to(
-        jnp.where(live[:, 0], 0.0, -1e30).astype(f32)[:, None], (win_count, LANES)
-    )
-    spread, gather, head, squeeze, stretch = row_maps()
+        jnp.where(live[:, 0], 0.0, -1e30).astype(bf16)[:, None], (win_count, LANES)
+    )
+    spread, gather, squeeze, stretch = row_maps()
     plain, mixed_mask = head_masks()
-    bias_qkv = jnp.concatenate([bias_q, jnp.zeros_like(bias_q), bias_v])[None]
     gain1, bias1, gain2, bias2 = ln1_gain[None], ln1_bias[None], ln2_gain[None], ln2_bias[None]
     out, qkv, probs, joined, mixed, after, hidden, slope, qkv_r, probs_r, mixed_r = run_forward(
         order, keep, tokens.reshape(REG_SIDE, -1, WIDTH), regional[0], window_bias, region_bias,
-        spread, squeeze, plain, mixed_mask, gain1, bias1, w_qkv, bias_qkv, w_out, bias_out[None],
+        spread, squeeze, plain, mixed_mask, gain1, bias1, w_qkv, bias_q[None], bias_v[None], w_out, bias_out[None],
         gain2, bias2, w_fc1, bias_fc1[None], w_fc2, bias_fc2[None],
     )
     came = swap_tiles(out, devices)
@@ -1110,12 +1139,12 @@
     (_, pairs), = stage_moves(stages[0])
     early_came = swap(early_sent, pairs)
     attention = (
-        order, keep, own, qkv, probs, joined, grad_mixed, grad_after, plain, mixed_mask, head, gain1, bias1
+        order, keep, own, qkv, probs, joined, grad_mixed, grad_after, plain, mixed_mask, gain1, bias1
     )
     grad_qkv, *held = run_back_attention(*attention)
-    early = add_up([early, early_came])
+    early = split_sum([early, early_came], stages[1])
     held, early, came = lax.optimization_barrier((held, early, came))
-    early = sum_stage(early, stages[1])
+    early = add_up(sum_parts(early, stages[1]))
     grad_qkv, late, late_sent, regional_out = run_back_attention(
         *attention,
         held=(*held, grad_qkv),
@@ -1127,28 +1156,37 @@
     early = sum_stages(early, stages[2:])
     rows = (order, grad_qkv, joined, grad_after, gain1, w_qkv)
     windows = run_back_rows(*rows, 0, ROWS_FIRST)
-    windows, early, late_came = lax.optimization_barrier((windows, early, late_came))
-    late = sum_stage(add_up([late, late_came]), stages[1])
+    windows, late_came = lax.optimization_barrier((windows, late_came))
+    late = add_up(sum_parts(split_sum([late, late_came], stages[1]), stages[1]))
+    windows, early = lax.optimization_barrier((windows, early))
     for stage in reversed(stages[2:]):
         early = gather_stage(early, stage)
     windows = run_back_rows(*rows, ROWS_FIRST, win_count // TILE - ROWS_FIRST, held=windows)
     windows, early, late = lax.optimization_barrier((windows, early, late))
     late = sum_stages(late, stages[2:])
     moves = stage_moves(stages[1])
-    direct = [swap(early, moves[at][1]) for at in (0, 1)]
+    early = [early] + [swap(early, moves[at][1]) for at in range(2)]
+    early_far = [swap(early[0], pairs)]
     tokens_out = run_relay(gather, windows)
-    tokens_out, came, late, early, direct = lax.optimization_barrier((tokens_out, came, late, early, direct))
+    tokens_out, came, early, early_far, late = lax.optimization_barrier(
+        (tokens_out, came, early, early_far, late)
+    )
+    early += [swap(early[0], pairs) for _, pairs in moves[2:]]
+    early_far += [swap(piece, pairs) for piece in early[1:3]]
     for stage in reversed(stages[2:]):
         late = gather_stage(late, stage)
+    came, late = lax.optimization_barrier((came, late))
+    late = [late] + [swap(late, pairs) for _, pairs in moves]
+    early_far += [swap(piece, pairs) for piece in early[3:]]
+    late_far = [swap(late[0], pairs)]
+    grad_w_fc1, grad_w_fc2 = run_early_out(own, early + early_far, w_fc1.shape[1])
     out_regional, out_local = run_collect(pick_back, came)
-    early = jnp.concatenate([early] + direct + [swap(early, pairs) for _, pairs in moves[2:]], axis=0)
-    out_local, early, late = lax.optimization_barrier((out_local, early, late))
-    late = gather_stage(late, stages[1])
-    early_far = swap(early, pairs)
-    grad_w_fc1, grad_w_fc2 = run_early_out(own, early, early_far, w_fc1.shape[1])
-    grad_w_fc1, grad_w_fc2, late = lax.optimization_barrier((grad_w_fc1, grad_w_fc2, late))
-    late_far = swap(late, pairs)
-    grad_w_qkv, grad_w_out, vectors = run_late_out(own, late, late_far)
+    grad_w_fc1, grad_w_fc2, out_local, late, late_far = lax.optimization_barrier(
+        (grad_w_fc1, grad_w_fc2, out_local, late, late_far)
+    )
+    late_far += [swap(piece, pairs) for piece in late[1:]]
+    grad_w_qkv, grad_w_out, *vectors = run_late_out(own, late + late_far, w_fc1.shape[1])
+    vectors = [vector[0] for vector in vectors]
     return (
         jnp.swapaxes(out_local, 0, 1)[None],
         out_regional[None],
@@ -1164,7 +1202,7 @@
         vectors[5],
         vectors[6],
         grad_w_fc1,
-        vectors[8:12].reshape(-1),
+        vectors[8],
         grad_w_fc2,
         vectors[7],
     )

time: 312 us -> 296 us (0.949)
  local copies, waits for them, and re-layouts: 13.9 us -> 7.41 us
  waiting for transfers between devices: 30.6 us -> 25.9 us
  Pallas kernels: 206 us -> 202 us
    ppermute x28 -> x34, waiting for transfers between devices: 25.7 us -> 18.8 us  [swap(): return lax.ppermute(rows, ('dp', 'img'), pairs)]
    unnamed x28 -> x44, local copies, waits for them, and re-layouts: 6.82 us -> 4.18 us
    ppermute x28 -> x34, starting transfers between devices: 32.8 us -> 33.3 us  [swap(): return lax.ppermute(rows, ('dp', 'img'), pairs)]
  transfers between devices with their start and end apart: 30 -> 36, of which waited for: 9 -> 14; matrix products, arithmetic and copies ran while one was open for 4% -> 4% of each run, Pallas kernels for 62% -> 66%
where the time goes in v5:
time: 296 us; the launch traced here: 292 us
  Pallas kernels  202 us (68%)
  starting transfers between devices  45.3 us (15%)
  waiting for transfers between devices  25.9 us (9%)
  other arithmetic  9.38 us (3%)
  local copies, waits for them, and re-layouts  7.41 us (3%)
    pallas_call x1, Pallas kernels, run_forward(): pl.pallas_call(forward_kernel, grid_spec=pltpu.PrefetchScalarGridSpec(num...  61.4 us
    pallas_call x1, Pallas kernels, run_back_mlp(): pl.pallas_call(back_mlp_kernel, grid_spec=pltpu.PrefetchScalarGridSpec(nu...  54.9 us
    pallas_call x2, Pallas kernels, run_back_attention(): pl.pallas_call(functools.partial(back_attention_kernel, held is None, end...  40.5 us
    ppermute x34, starting transfers between devices, swap(): return lax.ppermute(rows, ('dp', 'img'), pairs)  33.3 us
    pallas_call x2, Pallas kernels, run_back_rows(): pl.pallas_call(functools.partial(back_rows_kernel, begin), grid_spec=pltp...  20.3 us
    ppermute x34, waiting for transfers between devices, swap(): return lax.ppermute(rows, ('dp', 'img'), pairs)  18.8 us
    all_to_all x2, starting transfers between devices, swap_tiles(): lax.all_to_all(tiles_sent, 'dp', split_axis=0, concat_axis=0, tiled=True)  12 us
    all_to_all x2, waiting for transfers between devices, swap_tiles(): lax.all_to_all(tiles_sent, 'dp', split_axis=0, concat_axis=0, tiled=True)  7.04 us
  transfers between devices with their start and end apart: 36, of which 14 were waited for; matrix products, arithmetic and copies ran while one was open for 4% of the time, Pallas kernels for 66%

profile of v5, /device:TPU:0, one launch (start us, length us, event | category | flops | bytes accessed | tf_op | source)
XLA Modules:
  0.0 292.3 jit_solution(6421889457008787085)
XLA Ops:
  2.6 4.7 %deal.1 = bf16[8,400,512]{2,1,0:T(8,128)(2,1)} custom-call(bf16[128,128]{1,0:T(8,128)(2,1)} %get-tuple-element.181.pick_ref, bf16[64,512]{1,0:T(8,128)(2,1)} %bitcast.64, bf16[49,64,512]{2,1,0:T(8,128)(2,1)} %bitcast.62), custom_call_target="tpu_custom_call" | custom-call | flops 5750000128 | bytes 1000000 | tf_op jit(solution)/shard_map/deal/pallas_call | solution.py:1017
  7.3 7.4 %all-to-all-start = ((bf16[8,400,512]{2,1,0:T(8,128)(2,1)}), bf16[8,400,512]{2,1,0:T(8,128)(2,1)S(1)}, u32[]{:S(2)}, u32[]{:S(2)}) async-start(bf16[8,400,512]{2,1,0:T(8,128)(2,1)} %deal.1), calls=%async_computation | async-start | bytes 6553600 | tf_op jit(solution)/shard_map/all_to_all | solution.py:1044
  20.2 61.4 %forward.1 = (bf16[8,400,512]{2,1,0:T(8,128)(2,1)}, bf16[64,12,64,128]{3,2,1,0:T(8,128)(2,1)}, bf16[64,8,64,128]{3,2,1,0:T(8,128)(2,1)}, bf16[64,64,512]{2,1,0:T...) custom-call(s32[64]{0:T(128)} %select_reduce_fusion.1.order_ref, ...), custom_call_target="tpu_custom_call" | custom-call | flops 70149996544 | bytes 1000000 | tf_op jit(solution)/shard_map/forward/pallas_call | solution.py:379
  81.7 6.5 %all-to-all-done.cot_ref = bf16[8,400,512]{2,1,0:T(8,128)(2,1)S(1)} async-done(((bf16[8,400,512]{2,1,0:T(8,128)(2,1)}), bf16[8,400,512]{2,1,0:T(8,128)(2,1)S(1)}, u32[]{:S(2)}, u32[]{:S(2)}) %all-to-all-start) | async-done | bytes 3276832 | tf_op jit(solution)/shard_map/all_to_all | solution.py:1044
  89.8 4.6 %all-to-all-start.1 = ((bf16[8,400,512]{2,1,0:T(8,128)(2,1)}), bf16[8,400,512]{2,1,0:T(8,128)(2,1)}, u32[]{:S(2)}, u32[]{:S(2)}) async-start(bf16[8,400,512]{2,1,0:T(8,128)(2,1)} %get-tuple-element.106), calls=%async_computation.1 | async-start | bytes 6553600 | tf_op jit(solution)/shard_map/all_to_all | solution.py:1044
  94.5 54.9 %back_mlp.1 = (f32[3584,512]{1,0:T(8,128)}, bf16[64,4,64,128]{3,2,1,0:T(8,128)(2,1)}, bf16[16,128,512]{2,1,0:T(8,128)(2,1)}, bf16[16,128,512]{2,1,0:T(8,128)(2,1...) custom-call(f32[1]{0:T(128)} %bitcast.3.keep_ref, s32[1]{0:T(128)} %bitcast.own_ref, ...), custom_call_target="tpu_custom_call" | custom-call | flops 63250001920 | bytes 1000000 | tf_op jit(solution)/shard_map/back_mlp/pallas_call | solution.py:496
  149.5 14.3 %back_attention.2 = (bf16[4096,1536]{1,0:T(8,128)(2,1)}, f32[528,1536]{1,0:T(8,128)}, f32[64,2048]{1,0:T(8,128)}, f32[64,512]{1,0:T(8,128)}) custom-call(s32[64]{0:T(128)} %select_reduce_fusion.1.order_ref, f32[1]{0:T(128)} %bitcast.3.keep_ref, s32[1]{0:T(128)} %bitcast.own_ref, bf16[64,12,64,128]{3,2,1,0:T(8,128)(2,1)} %get-tuple-element.92.qkv_ref, ...), custom_call_target="tpu_custom_call" | custom-call | flops 17250000896 | bytes 1000000 | tf_op jit(solution)/shard_map/back_attention/pallas_call | solution.py:695
  163.8 3.1 %add_convert_fusion.1 = (bf16[4,128,512]{2,1,0:T(8,128)(2,1)}, bf16[4,128,512]{2,1,0:T(8,128)(2,1)}, bf16[4,128,512]{2,1,0:T(8,128)(2,1)}, bf16[4,128,512]{2,1,0:T(8,128)(2,1)S(1)}) fusion(bf16[16,128,512]{2,1,0:T(8,128)(2,1)} %collective-permute-done, bf16[16,128,512]{2,1,0:T(8,128)(2,1)S(1)} %copy-done.1), kind=kLoop, calls=%fused_computation.1 | loop fusion | flops 4194304 | bytes 6291456 | tf_op jit(solution)/shard_map/convert_element_type | solution.py:967
  171.0 26.1 %back_attention.3 = (bf16[4096,1536]{1,0:T(8,128)(2,1)}, bf16[16,72,512]{2,1,0:T(8,128)(2,1)}, bf16[16,72,512]{2,1,0:T(8,128)(2,1)}, bf16[64,512]{1,0:T(8,128)(2,1)}) custom-call(s32[64]{0:T(128)} %select_reduce_fusion.1.order_ref, f32[1]{0:T(128)} %bitcast.3.keep_ref, s32[1]{0:T(128)} %bitcast.own_ref, ...), custom_call_target="tpu_custom_call", output_to_operand_aliasing={{0}: (15, {})} | custom-call | flops 28750000128 | bytes 1000000 | tf_op jit(solution)/shard_map/back_attention/pallas_call | solution.py:695
  199.0 2.4 collective-permute-start.7
  201.4 6.8 %back_rows.2.refs_0_ = bf16[64,64,512]{2,1,0:T(8,128)(2,1)} custom-call(s32[64]{0:T(128)} %select_reduce_fusion.1.order_ref, bf16[4096,1536]{1,0:T(8,128)(2,1)} %get-tuple-element.122.grad_qkv_ref, bf16[64,64,512]{2,1,0:T(8,128)(2,1)} %get-tuple-element.94.joined_ref, f32[3584,512]{1,0:T(8,128)} %get-tuple-element.100.grad_after_ref, f32[1,512]{1,0:T(1,128)} %bitcast.58, ...), custom_call_target="tpu_custom_call" | custom-call | flops 5750000128 | bytes 1000000 | tf_op jit(solution)/shard_map/back_rows/pallas_call | solution.py:762
  208.5 5.1 %collective-permute-done.6 = bf16[1,128,512]{2,1,0:T(8,128)(2,1)S(1)} collective-permute-done((bf16[1,128,512]{2,1,0:T(8,128)(2,1)S(1)}, bf16[1,128,512]{2,1,0:T(8,128)(2,1)S(1)}, u32[]{:S(2)}, u32[]{:S(2)}) %collective-permute-start.6) | collective-permute-done | bytes 131104 | tf_op jit(solution)/shard_map/ppermute | solution.py:963
  213.7 2.7 collective-permute-start.10
  223.6 13.5 %back_rows.3.windows_ref = bf16[64,64,512]{2,1,0:T(8,128)(2,1)} custom-call(s32[64]{0:T(128)} %select_reduce_fusion.1.order_ref, bf16[4096,1536]{1,0:T(8,128)(2,1)} %get-tuple-element.122.grad_qkv_ref, bf16[64,64,512]{2,1,0:T(8,128)(2,1)} %get-tuple-element.94.joined_ref, ...), custom_call_target="tpu_custom_call", output_to_operand_aliasing={{}: (6, {})} | custom-call | flops 17250000896 | bytes 1000000 | tf_op jit(solution)/shard_map/back_rows/pallas_call | solution.py:762
  242.2 1.9 collective-permute-start.19
  244.8 5.8 %relay.1 = bf16[8,392,512]{2,1,0:T(8,128)(2,1)} custom-call(bf16[392,512]{1,0:T(8,128)(2,1)} %constant.192.clone.gather_ref, bf16[64,64,512]{2,1,0:T(8,128)(2,1)} %back_rows.3.windows_ref), custom_call_target="tpu_custom_call" | custom-call | flops 5750000128 | bytes 1000000 | tf_op jit(solution)/shard_map/relay/pallas_call | solution.py:789
  251.9 2.5 collective-permute-done.15.refs_2_
  254.7 2.4 collective-permute-start.20
  261.6 2.5 collective-permute-done.26
  264.1 2.1 collective-permute-done.25
  267.0 2.0 collective-permute-done.20.refs_3_
  269.0 4.8 %collect.1 = (bf16[64,512]{1,0:T(8,128)(2,1)}, bf16[49,64,512]{2,1,0:T(8,128)(2,1)}) custom-call(bf16[128,128]{1,0:T(8,128)(2,1)} %get-tuple-element.180.pick_ref, bf16[8,400,512]{2,1,0:T(8,128)(2,1)} %all-to-all-done.1.came_ref), custom_call_target="tpu_custom_call" | custom-call | flops 5750000128 | bytes 1000000 | tf_op jit(solution)/shard_map/collect/pallas_call | solution.py:1028
  277.9 5.6 %early_out.1 = (f32[512,2048]{1,0:T(8,128)}, f32[2048,512]{1,0:T(8,128)}) custom-call(s32[1]{0:T(128)} %bitcast.own_ref, bf16[4,128,512]{2,1,0:T(8,128)(2,1)} %copy-done.3, bf16[4,128,512]{2,1,0:T(8,128)(2,1)} %copy-done.10, bf16[4,128,512]{2,1,0:T(8,128)(2,1)} %copy-done.9, bf16[4,128,512]{2,1,0:T(8,128)(2,1)} %copy-done.11, ...), custom_call_target="tpu_custom_call" | custom-call | flops 5750000128 | bytes 1000000 | tf_op jit(solution)/shard_map/early_out/pallas_call | solution.py:837
  287.7 4.3 %late_out.1 = (f32[512,1536]{1,0:T(8,128)}, f32[512,512]{1,0:T(8,128)}, f32[1,512]{1,0:T(1,128)}, f32[1,512]{1,0:T(1,128)}, f32[1,512]{1,0:T(1,128)}, /*index=5*...) custom-call(s32[1]{0:T(128)} %bitcast.own_ref, ...), custom_call_target="tpu_custom_call" | custom-call | flops 3449999872 | bytes 1000000 | tf_op jit(solution)/shard_map/late_out/pallas_call | solution.py:900
  (136 shorter events, 42.6 us)
Async XLA Ops:
  7.3 80.9 %all-to-all-start = ((bf16[8,400,512]{2,1,0:T(8,128)(2,1)}), bf16[8,400,512]{2,1,0:T(8,128)(2,1)S(1)}, u32[]{:S(2)}, u32[]{:S(2)}) async-start(bf16[8,400,512]{2,1,0:T(8,128)(2,1)} %deal.1), calls=%async_computation | async-start | bytes 6553600 | tf_op jit(solution)/shard_map/all_to_all | solution.py:1044
  89.8 77.6 %all-to-all-start.1 = ((bf16[8,400,512]{2,1,0:T(8,128)(2,1)}), bf16[8,400,512]{2,1,0:T(8,128)(2,1)}, u32[]{:S(2)}, u32[]{:S(2)}) async-start(bf16[8,400,512]{2,1,0:T(8,128)(2,1)} %get-tuple-element.106), calls=%async_computation.1 | async-start | bytes 6553600 | tf_op jit(solution)/shard_map/all_to_all | solution.py:1044
  149.4 14.4 %collective-permute-start = (bf16[16,128,512]{2,1,0:T(8,128)(2,1)}, bf16[16,128,512]{2,1,0:T(8,128)(2,1)}, u32[]{:S(2)}, u32[]{:S(2)}) collective-permute-start(bf16[16,128,512]{2,1,0:T(8,128)(2,1)} %get-tuple-element.105), channel_id=1, source_target_pairs={{0,1},{1,0},{2,3},{3,2},{4,5},{5,4},{6,7},{7,6},{8,9},{9,8},{10,11... | collective-permute-start | bytes 6291464 | tf_op jit(solution)/shard_map/ppermute | solution.py:963
  167.5 29.7 %collective-permute-start.1 = (bf16[4,128,512]{2,1,0:T(8,128)(2,1)}, bf16[4,128,512]{2,1,0:T(8,128)(2,1)S(1)}, u32[]{:S(2)}, u32[]{:S(2)}) collective-permute-start(bf16[4,128,512]{2,1,0:T(8,128)(2,1)} %get-tuple-element.119), channel_id=1, source_target_pairs={{0,2},{1,3},{2,0},{3,1},{4,6},{5,7},{6,4},{7,5},{8,10},{9,11},{10,... | collective-permute-start | bytes 1572872 | tf_op jit(solution)/shard_map/ppermute | solution.py:963
  169.0 28.2 %collective-permute-start.2 = (bf16[4,128,512]{2,1,0:T(8,128)(2,1)}, bf16[4,128,512]{2,1,0:T(8,128)(2,1)S(1)}, u32[]{:S(2)}, u32[]{:S(2)}) collective-permute-start(bf16[4,128,512]{2,1,0:T(8,128)(2,1)} %get-tuple-element.120), channel_id=1, source_target_pairs={{0,4},{1,5},{2,6},{3,7},{4,0},{5,1},{6,2},{7,3},{8,12},{9,13},{10,... | collective-permute-start | bytes 1572872 | tf_op jit(solution)/shard_map/ppermute | solution.py:963
  170.4 26.8 %collective-permute-start.3 = (bf16[4,128,512]{2,1,0:T(8,128)(2,1)}, bf16[4,128,512]{2,1,0:T(8,128)(2,1)S(1)}, u32[]{:S(2)}, u32[]{:S(2)}) collective-permute-start(bf16[4,128,512]{2,1,0:T(8,128)(2,1)} %get-tuple-element.121), channel_id=1, source_target_pairs={{0,6},{1,7},{2,4},{3,5},{4,2},{5,3},{6,0},{7,1},{8,14},{9,15},{10,... | collective-permute-start | bytes 1572872 | tf_op jit(solution)/shard_map/ppermute | solution.py:963
  197.1 16.6 %collective-permute-start.4 = (bf16[16,72,512]{2,1,0:T(8,128)(2,1)}, bf16[16,72,512]{2,1,0:T(8,128)(2,1)S(1)}, u32[]{:S(2)}, u32[]{:S(2)}) collective-permute-start(bf16[16,72,512]{2,1,0:T(8,128)(2,1)} %get-tuple-element.123), channel_id=1, source_target_pairs={{0,1},{1,0},{2,3},{3,2},{4,5},{5,4},{6,7},{7,6},{8,9},{9,8},{10,11... | collective-permute-start | bytes 3538952 | tf_op jit(solution)/shard_map/ppermute | solution.py:963
  197.5 10.6 %collective-permute-start.5 = (bf16[1,128,512]{2,1,0:T(8,128)(2,1)S(1)}, bf16[1,128,512]{2,1,0:T(8,128)(2,1)S(1)}, u32[]{:S(2)}, u32[]{:S(2)}) collective-permute-start(bf16[1,128,512]{2,1,0:T(8,128)(2,1)S(1)} %get-tuple-element.174), channel_id=1, source_target_pairs={{0,8},{1,9},{2,10},{3,11},{4,12},{5,13},{6,14},{7,15},{8,0},{9,1},... | collective-permute-start | bytes 393224 | tf_op jit(solution)/shard_map/ppermute | solution.py:963
  199.0 9.6 %collective-permute-start.7 = (bf16[1,128,512]{2,1,0:T(8,128)(2,1)S(1)}, bf16[1,128,512]{2,1,0:T(8,128)(2,1)S(1)}, u32[]{:S(2)}, u32[]{:S(2)}) collective-permute-start(bf16[1,128,512]{2,1,0:T(8,128)(2,1)S(1)} %get-tuple-element.175), channel_id=1, source_target_pairs={{0,24},{1,25},{2,26},{3,27},{4,28},{5,29},{6,30},{7,31},{8,16},{9,... | collective-permute-start | bytes 393224 | tf_op jit(solution)/shard_map/ppermute | solution.py:963
  201.4 12.3 %collective-permute-start.6 = (bf16[1,128,512]{2,1,0:T(8,128)(2,1)S(1)}, bf16[1,128,512]{2,1,0:T(8,128)(2,1)S(1)}, u32[]{:S(2)}, u32[]{:S(2)}) collective-permute-start(bf16[1,128,512]{2,1,0:T(8,128)(2,1)S(1)} %get-tuple-element.176), channel_id=1, source_target_pairs={{0,16},{1,17},{2,18},{3,19},{4,20},{5,21},{6,22},{7,23},{8,24},{9,... | collective-permute-start | bytes 393224 | tf_op jit(solution)/shard_map/ppermute | solution.py:963
  216.5 20.6 %collective-permute-start.9 = (bf16[1,128,512]{2,1,0:T(8,128)(2,1)S(1)}, bf16[1,128,512]{2,1,0:T(8,128)(2,1)S(1)}, u32[]{:S(2)}, u32[]{:S(2)}) collective-permute-start(bf16[1,128,512]{2,1,0:T(8,128)(2,1)S(1)} %add_convert_fusion.10), channel_id=1, source_target_pairs={{0,16},{1,17},{2,18},{3,19},{4,20},{5,21},{6,22},{7,23},{8,24},{9,... | collective-permute-start | bytes 393224 | tf_op jit(solution)/shard_map/ppermute | solution.py:963
  216.5 21.3 %collective-permute-start.8 = (bf16[1,128,512]{2,1,0:T(8,128)(2,1)S(1)}, bf16[1,128,512]{2,1,0:T(8,128)(2,1)}, u32[]{:S(2)}, u32[]{:S(2)}) collective-permute-start(bf16[1,128,512]{2,1,0:T(8,128)(2,1)S(1)} %add_convert_fusion.10), channel_id=1, source_target_pairs={{0,8},{1,9},{2,10},{3,11},{4,12},{5,13},{6,14},{7,15},{8,0},{9,1},... | collective-permute-start | bytes 393224 | tf_op jit(solution)/shard_map/ppermute | solution.py:963
  219.2 19.6 %collective-permute-start.11 = (bf16[4,72,512]{2,1,0:T(8,128)(2,1)}, bf16[4,72,512]{2,1,0:T(8,128)(2,1)S(1)}, u32[]{:S(2)}, u32[]{:S(2)}) collective-permute-start(bf16[4,72,512]{2,1,0:T(8,128)(2,1)} %get-tuple-element.171), channel_id=1, source_target_pairs={{0,2},{1,3},{2,0},{3,1},{4,6},{5,7},{6,4},{7,5},{8,10},{9,11},{10,... | collective-permute-start | bytes 884744 | tf_op jit(solution)/shard_map/ppermute | solution.py:963
  220.8 18.1 %collective-permute-start.13 = (bf16[4,72,512]{2,1,0:T(8,128)(2,1)}, bf16[4,72,512]{2,1,0:T(8,128)(2,1)S(1)}, u32[]{:S(2)}, u32[]{:S(2)}) collective-permute-start(bf16[4,72,512]{2,1,0:T(8,128)(2,1)} %get-tuple-element.172), channel_id=1, source_target_pairs={{0,6},{1,7},{2,4},{3,5},{4,2},{5,3},{6,0},{7,1},{8,14},{9,15},{10,... | collective-permute-start | bytes 884744 | tf_op jit(solution)/shard_map/ppermute | solution.py:963
  222.2 16.7 %collective-permute-start.12 = (bf16[4,72,512]{2,1,0:T(8,128)(2,1)}, bf16[4,72,512]{2,1,0:T(8,128)(2,1)S(1)}, u32[]{:S(2)}, u32[]{:S(2)}) collective-permute-start(bf16[4,72,512]{2,1,0:T(8,128)(2,1)} %get-tuple-element.173), channel_id=1, source_target_pairs={{0,4},{1,5},{2,6},{3,7},{4,0},{5,1},{6,2},{7,3},{8,12},{9,13},{10,... | collective-permute-start | bytes 884744 | tf_op jit(solution)/shard_map/ppermute | solution.py:963
  240.1 11.8 %collective-permute-start.16 = (bf16[4,128,512]{2,1,0:T(8,128)(2,1)S(1)}, bf16[4,128,512]{2,1,0:T(8,128)(2,1)S(1)}, u32[]{:S(2)}, u32[]{:S(2)}) collective-permute-start(bf16[4,128,512]{2,1,0:T(8,128)(2,1)S(1)} %pad_maximum_fusion.refs_0_), channel_id=1, source_target_pairs={{0,1},{1,0},{2,3},{3,2},{4,5},{5,4},{6,7},{7,6},{8,9},{9,8},{10,11... | collective-permute-start | bytes 1572872 | tf_op jit(solution)/shard_map/ppermute | solution.py:963
  240.1 14.3 %collective-permute-start.15 = (bf16[4,128,512]{2,1,0:T(8,128)(2,1)S(1)}, bf16[4,128,512]{2,1,0:T(8,128)(2,1)S(1)}, u32[]{:S(2)}, u32[]{:S(2)}) collective-permute-start(bf16[4,128,512]{2,1,0:T(8,128)(2,1)S(1)} %pad_maximum_fusion.refs_0_), channel_id=1, source_target_pairs={{0,4},{1,5},{2,6},{3,7},{4,0},{5,1},{6,2},{7,3},{8,12},{9,13},{10,... | collective-permute-start | bytes 1572872 | tf_op jit(solution)/shard_map/ppermute | solution.py:963
  240.7 14.1 %collective-permute-start.14 = (bf16[4,128,512]{2,1,0:T(8,128)(2,1)S(1)}, bf16[4,128,512]{2,1,0:T(8,128)(2,1)S(1)}, u32[]{:S(2)}, u32[]{:S(2)}) collective-permute-start(bf16[4,128,512]{2,1,0:T(8,128)(2,1)S(1)} %pad_maximum_fusion.refs_0_), channel_id=1, source_target_pairs={{0,2},{1,3},{2,0},{3,1},{4,6},{5,7},{6,4},{7,5},{8,10},{9,11},{10,... | collective-permute-start | bytes 1572872 | tf_op jit(solution)/shard_map/ppermute | solution.py:963
  254.7 14.3 %collective-permute-start.20 = (bf16[4,128,512]{2,1,0:T(8,128)(2,1)S(1)}, bf16[4,128,512]{2,1,0:T(8,128)(2,1)S(1)}, u32[]{:S(2)}, u32[]{:S(2)}) collective-permute-start(bf16[4,128,512]{2,1,0:T(8,128)(2,1)S(1)} %pad_maximum_fusion.refs_0_), channel_id=1, source_target_pairs={{0,6},{1,7},{2,4},{3,5},{4,2},{5,3},{6,0},{7,1},{8,14},{9,15},{10,... | collective-permute-start | bytes 1572872 | tf_op jit(solution)/shard_map/ppermute | solution.py:963
  261.6 12.3 %collective-permute-start.21 = (bf16[4,128,512]{2,1,0:T(8,128)(2,1)S(1)}, bf16[4,128,512]{2,1,0:T(8,128)(2,1)S(1)}, u32[]{:S(2)}, u32[]{:S(2)}) collective-permute-start(bf16[4,128,512]{2,1,0:T(8,128)(2,1)S(1)} %collective-permute-done.14.refs_1_), channel_id=1, source_target_pairs={{0,1},{1,0},{2,3},{3,2},{4,5},{5,4},{6,7},{7,6},{8,9},{9,8},{10,11... | collective-permute-start | bytes 1572872 | tf_op jit(solution)/shard_map/ppermute | solution.py:963
  264.1 11.2 %collective-permute-start.22 = (bf16[4,128,512]{2,1,0:T(8,128)(2,1)S(1)}, bf16[4,128,512]{2,1,0:T(8,128)(2,1)}, u32[]{:S(2)}, u32[]{:S(2)}) collective-permute-start(bf16[4,128,512]{2,1,0:T(8,128)(2,1)S(1)} %collective-permute-done.15.refs_2_), channel_id=1, source_target_pairs={{0,1},{1,0},{2,3},{3,2},{4,5},{5,4},{6,7},{7,6},{8,9},{9,8},{10,11... | collective-permute-start | bytes 1572872 | tf_op jit(solution)/shard_map/ppermute | solution.py:963
  266.3 17.2 %collective-permute-start.30 = (bf16[4,72,512]{2,1,0:T(8,128)(2,1)S(1)}, bf16[4,72,512]{2,1,0:T(8,128)(2,1)S(1)}, u32[]{:S(2)}, u32[]{:S(2)}) collective-permute-start(bf16[4,72,512]{2,1,0:T(8,128)(2,1)S(1)} %pad_maximum_fusion.1.refs_0_), channel_id=1, source_target_pairs={{0,1},{1,0},{2,3},{3,2},{4,5},{5,4},{6,7},{7,6},{8,9},{9,8},{10,11... | collective-permute-start | bytes 884744 | tf_op jit(solution)/shard_map/ppermute | solution.py:963
  266.4 17.1 %collective-permute-start.29 = (bf16[4,72,512]{2,1,0:T(8,128)(2,1)S(1)}, bf16[4,72,512]{2,1,0:T(8,128)(2,1)S(1)}, u32[]{:S(2)}, u32[]{:S(2)}) collective-permute-start(bf16[4,72,512]{2,1,0:T(8,128)(2,1)S(1)} %pad_maximum_fusion.1.refs_0_), channel_id=1, source_target_pairs={{0,6},{1,7},{2,4},{3,5},{4,2},{5,3},{6,0},{7,1},{8,14},{9,15},{10,... | collective-permute-start | bytes 884744 | tf_op jit(solution)/shard_map/ppermute | solution.py:963
  273.9 9.6 %collective-permute-start.28 = (bf16[4,72,512]{2,1,0:T(8,128)(2,1)S(1)}, bf16[4,72,512]{2,1,0:T(8,128)(2,1)S(1)}, u32[]{:S(2)}, u32[]{:S(2)}) collective-permute-start(bf16[4,72,512]{2,1,0:T(8,128)(2,1)S(1)} %pad_maximum_fusion.1.refs_0_), channel_id=1, source_target_pairs={{0,4},{1,5},{2,6},{3,7},{4,0},{5,1},{6,2},{7,3},{8,12},{9,13},{10,... | collective-permute-start | bytes 884744 | tf_op jit(solution)/shard_map/ppermute | solution.py:963
  (34 other events, 240.2 us)

commit v6 on v5

--- a/solution.py
+++ b/solution.py
@@ -25,11 +25,13 @@
 GROUPS = HEADS // GROUP
 TOGETHER = 8
 LANES = 128
+DEAL_PARTS = 5
+ATTENTION_FIRST = 3
 ROWS_FIRST = 2
-FIRST_TILES = 3
 ONES = 16
 CHUNK = 512
-VMEM_LIMIT = 60 * 1024 * 1024
+MIB = 1024 * 1024
+VMEM_LIMIT = 60 * MIB
 
 f32 = jnp.float32
 
@@ -393,7 +395,7 @@
         out_shape=[jax.ShapeDtypeStruct(s, d) for s, d, _ in outs]
         + [jax.ShapeDtypeStruct(s, d) for s, d in fixed],
         compiler_params=pltpu.CompilerParams(
-            dimension_semantics=("arbitrary",), vmem_limit_bytes=VMEM_LIMIT
+            dimension_semantics=("arbitrary",), vmem_limit_bytes=62 * MIB
         ),
         cost_estimate=took(61),
         name="forward",
@@ -520,13 +522,13 @@
 
 
 def back_attention_kernel(
-    first, last, order_ref, keep_ref, own_ref,
+    begin, last, order_ref, keep_ref, own_ref,
     qkv_ref, probs_ref, joined_ref, grad_mixed_ref, grad_after_ref,
     plain_ref, mixed_mask_ref, gain1_ref, bias1_ref, *refs,
 ):
-    if first:
-        held_in = ()
-    else:
+    first = begin == 0
+    held_in = ()
+    if not first:
         held_in, refs = refs[:3], refs[4:]
     if last:
         ending, refs = refs[:10], refs[10:]
@@ -540,7 +542,7 @@
     mixed = mixed_mask_ref[...]
 
     @pl.when(step == 0)
-    def begin():
+    def open_sums():
         for at, ref in enumerate((sum_qkv, heads, after_heads)):
             ref[...] = jnp.zeros_like(ref) if first else held_in[at][...]
 
@@ -567,7 +569,7 @@
     normed = (unit * gain1_ref[...] + bias1_ref[...]).astype(bf16)
     turned = jnp.concatenate([normed.T, jnp.ones((ONES, TILE * SLOT), bf16)], axis=0)
     sum_qkv[...] += dot(turned, grad_qkv_ref[...])
-    rows = pl.ds(pl.multiple_of((step + (0 if first else FIRST_TILES)) * TILE, TILE), TILE)
+    rows = pl.ds(pl.multiple_of((step + begin) * TILE, TILE), TILE)
     heads[rows, : 3 * WIDTH] = jnp.concatenate(
         [grad_qkv_ref[at * SLOT : at * SLOT + 16].astype(f32)[:1] for at in range(TILE)], axis=0
     )
@@ -650,13 +652,11 @@
         ).astype(bf16)
 
 
-def run_back_attention(order, keep, own, qkv, probs, joined, grad_mixed, grad_after, plain, mixed, gain1, bias1,
-                       held=None, ending=None, parts=1):
+def run_back_attention(begin, count, order, keep, own, qkv, probs, joined, grad_mixed, grad_after, plain, mixed, gain1,
+                       bias1, held=None, ending=None, parts=1):
     windows = qkv.shape[0]
     steps = windows // TILE
     rows = TILE * TALL
-    begin = 0 if held is None else FIRST_TILES
-    count = FIRST_TILES if held is None else steps - FIRST_TILES
 
     def tile(shape):
         return pl.BlockSpec(shape, lambda step, *_: (step + begin,) + (0,) * (len(shape) - 1))
@@ -693,7 +693,7 @@
         ]
         scratch = [pltpu.VMEM(s, f32) for s in held_shapes] + [pltpu.VMEM((4 * WIDTH, WIDTH), bf16)]
     return pl.pallas_call(
-        functools.partial(back_attention_kernel, held is None, ending is not None),
+        functools.partial(back_attention_kernel, begin, ending is not None),
         grid_spec=pltpu.PrefetchScalarGridSpec(
             num_scalar_prefetch=3,
             grid=(count,),
@@ -795,68 +795,94 @@
         compiler_params=pltpu.CompilerParams(
             dimension_semantics=("arbitrary",), vmem_limit_bytes=VMEM_LIMIT
         ),
-        cost_estimate=took(5),
+        cost_estimate=took(0.3),
         name="relay",
     )(gather, windows)
 
 
-def early_out_kernel(own_ref, *refs):
-    pieces, (fc1_ref, fc2_ref, wide, done) = refs[:-4], refs[-4:]
-    per, share, _ = pieces[0].shape
-    own = own_ref[0]
-    half = len(pieces) // 2
-
-    def copy_first(block):
-        columns = pl.ds(pl.multiple_of(block * WIDTH, WIDTH), WIDTH)
-        return pltpu.make_async_copy(wide.at[block], fc1_ref.at[:, columns], done.at[block])
-
-    def copy_second(block):
-        rows = pl.ds(pl.multiple_of((block - half) * WIDTH, WIDTH), WIDTH)
-        return pltpu.make_async_copy(wide.at[block], fc2_ref.at[rows, :], done.at[block])
-
-    for at, piece in enumerate(pieces):
-        block = at ^ (own // per)
+def widen_early(own, pieces, first, fc1_ref, fc2_ref, wide, done):
+    half = 4
+
+    def copies(place, slot):
+        block = place ^ first
+        columns = pl.ds(pl.multiple_of(block % half * WIDTH, WIDTH), WIDTH)
+        copy_first = pltpu.make_async_copy(wide.at[slot], fc1_ref.at[:, columns], done.at[slot])
+        copy_second = pltpu.make_async_copy(wide.at[slot], fc2_ref.at[columns, :], done.at[slot])
+        return block, copy_first, copy_second
+
+    for slot, (place, piece, low) in enumerate(pieces):
+        share = piece.shape[1]
+        per = WIDTH // share
         for chunk in range(per):
             row = pl.multiple_of((chunk ^ (own % per)) * share, share)
-            wide[block, pl.ds(row, share)] = piece[chunk].astype(f32)
+            wide[slot, pl.ds(row, share)] = piece[low + chunk].astype(f32)
+        block, copy_first, copy_second = copies(place, slot)
 
         @pl.when(block < half)
-        def first(block=block):
-            copy_first(block).start()
+        def start_first(copy=copy_first):
+            copy.start()
 
         @pl.when(block >= half)
-        def second(block=block):
-            copy_second(block).start()
-
-    for block in range(len(pieces)):
-        (copy_first if block < half else copy_second)(block).wait()
-
-
-def run_early_out(own, pieces, units):
-    count = len(pieces)
+        def start_second(copy=copy_second):
+            copy.start()
+
+    def finish():
+        for slot, (place, _, _) in enumerate(pieces):
+            block, copy_first, copy_second = copies(place, slot)
+
+            @pl.when(block < half)
+            def wait_first(copy=copy_first):
+                copy.wait()
+
+            @pl.when(block >= half)
+            def wait_second(copy=copy_second):
+                copy.wait()
+
+    return finish
+
+
+def early_out_kernel(own_ref, near_ref, far_ref, fc1_ref, fc2_ref, wide, done):
+    own = own_ref[0]
+    per = near_ref.shape[0] // 3
+    pieces = [(4 * half + at, ref, at * per) for half, ref in enumerate((near_ref, far_ref)) for at in range(3)]
+    widen_early(own, pieces, own // per, fc1_ref, fc2_ref, wide, done)()
+
+
+def run_early_out(own, near, far, units):
     return pl.pallas_call(
         early_out_kernel,
-        in_specs=[pl.BlockSpec(memory_space=pltpu.SMEM)] + [pl.BlockSpec(memory_space=pltpu.VMEM)] * count,
+        in_specs=[pl.BlockSpec(memory_space=pltpu.SMEM)] + [pl.BlockSpec(memory_space=pltpu.VMEM)] * 2,
         out_specs=[pl.BlockSpec(memory_space=pl.ANY)] * 2,
         out_shape=[
             jax.ShapeDtypeStruct((WIDTH, units), f32),
             jax.ShapeDtypeStruct((units, WIDTH), f32),
         ],
-        scratch_shapes=[pltpu.VMEM((count, WIDTH, WIDTH), f32), pltpu.SemaphoreType.DMA((count,))],
-        compiler_params=pltpu.CompilerParams(vmem_limit_bytes=VMEM_LIMIT),
-        cost_estimate=took(5),
+        scratch_shapes=[pltpu.VMEM((6, WIDTH, WIDTH), f32), pltpu.SemaphoreType.DMA((6,))],
+        compiler_params=pltpu.CompilerParams(vmem_limit_bytes=20 * MIB),
+        cost_estimate=took(0.3),
         name="early_out",
-    )(own, *pieces)
-
-
-def late_out_kernel(own_ref, *refs):
-    pieces, (qkv_ref, out_ref), small_refs, (wide, done) = refs[:-13], refs[-13:-11], refs[-11:-2], refs[-2:]
+    )(own, near, far)
+
+
+def late_out_kernel(places, own_ref, *refs):
+    pieces, refs = refs[:8], refs[8:]
+    early, refs = refs[: len(places)], refs[len(places) + 2 :]
+    (qkv_ref, out_ref), small_refs, (fc1_ref, fc2_ref, wide, wide_early, done, done_early) = refs[:2], refs[2:11], refs[11:]
     per, share, _ = pieces[0].shape
     share -= 8
     own = own_ref[0]
     count = len(pieces)
     height = per * share
     split = WIDTH // height
+    finish = widen_early(
+        own,
+        [(place, piece, 0) for place, piece in zip(places, early)],
+        own // early[0].shape[0],
+        fc1_ref,
+        fc2_ref,
+        wide_early,
+        done_early,
+    )
 
     def copy_first(block):
         rows = pl.ds(pl.multiple_of(block % split * height, height), height)
@@ -892,29 +918,40 @@
 
     for block in range(count):
         (copy_first if block < 3 * split else copy_second)(block).wait()
-
-
-def run_late_out(own, pieces, units):
+    finish()
+
+
+def run_late_out(own, pieces, early, grad_w_fc1, grad_w_fc2):
+    places = (3, 7)
     count = len(pieces)
     per, share, _ = pieces[0].shape
+    units = grad_w_fc1.shape[1]
+    anywhere = pl.BlockSpec(memory_space=pl.ANY)
+    kept = pl.BlockSpec(memory_space=pltpu.VMEM)
+    inputs = [own, *pieces, *early, grad_w_fc1, grad_w_fc2]
     return pl.pallas_call(
-        late_out_kernel,
-        in_specs=[pl.BlockSpec(memory_space=pltpu.SMEM)] + [pl.BlockSpec(memory_space=pltpu.VMEM)] * count,
-        out_specs=[pl.BlockSpec(memory_space=pl.ANY)] * 2 + [pl.BlockSpec(memory_space=pltpu.VMEM)] * 9,
+        functools.partial(late_out_kernel, places),
+        in_specs=[pl.BlockSpec(memory_space=pltpu.SMEM)] + [kept] * (count + len(places)) + [anywhere] * 2,
+        out_specs=[anywhere] * 2 + [kept] * 9 + [anywhere] * 2,
         out_shape=[
             jax.ShapeDtypeStruct((WIDTH, 3 * WIDTH), f32),
             jax.ShapeDtypeStruct((WIDTH, WIDTH), f32),
             *[jax.ShapeDtypeStruct((1, WIDTH), f32)] * 8,
             jax.ShapeDtypeStruct((1, units), f32),
+            jax.ShapeDtypeStruct((WIDTH, units), f32),
+            jax.ShapeDtypeStruct((units, WIDTH), f32),
         ],
+        input_output_aliases={len(inputs) - 2: 11, len(inputs) - 1: 12},
         scratch_shapes=[
             pltpu.VMEM((count, per * (share - 8), WIDTH), f32),
+            pltpu.VMEM((len(places), WIDTH, WIDTH), f32),
             pltpu.SemaphoreType.DMA((count,)),
+            pltpu.SemaphoreType.DMA((len(places),)),
         ],
-        compiler_params=pltpu.CompilerParams(vmem_limit_bytes=VMEM_LIMIT),
+        compiler_params=pltpu.CompilerParams(vmem_limit_bytes=20 * MIB),
         cost_estimate=took(3),
         name="late_out",
-    )(own, *pieces)
+    )(*inputs)
 
 
 def band_to_windows(band_values, win_count):
@@ -980,8 +1017,12 @@
     return add_up(sum_parts(rows.reshape((1 << len(stage), -1) + rows.shape[1:]), stage))
 
 
+def gather_parts(rows, stage):
+    return [rows] + [swap(rows, pairs) for _, pairs in stage_moves(stage)]
+
+
 def gather_stage(rows, stage):
-    return jnp.concatenate([rows] + [swap(rows, pairs) for _, pairs in stage_moves(stage)], axis=0)
+    return jnp.concatenate(gather_parts(rows, stage), axis=0)
 
 
 def sum_stages(rows, stages):
@@ -990,49 +1031,123 @@
     return rows
 
 
-def deal_kernel(pick_ref, region_ref, local_ref, out_ref):
+def deal_kernel(pick_ref, region_ref, local_ref, out_ref, rows_in, rows_out, came, gone):
     groups = out_ref.shape[0]
-    for pair in range(out_ref.shape[1] // 16):
-        head = region_ref[...] if pair == 0 else local_ref[2 * pair - 1]
-        rows = jnp.concatenate([head, local_ref[2 * pair]], axis=0)
-        out_ref[:, 16 * pair : 16 * pair + 16, :] = (
-            dot(pick_ref[...], rows).astype(bf16).reshape(groups, 16, WIDTH)
-        )
-
-
-def collect_kernel(pick_ref, came_ref, region_ref, local_ref):
+    positions = rows_in.shape[0]
+    part = positions // DEAL_PARTS
+
+    def copy_in(at):
+        low = at * part
+        if at == 0:
+            return [
+                pltpu.make_async_copy(region_ref, rows_in.at[0], came.at[DEAL_PARTS]),
+                pltpu.make_async_copy(local_ref.at[: part - 1], rows_in.at[1:part], came.at[0]),
+            ]
+        return [
+            pltpu.make_async_copy(local_ref.at[low - 1 : low + part - 1], rows_in.at[low : low + part], came.at[at])
+        ]
+
+    def copy_out(at):
+        rows = slice(at * part * TILE, (at + 1) * part * TILE)
+        return pltpu.make_async_copy(rows_out.at[:, rows, :], out_ref.at[:, rows, :], gone.at[at])
+
+    for at in range(DEAL_PARTS):
+        for copy in copy_in(at):
+            copy.start()
+    for at in range(DEAL_PARTS):
+        for copy in copy_in(at):
+            copy.wait()
+        pairs = range(at * part // 2, (at + 1) * part // 2)
+        dealt = [
+            dot(pick_ref[...], jnp.concatenate([rows_in[2 * pair], rows_in[2 * pair + 1]], axis=0))
+            for pair in pairs
+        ]
+        for pair, rows in zip(pairs, dealt):
+            rows_out[:, 16 * pair : 16 * pair + 16, :] = rows.astype(bf16).reshape(groups, 16, WIDTH)
+        copy_out(at).start()
+    for at in range(DEAL_PARTS):
+        copy_out(at).wait()
+
+
+def collect_kernel(pick_ref, came_ref, region_ref, local_ref, rows_in, rows_out, came, gone):
     slots = region_ref.shape[0]
-    for pair in range(came_ref.shape[1] // 16):
-        rows = came_ref[:, 16 * pair : 16 * pair + 16, :].reshape(2 * slots, WIDTH)
-        rows = dot(pick_ref[...], rows).astype(bf16)
-        if pair == 0:
-            region_ref[...] = rows[:slots]
-        else:
-            local_ref[2 * pair - 1] = rows[:slots]
-        local_ref[2 * pair] = rows[slots:]
+    positions = rows_out.shape[0]
+    part = positions // DEAL_PARTS
+
+    def copy_in(at):
+        rows = slice(at * part * TILE, (at + 1) * part * TILE)
+        return pltpu.make_async_copy(came_ref.at[:, rows, :], rows_in.at[:, rows, :], came.at[at])
+
+    def copy_out(at):
+        low = at * part
+        if at == 0:
+            return [
+                pltpu.make_async_copy(rows_out.at[0], region_ref, gone.at[DEAL_PARTS]),
+                pltpu.make_async_copy(rows_out.at[1:part], local_ref.at[: part - 1], gone.at[0]),
+            ]
+        return [
+            pltpu.make_async_copy(rows_out.at[low : low + part], local_ref.at[low - 1 : low + part - 1], gone.at[at])
+        ]
+
+    for at in range(DEAL_PARTS):
+        copy_in(at).start()
+    for at in range(DEAL_PARTS):
+        copy_in(at).wait()
+        pairs = range(at * part // 2, (at + 1) * part // 2)
+        dealt = [
+            dot(pick_ref[...], rows_in[:, 16 * pair : 16 * pair + 16, :].reshape(2 * slots, WIDTH)) for pair in pairs
+        ]
+        for pair, rows in zip(pairs, dealt):
+            rows = rows.astype(bf16)
+            rows_out[2 * pair] = rows[:slots]
+            rows_out[2 * pair + 1] = rows[slots:]
+        for copy in copy_out(at):
+            copy.start()
+    for at in range(DEAL_PARTS):
+        for copy in copy_out(at):
+            copy.wait()
 
 
 def run_deal(pick, region, local):
-    count = region.shape[0] // TILE
+    slots = region.shape[0]
+    count, positions = slots // TILE, local.shape[0] + 1
     return pl.pallas_call(
         deal_kernel,
-        out_shape=jax.ShapeDtypeStruct((count, (local.shape[0] + 1) * TILE, WIDTH), bf16),
+        in_specs=[pl.BlockSpec(memory_space=pltpu.VMEM)] + [pl.BlockSpec(memory_space=pl.ANY)] * 2,
+        out_specs=pl.BlockSpec(memory_space=pl.ANY),
+        out_shape=jax.ShapeDtypeStruct((count, positions * TILE, WIDTH), bf16),
+        scratch_shapes=[
+            pltpu.VMEM((positions, slots, WIDTH), bf16),
+            pltpu.VMEM((count, positions * TILE, WIDTH), bf16),
+            pltpu.SemaphoreType.DMA((DEAL_PARTS + 1,)),
+            pltpu.SemaphoreType.DMA((DEAL_PARTS,)),
+        ],
         compiler_params=pltpu.CompilerParams(vmem_limit_bytes=VMEM_LIMIT),
-        cost_estimate=took(5),
+        cost_estimate=took(4),
         name="deal",
     )(pick, region, local)
 
 
 def run_collect(pick, came):
-    slots = came.shape[0] * TILE
+    count, rows, _ = came.shape
+    slots, positions = count * TILE, rows // TILE
+    anywhere = pl.BlockSpec(memory_space=pl.ANY)
     return pl.pallas_call(
         collect_kernel,
+        in_specs=[pl.BlockSpec(memory_space=pltpu.VMEM), anywhere],
+        out_specs=[anywhere] * 2,
         out_shape=[
             jax.ShapeDtypeStruct((slots, WIDTH), bf16),
-            jax.ShapeDtypeStruct((came.shape[1] // TILE - 1, slots, WIDTH), bf16),
+            jax.ShapeDtypeStruct((positions - 1, slots, WIDTH), bf16),
+        ],
+        scratch_shapes=[
+            pltpu.VMEM((count, rows, WIDTH), bf16),
+            pltpu.VMEM((positions, slots, WIDTH), bf16),
+            pltpu.SemaphoreType.DMA((DEAL_PARTS,)),
+            pltpu.SemaphoreType.DMA((DEAL_PARTS + 1,)),
         ],
         compiler_params=pltpu.CompilerParams(vmem_limit_bytes=VMEM_LIMIT),
-        cost_estimate=took(5),
+        cost_estimate=took(0.3),
         name="collect",
     )(pick, came)
 
@@ -1141,11 +1256,15 @@
     attention = (
         order, keep, own, qkv, probs, joined, grad_mixed, grad_after, plain, mixed_mask, gain1, bias1
     )
-    grad_qkv, *held = run_back_attention(*attention)
-    early = split_sum([early, early_came], stages[1])
+    tile_count = win_count // TILE
+    xy_stage, (z_stage, *more) = stages[1], stages[2:]
+    grad_qkv, *held = run_back_attention(0, ATTENTION_FIRST, *attention)
+    early = split_sum([early, early_came], xy_stage)
     held, early, came = lax.optimization_barrier((held, early, came))
-    early = add_up(sum_parts(early, stages[1]))
+    early = add_up(sum_parts(early, xy_stage))
     grad_qkv, late, late_sent, regional_out = run_back_attention(
+        ATTENTION_FIRST,
+        tile_count - ATTENTION_FIRST,
         *attention,
         held=(*held, grad_qkv),
         ending=(grad_out, order[None], regional[0], qkv_r, probs_r, mixed_r, w_qkv, w_out, small, row_fc1),
@@ -1153,39 +1272,45 @@
     )
     late_came = swap(late_sent, pairs)
     grad_qkv, early = lax.optimization_barrier((grad_qkv, early))
-    early = sum_stages(early, stages[2:])
+    early = sum_parts(split_sum([early], z_stage), z_stage)
     rows = (order, grad_qkv, joined, grad_after, gain1, w_qkv)
     windows = run_back_rows(*rows, 0, ROWS_FIRST)
     windows, late_came = lax.optimization_barrier((windows, late_came))
-    late = add_up(sum_parts(split_sum([late, late_came], stages[1]), stages[1]))
+    late = sum_parts(split_sum([late, late_came], xy_stage), xy_stage)
     windows, early = lax.optimization_barrier((windows, early))
-    for stage in reversed(stages[2:]):
+    early = sum_stages(add_up(early), more)
+    for stage in reversed(more):
         early = gather_stage(early, stage)
-    windows = run_back_rows(*rows, ROWS_FIRST, win_count // TILE - ROWS_FIRST, held=windows)
+    early = gather_parts(early, z_stage)
+    windows = run_back_rows(*rows, ROWS_FIRST, tile_count - ROWS_FIRST, held=windows)
     windows, early, late = lax.optimization_barrier((windows, early, late))
-    late = sum_stages(late, stages[2:])
-    moves = stage_moves(stages[1])
+    late = sum_parts(split_sum([add_up(late)], z_stage), z_stage)
+    early = jnp.concatenate(early, axis=0)
+    moves = stage_moves(xy_stage)
     early = [early] + [swap(early, moves[at][1]) for at in range(2)]
-    early_far = [swap(early[0], pairs)]
     tokens_out = run_relay(gather, windows)
-    tokens_out, came, early, early_far, late = lax.optimization_barrier(
-        (tokens_out, came, early, early_far, late)
-    )
-    early += [swap(early[0], pairs) for _, pairs in moves[2:]]
-    early_far += [swap(piece, pairs) for piece in early[1:3]]
-    for stage in reversed(stages[2:]):
+    tokens_out, came, early, late = lax.optimization_barrier((tokens_out, came, early, late))
+    late = sum_stages(add_up(late), more)
+    for stage in reversed(more):
         late = gather_stage(late, stage)
-    came, late = lax.optimization_barrier((came, late))
-    late = [late] + [swap(late, pairs) for _, pairs in moves]
-    early_far += [swap(piece, pairs) for piece in early[3:]]
+    late = gather_parts(late, z_stage)
+    (_, across), = moves[2:]
+    early_last = swap(early[0], across)
+    early = jnp.concatenate(early, axis=0)
+    early_far = swap(early, pairs)
+    came, early_far, late = lax.optimization_barrier((came, early_far, late))
+    late = gather_parts(jnp.concatenate(late, axis=0), xy_stage)
+    grad_w_fc1, grad_w_fc2 = run_early_out(own, early, early_far, w_fc1.shape[1])
+    out_regional, out_local = run_collect(pick_back, came)
     late_far = [swap(late[0], pairs)]
-    grad_w_fc1, grad_w_fc2 = run_early_out(own, early + early_far, w_fc1.shape[1])
-    out_regional, out_local = run_collect(pick_back, came)
-    grad_w_fc1, grad_w_fc2, out_local, late, late_far = lax.optimization_barrier(
-        (grad_w_fc1, grad_w_fc2, out_local, late, late_far)
-    )
+    grad_w_fc1, grad_w_fc2, out_local, early_last, late, late_far = lax.optimization_barrier(
+        (grad_w_fc1, grad_w_fc2, out_local, early_last, late, late_far)
+    )
+    early_last = [early_last, swap(early_last, pairs)]
     late_far += [swap(piece, pairs) for piece in late[1:]]
-    grad_w_qkv, grad_w_out, *vectors = run_late_out(own, late + late_far, w_fc1.shape[1])
+    grad_w_qkv, grad_w_out, *vectors, grad_w_fc1, grad_w_fc2 = run_late_out(
+        own, late + late_far, early_last, grad_w_fc1, grad_w_fc2
+    )
     vectors = [vector[0] for vector in vectors]
     return (
         jnp.swapaxes(out_local, 0, 1)[None],

time: 296 us -> 293 us (0.990)
  Pallas kernels: 202 us -> 198 us
    ppermute x34 -> x32, waiting for transfers between devices: 18.8 us -> 21.6 us  [swap(): return lax.ppermute(rows, ('dp', 'img'), pairs)]
    ppermute x34 -> x32, starting transfers between devices: 33.3 us -> 34.3 us  [swap(): return lax.ppermute(rows, ('dp', 'img'), pairs)]
  transfers between devices with their start and end apart: 36 -> 34, of which waited for: 14 -> 11; matrix products, arithmetic and copies ran while one was open for 4% -> 4% of each run, Pallas kernels for 66% -> 66%
where the time goes in v6:
time: 293 us; the launch traced here: 290 us
  Pallas kernels  198 us (68%)
  starting transfers between devices  45.5 us (16%)
  waiting for transfers between devices  28.8 us (10%)
  other arithmetic  9.7 us (3%)
  local copies, waits for them, and re-layouts  5.87 us (2%)
    pallas_call x1, Pallas kernels, run_forward(): pl.pallas_call(forward_kernel, grid_spec=pltpu.PrefetchScalarGridSpec(num...  61.4 us
    pallas_call x1, Pallas kernels, run_back_mlp(): pl.pallas_call(back_mlp_kernel, grid_spec=pltpu.PrefetchScalarGridSpec(nu...  54.9 us
    pallas_call x2, Pallas kernels, run_back_attention(): pl.pallas_call(functools.partial(back_attention_kernel, begin, ending is...  40.5 us
    ppermute x32, starting transfers between devices, swap(): return lax.ppermute(rows, ('dp', 'img'), pairs)  34.3 us
    ppermute x32, waiting for transfers between devices, swap(): return lax.ppermute(rows, ('dp', 'img'), pairs)  21.6 us
    pallas_call x2, Pallas kernels, run_back_rows(): pl.pallas_call(functools.partial(back_rows_kernel, begin), grid_spec=pltp...  20.2 us
    all_to_all x2, starting transfers between devices, swap_tiles(): lax.all_to_all(tiles_sent, 'dp', split_axis=0, concat_axis=0, tiled=True)  11.2 us
    all_to_all x2, waiting for transfers between devices, swap_tiles(): lax.all_to_all(tiles_sent, 'dp', split_axis=0, concat_axis=0, tiled=True)  7.19 us
  transfers between devices with their start and end apart: 34, of which 11 were waited for; matrix products, arithmetic and copies ran while one was open for 4% of the time, Pallas kernels for 66%

profile of v6, /device:TPU:0, one launch (start us, length us, event | category | flops | bytes accessed | tf_op | source)
XLA Modules:
  0.0 289.7 jit_solution(7936589720215676893)
XLA Ops:
  2.6 4.4 %deal.1 = bf16[8,400,512]{2,1,0:T(8,128)(2,1)} custom-call(bf16[128,128]{1,0:T(8,128)(2,1)} %get-tuple-element.220.pick_ref, bf16[64,512]{1,0:T(8,128)(2,1)} %bitcast.66, bf16[49,64,512]{2,1,0:T(8,128)(2,1)} %bitcast.63), custom_call_target="tpu_custom_call" | custom-call | flops 4600000000 | bytes 1000000 | tf_op jit(solution)/shard_map/deal/pallas_call | solution.py:1114
  7.0 7.4 %all-to-all-start = ((bf16[8,400,512]{2,1,0:T(8,128)(2,1)}), bf16[8,400,512]{2,1,0:T(8,128)(2,1)}, u32[]{:S(2)}, u32[]{:S(2)}) async-start(bf16[8,400,512]{2,1,0:T(8,128)(2,1)} %deal.1), calls=%async_computation | async-start | bytes 6553600 | tf_op jit(solution)/shard_map/all_to_all | solution.py:1159
  20.0 61.4 %forward.1 = (bf16[8,400,512]{2,1,0:T(8,128)(2,1)}, bf16[64,12,64,128]{3,2,1,0:T(8,128)(2,1)}, bf16[64,8,64,128]{3,2,1,0:T(8,128)(2,1)}, bf16[64,64,512]{2,1,0:T...) custom-call(s32[64]{0:T(128)} %select_reduce_fusion.1.order_ref, ...), custom_call_target="tpu_custom_call" | custom-call | flops 70149996544 | bytes 1000000 | tf_op jit(solution)/shard_map/forward/pallas_call | solution.py:381
  81.4 6.6 %all-to-all-done.cot_ref = bf16[8,400,512]{2,1,0:T(8,128)(2,1)} async-done(((bf16[8,400,512]{2,1,0:T(8,128)(2,1)}), bf16[8,400,512]{2,1,0:T(8,128)(2,1)}, u32[]{:S(2)}, u32[]{:S(2)}) %all-to-all-start) | async-done | bytes 3276832 | tf_op jit(solution)/shard_map/all_to_all | solution.py:1159
  88.0 3.8 %all-to-all-start.1 = ((bf16[8,400,512]{2,1,0:T(8,128)(2,1)}), bf16[8,400,512]{2,1,0:T(8,128)(2,1)S(1)}, u32[]{:S(2)}, u32[]{:S(2)}) async-start(bf16[8,400,512]{2,1,0:T(8,128)(2,1)} %get-tuple-element.124), calls=%async_computation.1 | async-start | bytes 6553600 | tf_op jit(solution)/shard_map/all_to_all | solution.py:1159
  91.9 54.9 %back_mlp.1 = (f32[3584,512]{1,0:T(8,128)}, bf16[64,4,64,128]{3,2,1,0:T(8,128)(2,1)}, bf16[16,128,512]{2,1,0:T(8,128)(2,1)}, bf16[16,128,512]{2,1,0:T(8,128)(2,1...) custom-call(f32[1]{0:T(128)} %bitcast.3.keep_ref, s32[1]{0:T(128)} %bitcast.own_ref, ...), custom_call_target="tpu_custom_call" | custom-call | flops 63250001920 | bytes 1000000 | tf_op jit(solution)/shard_map/back_mlp/pallas_call | solution.py:498
  146.8 14.2 %back_attention.2 = (bf16[4096,1536]{1,0:T(8,128)(2,1)}, f32[528,1536]{1,0:T(8,128)}, f32[64,2048]{1,0:T(8,128)}, f32[64,512]{1,0:T(8,128)}) custom-call(s32[64]{0:T(128)} %select_reduce_fusion.1.order_ref, f32[1]{0:T(128)} %bitcast.3.keep_ref, s32[1]{0:T(128)} %bitcast.own_ref, bf16[64,12,64,128]{3,2,1,0:T(8,128)(2,1)} %get-tuple-element.110.qkv_ref, ...), custom_call_target="tpu_custom_call" | custom-call | flops 17250000896 | bytes 1000000 | tf_op jit(solution)/shard_map/back_attention/pallas_call | solution.py:695
  161.1 3.9 %add_convert_fusion.1 = (bf16[4,128,512]{2,1,0:T(8,128)(2,1)}, bf16[4,128,512]{2,1,0:T(8,128)(2,1)}, bf16[4,128,512]{2,1,0:T(8,128)(2,1)}, bf16[4,128,512]{2,1,0:T(8,128)(2,1)}) fusion(bf16[16,128,512]{2,1,0:T(8,128)(2,1)} %collective-permute-done, bf16[16,128,512]{2,1,0:T(8,128)(2,1)} %get-tuple-element.122), kind=kLoop, calls=%fused_computation.1 | loop fusion | flops 4194304 | bytes 6291456 | tf_op jit(solution)/shard_map/convert_element_type | solution.py:1004
  169.0 26.3 %back_attention.3 = (bf16[4096,1536]{1,0:T(8,128)(2,1)}, bf16[16,72,512]{2,1,0:T(8,128)(2,1)}, bf16[16,72,512]{2,1,0:T(8,128)(2,1)}, bf16[64,512]{1,0:T(8,128)(2,1)}) custom-call(s32[64]{0:T(128)} %select_reduce_fusion.1.order_ref, f32[1]{0:T(128)} %bitcast.3.keep_ref, s32[1]{0:T(128)} %bitcast.own_ref, ...), custom_call_target="tpu_custom_call", output_to_operand_aliasing={{0}: (15, {})} | custom-call | flops 28750000128 | bytes 1000000 | tf_op jit(solution)/shard_map/back_attention/pallas_call | solution.py:695
  197.1 3.4 %collective-permute-start.7 = (bf16[1,128,512]{2,1,0:T(8,128)(2,1)S(1)}, bf16[1,128,512]{2,1,0:T(8,128)(2,1)S(1)}, u32[]{:S(2)}, u32[]{:S(2)}) collective-permute-start(bf16[1,128,512]{2,1,0:T(8,128)(2,1)S(1)} %get-tuple-element.211), channel_id=1, source_target_pairs={{0,24},{1,25},{2,26},{3,27},{4,28},{5,29},{6,30},{7,31},{8,16},{9,... | collective-permute-start | bytes 393224 | tf_op jit(solution)/shard_map/ppermute | solution.py:1000
  201.5 6.6 %back_rows.2.refs_0_ = bf16[64,64,512]{2,1,0:T(8,128)(2,1)} custom-call(s32[64]{0:T(128)} %select_reduce_fusion.1.order_ref, bf16[4096,1536]{1,0:T(8,128)(2,1)} %get-tuple-element.140.grad_qkv_ref, bf16[64,64,512]{2,1,0:T(8,128)(2,1)} %get-tuple-element.112.joined_ref, f32[3584,512]{1,0:T(8,128)} %get-tuple-element.118.grad_after_ref, f32[1,512]{1,0:T(1,128)} %bitcast.59, ...), custom_call_target="tpu_custom_call" | custom-call | flops 5750000128 | bytes 1000000 | tf_op jit(solution)/shard_map/back_rows/pallas_call | solution.py:762
  208.2 4.2 %collective-permute-done.6 = bf16[1,128,512]{2,1,0:T(8,128)(2,1)S(1)} collective-permute-done((bf16[1,128,512]{2,1,0:T(8,128)(2,1)S(1)}, bf16[1,128,512]{2,1,0:T(8,128)(2,1)S(1)}, u32[]{:S(2)}, u32[]{:S(2)}) %collective-permute-start.6) | collective-permute-done | bytes 131104 | tf_op jit(solution)/shard_map/ppermute | solution.py:1000
  212.5 2.4 collective-permute-start.10
  217.3 2.5 collective-permute-start.13
  222.4 13.5 %back_rows.3.windows_ref = bf16[64,64,512]{2,1,0:T(8,128)(2,1)} custom-call(s32[64]{0:T(128)} %select_reduce_fusion.1.order_ref, bf16[4096,1536]{1,0:T(8,128)(2,1)} %get-tuple-element.140.grad_qkv_ref, bf16[64,64,512]{2,1,0:T(8,128)(2,1)} %get-tuple-element.112.joined_ref, ...), custom_call_target="tpu_custom_call", output_to_operand_aliasing={{}: (6, {})} | custom-call | flops 17250000896 | bytes 1000000 | tf_op jit(solution)/shard_map/back_rows/pallas_call | solution.py:762
  240.7 2.4 collective-permute-start.18
  245.1 5.8 %relay.1 = bf16[8,392,512]{2,1,0:T(8,128)(2,1)} custom-call(bf16[392,512]{1,0:T(8,128)(2,1)} %constant.192.clone.gather_ref, bf16[64,64,512]{2,1,0:T(8,128)(2,1)} %back_rows.3.windows_ref), custom_call_target="tpu_custom_call" | custom-call | flops 345000000 | bytes 1000000 | tf_op jit(solution)/shard_map/relay/pallas_call | solution.py:789
  251.3 2.4 collective-permute-start.22
  258.3 2.7 collective-permute-done.21
  264.6 2.8 early_out.1
  267.4 4.4 %collect.1 = (bf16[64,512]{1,0:T(8,128)(2,1)}, bf16[49,64,512]{2,1,0:T(8,128)(2,1)}) custom-call(bf16[128,128]{1,0:T(8,128)(2,1)} %get-tuple-element.219.pick_ref, bf16[8,400,512]{2,1,0:T(8,128)(2,1)} %copy-done), custom_call_target="tpu_custom_call" | custom-call | flops 345000000 | bytes 1000000 | tf_op jit(solution)/shard_map/collect/pallas_call | solution.py:1135
  271.8 6.0 %collective-permute-done.26.refs_3_ = bf16[4,72,512]{2,1,0:T(8,128)(2,1)S(1)} collective-permute-done((bf16[4,72,512]{2,1,0:T(8,128)(2,1)S(1)}, bf16[4,72,512]{2,1,0:T(8,128)(2,1)S(1)}, u32[]{:S(2)}, u32[]{:S(2)}) %collective-permute-start.26) | collective-permute-done | bytes 294944 | tf_op jit(solution)/shard_map/ppermute | solution.py:1000
  277.8 5.0 %collective-permute-done.25.refs_2_ = bf16[4,72,512]{2,1,0:T(8,128)(2,1)S(1)} collective-permute-done((bf16[4,72,512]{2,1,0:T(8,128)(2,1)S(1)}, bf16[4,72,512]{2,1,0:T(8,128)(2,1)S(1)}, u32[]{:S(2)}, u32[]{:S(2)}) %collective-permute-start.25) | collective-permute-done | bytes 294944 | tf_op jit(solution)/shard_map/ppermute | solution.py:1000
  286.0 3.5 %late_out.1 = (f32[512,1536]{1,0:T(8,128)}, f32[512,512]{1,0:T(8,128)}, f32[1,512]{1,0:T(1,128)}, f32[1,512]{1,0:T(1,128)}, f32[1,512]{1,0:T(1,128)}, /*index=5*...) custom-call(s32[1]{0:T(128)} %bitcast.own_ref, ...), custom_call_target="tpu_custom_call", output_to_operand_aliasing={{11}: (11, {}), {12}: (12, {})} | custom-call | flops 3449999872 | bytes 1000000 | tf_op jit(solution)/shard_map/late_out/pallas_call | solution.py:932
  (111 shorter events, 37.0 us)
Async XLA Ops:
  7.0 81.0 %all-to-all-start = ((bf16[8,400,512]{2,1,0:T(8,128)(2,1)}), bf16[8,400,512]{2,1,0:T(8,128)(2,1)}, u32[]{:S(2)}, u32[]{:S(2)}) async-start(bf16[8,400,512]{2,1,0:T(8,128)(2,1)} %deal.1), calls=%async_computation | async-start | bytes 6553600 | tf_op jit(solution)/shard_map/all_to_all | solution.py:1159
  88.0 77.5 %all-to-all-start.1 = ((bf16[8,400,512]{2,1,0:T(8,128)(2,1)}), bf16[8,400,512]{2,1,0:T(8,128)(2,1)S(1)}, u32[]{:S(2)}, u32[]{:S(2)}) async-start(bf16[8,400,512]{2,1,0:T(8,128)(2,1)} %get-tuple-element.124), calls=%async_computation.1 | async-start | bytes 6553600 | tf_op jit(solution)/shard_map/all_to_all | solution.py:1159
  146.8 14.3 %collective-permute-start = (bf16[16,128,512]{2,1,0:T(8,128)(2,1)}, bf16[16,128,512]{2,1,0:T(8,128)(2,1)}, u32[]{:S(2)}, u32[]{:S(2)}) collective-permute-start(bf16[16,128,512]{2,1,0:T(8,128)(2,1)} %get-tuple-element.123), channel_id=1, source_target_pairs={{0,1},{1,0},{2,3},{3,2},{4,5},{5,4},{6,7},{7,6},{8,9},{9,8},{10,11... | collective-permute-start | bytes 6291464 | tf_op jit(solution)/shard_map/ppermute | solution.py:1000
  165.5 29.8 %collective-permute-start.1 = (bf16[4,128,512]{2,1,0:T(8,128)(2,1)}, bf16[4,128,512]{2,1,0:T(8,128)(2,1)}, u32[]{:S(2)}, u32[]{:S(2)}) collective-permute-start(bf16[4,128,512]{2,1,0:T(8,128)(2,1)} %get-tuple-element.137), channel_id=1, source_target_pairs={{0,2},{1,3},{2,0},{3,1},{4,6},{5,7},{6,4},{7,5},{8,10},{9,11},{10,... | collective-permute-start | bytes 1572872 | tf_op jit(solution)/shard_map/ppermute | solution.py:1000
  167.0 28.3 %collective-permute-start.2 = (bf16[4,128,512]{2,1,0:T(8,128)(2,1)}, bf16[4,128,512]{2,1,0:T(8,128)(2,1)}, u32[]{:S(2)}, u32[]{:S(2)}) collective-permute-start(bf16[4,128,512]{2,1,0:T(8,128)(2,1)} %get-tuple-element.138), channel_id=1, source_target_pairs={{0,4},{1,5},{2,6},{3,7},{4,0},{5,1},{6,2},{7,3},{8,12},{9,13},{10,... | collective-permute-start | bytes 1572872 | tf_op jit(solution)/shard_map/ppermute | solution.py:1000
  168.6 26.8 %collective-permute-start.3 = (bf16[4,128,512]{2,1,0:T(8,128)(2,1)}, bf16[4,128,512]{2,1,0:T(8,128)(2,1)}, u32[]{:S(2)}, u32[]{:S(2)}) collective-permute-start(bf16[4,128,512]{2,1,0:T(8,128)(2,1)} %get-tuple-element.139), channel_id=1, source_target_pairs={{0,6},{1,7},{2,4},{3,5},{4,2},{5,3},{6,0},{7,1},{8,14},{9,15},{10,... | collective-permute-start | bytes 1572872 | tf_op jit(solution)/shard_map/ppermute | solution.py:1000
  195.3 12.9 %collective-permute-start.4 = (bf16[16,72,512]{2,1,0:T(8,128)(2,1)}, bf16[16,72,512]{2,1,0:T(8,128)(2,1)S(1)}, u32[]{:S(2)}, u32[]{:S(2)}) collective-permute-start(bf16[16,72,512]{2,1,0:T(8,128)(2,1)} %get-tuple-element.141), channel_id=1, source_target_pairs={{0,1},{1,0},{2,3},{3,2},{4,5},{5,4},{6,7},{7,6},{8,9},{9,8},{10,11... | collective-permute-start | bytes 3538952 | tf_op jit(solution)/shard_map/ppermute | solution.py:1000
  197.1 11.1 %collective-permute-start.7 = (bf16[1,128,512]{2,1,0:T(8,128)(2,1)S(1)}, bf16[1,128,512]{2,1,0:T(8,128)(2,1)S(1)}, u32[]{:S(2)}, u32[]{:S(2)}) collective-permute-start(bf16[1,128,512]{2,1,0:T(8,128)(2,1)S(1)} %get-tuple-element.211), channel_id=1, source_target_pairs={{0,24},{1,25},{2,26},{3,27},{4,28},{5,29},{6,30},{7,31},{8,16},{9,... | collective-permute-start | bytes 393224 | tf_op jit(solution)/shard_map/ppermute | solution.py:1000
  200.5 11.9 %collective-permute-start.6 = (bf16[1,128,512]{2,1,0:T(8,128)(2,1)S(1)}, bf16[1,128,512]{2,1,0:T(8,128)(2,1)S(1)}, u32[]{:S(2)}, u32[]{:S(2)}) collective-permute-start(bf16[1,128,512]{2,1,0:T(8,128)(2,1)S(1)} %get-tuple-element.212), channel_id=1, source_target_pairs={{0,16},{1,17},{2,18},{3,19},{4,20},{5,21},{6,22},{7,23},{8,24},{9,... | collective-permute-start | bytes 393224 | tf_op jit(solution)/shard_map/ppermute | solution.py:1000
  200.5 11.9 %collective-permute-start.5 = (bf16[1,128,512]{2,1,0:T(8,128)(2,1)S(1)}, bf16[1,128,512]{2,1,0:T(8,128)(2,1)S(1)}, u32[]{:S(2)}, u32[]{:S(2)}) collective-permute-start(bf16[1,128,512]{2,1,0:T(8,128)(2,1)S(1)} %get-tuple-element.213), channel_id=1, source_target_pairs={{0,8},{1,9},{2,10},{3,11},{4,12},{5,13},{6,14},{7,15},{8,0},{9,1},... | collective-permute-start | bytes 393224 | tf_op jit(solution)/shard_map/ppermute | solution.py:1000
  214.9 21.0 %collective-permute-start.9 = (bf16[1,128,512]{2,1,0:T(8,128)(2,1)S(1)}, bf16[1,128,512]{2,1,0:T(8,128)(2,1)S(1)}, u32[]{:S(2)}, u32[]{:S(2)}) collective-permute-start(bf16[1,128,512]{2,1,0:T(8,128)(2,1)S(1)} %add_convert_fusion.10), channel_id=1, source_target_pairs={{0,16},{1,17},{2,18},{3,19},{4,20},{5,21},{6,22},{7,23},{8,24},{9,... | collective-permute-start | bytes 393224 | tf_op jit(solution)/shard_map/ppermute | solution.py:1000
  214.9 21.0 %collective-permute-start.8 = (bf16[1,128,512]{2,1,0:T(8,128)(2,1)S(1)}, bf16[1,128,512]{2,1,0:T(8,128)(2,1)}, u32[]{:S(2)}, u32[]{:S(2)}) collective-permute-start(bf16[1,128,512]{2,1,0:T(8,128)(2,1)S(1)} %add_convert_fusion.10), channel_id=1, source_target_pairs={{0,8},{1,9},{2,10},{3,11},{4,12},{5,13},{6,14},{7,15},{8,0},{9,1},... | collective-permute-start | bytes 393224 | tf_op jit(solution)/shard_map/ppermute | solution.py:1000
  217.3 18.6 %collective-permute-start.13 = (bf16[4,72,512]{2,1,0:T(8,128)(2,1)S(1)}, bf16[4,72,512]{2,1,0:T(8,128)(2,1)S(1)}, u32[]{:S(2)}, u32[]{:S(2)}) collective-permute-start(bf16[4,72,512]{2,1,0:T(8,128)(2,1)S(1)} %get-tuple-element.207), channel_id=1, source_target_pairs={{0,6},{1,7},{2,4},{3,5},{4,2},{5,3},{6,0},{7,1},{8,14},{9,15},{10,... | collective-permute-start | bytes 884744 | tf_op jit(solution)/shard_map/ppermute | solution.py:1000
  219.8 16.2 %collective-permute-start.12 = (bf16[4,72,512]{2,1,0:T(8,128)(2,1)S(1)}, bf16[4,72,512]{2,1,0:T(8,128)(2,1)S(1)}, u32[]{:S(2)}, u32[]{:S(2)}) collective-permute-start(bf16[4,72,512]{2,1,0:T(8,128)(2,1)S(1)} %get-tuple-element.208), channel_id=1, source_target_pairs={{0,4},{1,5},{2,6},{3,7},{4,0},{5,1},{6,2},{7,3},{8,12},{9,13},{10,... | collective-permute-start | bytes 884744 | tf_op jit(solution)/shard_map/ppermute | solution.py:1000
  220.9 15.1 %collective-permute-start.11 = (bf16[4,72,512]{2,1,0:T(8,128)(2,1)S(1)}, bf16[4,72,512]{2,1,0:T(8,128)(2,1)S(1)}, u32[]{:S(2)}, u32[]{:S(2)}) collective-permute-start(bf16[4,72,512]{2,1,0:T(8,128)(2,1)S(1)} %get-tuple-element.209), channel_id=1, source_target_pairs={{0,2},{1,3},{2,0},{3,1},{4,6},{5,7},{6,4},{7,5},{8,10},{9,11},{10,... | collective-permute-start | bytes 884744 | tf_op jit(solution)/shard_map/ppermute | solution.py:1000
  238.5 12.5 %collective-permute-start.15 = (bf16[4,128,512]{2,1,0:T(8,128)(2,1)S(1)}, bf16[4,128,512]{2,1,0:T(8,128)(2,1)S(1)}, u32[]{:S(2)}, u32[]{:S(2)}) collective-permute-start(bf16[4,128,512]{2,1,0:T(8,128)(2,1)S(1)} %constant_dynamic-update-slice_fusion), channel_id=1, source_target_pairs={{0,4},{1,5},{2,6},{3,7},{4,0},{5,1},{6,2},{7,3},{8,12},{9,13},{10,... | collective-permute-start | bytes 1572872 | tf_op jit(solution)/shard_map/ppermute | solution.py:1000
  240.0 11.0 %collective-permute-start.14 = (bf16[4,128,512]{2,1,0:T(8,128)(2,1)S(1)}, bf16[4,128,512]{2,1,0:T(8,128)(2,1)S(1)}, u32[]{:S(2)}, u32[]{:S(2)}) collective-permute-start(bf16[4,128,512]{2,1,0:T(8,128)(2,1)S(1)} %constant_dynamic-update-slice_fusion), channel_id=1, source_target_pairs={{0,2},{1,3},{2,0},{3,1},{4,6},{5,7},{6,4},{7,5},{8,10},{9,11},{10,... | collective-permute-start | bytes 1572872 | tf_op jit(solution)/shard_map/ppermute | solution.py:1000
  240.7 10.3 %collective-permute-start.18 = (bf16[1,72,512]{2,1,0:T(8,128)(2,1)S(1)}, bf16[1,72,512]{2,1,0:T(8,128)(2,1)S(1)}, u32[]{:S(2)}, u32[]{:S(2)}) collective-permute-start(bf16[1,72,512]{2,1,0:T(8,128)(2,1)S(1)} %get-tuple-element.215), channel_id=1, source_target_pairs={{0,24},{1,25},{2,26},{3,27},{4,28},{5,29},{6,30},{7,31},{8,16},{9,... | collective-permute-start | bytes 221192 | tf_op jit(solution)/shard_map/ppermute | solution.py:1000
  251.1 9.8 %collective-permute-start.19 = (bf16[12,128,512]{2,1,0:T(8,128)(2,1)S(1)}, bf16[12,128,512]{2,1,0:T(8,128)(2,1)S(1)}, u32[]{:S(2)}, u32[]{:S(2)}) collective-permute-start(bf16[12,128,512]{2,1,0:T(8,128)(2,1)S(1)} %constant_dynamic-update-slice_fusion.4.near_ref), channel_id=1, source_target_pairs={{0,1},{1,0},{2,3},{3,2},{4,5},{5,4},{6,7},{7,6},{8,9},{9,8},{10,11... | collective-permute-start | bytes 4718600 | tf_op jit(solution)/shard_map/ppermute | solution.py:1000
  255.7 16.1 %collective-permute-start.23 = (bf16[4,128,512]{2,1,0:T(8,128)(2,1)S(1)}, bf16[4,128,512]{2,1,0:T(8,128)(2,1)S(1)}, u32[]{:S(2)}, u32[]{:S(2)}) collective-permute-start(bf16[4,128,512]{2,1,0:T(8,128)(2,1)S(1)} %constant_dynamic-update-slice_fusion), channel_id=1, source_target_pairs={{0,6},{1,7},{2,4},{3,5},{4,2},{5,3},{6,0},{7,1},{8,14},{9,15},{10,... | collective-permute-start | bytes 1572872 | tf_op jit(solution)/shard_map/ppermute | solution.py:1000
  261.0 10.8 %collective-permute-start.27 = (bf16[4,72,512]{2,1,0:T(8,128)(2,1)S(1)}, bf16[4,72,512]{2,1,0:T(8,128)(2,1)S(1)}, u32[]{:S(2)}, u32[]{:S(2)}) collective-permute-start(bf16[4,72,512]{2,1,0:T(8,128)(2,1)S(1)} %constant_dynamic-update-slice_fusion.7.refs_0_), channel_id=1, source_target_pairs={{0,1},{1,0},{2,3},{3,2},{4,5},{5,4},{6,7},{7,6},{8,9},{9,8},{10,11... | collective-permute-start | bytes 884744 | tf_op jit(solution)/shard_map/ppermute | solution.py:1000
  261.1 16.7 %collective-permute-start.26 = (bf16[4,72,512]{2,1,0:T(8,128)(2,1)S(1)}, bf16[4,72,512]{2,1,0:T(8,128)(2,1)S(1)}, u32[]{:S(2)}, u32[]{:S(2)}) collective-permute-start(bf16[4,72,512]{2,1,0:T(8,128)(2,1)S(1)} %constant_dynamic-update-slice_fusion.7.refs_0_), channel_id=1, source_target_pairs={{0,6},{1,7},{2,4},{3,5},{4,2},{5,3},{6,0},{7,1},{8,14},{9,15},{10,... | collective-permute-start | bytes 884744 | tf_op jit(solution)/shard_map/ppermute | solution.py:1000
  262.7 20.1 %collective-permute-start.25 = (bf16[4,72,512]{2,1,0:T(8,128)(2,1)S(1)}, bf16[4,72,512]{2,1,0:T(8,128)(2,1)S(1)}, u32[]{:S(2)}, u32[]{:S(2)}) collective-permute-start(bf16[4,72,512]{2,1,0:T(8,128)(2,1)S(1)} %constant_dynamic-update-slice_fusion.7.refs_0_), channel_id=1, source_target_pairs={{0,4},{1,5},{2,6},{3,7},{4,0},{5,1},{6,2},{7,3},{8,12},{9,13},{10,... | collective-permute-start | bytes 884744 | tf_op jit(solution)/shard_map/ppermute | solution.py:1000
  264.1 18.7 %collective-permute-start.24 = (bf16[4,72,512]{2,1,0:T(8,128)(2,1)S(1)}, bf16[4,72,512]{2,1,0:T(8,128)(2,1)S(1)}, u32[]{:S(2)}, u32[]{:S(2)}) collective-permute-start(bf16[4,72,512]{2,1,0:T(8,128)(2,1)S(1)} %constant_dynamic-update-slice_fusion.7.refs_0_), channel_id=1, source_target_pairs={{0,2},{1,3},{2,0},{3,1},{4,6},{5,7},{6,4},{7,5},{8,10},{9,11},{10,... | collective-permute-start | bytes 884744 | tf_op jit(solution)/shard_map/ppermute | solution.py:1000
  (17 other events, 154.6 us)

commit v7 on v6

--- a/solution.py
+++ b/solution.py
@@ -29,6 +29,7 @@
 ATTENTION_FIRST = 3
 ROWS_FIRST = 2
 ONES = 16
+BACK_CHUNK = 1024
 CHUNK = 512
 MIB = 1024 * 1024
 VMEM_LIMIT = 60 * MIB
@@ -442,7 +443,7 @@
     grad_turned = grad_mlp.T
     sums[0:1] += column_sum(grad_mlp.astype(f32))
     grad_norm = jnp.zeros(after_ref.shape, f32)
-    chunks = [slice(at, at + CHUNK) for at in range(0, w_fc1_ref.shape[1], CHUNK)]
+    chunks = [slice(at, at + BACK_CHUNK) for at in range(0, w_fc1_ref.shape[1], BACK_CHUNK)]
     ahead = dot_nt(grad_mlp, w_fc2_ref[chunks[0], :])
     for at, cols in enumerate(chunks):
         grad_hidden = ahead

time: 293 us -> 293 us (level)
  no operation moved by 1% of the time
where the time goes in v7:
time: 293 us; the launch traced here: 290 us
  Pallas kernels  198 us (68%)
  starting transfers between devices  45.5 us (16%)
  waiting for transfers between devices  28.8 us (10%)
  other arithmetic  9.7 us (3%)
  local copies, waits for them, and re-layouts  5.87 us (2%)
    pallas_call x1, Pallas kernels, run_forward(): pl.pallas_call(forward_kernel, grid_spec=pltpu.PrefetchScalarGridSpec(num...  61.4 us
    pallas_call x1, Pallas kernels, run_back_mlp(): pl.pallas_call(back_mlp_kernel, grid_spec=pltpu.PrefetchScalarGridSpec(nu...  54.7 us
    pallas_call x2, Pallas kernels, run_back_attention(): pl.pallas_call(functools.partial(back_attention_kernel, begin, ending is...  40.5 us
    ppermute x32, starting transfers between devices, swap(): return lax.ppermute(rows, ('dp', 'img'), pairs)  34.3 us
    ppermute x32, waiting for transfers between devices, swap(): return lax.ppermute(rows, ('dp', 'img'), pairs)  21.5 us
    pallas_call x2, Pallas kernels, run_back_rows(): pl.pallas_call(functools.partial(back_rows_kernel, begin), grid_spec=pltp...  20.2 us
    all_to_all x2, starting transfers between devices, swap_tiles(): lax.all_to_all(tiles_sent, 'dp', split_axis=0, concat_axis=0, tiled=True)  11.2 us
    all_to_all x2, waiting for transfers between devices, swap_tiles(): lax.all_to_all(tiles_sent, 'dp', split_axis=0, concat_axis=0, tiled=True)  7.33 us
  transfers between devices with their start and end apart: 34, of which 11 were waited for; matrix products, arithmetic and copies ran while one was open for 4% of the time, Pallas kernels for 66%

profile of v7, /device:TPU:0, one launch (start us, length us, event | category | flops | bytes accessed | tf_op | source)
XLA Modules:
  0.0 289.6 jit_solution(8187308309299382922)
XLA Ops:
  2.6 4.4 %deal.1 = bf16[8,400,512]{2,1,0:T(8,128)(2,1)} custom-call(bf16[128,128]{1,0:T(8,128)(2,1)} %get-tuple-element.220.pick_ref, bf16[64,512]{1,0:T(8,128)(2,1)} %bitcast.66, bf16[49,64,512]{2,1,0:T(8,128)(2,1)} %bitcast.63), custom_call_target="tpu_custom_call" | custom-call | flops 4600000000 | bytes 1000000 | tf_op jit(solution)/shard_map/deal/pallas_call | solution.py:1115
  7.0 7.4 %all-to-all-start = ((bf16[8,400,512]{2,1,0:T(8,128)(2,1)}), bf16[8,400,512]{2,1,0:T(8,128)(2,1)}, u32[]{:S(2)}, u32[]{:S(2)}) async-start(bf16[8,400,512]{2,1,0:T(8,128)(2,1)} %deal.1), calls=%async_computation | async-start | bytes 6553600 | tf_op jit(solution)/shard_map/all_to_all | solution.py:1160
  20.0 61.4 %forward.1 = (bf16[8,400,512]{2,1,0:T(8,128)(2,1)}, bf16[64,12,64,128]{3,2,1,0:T(8,128)(2,1)}, bf16[64,8,64,128]{3,2,1,0:T(8,128)(2,1)}, bf16[64,64,512]{2,1,0:T...) custom-call(s32[64]{0:T(128)} %select_reduce_fusion.1.order_ref, ...), custom_call_target="tpu_custom_call" | custom-call | flops 70149996544 | bytes 1000000 | tf_op jit(solution)/shard_map/forward/pallas_call | solution.py:382
  81.4 6.6 %all-to-all-done.cot_ref = bf16[8,400,512]{2,1,0:T(8,128)(2,1)} async-done(((bf16[8,400,512]{2,1,0:T(8,128)(2,1)}), bf16[8,400,512]{2,1,0:T(8,128)(2,1)}, u32[]{:S(2)}, u32[]{:S(2)}) %all-to-all-start) | async-done | bytes 3276832 | tf_op jit(solution)/shard_map/all_to_all | solution.py:1160
  88.0 3.8 %all-to-all-start.1 = ((bf16[8,400,512]{2,1,0:T(8,128)(2,1)}), bf16[8,400,512]{2,1,0:T(8,128)(2,1)S(1)}, u32[]{:S(2)}, u32[]{:S(2)}) async-start(bf16[8,400,512]{2,1,0:T(8,128)(2,1)} %get-tuple-element.124), calls=%async_computation.1 | async-start | bytes 6553600 | tf_op jit(solution)/shard_map/all_to_all | solution.py:1160
  91.9 54.7 %back_mlp.1 = (f32[3584,512]{1,0:T(8,128)}, bf16[64,4,64,128]{3,2,1,0:T(8,128)(2,1)}, bf16[16,128,512]{2,1,0:T(8,128)(2,1)}, bf16[16,128,512]{2,1,0:T(8,128)(2,1...) custom-call(f32[1]{0:T(128)} %bitcast.3.keep_ref, s32[1]{0:T(128)} %bitcast.own_ref, ...), custom_call_target="tpu_custom_call" | custom-call | flops 63250001920 | bytes 1000000 | tf_op jit(solution)/shard_map/back_mlp/pallas_call | solution.py:499
  146.7 14.2 %back_attention.2 = (bf16[4096,1536]{1,0:T(8,128)(2,1)}, f32[528,1536]{1,0:T(8,128)}, f32[64,2048]{1,0:T(8,128)}, f32[64,512]{1,0:T(8,128)}) custom-call(s32[64]{0:T(128)} %select_reduce_fusion.1.order_ref, f32[1]{0:T(128)} %bitcast.3.keep_ref, s32[1]{0:T(128)} %bitcast.own_ref, bf16[64,12,64,128]{3,2,1,0:T(8,128)(2,1)} %get-tuple-element.110.qkv_ref, ...), custom_call_target="tpu_custom_call" | custom-call | flops 17250000896 | bytes 1000000 | tf_op jit(solution)/shard_map/back_attention/pallas_call | solution.py:696
  160.9 3.9 %add_convert_fusion.1 = (bf16[4,128,512]{2,1,0:T(8,128)(2,1)}, bf16[4,128,512]{2,1,0:T(8,128)(2,1)}, bf16[4,128,512]{2,1,0:T(8,128)(2,1)}, bf16[4,128,512]{2,1,0:T(8,128)(2,1)}) fusion(bf16[16,128,512]{2,1,0:T(8,128)(2,1)} %collective-permute-done, bf16[16,128,512]{2,1,0:T(8,128)(2,1)} %get-tuple-element.122), kind=kLoop, calls=%fused_computation.1 | loop fusion | flops 4194304 | bytes 6291456 | tf_op jit(solution)/shard_map/convert_element_type | solution.py:1005
  169.0 26.3 %back_attention.3 = (bf16[4096,1536]{1,0:T(8,128)(2,1)}, bf16[16,72,512]{2,1,0:T(8,128)(2,1)}, bf16[16,72,512]{2,1,0:T(8,128)(2,1)}, bf16[64,512]{1,0:T(8,128)(2,1)}) custom-call(s32[64]{0:T(128)} %select_reduce_fusion.1.order_ref, f32[1]{0:T(128)} %bitcast.3.keep_ref, s32[1]{0:T(128)} %bitcast.own_ref, ...), custom_call_target="tpu_custom_call", output_to_operand_aliasing={{0}: (15, {})} | custom-call | flops 28750000128 | bytes 1000000 | tf_op jit(solution)/shard_map/back_attention/pallas_call | solution.py:696
  197.1 3.3 %collective-permute-start.7 = (bf16[1,128,512]{2,1,0:T(8,128)(2,1)S(1)}, bf16[1,128,512]{2,1,0:T(8,128)(2,1)S(1)}, u32[]{:S(2)}, u32[]{:S(2)}) collective-permute-start(bf16[1,128,512]{2,1,0:T(8,128)(2,1)S(1)} %get-tuple-element.211), channel_id=1, source_target_pairs={{0,24},{1,25},{2,26},{3,27},{4,28},{5,29},{6,30},{7,31},{8,16},{9,... | collective-permute-start | bytes 393224 | tf_op jit(solution)/shard_map/ppermute | solution.py:1001
  201.5 6.6 %back_rows.2.refs_0_ = bf16[64,64,512]{2,1,0:T(8,128)(2,1)} custom-call(s32[64]{0:T(128)} %select_reduce_fusion.1.order_ref, bf16[4096,1536]{1,0:T(8,128)(2,1)} %get-tuple-element.140.grad_qkv_ref, bf16[64,64,512]{2,1,0:T(8,128)(2,1)} %get-tuple-element.112.joined_ref, f32[3584,512]{1,0:T(8,128)} %get-tuple-element.118.grad_after_ref, f32[1,512]{1,0:T(1,128)} %bitcast.59, ...), custom_call_target="tpu_custom_call" | custom-call | flops 5750000128 | bytes 1000000 | tf_op jit(solution)/shard_map/back_rows/pallas_call | solution.py:763
  208.2 4.1 %collective-permute-done.6 = bf16[1,128,512]{2,1,0:T(8,128)(2,1)S(1)} collective-permute-done((bf16[1,128,512]{2,1,0:T(8,128)(2,1)S(1)}, bf16[1,128,512]{2,1,0:T(8,128)(2,1)S(1)}, u32[]{:S(2)}, u32[]{:S(2)}) %collective-permute-start.6) | collective-permute-done | bytes 131104 | tf_op jit(solution)/shard_map/ppermute | solution.py:1001
  212.4 2.4 collective-permute-start.10
  217.2 2.5 collective-permute-start.13
  222.2 13.5 %back_rows.3.windows_ref = bf16[64,64,512]{2,1,0:T(8,128)(2,1)} custom-call(s32[64]{0:T(128)} %select_reduce_fusion.1.order_ref, bf16[4096,1536]{1,0:T(8,128)(2,1)} %get-tuple-element.140.grad_qkv_ref, bf16[64,64,512]{2,1,0:T(8,128)(2,1)} %get-tuple-element.112.joined_ref, ...), custom_call_target="tpu_custom_call", output_to_operand_aliasing={{}: (6, {})} | custom-call | flops 17250000896 | bytes 1000000 | tf_op jit(solution)/shard_map/back_rows/pallas_call | solution.py:763
  240.5 2.4 collective-permute-start.18
  245.0 5.8 %relay.1 = bf16[8,392,512]{2,1,0:T(8,128)(2,1)} custom-call(bf16[392,512]{1,0:T(8,128)(2,1)} %constant.192.clone.gather_ref, bf16[64,64,512]{2,1,0:T(8,128)(2,1)} %back_rows.3.windows_ref), custom_call_target="tpu_custom_call" | custom-call | flops 345000000 | bytes 1000000 | tf_op jit(solution)/shard_map/relay/pallas_call | solution.py:790
  251.1 2.4 collective-permute-start.22
  258.1 2.7 collective-permute-done.21
  264.5 2.8 early_out.1
  267.3 4.4 %collect.1 = (bf16[64,512]{1,0:T(8,128)(2,1)}, bf16[49,64,512]{2,1,0:T(8,128)(2,1)}) custom-call(bf16[128,128]{1,0:T(8,128)(2,1)} %get-tuple-element.219.pick_ref, bf16[8,400,512]{2,1,0:T(8,128)(2,1)} %copy-done), custom_call_target="tpu_custom_call" | custom-call | flops 345000000 | bytes 1000000 | tf_op jit(solution)/shard_map/collect/pallas_call | solution.py:1136
  271.7 6.0 %collective-permute-done.26.refs_3_ = bf16[4,72,512]{2,1,0:T(8,128)(2,1)S(1)} collective-permute-done((bf16[4,72,512]{2,1,0:T(8,128)(2,1)S(1)}, bf16[4,72,512]{2,1,0:T(8,128)(2,1)S(1)}, u32[]{:S(2)}, u32[]{:S(2)}) %collective-permute-start.26) | collective-permute-done | bytes 294944 | tf_op jit(solution)/shard_map/ppermute | solution.py:1001
  277.7 5.0 %collective-permute-done.25.refs_2_ = bf16[4,72,512]{2,1,0:T(8,128)(2,1)S(1)} collective-permute-done((bf16[4,72,512]{2,1,0:T(8,128)(2,1)S(1)}, bf16[4,72,512]{2,1,0:T(8,128)(2,1)S(1)}, u32[]{:S(2)}, u32[]{:S(2)}) %collective-permute-start.25) | collective-permute-done | bytes 294944 | tf_op jit(solution)/shard_map/ppermute | solution.py:1001
  285.9 3.5 %late_out.1 = (f32[512,1536]{1,0:T(8,128)}, f32[512,512]{1,0:T(8,128)}, f32[1,512]{1,0:T(1,128)}, f32[1,512]{1,0:T(1,128)}, f32[1,512]{1,0:T(1,128)}, /*index=5*...) custom-call(s32[1]{0:T(128)} %bitcast.own_ref, ...), custom_call_target="tpu_custom_call", output_to_operand_aliasing={{11}: (11, {}), {12}: (12, {})} | custom-call | flops 3449999872 | bytes 1000000 | tf_op jit(solution)/shard_map/late_out/pallas_call | solution.py:933
  (111 shorter events, 37.3 us)
Async XLA Ops:
  7.0 81.0 %all-to-all-start = ((bf16[8,400,512]{2,1,0:T(8,128)(2,1)}), bf16[8,400,512]{2,1,0:T(8,128)(2,1)}, u32[]{:S(2)}, u32[]{:S(2)}) async-start(bf16[8,400,512]{2,1,0:T(8,128)(2,1)} %deal.1), calls=%async_computation | async-start | bytes 6553600 | tf_op jit(solution)/shard_map/all_to_all | solution.py:1160
  88.0 77.5 %all-to-all-start.1 = ((bf16[8,400,512]{2,1,0:T(8,128)(2,1)}), bf16[8,400,512]{2,1,0:T(8,128)(2,1)S(1)}, u32[]{:S(2)}, u32[]{:S(2)}) async-start(bf16[8,400,512]{2,1,0:T(8,128)(2,1)} %get-tuple-element.124), calls=%async_computation.1 | async-start | bytes 6553600 | tf_op jit(solution)/shard_map/all_to_all | solution.py:1160
  146.6 14.3 %collective-permute-start = (bf16[16,128,512]{2,1,0:T(8,128)(2,1)}, bf16[16,128,512]{2,1,0:T(8,128)(2,1)}, u32[]{:S(2)}, u32[]{:S(2)}) collective-permute-start(bf16[16,128,512]{2,1,0:T(8,128)(2,1)} %get-tuple-element.123), channel_id=1, source_target_pairs={{0,1},{1,0},{2,3},{3,2},{4,5},{5,4},{6,7},{7,6},{8,9},{9,8},{10,11... | collective-permute-start | bytes 6291464 | tf_op jit(solution)/shard_map/ppermute | solution.py:1001
  165.5 29.8 %collective-permute-start.1 = (bf16[4,128,512]{2,1,0:T(8,128)(2,1)}, bf16[4,128,512]{2,1,0:T(8,128)(2,1)}, u32[]{:S(2)}, u32[]{:S(2)}) collective-permute-start(bf16[4,128,512]{2,1,0:T(8,128)(2,1)} %get-tuple-element.137), channel_id=1, source_target_pairs={{0,2},{1,3},{2,0},{3,1},{4,6},{5,7},{6,4},{7,5},{8,10},{9,11},{10,... | collective-permute-start | bytes 1572872 | tf_op jit(solution)/shard_map/ppermute | solution.py:1001
  167.0 28.3 %collective-permute-start.2 = (bf16[4,128,512]{2,1,0:T(8,128)(2,1)}, bf16[4,128,512]{2,1,0:T(8,128)(2,1)}, u32[]{:S(2)}, u32[]{:S(2)}) collective-permute-start(bf16[4,128,512]{2,1,0:T(8,128)(2,1)} %get-tuple-element.138), channel_id=1, source_target_pairs={{0,4},{1,5},{2,6},{3,7},{4,0},{5,1},{6,2},{7,3},{8,12},{9,13},{10,... | collective-permute-start | bytes 1572872 | tf_op jit(solution)/shard_map/ppermute | solution.py:1001
  168.5 26.9 %collective-permute-start.3 = (bf16[4,128,512]{2,1,0:T(8,128)(2,1)}, bf16[4,128,512]{2,1,0:T(8,128)(2,1)}, u32[]{:S(2)}, u32[]{:S(2)}) collective-permute-start(bf16[4,128,512]{2,1,0:T(8,128)(2,1)} %get-tuple-element.139), channel_id=1, source_target_pairs={{0,6},{1,7},{2,4},{3,5},{4,2},{5,3},{6,0},{7,1},{8,14},{9,15},{10,... | collective-permute-start | bytes 1572872 | tf_op jit(solution)/shard_map/ppermute | solution.py:1001
  195.3 12.9 %collective-permute-start.4 = (bf16[16,72,512]{2,1,0:T(8,128)(2,1)}, bf16[16,72,512]{2,1,0:T(8,128)(2,1)S(1)}, u32[]{:S(2)}, u32[]{:S(2)}) collective-permute-start(bf16[16,72,512]{2,1,0:T(8,128)(2,1)} %get-tuple-element.141), channel_id=1, source_target_pairs={{0,1},{1,0},{2,3},{3,2},{4,5},{5,4},{6,7},{7,6},{8,9},{9,8},{10,11... | collective-permute-start | bytes 3538952 | tf_op jit(solution)/shard_map/ppermute | solution.py:1001
  197.1 11.1 %collective-permute-start.7 = (bf16[1,128,512]{2,1,0:T(8,128)(2,1)S(1)}, bf16[1,128,512]{2,1,0:T(8,128)(2,1)S(1)}, u32[]{:S(2)}, u32[]{:S(2)}) collective-permute-start(bf16[1,128,512]{2,1,0:T(8,128)(2,1)S(1)} %get-tuple-element.211), channel_id=1, source_target_pairs={{0,24},{1,25},{2,26},{3,27},{4,28},{5,29},{6,30},{7,31},{8,16},{9,... | collective-permute-start | bytes 393224 | tf_op jit(solution)/shard_map/ppermute | solution.py:1001
  200.4 11.9 %collective-permute-start.6 = (bf16[1,128,512]{2,1,0:T(8,128)(2,1)S(1)}, bf16[1,128,512]{2,1,0:T(8,128)(2,1)S(1)}, u32[]{:S(2)}, u32[]{:S(2)}) collective-permute-start(bf16[1,128,512]{2,1,0:T(8,128)(2,1)S(1)} %get-tuple-element.212), channel_id=1, source_target_pairs={{0,16},{1,17},{2,18},{3,19},{4,20},{5,21},{6,22},{7,23},{8,24},{9,... | collective-permute-start | bytes 393224 | tf_op jit(solution)/shard_map/ppermute | solution.py:1001
  200.4 11.9 %collective-permute-start.5 = (bf16[1,128,512]{2,1,0:T(8,128)(2,1)S(1)}, bf16[1,128,512]{2,1,0:T(8,128)(2,1)S(1)}, u32[]{:S(2)}, u32[]{:S(2)}) collective-permute-start(bf16[1,128,512]{2,1,0:T(8,128)(2,1)S(1)} %get-tuple-element.213), channel_id=1, source_target_pairs={{0,8},{1,9},{2,10},{3,11},{4,12},{5,13},{6,14},{7,15},{8,0},{9,1},... | collective-permute-start | bytes 393224 | tf_op jit(solution)/shard_map/ppermute | solution.py:1001
  214.8 21.0 %collective-permute-start.9 = (bf16[1,128,512]{2,1,0:T(8,128)(2,1)S(1)}, bf16[1,128,512]{2,1,0:T(8,128)(2,1)S(1)}, u32[]{:S(2)}, u32[]{:S(2)}) collective-permute-start(bf16[1,128,512]{2,1,0:T(8,128)(2,1)S(1)} %add_convert_fusion.10), channel_id=1, source_target_pairs={{0,16},{1,17},{2,18},{3,19},{4,20},{5,21},{6,22},{7,23},{8,24},{9,... | collective-permute-start | bytes 393224 | tf_op jit(solution)/shard_map/ppermute | solution.py:1001
  214.8 21.0 %collective-permute-start.8 = (bf16[1,128,512]{2,1,0:T(8,128)(2,1)S(1)}, bf16[1,128,512]{2,1,0:T(8,128)(2,1)}, u32[]{:S(2)}, u32[]{:S(2)}) collective-permute-start(bf16[1,128,512]{2,1,0:T(8,128)(2,1)S(1)} %add_convert_fusion.10), channel_id=1, source_target_pairs={{0,8},{1,9},{2,10},{3,11},{4,12},{5,13},{6,14},{7,15},{8,0},{9,1},... | collective-permute-start | bytes 393224 | tf_op jit(solution)/shard_map/ppermute | solution.py:1001
  217.2 18.6 %collective-permute-start.13 = (bf16[4,72,512]{2,1,0:T(8,128)(2,1)S(1)}, bf16[4,72,512]{2,1,0:T(8,128)(2,1)S(1)}, u32[]{:S(2)}, u32[]{:S(2)}) collective-permute-start(bf16[4,72,512]{2,1,0:T(8,128)(2,1)S(1)} %get-tuple-element.207), channel_id=1, source_target_pairs={{0,6},{1,7},{2,4},{3,5},{4,2},{5,3},{6,0},{7,1},{8,14},{9,15},{10,... | collective-permute-start | bytes 884744 | tf_op jit(solution)/shard_map/ppermute | solution.py:1001
  219.7 16.1 %collective-permute-start.12 = (bf16[4,72,512]{2,1,0:T(8,128)(2,1)S(1)}, bf16[4,72,512]{2,1,0:T(8,128)(2,1)S(1)}, u32[]{:S(2)}, u32[]{:S(2)}) collective-permute-start(bf16[4,72,512]{2,1,0:T(8,128)(2,1)S(1)} %get-tuple-element.208), channel_id=1, source_target_pairs={{0,4},{1,5},{2,6},{3,7},{4,0},{5,1},{6,2},{7,3},{8,12},{9,13},{10,... | collective-permute-start | bytes 884744 | tf_op jit(solution)/shard_map/ppermute | solution.py:1001
  220.7 15.1 %collective-permute-start.11 = (bf16[4,72,512]{2,1,0:T(8,128)(2,1)S(1)}, bf16[4,72,512]{2,1,0:T(8,128)(2,1)S(1)}, u32[]{:S(2)}, u32[]{:S(2)}) collective-permute-start(bf16[4,72,512]{2,1,0:T(8,128)(2,1)S(1)} %get-tuple-element.209), channel_id=1, source_target_pairs={{0,2},{1,3},{2,0},{3,1},{4,6},{5,7},{6,4},{7,5},{8,10},{9,11},{10,... | collective-permute-start | bytes 884744 | tf_op jit(solution)/shard_map/ppermute | solution.py:1001
  238.3 12.5 %collective-permute-start.15 = (bf16[4,128,512]{2,1,0:T(8,128)(2,1)S(1)}, bf16[4,128,512]{2,1,0:T(8,128)(2,1)S(1)}, u32[]{:S(2)}, u32[]{:S(2)}) collective-permute-start(bf16[4,128,512]{2,1,0:T(8,128)(2,1)S(1)} %constant_dynamic-update-slice_fusion), channel_id=1, source_target_pairs={{0,4},{1,5},{2,6},{3,7},{4,0},{5,1},{6,2},{7,3},{8,12},{9,13},{10,... | collective-permute-start | bytes 1572872 | tf_op jit(solution)/shard_map/ppermute | solution.py:1001
  239.8 11.0 %collective-permute-start.14 = (bf16[4,128,512]{2,1,0:T(8,128)(2,1)S(1)}, bf16[4,128,512]{2,1,0:T(8,128)(2,1)S(1)}, u32[]{:S(2)}, u32[]{:S(2)}) collective-permute-start(bf16[4,128,512]{2,1,0:T(8,128)(2,1)S(1)} %constant_dynamic-update-slice_fusion), channel_id=1, source_target_pairs={{0,2},{1,3},{2,0},{3,1},{4,6},{5,7},{6,4},{7,5},{8,10},{9,11},{10,... | collective-permute-start | bytes 1572872 | tf_op jit(solution)/shard_map/ppermute | solution.py:1001
  240.5 10.3 %collective-permute-start.18 = (bf16[1,72,512]{2,1,0:T(8,128)(2,1)S(1)}, bf16[1,72,512]{2,1,0:T(8,128)(2,1)S(1)}, u32[]{:S(2)}, u32[]{:S(2)}) collective-permute-start(bf16[1,72,512]{2,1,0:T(8,128)(2,1)S(1)} %get-tuple-element.215), channel_id=1, source_target_pairs={{0,24},{1,25},{2,26},{3,27},{4,28},{5,29},{6,30},{7,31},{8,16},{9,... | collective-permute-start | bytes 221192 | tf_op jit(solution)/shard_map/ppermute | solution.py:1001
  251.0 9.8 %collective-permute-start.19 = (bf16[12,128,512]{2,1,0:T(8,128)(2,1)S(1)}, bf16[12,128,512]{2,1,0:T(8,128)(2,1)S(1)}, u32[]{:S(2)}, u32[]{:S(2)}) collective-permute-start(bf16[12,128,512]{2,1,0:T(8,128)(2,1)S(1)} %constant_dynamic-update-slice_fusion.4.near_ref), channel_id=1, source_target_pairs={{0,1},{1,0},{2,3},{3,2},{4,5},{5,4},{6,7},{7,6},{8,9},{9,8},{10,11... | collective-permute-start | bytes 4718600 | tf_op jit(solution)/shard_map/ppermute | solution.py:1001
  255.6 16.1 %collective-permute-start.23 = (bf16[4,128,512]{2,1,0:T(8,128)(2,1)S(1)}, bf16[4,128,512]{2,1,0:T(8,128)(2,1)S(1)}, u32[]{:S(2)}, u32[]{:S(2)}) collective-permute-start(bf16[4,128,512]{2,1,0:T(8,128)(2,1)S(1)} %constant_dynamic-update-slice_fusion), channel_id=1, source_target_pairs={{0,6},{1,7},{2,4},{3,5},{4,2},{5,3},{6,0},{7,1},{8,14},{9,15},{10,... | collective-permute-start | bytes 1572872 | tf_op jit(solution)/shard_map/ppermute | solution.py:1001
  260.9 10.8 %collective-permute-start.27 = (bf16[4,72,512]{2,1,0:T(8,128)(2,1)S(1)}, bf16[4,72,512]{2,1,0:T(8,128)(2,1)S(1)}, u32[]{:S(2)}, u32[]{:S(2)}) collective-permute-start(bf16[4,72,512]{2,1,0:T(8,128)(2,1)S(1)} %constant_dynamic-update-slice_fusion.7.refs_0_), channel_id=1, source_target_pairs={{0,1},{1,0},{2,3},{3,2},{4,5},{5,4},{6,7},{7,6},{8,9},{9,8},{10,11... | collective-permute-start | bytes 884744 | tf_op jit(solution)/shard_map/ppermute | solution.py:1001
  261.0 16.7 %collective-permute-start.26 = (bf16[4,72,512]{2,1,0:T(8,128)(2,1)S(1)}, bf16[4,72,512]{2,1,0:T(8,128)(2,1)S(1)}, u32[]{:S(2)}, u32[]{:S(2)}) collective-permute-start(bf16[4,72,512]{2,1,0:T(8,128)(2,1)S(1)} %constant_dynamic-update-slice_fusion.7.refs_0_), channel_id=1, source_target_pairs={{0,6},{1,7},{2,4},{3,5},{4,2},{5,3},{6,0},{7,1},{8,14},{9,15},{10,... | collective-permute-start | bytes 884744 | tf_op jit(solution)/shard_map/ppermute | solution.py:1001
  262.5 20.2 %collective-permute-start.25 = (bf16[4,72,512]{2,1,0:T(8,128)(2,1)S(1)}, bf16[4,72,512]{2,1,0:T(8,128)(2,1)S(1)}, u32[]{:S(2)}, u32[]{:S(2)}) collective-permute-start(bf16[4,72,512]{2,1,0:T(8,128)(2,1)S(1)} %constant_dynamic-update-slice_fusion.7.refs_0_), channel_id=1, source_target_pairs={{0,4},{1,5},{2,6},{3,7},{4,0},{5,1},{6,2},{7,3},{8,12},{9,13},{10,... | collective-permute-start | bytes 884744 | tf_op jit(solution)/shard_map/ppermute | solution.py:1001
  264.0 18.7 %collective-permute-start.24 = (bf16[4,72,512]{2,1,0:T(8,128)(2,1)S(1)}, bf16[4,72,512]{2,1,0:T(8,128)(2,1)S(1)}, u32[]{:S(2)}, u32[]{:S(2)}) collective-permute-start(bf16[4,72,512]{2,1,0:T(8,128)(2,1)S(1)} %constant_dynamic-update-slice_fusion.7.refs_0_), channel_id=1, source_target_pairs={{0,2},{1,3},{2,0},{3,1},{4,6},{5,7},{6,4},{7,5},{8,10},{9,11},{10,... | collective-permute-start | bytes 884744 | tf_op jit(solution)/shard_map/ppermute | solution.py:1001
  (17 other events, 154.6 us)
